TPU v7x, 32 devices: a whole 2x2x4 slice. The times are simulated.
32 devices in a mesh: doc: 4 (over y, core), seq: 8 (over z, x).
Axes of the slice: x: 2, y: 2, z: 4, core: 2. Of those that a mesh axis runs over, the one named last changes fastest.
Arguments:
- queries: bfloat16 [4096, 512], P(('doc', 'seq')), parts along dimension 0, may hold values from -26 to 26
- key_vectors: bfloat16 [4096, 512], P(('doc', 'seq')), parts along dimension 0, may hold values from -26 to 26
- value_vectors: bfloat16 [4096, 512], P(('doc', 'seq')), parts along dimension 0, may hold values from -6 to 6
- output_grad: bfloat16 [4096, 512], P(('doc', 'seq')), parts along dimension 0, may hold values from -6 to 6
- rand_pick: int32 [64, 3], P('doc'), parts along dimension 0, may hold values from 0 to 1
- global_ids: int32 [8], P('doc'), parts along dimension 0, may hold values from 0 to 15
Outputs:
- grad_queries: bfloat16 [4096, 512], P(('doc', 'seq')), parts along dimension 0
- grad_keys: bfloat16 [4096, 512], P(('doc', 'seq')), parts along dimension 0
- grad_values: bfloat16 [4096, 512], P(('doc', 'seq')), parts along dimension 0
There are 4 independent parts, one for each index of `doc`. A program takes and returns all parts, laid end to end along the dimension named above; each array names one. Nothing has to cross between parts.
All inputs are finite; a program needn't handle non-finite values.
Results may differ from a plain program's by a relative error of at most 0.012.
Values may be sent and summed in bfloat16 or wider, within the bound.
No kernel may reach another device: no remote copies, remote signals or barrier semaphores. Data moves between devices by JAX's collectives and lax.ppermute only.
A program may use at most 64 MiB of HBM per device.

v0:
```python
import math

import jax
import jax.numpy as jnp
from jax import lax
from jax.sharding import PartitionSpec as P

HEADS = 8
BLOCK = 64
RAND = 3
GLOBAL = 2


def extended_2(block, sides, width):
    for axis, dim in sides:
        count = lax.axis_size(axis)
        forward = [(i, i + 1) for i in range(count - 1)]
        backward = [(target, source) for source, target in forward]
        low = lax.ppermute(
            lax.slice_in_dim(block, block.shape[dim] - width, None, axis=dim), axis, forward
        )
        high = lax.ppermute(lax.slice_in_dim(block, 0, width, axis=dim), axis, backward)
        block = jnp.concatenate([low, block, high], axis=dim)
    return block


def shifted(block, axis, distance):
    devices = range(lax.axis_size(axis))
    route = [((i - distance) % len(devices), i) for i in devices]
    return lax.ppermute(block, axis, route)


def broadcast(block, axis, holder):
    block = jnp.where(lax.axis_index(axis) == holder, block, jnp.zeros_like(block))
    return lax.psum(block, axis)


def key_grads(probs_half, grad_half, query_block, grad_block, scale):
    width = query_block.shape[-1]
    head_size = width // HEADS
    query_heads = query_block.reshape(-1, HEADS, head_size)
    grad_heads = grad_block.reshape(-1, HEADS, head_size)
    grad_key = (
        jnp.einsum("hqk,qhe->khe", grad_half, query_heads, preferred_element_type=jnp.float32)
        * scale
    )
    grad_value = jnp.einsum(
        "hqk,qhe->khe", probs_half, grad_heads, preferred_element_type=jnp.float32
    )
    count = grad_key.shape[0]
    return jnp.concatenate(
        [grad_key.reshape(count, width), grad_value.reshape(count, width)], axis=1
    )


def attend(query_block, grad_block, listed, valid, scale):
    width = query_block.shape[-1]
    head_size = width // HEADS
    query_heads = query_block.reshape(-1, HEADS, head_size)
    grad_heads = grad_block.reshape(-1, HEADS, head_size)
    key_heads = listed[:, :width].reshape(-1, HEADS, head_size)
    value_heads = listed[:, width:].reshape(-1, HEADS, head_size)
    scores = (
        jnp.einsum("qhe,khe->hqk", query_heads, key_heads, preferred_element_type=jnp.float32)
        * scale
    )
    scores = jnp.where(valid[None, None, :], scores, -1e30)
    row_max = jnp.max(scores, axis=-1, keepdims=True)
    expo = jnp.exp(scores - row_max)
    row_total = jnp.sum(expo, axis=-1, keepdims=True)
    probs = expo / row_total
    probs_half = probs.astype(jnp.bfloat16)
    attended = jnp.einsum(
        "hqk,khe->qhe", probs_half, value_heads, preferred_element_type=jnp.float32
    )
    row_dot = jnp.sum(grad_heads.astype(jnp.float32) * attended, axis=-1).T
    grad_probs = jnp.einsum(
        "qhe,khe->hqk", grad_heads, value_heads, preferred_element_type=jnp.float32
    )
    grad_scores = probs * (grad_probs - row_dot[:, :, None])
    grad_half = grad_scores.astype(jnp.bfloat16)
    grad_query = (
        jnp.einsum("hqk,khe->qhe", grad_half, key_heads, preferred_element_type=jnp.float32) * scale
    )
    return (probs_half, grad_half, grad_query.reshape(-1, width), row_max, row_total, row_dot)


def on_device(queries, key_vectors, value_vectors, output_grad, rand_pick, global_ids):
    group = lax.axis_size("seq")
    position = lax.axis_index("seq")
    rows, width = queries.shape
    local_blocks = rows // BLOCK
    head_size = width // HEADS
    scale = 1.0 / math.sqrt(head_size)
    all_blocks = local_blocks * group
    near = (3 + GLOBAL) * BLOCK
    pairs = jnp.concatenate([key_vectors, value_vectors], axis=1)
    padded = extended_2(pairs, (("seq", 0),), BLOCK)
    extended = padded.reshape(local_blocks + 2, BLOCK, 2 * width)
    own_pairs = extended[1:-1]
    block_range = jnp.arange(local_blocks, dtype=jnp.int32)
    routes = []
    fetched = []
    for slot_idx in range(RAND):
        distance = (slot_idx + 1) * group // 4
        arrived = None
        for lag in range(2):
            target = (position + distance + lag) % group
            picks = lax.dynamic_slice_in_dim(rand_pick, target * local_blocks, local_blocks, 0)[
                :, slot_idx
            ]
            behind = block_range - picks
            if lag == 0:
                inside = behind >= 0
                local_index = jnp.clip(behind, 0, local_blocks - 1)
            else:
                inside = behind < 0
                local_index = jnp.clip(behind + local_blocks, 0, local_blocks - 1)
            routes.append((slot_idx, distance + lag, inside, local_index))
            outgoing = jnp.where(
                inside[:, None, None],
                jnp.take(own_pairs, local_index, axis=0),
                jnp.zeros((), own_pairs.dtype),
            )
            moved = shifted(outgoing, "seq", distance + lag)
            arrived = moved if arrived is None else arrived + moved
        fetched.append(arrived)
    random_pairs = jnp.stack(fetched, axis=1).reshape(local_blocks, RAND * BLOCK, 2 * width)
    roots = global_ids // local_blocks
    offsets = global_ids % local_blocks
    global_list = []
    for slot_idx in range(GLOBAL):
        picked = lax.dynamic_index_in_dim(own_pairs, offsets[slot_idx], 0, keepdims=False)
        global_list.append(broadcast(picked, "seq", roots[slot_idx]))
    global_pairs = jnp.concatenate(global_list, axis=0)
    segment = jnp.arange((3 + GLOBAL + RAND) * BLOCK) // BLOCK
    query_blocks = queries.reshape(local_blocks, BLOCK, width)
    grad_blocks = output_grad.reshape(local_blocks, BLOCK, width)

    def visit(global_acc, inputs):
        query_block, grad_block, remote_keys, block_idx = inputs
        window = lax.dynamic_slice_in_dim(extended, block_idx, 3, 0).reshape(3 * BLOCK, 2 * width)
        listed = jnp.concatenate([window, global_pairs, remote_keys], axis=0)
        overall = position * local_blocks + block_idx
        valid = ((segment != 0) | (overall > 0)) & ((segment != 2) | (overall < all_blocks - 1))
        probs_half, grad_half, grad_query, row_max, row_total, row_dot = attend(
            query_block, grad_block, listed, valid, scale
        )
        grads = key_grads(probs_half, grad_half, query_block, grad_block, scale)
        extra = grads[near:].reshape(RAND, BLOCK, 2 * width)
        window_part = grads[: 3 * BLOCK].reshape(3, BLOCK, 2 * width)
        global_acc = global_acc + grads[3 * BLOCK : near].reshape(GLOBAL, BLOCK, 2 * width)
        return (global_acc, (grad_query.astype(jnp.bfloat16), window_part, extra))

    start = jnp.zeros((GLOBAL, BLOCK, 2 * width), jnp.float32)
    steps_in = (query_blocks, grad_blocks, random_pairs, block_range)
    global_acc, (grad_query, window_parts, extra) = lax.scan(visit, start, steps_in)
    window_acc = jnp.pad(window_parts[:, 0], ((0, 2), (0, 0), (0, 0)))
    window_acc = window_acc + jnp.pad(window_parts[:, 1], ((1, 1), (0, 0), (0, 0)))
    window_acc = window_acc + jnp.pad(window_parts[:, 2], ((2, 0), (0, 0), (0, 0)))
    rims = jnp.concatenate([window_acc[0], window_acc[-1]], axis=0)
    returned = extended_2(rims, (("seq", 0),), BLOCK)
    totals = window_acc[1:-1]
    totals = totals.at[0].add(returned[:BLOCK]).at[-1].add(returned[-BLOCK:])
    for slot_idx, reach, inside, local_index in routes:
        back = shifted(extra[:, slot_idx], "seq", -reach)
        back = jnp.where(inside[:, None, None], back, 0.0)
        onehot = ((local_index[:, None] == block_range[None, :]) & inside[:, None]).astype(
            jnp.float32
        )
        totals = totals + jnp.einsum("jo,jbf->obf", onehot, back, precision=lax.Precision.HIGHEST)
    global_total = lax.psum(global_acc, "seq")
    owners = ((offsets[:, None] == block_range[None, :]) & (roots[:, None] == position)).astype(
        jnp.float32
    )
    totals = totals + jnp.einsum(
        "go,gbf->obf", owners, global_total, precision=lax.Precision.HIGHEST
    )
    flat = totals.reshape(rows, 2 * width)
    return (
        grad_query.reshape(rows, width),
        flat[:, :width].astype(jnp.bfloat16),
        flat[:, width:].astype(jnp.bfloat16),
    )


def solution(mesh):
    return jax.shard_map(
        on_device,
        mesh=mesh,
        in_specs=(
            P(("doc", "seq"), None),
            P(("doc", "seq"), None),
            P(("doc", "seq"), None),
            P(("doc", "seq"), None),
            P("doc", None),
            P("doc"),
        ),
        out_specs=(P(("doc", "seq"), None), P(("doc", "seq"), None), P(("doc", "seq"), None)),
        check_vma=False,
    )
```

profile of v0, /device:TPU:0, one launch (start us, length us, event | category | flops | bytes accessed | tf_op | source)
XLA Modules:
  0.0 315.8 jit_solution(8659020763328884440)
XLA Ops:
  9.1 4.8 %collective-permute-start = (bf16[64,1024]{1,0:T(8,128)(2,1)S(1)}, bf16[64,1024]{1,0:T(8,128)(2,1)S(1)}, u32[]{:S(2)}, u32[]{:S(2)}) collective-permute-start(bf16[64,1024]{1,0:T(8,128)(2,1)S(1)} %get-tuple-element.336), channel_id=1, source_target_pairs={{0,1},{1,2},{2,3},{3,4},{4,5},{5,6},{6,7},{8,9},{9,10},{10,11},{11... | collective-permute-start | bytes 393224 | tf_op jit(solution)/shard_map/ppermute | solution.py:19
  17.0 3.7 %collective-permute-start.2 = (bf16[2,64,1024]{2,1,0:T(8,128)(2,1)S(1)}, bf16[2,64,1024]{2,1,0:T(8,128)(2,1)S(1)}, u32[]{:S(2)}, u32[]{:S(2)}) collective-permute-start(bf16[2,64,1024]{2,1,0:T(8,128)(2,1)S(1)} %select_select_fusion.5), channel_id=1, source_target_pairs={{6,0},{7,1},{0,2},{1,3},{2,4},{3,5},{4,6},{5,7},{14,8},{15,9},{8,1... | collective-permute-start | bytes 786440 | tf_op jit(solution)/shard_map/ppermute | solution.py:30
  21.4 1.7 collective-permute-start.3
  38.8 3.6 %collective-permute-start.5 = (bf16[2,64,1024]{2,1,0:T(8,128)(2,1)S(1)}, bf16[2,64,1024]{2,1,0:T(8,128)(2,1)S(1)}, u32[]{:S(2)}, u32[]{:S(2)}) collective-permute-start(bf16[2,64,1024]{2,1,0:T(8,128)(2,1)S(1)} %select_select_fusion.2), channel_id=1, source_target_pairs={{3,0},{4,1},{5,2},{6,3},{7,4},{0,5},{1,6},{2,7},{11,8},{12,9},{13,... | collective-permute-start | bytes 786440 | tf_op jit(solution)/shard_map/ppermute | solution.py:30
  44.3 3.1 collective-permute-done.3
  47.5 7.3 %collective-permute-done.4 = bf16[2,64,1024]{2,1,0:T(8,128)(2,1)S(1)} collective-permute-done((bf16[2,64,1024]{2,1,0:T(8,128)(2,1)S(1)}, bf16[2,64,1024]{2,1,0:T(8,128)(2,1)S(1)}, u32[]{:S(2)}, u32[]{:S(2)}) %collective-permute-start.4) | collective-permute-done | bytes 262176 | tf_op jit(solution)/shard_map/ppermute | solution.py:30
  54.8 5.0 %collective-permute-done.5 = bf16[2,64,1024]{2,1,0:T(8,128)(2,1)S(1)} collective-permute-done((bf16[2,64,1024]{2,1,0:T(8,128)(2,1)S(1)}, bf16[2,64,1024]{2,1,0:T(8,128)(2,1)S(1)}, u32[]{:S(2)}, u32[]{:S(2)}) %collective-permute-start.5) | collective-permute-done | bytes 262176 | tf_op jit(solution)/shard_map/ppermute | solution.py:30
  59.9 3.2 %collective-permute-done.6 = bf16[2,64,1024]{2,1,0:T(8,128)(2,1)S(1)} collective-permute-done((bf16[2,64,1024]{2,1,0:T(8,128)(2,1)S(1)}, bf16[2,64,1024]{2,1,0:T(8,128)(2,1)S(1)}, u32[]{:S(2)}, u32[]{:S(2)}) %collective-permute-start.6) | collective-permute-done | bytes 262176 | tf_op jit(solution)/shard_map/ppermute | solution.py:30
  63.2 60.9 %all-reduce.9.cloned.1.call-done = (bf16[64,1024]{1,0:T(8,128)(2,1)}, bf16[64,1024]{1,0:T(8,128)(2,1)}) async-done(((bf16[64,1024]{1,0:T(8,128)(2,1)}, bf16[64,1024]{1,0:T(8,128)(2,1)}), (bf16[64,1024]{1,0:T(8,128)(2,1)}, bf16[64,1024]{1,0:T(8,128)(2,1)})) %all-reduce.9.cloned.1.call-update) | async-done | bytes 262160 | tf_op jit(solution)/shard_map/psum | solution.py:35
  124.2 32.2 %while.22 = (s32[]{:T(128)}, f32[2,64,1024]{2,1,0:T(8,128)}, bf16[2,64,512]{2,1,0:T(8,128)(2,1)}, f32[2,3,64,1024]{3,2,0,1:T(8,128)}, f32[2,3,64,1024]{3,2,0,1:T...) while((s32[]{:T(128)}, f32[2,64,1024]{2,1,0:T(8,128)}, ...), condition=%wide.region_6.8_spmd.clone.clone, body=%wide.region_2.7_spmd.clone.clone.sunk | while | flops 209885696 | bytes 83506968 | solution.py:157
  131.6 1.7 fusion.147
  147.7 1.7 fusion.147
  156.3 1.5 slice_bitcast_fusion.5
  158.8 2.8 collective-permute-start.8
  162.8 3.1 collective-permute-start.11
  167.8 3.1 collective-permute-start.10
  173.3 12.1 %collective-permute-start.12 = (f32[2,64,1024]{2,1,0:T(8,128)}, f32[2,64,1024]{2,1,0:T(8,128)}, u32[]{:S(2)}, u32[]{:S(2)}) collective-permute-start(f32[2,64,1024]{2,1,0:T(8,128)} %get-tuple-element.328), channel_id=1, source_target_pairs={{4,0},{5,1},{6,2},{7,3},{0,4},{1,5},{2,6},{3,7},{12,8},{13,9},{14,... | collective-permute-start | bytes 1572872 | tf_op jit(solution)/shard_map/ppermute | solution.py:30
  185.4 3.2 %collective-permute-start.15 = (f32[2,64,1024]{2,1,0:T(8,128)}, f32[2,64,1024]{2,1,0:T(8,128)S(1)}, u32[]{:S(2)}, u32[]{:S(2)}) collective-permute-start(f32[2,64,1024]{2,1,0:T(8,128)} %get-tuple-element.329), channel_id=1, source_target_pairs={{7,0},{0,1},{1,2},{2,3},{3,4},{4,5},{5,6},{6,7},{15,8},{8,9},{9,10... | collective-permute-start | bytes 1572872 | tf_op jit(solution)/shard_map/ppermute | solution.py:30
  189.4 1.9 scatter-add.9
  191.3 47.6 %collective-permute-start.14 = (f32[2,64,1024]{2,1,0:T(8,128)}, f32[2,64,1024]{2,1,0:T(8,128)S(1)}, u32[]{:S(2)}, u32[]{:S(2)}) collective-permute-start(f32[2,64,1024]{2,1,0:T(8,128)} %get-tuple-element.329), channel_id=1, source_target_pairs={{6,0},{7,1},{0,2},{1,3},{2,4},{3,5},{4,6},{5,7},{14,8},{15,9},{8,1... | collective-permute-start | bytes 1572872 | tf_op jit(solution)/shard_map/ppermute | solution.py:30
  240.0 17.2 %collective-permute-done.13 = f32[2,64,1024]{2,1,0:T(8,128)} collective-permute-done((f32[2,64,1024]{2,1,0:T(8,128)}, f32[2,64,1024]{2,1,0:T(8,128)}, u32[]{:S(2)}, u32[]{:S(2)}) %collective-permute-start.13) | collective-permute-done | bytes 524320 | tf_op jit(solution)/shard_map/ppermute | solution.py:30
  266.5 36.6 %all-reduce.7.cloned.1.call-done = f32[2,64,1024]{2,0,1:T(2,128)} async-done(((f32[2,64,1024]{2,0,1:T(2,128)}), f32[2,64,1024]{2,0,1:T(2,128)}) %all-reduce.7.cloned.1.call-update) | async-done | bytes 524304 | tf_op jit(solution)/shard_map/psum | solution.py:172
  303.1 2.1 fusion.45
  305.2 3.0 fusion.32
  (255 shorter events, 59.4 us)
Async XLA Ops:
  7.2 117.0 %all-reduce.9.cloned.1.call-start = ((), (), s32[]{:S(2)}) async-start(), calls=%async_computation.1 | async-start | bytes 524288 | tf_op jit(solution)/shard_map/psum | solution.py:35
  9.1 29.8 %collective-permute-start = (bf16[64,1024]{1,0:T(8,128)(2,1)S(1)}, bf16[64,1024]{1,0:T(8,128)(2,1)S(1)}, u32[]{:S(2)}, u32[]{:S(2)}) collective-permute-start(bf16[64,1024]{1,0:T(8,128)(2,1)S(1)} %get-tuple-element.336), channel_id=1, source_target_pairs={{0,1},{1,2},{2,3},{3,4},{4,5},{5,6},{6,7},{8,9},{9,10},{10,11},{11... | collective-permute-start | bytes 393224 | tf_op jit(solution)/shard_map/ppermute | solution.py:19
  13.9 28.5 %collective-permute-start.1 = (bf16[64,1024]{1,0:T(8,128)(2,1)S(1)}, bf16[64,1024]{1,0:T(8,128)(2,1)S(1)}, u32[]{:S(2)}, u32[]{:S(2)}) collective-permute-start(bf16[64,1024]{1,0:T(8,128)(2,1)S(1)} %get-tuple-element.337), channel_id=1, source_target_pairs={{1,0},{2,1},{3,2},{4,3},{5,4},{6,5},{7,6},{9,8},{10,9},{11,10},{12... | collective-permute-start | bytes 393224 | tf_op jit(solution)/shard_map/ppermute | solution.py:22
  16.3 21.9 %copy-start.22 = (s32[2,3]{0,1:T(4,128)}, s32[2,3]{0,1:T(4,128)S(1)}, u32[]{:S(2)}) copy-start(s32[2,3]{0,1:T(4,128)S(1)} %get-tuple-element.342) | copy-start | bytes 76
  17.0 26.8 %collective-permute-start.2 = (bf16[2,64,1024]{2,1,0:T(8,128)(2,1)S(1)}, bf16[2,64,1024]{2,1,0:T(8,128)(2,1)S(1)}, u32[]{:S(2)}, u32[]{:S(2)}) collective-permute-start(bf16[2,64,1024]{2,1,0:T(8,128)(2,1)S(1)} %select_select_fusion.5), channel_id=1, source_target_pairs={{6,0},{7,1},{0,2},{1,3},{2,4},{3,5},{4,6},{5,7},{14,8},{15,9},{8,1... | collective-permute-start | bytes 786440 | tf_op jit(solution)/shard_map/ppermute | solution.py:30
  21.4 26.0 %collective-permute-start.3 = (bf16[2,64,1024]{2,1,0:T(8,128)(2,1)S(1)}, bf16[2,64,1024]{2,1,0:T(8,128)(2,1)S(1)}, u32[]{:S(2)}, u32[]{:S(2)}) collective-permute-start(bf16[2,64,1024]{2,1,0:T(8,128)(2,1)S(1)} %select_select_fusion.4), channel_id=1, source_target_pairs={{5,0},{6,1},{7,2},{0,3},{1,4},{2,5},{3,6},{4,7},{13,8},{14,9},{15,... | collective-permute-start | bytes 786440 | tf_op jit(solution)/shard_map/ppermute | solution.py:30
  23.8 31.1 %collective-permute-start.4 = (bf16[2,64,1024]{2,1,0:T(8,128)(2,1)S(1)}, bf16[2,64,1024]{2,1,0:T(8,128)(2,1)S(1)}, u32[]{:S(2)}, u32[]{:S(2)}) collective-permute-start(bf16[2,64,1024]{2,1,0:T(8,128)(2,1)S(1)} %select_select_fusion.3), channel_id=1, source_target_pairs={{4,0},{5,1},{6,2},{7,3},{0,4},{1,5},{2,6},{3,7},{12,8},{13,9},{14,... | collective-permute-start | bytes 786440 | tf_op jit(solution)/shard_map/ppermute | solution.py:30
  32.6 270.5 %all-reduce.7.cloned.1.call-start = ((), (), s32[]{:S(2)}) async-start(), calls=%async_computation | async-start | bytes 1048576 | tf_op jit(solution)/shard_map/psum | solution.py:172
  38.8 21.0 %collective-permute-start.5 = (bf16[2,64,1024]{2,1,0:T(8,128)(2,1)S(1)}, bf16[2,64,1024]{2,1,0:T(8,128)(2,1)S(1)}, u32[]{:S(2)}, u32[]{:S(2)}) collective-permute-start(bf16[2,64,1024]{2,1,0:T(8,128)(2,1)S(1)} %select_select_fusion.2), channel_id=1, source_target_pairs={{3,0},{4,1},{5,2},{6,3},{7,4},{0,5},{1,6},{2,7},{11,8},{12,9},{13,... | collective-permute-start | bytes 786440 | tf_op jit(solution)/shard_map/ppermute | solution.py:30
  42.4 20.6 %collective-permute-start.6 = (bf16[2,64,1024]{2,1,0:T(8,128)(2,1)S(1)}, bf16[2,64,1024]{2,1,0:T(8,128)(2,1)S(1)}, u32[]{:S(2)}, u32[]{:S(2)}) collective-permute-start(bf16[2,64,1024]{2,1,0:T(8,128)(2,1)S(1)} %select_select_fusion.1), channel_id=1, source_target_pairs={{2,0},{3,1},{4,2},{5,3},{6,4},{7,5},{0,6},{1,7},{10,8},{11,9},{12,... | collective-permute-start | bytes 786440 | tf_op jit(solution)/shard_map/ppermute | solution.py:30
  43.8 19.2 %collective-permute-start.7 = (bf16[2,64,1024]{2,1,0:T(8,128)(2,1)S(1)}, bf16[2,64,1024]{2,1,0:T(8,128)(2,1)S(1)}, u32[]{:S(2)}, u32[]{:S(2)}) collective-permute-start(bf16[2,64,1024]{2,1,0:T(8,128)(2,1)S(1)} %select_select_fusion), channel_id=1, source_target_pairs={{1,0},{2,1},{3,2},{4,3},{5,4},{6,5},{7,6},{0,7},{9,8},{10,9},{11,1... | collective-permute-start | bytes 786440 | tf_op jit(solution)/shard_map/ppermute | solution.py:30
  158.8 14.5 %collective-permute-start.8 = (f32[64,1024]{1,0:T(8,128)}, f32[64,1024]{1,0:T(8,128)S(1)}, u32[]{:S(2)}, u32[]{:S(2)}) collective-permute-start(f32[64,1024]{1,0:T(8,128)} %get-tuple-element.331), channel_id=1, source_target_pairs={{0,1},{1,2},{2,3},{3,4},{4,5},{5,6},{6,7},{8,9},{9,10},{10,11},{11... | collective-permute-start | bytes 786440 | tf_op jit(solution)/shard_map/ppermute | solution.py:19
  162.8 28.5 %collective-permute-start.11 = (f32[2,64,1024]{2,1,0:T(8,128)}, f32[2,64,1024]{2,1,0:T(8,128)S(1)}, u32[]{:S(2)}, u32[]{:S(2)}) collective-permute-start(f32[2,64,1024]{2,1,0:T(8,128)} %get-tuple-element.327), channel_id=1, source_target_pairs={{3,0},{4,1},{5,2},{6,3},{7,4},{0,5},{1,6},{2,7},{11,8},{12,9},{13,... | collective-permute-start | bytes 1572872 | tf_op jit(solution)/shard_map/ppermute | solution.py:30
  165.9 19.6 %collective-permute-start.9 = (f32[64,1024]{1,0:T(8,128)S(1)}, f32[64,1024]{1,0:T(8,128)S(1)}, u32[]{:S(2)}, u32[]{:S(2)}) collective-permute-start(f32[64,1024]{1,0:T(8,128)S(1)} %get-tuple-element.330), channel_id=1, source_target_pairs={{1,0},{2,1},{3,2},{4,3},{5,4},{6,5},{7,6},{9,8},{10,9},{11,10},{12... | collective-permute-start | bytes 786440 | tf_op jit(solution)/shard_map/ppermute | solution.py:22
  167.8 71.2 %collective-permute-start.10 = (f32[2,64,1024]{2,1,0:T(8,128)}, f32[2,64,1024]{2,1,0:T(8,128)S(1)}, u32[]{:S(2)}, u32[]{:S(2)}) collective-permute-start(f32[2,64,1024]{2,1,0:T(8,128)} %get-tuple-element.327), channel_id=1, source_target_pairs={{2,0},{3,1},{4,2},{5,3},{6,4},{7,5},{0,6},{1,7},{10,8},{11,9},{12,... | collective-permute-start | bytes 1572872 | tf_op jit(solution)/shard_map/ppermute | solution.py:30
  172.2 85.0 %collective-permute-start.13 = (f32[2,64,1024]{2,1,0:T(8,128)}, f32[2,64,1024]{2,1,0:T(8,128)}, u32[]{:S(2)}, u32[]{:S(2)}) collective-permute-start(f32[2,64,1024]{2,1,0:T(8,128)} %get-tuple-element.328), channel_id=1, source_target_pairs={{5,0},{6,1},{7,2},{0,3},{1,4},{2,5},{3,6},{4,7},{13,8},{14,9},{15,... | collective-permute-start | bytes 1572872 | tf_op jit(solution)/shard_map/ppermute | solution.py:30
  173.3 85.1 %collective-permute-start.12 = (f32[2,64,1024]{2,1,0:T(8,128)}, f32[2,64,1024]{2,1,0:T(8,128)}, u32[]{:S(2)}, u32[]{:S(2)}) collective-permute-start(f32[2,64,1024]{2,1,0:T(8,128)} %get-tuple-element.328), channel_id=1, source_target_pairs={{4,0},{5,1},{6,2},{7,3},{0,4},{1,5},{2,6},{3,7},{12,8},{13,9},{14,... | collective-permute-start | bytes 1572872 | tf_op jit(solution)/shard_map/ppermute | solution.py:30
  185.4 75.4 %collective-permute-start.15 = (f32[2,64,1024]{2,1,0:T(8,128)}, f32[2,64,1024]{2,1,0:T(8,128)S(1)}, u32[]{:S(2)}, u32[]{:S(2)}) collective-permute-start(f32[2,64,1024]{2,1,0:T(8,128)} %get-tuple-element.329), channel_id=1, source_target_pairs={{7,0},{0,1},{1,2},{2,3},{3,4},{4,5},{5,6},{6,7},{15,8},{8,9},{9,10... | collective-permute-start | bytes 1572872 | tf_op jit(solution)/shard_map/ppermute | solution.py:30
  189.4 67.8 %copy-start.17 = (pred[2]{0:T(512)(128)(4,1)S(1)}, pred[2]{0:T(512)(128)(4,1)}, u32[]{:S(2)}) copy-start(pred[2]{0:T(512)(128)(4,1)} %copy-done.16) | copy-start | bytes 10
  191.3 72.4 %collective-permute-start.14 = (f32[2,64,1024]{2,1,0:T(8,128)}, f32[2,64,1024]{2,1,0:T(8,128)S(1)}, u32[]{:S(2)}, u32[]{:S(2)}) collective-permute-start(f32[2,64,1024]{2,1,0:T(8,128)} %get-tuple-element.329), channel_id=1, source_target_pairs={{6,0},{7,1},{0,2},{1,3},{2,4},{3,5},{4,6},{5,7},{14,8},{15,9},{8,1... | collective-permute-start | bytes 1572872 | tf_op jit(solution)/shard_map/ppermute | solution.py:30
  239.0 20.5 %copy-start.32 = (pred[2]{0:T(512)(128)(4,1)S(1)}, pred[2]{0:T(512)(128)(4,1)}, u32[]{:S(2)}) copy-start(pred[2]{0:T(512)(128)(4,1)} %compare_bitcast_fusion.4) | copy-start | bytes 10
  240.0 20.9 %copy-start.21 = (pred[2]{0:T(512)(128)(4,1)S(1)}, pred[2]{0:T(512)(128)(4,1)}, u32[]{:S(2)}) copy-start(pred[2]{0:T(512)(128)(4,1)} %copy-done.20) | copy-start | bytes 10
  263.7 39.4 %copy-start.23 = (pred[2]{0:T(512)(128)(4,1)S(1)}, pred[2]{0:T(512)(128)(4,1)}, u32[]{:S(2)}) copy-start(pred[2]{0:T(512)(128)(4,1)} %get-tuple-element.302) | copy-start | bytes 10
  263.9 41.3 %copy-start.37 = (pred[2]{0:T(512)(128)(4,1)S(1)}, pred[2]{0:T(512)(128)(4,1)}, u32[]{:S(2)}) copy-start(pred[2]{0:T(512)(128)(4,1)} %compare_bitcast_fusion.5) | copy-start | bytes 10
  (51 other events, 214.6 us)
Sparse Core Ops, SparseCore 0:
  32.8 91.3 all-reduce.8
  172.3 130.7 all-reduce.6
where the time goes:
time: 317 us; the launch traced here: 316 us
  waiting for transfers between devices  133 us (42%)
  starting transfers between devices  92.5 us (29%)
  local copies, waits for them, and re-layouts  33.9 us (11%)
  between operations  20 us (6%)
  matrix products  18.6 us (6%)
  other arithmetic  11.7 us (4%)
  loops' own time  5.71 us (2%)
    ppermute x12, starting transfers between devices, shifted(): return lax.ppermute(block, axis, route)  82.2 us
    psum x1, waiting for transfers between devices, broadcast(): return lax.psum(block, axis)  60.9 us
    psum x1, waiting for transfers between devices, on_device(): global_total = lax.psum(global_acc, 'seq')  36.6 us
    ppermute x12, waiting for transfers between devices, shifted(): return lax.ppermute(block, axis, route)  35.8 us
    dot_general x6, matrix products, on_device(): jnp.einsum('jo,jbf->obf', onehot, back, precision=lax.Precision.HIGHEST)  9.52 us
    while x64, local copies, waits for them, and re-layouts  9.26 us
    ppermute x2, starting transfers between devices, extended_2(): lax.ppermute(lax.slice_in_dim(block, block.shape[dim] - width, None, axis...  7.68 us
  transfers between devices with their start and end apart: 18, of which 7 were waited for; matrix products, arithmetic and copies ran while one was open for 9% of the time, Pallas kernels for 0%

commit v1 on v0

v1 whole, which is shorter than its diff:
```python
import functools
import math

import jax
import jax.numpy as jnp
from jax import lax
from jax.experimental import pallas as pl
from jax.experimental.pallas import tpu as pltpu
from jax.sharding import PartitionSpec as P

HEADS = 8
BLOCK = 64
RAND = 3
GLOBAL = 2
HEAD = 64
LANES = 2 * HEAD
WINDOW = 4
ENTRIES = WINDOW + GLOBAL + 2 * RAND
MASKED = -1e30


def low_lanes(shape):
    return lax.broadcasted_iota(jnp.int32, shape, len(shape) - 1) < HEAD


def swap_halves(block):
    return pltpu.roll(block, HEAD, 1)


def pack_kernel(q_ref, k_ref, v_ref, g_ref, out_ref):
    rows = q_ref.shape[0]
    low = low_lanes((rows, LANES))
    for pair in range(HEADS // 2):
        lanes = slice(pair * LANES, (pair + 1) * LANES)
        for place, (first_ref, second_ref) in enumerate(((k_ref, v_ref), (q_ref, g_ref))):
            first = first_ref[:, lanes].astype(jnp.float32)
            second = second_ref[:, lanes].astype(jnp.float32)
            even = jnp.where(low, first, swap_halves(second))
            odd = jnp.where(low, swap_halves(first), second)
            for half, tile in enumerate((even, odd)):
                out_ref[2 * pair + half, place] = tile.astype(jnp.bfloat16)


def unpack_kernel(in_ref, gq_ref, gk_ref, gv_ref):
    rows = gq_ref.shape[0]
    low = low_lanes((rows, LANES))
    low_block = low_lanes((BLOCK, LANES))
    for pair in range(HEADS // 2):
        lanes = slice(pair * LANES, (pair + 1) * LANES)
        even = in_ref[2 * pair].astype(jnp.float32)
        odd = in_ref[2 * pair + 1].astype(jnp.float32)
        gk = jnp.where(low, even[:rows], swap_halves(odd[:rows]))
        gv = jnp.where(low, swap_halves(even[:rows]), odd[:rows])
        gk_ref[:, lanes] = gk.astype(jnp.bfloat16)
        gv_ref[:, lanes] = gv.astype(jnp.bfloat16)
        first = jnp.where(low_block, even[rows:], swap_halves(odd[rows:]))
        second = jnp.where(low_block, swap_halves(even[rows:]), odd[rows:])
        gq_ref[:BLOCK, lanes] = first.astype(jnp.bfloat16)
        gq_ref[BLOCK:, lanes] = second.astype(jnp.bfloat16)


def attend_kernel(alone, scale, picks_ref, globals_ref, range_ref, sent_ref, *rest):
    if alone:
        out_ref, acc_ref = rest
        pool_ref = None
    else:
        pool_ref, gq_ref, acc_ref = rest
    tiles = sent_ref.shape[0]
    blocks = 2 * tiles
    queries = 2 * BLOCK
    low = low_lanes((BLOCK, queries))
    low_rows = low_lanes((queries, LANES))
    acc_ref[...] = jnp.zeros_like(acc_ref)

    def pooled(entry):
        if alone:
            return sent_ref[entry // 2, 0, entry % 2]
        return pool_ref[entry]

    def chosen(tile):
        first = 2 * tile
        if alone:
            window = [max(first - 1, 0), first, first + 1, min(first + 2, blocks - 1)]
            everywhere = [globals_ref[slot] for slot in range(GLOBAL)]
        else:
            window = [first - 1 if tile > 0 else blocks, first, first + 1]
            window += [first + 2 if tile < tiles - 1 else blocks + 1]
            everywhere = [blocks + 2 + slot for slot in range(GLOBAL)]
        picked = []
        for block in (first, first + 1):
            for slot in range(RAND):
                pick = picks_ref[block, slot]
                if alone:
                    behind = block + blocks - (slot + 1) * blocks // 4 - pick
                    picked.append(lax.rem(behind, blocks))
                else:
                    base = blocks + 2 + GLOBAL + slot * (blocks + 1)
                    picked.append(base + block + 1 - pick)
        return window + everywhere + picked

    for tile in range(tiles):
        entries = chosen(tile)
        keys = jnp.concatenate([pooled(entry) for entry in entries], axis=0)
        both = sent_ref[tile, 1].reshape(queries, LANES)
        zero = jnp.zeros_like(both)
        sides = jnp.concatenate(
            [jnp.where(low_rows, both * scale, zero), jnp.where(low_rows, zero, both)], axis=0
        )
        products = lax.dot_general(
            keys, sides, (((1,), (1,)), ((), ())), preferred_element_type=jnp.float32
        )
        grad_probs = products[:, queries:]
        parts = []
        for place in range(ENTRIES):
            part = products[place * BLOCK : (place + 1) * BLOCK, :queries]
            keep = None
            if place == 0:
                keep = low
                if tile == 0:
                    keep = jnp.logical_and(low, False if alone else range_ref[0] > 0)
            elif place == WINDOW - 1:
                keep = jnp.logical_not(low)
                if tile == tiles - 1:
                    inside = False if alone else range_ref[0] < range_ref[1] - 1
                    keep = jnp.logical_and(keep, inside)
            elif place >= WINDOW + GLOBAL + RAND:
                keep = jnp.logical_not(low)
            elif place >= WINDOW + GLOBAL:
                keep = low
            parts.append(part if keep is None else jnp.where(keep, part, MASKED))
        scores = jnp.concatenate(parts, axis=0)
        row_max = jnp.max(scores, axis=0, keepdims=True)
        expo = jnp.exp(scores - row_max)
        row_total = jnp.sum(expo, axis=0, keepdims=True)
        probs = expo * (1.0 / row_total)
        probs_half = probs.astype(jnp.bfloat16)
        row_dot = jnp.sum(probs_half.astype(jnp.float32) * grad_probs, axis=0, keepdims=True)
        grad_half = (probs * (grad_probs - row_dot)).astype(jnp.bfloat16)
        pair = jnp.concatenate([grad_half, probs_half], axis=1)
        key_grads = jnp.dot(pair, sides, preferred_element_type=jnp.float32)
        grad_query = lax.dot_general(
            grad_half, keys, (((0,), (0,)), ((), ())), preferred_element_type=jnp.float32
        )
        grad_query = grad_query * scale
        folded = jnp.where(
            low_lanes((BLOCK, LANES)), grad_query[:BLOCK], swap_halves(grad_query[BLOCK:])
        ).astype(jnp.bfloat16)
        if alone:
            out_ref[tile, queries:] = folded
        else:
            gq_ref[tile] = folded
        for place, entry in enumerate(entries):
            acc_ref[entry] += key_grads[place * BLOCK : (place + 1) * BLOCK]
    if alone:
        for tile in range(tiles):
            for half in range(2):
                grads = acc_ref[2 * tile + half].astype(jnp.bfloat16)
                out_ref[tile, half * BLOCK : (half + 1) * BLOCK] = grads


def exchange(block, ways, groups):
    return lax.all_to_all(block, "seq", 0, 0, axis_index_groups=groups)


def moved(block, ranges, distance, ways, wrap=True):
    route = []
    for source in range(ranges):
        target = source + distance
        if wrap:
            target %= ranges
        if 0 <= target < ranges:
            route += [(source * ways + head, target * ways + head) for head in range(ways)]
    return lax.ppermute(block, "seq", route)


def on_device(queries, key_vectors, value_vectors, output_grad, rand_pick, global_ids):
    group = lax.axis_size("seq")
    rows, width = queries.shape
    ways = HEADS
    ranges = group // ways
    alone = ranges == 1
    blocks = ways * rows // BLOCK
    scale = 1.0 / math.sqrt(width // HEADS)
    vmem = pl.BlockSpec(memory_space=pltpu.VMEM)
    smem = pl.BlockSpec(memory_space=pltpu.SMEM)
    half_type = jnp.bfloat16
    groups = None
    if not alone:
        groups = [[r * ways + head for head in range(ways)] for r in range(ranges)]

    packed = pl.pallas_call(
        pack_kernel,
        out_shape=jax.ShapeDtypeStruct((HEADS, 2, rows, LANES), half_type),
        in_specs=[vmem] * 4,
        out_specs=vmem,
        name="pack",
    )(queries, key_vectors, value_vectors, output_grad)
    sent = exchange(packed, ways, groups).reshape(ways, 2, 2, BLOCK, LANES)

    kernel = functools.partial(attend_kernel, alone, scale)
    back_shape = (ways, rows + BLOCK, LANES)
    if alone:
        back = pl.pallas_call(
            kernel,
            out_shape=jax.ShapeDtypeStruct(back_shape, half_type),
            in_specs=[smem, smem, smem, vmem],
            out_specs=vmem,
            scratch_shapes=[pltpu.VMEM((blocks, BLOCK, LANES), jnp.float32)],
            compiler_params=pltpu.CompilerParams(vmem_limit_bytes=48 * 2**20),
            name="attend",
        )(rand_pick, global_ids, jnp.zeros((2,), jnp.int32), sent)
    else:
        back = spread_out(
            kernel, sent, rand_pick, global_ids, ways, ranges, blocks, back_shape, groups
        )
    received = exchange(back, ways, groups)
    return pl.pallas_call(
        unpack_kernel,
        out_shape=[jax.ShapeDtypeStruct((rows, width), half_type)] * 3,
        in_specs=[vmem],
        out_specs=[vmem] * 3,
        name="unpack",
    )(received)


def spread_out(kernel, sent, rand_pick, global_ids, ways, ranges, blocks, back_shape, groups):
    vmem = pl.BlockSpec(memory_space=pltpu.VMEM)
    smem = pl.BlockSpec(memory_space=pltpu.SMEM)
    mine = lax.axis_index("seq") // ways
    own = sent[:, 0].reshape(blocks, BLOCK, LANES)
    lags = [(slot + 1) * ranges // 4 for slot in range(RAND)]
    heads = [[r * ways + head for r in range(ranges)] for head in range(ways)]
    roots = global_ids // blocks
    offsets = global_ids % blocks
    pool = [own, moved(own[-1:], ranges, 1, ways, False), moved(own[:1], ranges, -1, ways, False)]
    chosen = jnp.where((roots == mine)[:, None, None], jnp.take(own, offsets, axis=0), 0)
    pool.append(lax.psum(chosen.astype(own.dtype), "seq", axis_index_groups=heads))
    for lag in lags:
        pool.append(moved(own[-1:], ranges, lag + 1, ways))
        pool.append(moved(own, ranges, lag, ways))
    pool = jnp.concatenate(pool, axis=0)
    picks = lax.dynamic_slice_in_dim(rand_pick, mine * blocks, blocks, 0)
    where = jnp.stack([mine, jnp.int32(ranges)]).astype(jnp.int32)
    grad_query, totals = pl.pallas_call(
        kernel,
        out_shape=[
            jax.ShapeDtypeStruct((ways, BLOCK, LANES), jnp.bfloat16),
            jax.ShapeDtypeStruct(pool.shape, jnp.float32),
        ],
        in_specs=[smem, smem, smem, vmem, vmem],
        out_specs=[vmem] * 2,
        compiler_params=pltpu.CompilerParams(vmem_limit_bytes=48 * 2**20),
        name="attend",
    )(picks, global_ids, where, sent, pool)
    total = totals[:blocks]
    total = total.at[-1].add(moved(totals[blocks], ranges, -1, ways, False))
    total = total.at[0].add(moved(totals[blocks + 1], ranges, 1, ways, False))
    base = blocks + 2
    summed = lax.psum(totals[base : base + GLOBAL], "seq", axis_index_groups=heads)
    for slot in range(GLOBAL):
        owned = jnp.where(roots[slot] == mine, summed[slot], 0.0)
        total = total.at[offsets[slot]].add(owned)
    base += GLOBAL
    for lag in lags:
        total = total.at[-1].add(moved(totals[base], ranges, -lag - 1, ways))
        total = total + moved(totals[base + 1 : base + 1 + blocks], ranges, -lag, ways)
        base += blocks + 1
    grads = total.astype(jnp.bfloat16).reshape(ways, 2 * BLOCK, LANES)
    return jnp.concatenate([grads, grad_query], axis=1).reshape(back_shape)


def solution(mesh):
    whole = P(("doc", "seq"), None)
    return jax.shard_map(
        on_device,
        mesh=mesh,
        in_specs=(whole, whole, whole, whole, P("doc", None), P("doc")),
        out_specs=(whole, whole, whole),
        check_vma=False,
    )
```

time: 317 us -> 50.7 us (0.16)
  waiting for transfers between devices: 133 us -> 14.4 us
  starting transfers between devices: 92.5 us -> 7.38 us
  local copies, waits for them, and re-layouts: 33.9 us -> 0.74 us
  between operations: 20 us -> 0.64 us
  matrix products: 18.6 us -> 0 us
  blocking collectives: 0 us -> 15.8 us
  other arithmetic: 11.7 us -> 0 us
  Pallas kernels: 0 us -> 11.4 us
  loops' own time: 5.71 us -> 0 us
    psum x2 -> x0, waiting for transfers between devices: 97.5 us -> none  [the longest x1 60.9 us: broadcast(): return lax.psum(block, axis)]
    ppermute x16 -> x0, starting transfers between devices: 92.4 us -> none  [the longest x12 82.2 us: shifted(): return lax.ppermute(block, axis, route)]
    ppermute x16 -> x0, waiting for transfers between devices: 35.9 us -> none  [the longest x12 35.8 us: shifted(): return lax.ppermute(block, axis, route)]
    dot_general x17 -> x0, matrix products: 17.5 us -> none  [the longest x6 9.52 us: on_device(): jnp.einsum('jo,jbf->obf', onehot, back, precision=lax.Precision.HIGHEST)]
    all_to_all x0 -> x1, blocking collectives: none -> 15.8 us  [exchange(): return lax.all_to_all(block, 'seq', 0, 0, axis_index_groups=groups)]
    all_to_all x0 -> x1, waiting for transfers between devices: none -> 14.4 us  [exchange(): return lax.all_to_all(block, 'seq', 0, 0, axis_index_groups=groups)]
    pallas_call x0 -> x3, Pallas kernels: none -> 11.4 us  [the longest x1 7.39 us: on_device(): pl.pallas_call(kernel, out_shape=jax.ShapeDtypeStruct(back_shape, half_ty...]
    while x65 -> x0, local copies, waits for them, and re-layouts: 10.5 us -> none
  transfers between devices with their start and end apart: 18 -> 1, of which waited for: 7 -> 1; matrix products, arithmetic and copies ran while one was open for 9% -> 0% of each run, Pallas kernels for 0% -> 0%
where the time goes in v1:
time: 50.7 us; the launch traced here: 50.3 us
  blocking collectives  15.8 us (31%)
  waiting for transfers between devices  14.4 us (28%)
  Pallas kernels  11.4 us (22%)
  starting transfers between devices  7.38 us (15%)
  local copies, waits for them, and re-layouts  0.74 us (1%)
  between operations  0.64 us (1%)
    all_to_all x1, blocking collectives, exchange(): return lax.all_to_all(block, 'seq', 0, 0, axis_index_groups=groups)  15.8 us
    all_to_all x1, waiting for transfers between devices, exchange(): return lax.all_to_all(block, 'seq', 0, 0, axis_index_groups=groups)  14.4 us
    pallas_call x1, Pallas kernels, on_device(): pl.pallas_call(kernel, out_shape=jax.ShapeDtypeStruct(back_shape, half_ty...  7.39 us
    all_to_all x1, starting transfers between devices, exchange(): return lax.all_to_all(block, 'seq', 0, 0, axis_index_groups=groups)  7.38 us
    pallas_call x1, Pallas kernels, on_device(): pl.pallas_call(pack_kernel, out_shape=jax.ShapeDtypeStruct((HEADS, 2, row...  2.11 us
    pallas_call x1, Pallas kernels, on_device(): pl.pallas_call(unpack_kernel, out_shape=[jax.ShapeDtypeStruct((rows, widt...  1.9 us
  transfers between devices with their start and end apart: 1, of which 1 were waited for; matrix products, arithmetic and copies ran while one was open for 0% of the time, Pallas kernels for 0%

profile of v1, /device:TPU:0, one launch (start us, length us, event | category | flops | bytes accessed | tf_op | source)
XLA Modules:
  0.0 50.3 jit_solution(4513868272696640744)
XLA Ops:
  0.6 2.1 %pack.1 = bf16[8,2,128,128]{3,2,1,0:T(8,128)(2,1)} custom-call(bf16[128,512]{1,0:T(8,128)(2,1)} %q_ref.1, bf16[128,512]{1,0:T(8,128)(2,1)} %k_ref.1, bf16[128,512]{1,0:T(8,128)(2,1)} %v_ref.1, bf16[128,512]{1,0:T(8,128)(2,1)} %g_ref.1), custom_call_target="tpu_custom_call" | custom-call | tf_op jit(solution)/shard_map/pack/pallas_call | solution.py:191
  2.7 0.0 copy-start.1
  2.7 7.4 %all-to-all-start = ((bf16[8,2,128,128]{3,2,1,0:T(8,128)(2,1)}), bf16[8,2,128,128]{3,2,1,0:T(8,128)(2,1)S(1)}, u32[]{:S(2)}, u32[]{:S(2)}) async-start(bf16[8,2,128,128]{3,2,1,0:T(8,128)(2,1)} %pack.1), calls=%async_computation | async-start | bytes 1048576 | tf_op jit(solution)/shard_map/all_to_all | solution.py:162
  10.1 0.0 copy-done.1
  10.1 0.1 copy.9.picks_ref
  10.2 14.4 %all-to-all-done = bf16[8,2,128,128]{3,2,1,0:T(8,128)(2,1)S(1)} async-done(((bf16[8,2,128,128]{3,2,1,0:T(8,128)(2,1)}), bf16[8,2,128,128]{3,2,1,0:T(8,128)(2,1)S(1)}, u32[]{:S(2)}, u32[]{:S(2)}) %all-to-all-start) | async-done | bytes 524320 | tf_op jit(solution)/shard_map/all_to_all | solution.py:162
  24.6 0.0 copy-start
  24.6 0.7 %copy-done = s32[2]{0:T(128)S(1)} copy-done((s32[2]{0:T(128)S(1)}, s32[2]{0:T(128)}, u32[]{:S(2)}) %copy-start) | copy-done | bytes 32
  25.3 7.4 %attend.1 = bf16[8,192,128]{2,1,0:T(8,128)(2,1)S(1)} custom-call(s32[16,3]{1,0:T(8,128)S(1)} %copy.9.picks_ref, s32[2]{0:T(128)S(1)} %copy-done, s32[2]{0:T(128)S(1)} %broadcast_1_range_ref.2.range_ref, bf16[8,2,2,64,128]{4,3,2,1,0:T(8,128)(2,1)S(1)} %bitcast.1), custom_call_target="tpu_custom_call" | custom-call | tf_op jit(solution)/shard_map/attend/pallas_call | solution.py:203
  32.7 15.8 %all_to_all.10.in_ref = bf16[8,192,128]{2,1,0:T(8,128)(2,1)} all-to-all(bf16[8,192,128]{2,1,0:T(8,128)(2,1)S(1)} %attend.1), channel_id=1, replica_groups=mesh['doc'=4,'seq'=8] {'seq'}, dimensions={0} | all-to-all | bytes 786432 | tf_op jit(solution)/shard_map/all_to_all | solution.py:162
  48.4 1.9 %unpack.1 = (bf16[128,512]{1,0:T(8,128)(2,1)}, bf16[128,512]{1,0:T(8,128)(2,1)}, bf16[128,512]{1,0:T(8,128)(2,1)}) custom-call(bf16[8,192,128]{2,1,0:T(8,128)(2,1)} %all_to_all.10.in_ref), custom_call_target="tpu_custom_call" | custom-call | tf_op jit(solution)/shard_map/unpack/pallas_call | solution.py:217
  (1 shorter events, 0.0 us)
Async XLA Ops:
  2.7 7.4 %copy-start.1 = (s32[16,3]{0,1:T(4,128)S(1)}, s32[16,3]{0,1:T(4,128)}, u32[]{:S(2)}) copy-start(s32[16,3]{0,1:T(4,128)} %param.10) | copy-start | bytes 580
  2.7 21.9 %all-to-all-start = ((bf16[8,2,128,128]{3,2,1,0:T(8,128)(2,1)}), bf16[8,2,128,128]{3,2,1,0:T(8,128)(2,1)S(1)}, u32[]{:S(2)}, u32[]{:S(2)}) async-start(bf16[8,2,128,128]{3,2,1,0:T(8,128)(2,1)} %pack.1), calls=%async_computation | async-start | bytes 1048576 | tf_op jit(solution)/shard_map/all_to_all | solution.py:162
  24.6 0.7 %copy-start = (s32[2]{0:T(128)S(1)}, s32[2]{0:T(128)}, u32[]{:S(2)}) copy-start(s32[2]{0:T(128)} %globals_ref.1) | copy-start | bytes 28

commit v2 on v1

--- a/solution.py
+++ b/solution.py
@@ -14,8 +14,6 @@
 GLOBAL = 2
 HEAD = 64
 LANES = 2 * HEAD
-WINDOW = 4
-ENTRIES = WINDOW + GLOBAL + 2 * RAND
 MASKED = -1e30
 
 
@@ -59,7 +57,7 @@
         gq_ref[BLOCK:, lanes] = second.astype(jnp.bfloat16)
 
 
-def attend_kernel(alone, scale, picks_ref, globals_ref, range_ref, sent_ref, *rest):
+def attend_kernel(alone, scale, table_ref, sent_ref, *rest):
     if alone:
         out_ref, acc_ref = rest
         pool_ref = None
@@ -69,7 +67,8 @@
     blocks = 2 * tiles
     queries = 2 * BLOCK
     low = low_lanes((BLOCK, queries))
-    low_rows = low_lanes((queries, LANES))
+    zero = jnp.zeros((BLOCK, LANES), jnp.bfloat16)
+    fixed = blocks * RAND
     acc_ref[...] = jnp.zeros_like(acc_ref)
 
     def pooled(entry):
@@ -79,56 +78,63 @@
 
     def chosen(tile):
         first = 2 * tile
+        pairs = [(first, first), (first + 1, first + 1)]
+        for slot in range(GLOBAL):
+            entry = table_ref[fixed + slot] if alone else blocks + 2 + slot
+            pairs.append((entry, entry))
+        before, after = first - 1, first + 2
         if alone:
-            window = [max(first - 1, 0), first, first + 1, min(first + 2, blocks - 1)]
-            everywhere = [globals_ref[slot] for slot in range(GLOBAL)]
+            before, after = max(before, 0), min(after, blocks - 1)
         else:
-            window = [first - 1 if tile > 0 else blocks, first, first + 1]
-            window += [first + 2 if tile < tiles - 1 else blocks + 1]
-            everywhere = [blocks + 2 + slot for slot in range(GLOBAL)]
-        picked = []
-        for block in (first, first + 1):
-            for slot in range(RAND):
-                pick = picks_ref[block, slot]
+            before = before if tile > 0 else blocks
+            after = after if tile < tiles - 1 else blocks + 1
+        pairs.append((before, after))
+        for slot in range(RAND):
+            picked = []
+            for block in (first, first + 1):
+                pick = table_ref[block * RAND + slot]
                 if alone:
                     behind = block + blocks - (slot + 1) * blocks // 4 - pick
                     picked.append(lax.rem(behind, blocks))
                 else:
                     base = blocks + 2 + GLOBAL + slot * (blocks + 1)
                     picked.append(base + block + 1 - pick)
-        return window + everywhere + picked
-
-    for tile in range(tiles):
-        entries = chosen(tile)
-        keys = jnp.concatenate([pooled(entry) for entry in entries], axis=0)
-        both = sent_ref[tile, 1].reshape(queries, LANES)
-        zero = jnp.zeros_like(both)
-        sides = jnp.concatenate(
-            [jnp.where(low_rows, both * scale, zero), jnp.where(low_rows, zero, both)], axis=0
+            pairs.append(tuple(picked))
+        return pairs
+
+    def multiply(tile):
+        pairs = chosen(tile)
+        keys = jnp.concatenate(
+            [jnp.concatenate([pooled(a), pooled(b)], axis=1) for a, b in pairs], axis=0
         )
+        first, second = sent_ref[tile, 1, 0], sent_ref[tile, 1, 1]
+        rows = [
+            [jnp.where(low, first * scale, zero), zero],
+            [zero, jnp.where(low, second * scale, zero)],
+            [jnp.where(low, zero, first), zero],
+            [zero, jnp.where(low, zero, second)],
+        ]
+        sides = jnp.concatenate([jnp.concatenate(row, axis=1) for row in rows], axis=0)
         products = lax.dot_general(
             keys, sides, (((1,), (1,)), ((), ())), preferred_element_type=jnp.float32
         )
-        grad_probs = products[:, queries:]
-        parts = []
-        for place in range(ENTRIES):
-            part = products[place * BLOCK : (place + 1) * BLOCK, :queries]
-            keep = None
-            if place == 0:
+        return pairs, keys, sides, products
+
+    def weigh(tile, products):
+        scores, grad_probs = products[:, :queries], products[:, queries:]
+        edge = (2 + GLOBAL) * BLOCK
+        if tile == 0 or tile == tiles - 1:
+            if tile == 0:
+                keep = jnp.logical_not(low)
+                if not alone:
+                    keep = jnp.logical_or(keep, table_ref[fixed + GLOBAL] > 0)
+            else:
                 keep = low
-                if tile == 0:
-                    keep = jnp.logical_and(low, False if alone else range_ref[0] > 0)
-            elif place == WINDOW - 1:
-                keep = jnp.logical_not(low)
-                if tile == tiles - 1:
-                    inside = False if alone else range_ref[0] < range_ref[1] - 1
-                    keep = jnp.logical_and(keep, inside)
-            elif place >= WINDOW + GLOBAL + RAND:
-                keep = jnp.logical_not(low)
-            elif place >= WINDOW + GLOBAL:
-                keep = low
-            parts.append(part if keep is None else jnp.where(keep, part, MASKED))
-        scores = jnp.concatenate(parts, axis=0)
+                if not alone:
+                    last = table_ref[fixed + GLOBAL + 1] - 1
+                    keep = jnp.logical_or(keep, table_ref[fixed + GLOBAL] < last)
+            masked = jnp.where(keep, scores[edge : edge + BLOCK], MASKED)
+            scores = jnp.concatenate([scores[:edge], masked, scores[edge + BLOCK :]], axis=0)
         row_max = jnp.max(scores, axis=0, keepdims=True)
         expo = jnp.exp(scores - row_max)
         row_total = jnp.sum(expo, axis=0, keepdims=True)
@@ -136,21 +142,39 @@
         probs_half = probs.astype(jnp.bfloat16)
         row_dot = jnp.sum(probs_half.astype(jnp.float32) * grad_probs, axis=0, keepdims=True)
         grad_half = (probs * (grad_probs - row_dot)).astype(jnp.bfloat16)
-        pair = jnp.concatenate([grad_half, probs_half], axis=1)
-        key_grads = jnp.dot(pair, sides, preferred_element_type=jnp.float32)
+        return grad_half, probs_half
+
+    def gather(tile, pairs, keys, sides, grad_half, probs_half):
+        both = jnp.concatenate([grad_half, probs_half], axis=1)
+        key_grads = jnp.dot(both, sides, preferred_element_type=jnp.float32)
         grad_query = lax.dot_general(
             grad_half, keys, (((0,), (0,)), ((), ())), preferred_element_type=jnp.float32
         )
         grad_query = grad_query * scale
         folded = jnp.where(
-            low_lanes((BLOCK, LANES)), grad_query[:BLOCK], swap_halves(grad_query[BLOCK:])
+            low, grad_query[:BLOCK, :LANES], swap_halves(grad_query[BLOCK:, LANES:])
         ).astype(jnp.bfloat16)
         if alone:
             out_ref[tile, queries:] = folded
         else:
             gq_ref[tile] = folded
-        for place, entry in enumerate(entries):
-            acc_ref[entry] += key_grads[place * BLOCK : (place + 1) * BLOCK]
+        for place, (a, b) in enumerate(pairs):
+            part = key_grads[place * BLOCK : (place + 1) * BLOCK]
+            if place < 2 + GLOBAL:
+                acc_ref[a] += part[:, :LANES] + part[:, LANES:]
+            else:
+                acc_ref[a] += part[:, :LANES]
+                acc_ref[b] += part[:, LANES:]
+
+    ahead, weighed = {}, {}
+    for step in range(tiles + 2):
+        if step < tiles:
+            ahead[step] = multiply(step)
+        if 0 <= step - 1 < tiles:
+            weighed[step - 1] = weigh(step - 1, ahead[step - 1][-1])
+        if step >= 2:
+            pairs, keys, sides, _ = ahead.pop(step - 2)
+            gather(step - 2, pairs, keys, sides, *weighed.pop(step - 2))
     if alone:
         for tile in range(tiles):
             for half in range(2):
@@ -178,6 +202,7 @@
     rows, width = queries.shape
     ways = HEADS
     ranges = group // ways
+    assert group % ways == 0 and (ranges == 1 or ranges % 4 == 0)
     alone = ranges == 1
     blocks = ways * rows // BLOCK
     scale = 1.0 / math.sqrt(width // HEADS)
@@ -203,12 +228,12 @@
         back = pl.pallas_call(
             kernel,
             out_shape=jax.ShapeDtypeStruct(back_shape, half_type),
-            in_specs=[smem, smem, smem, vmem],
+            in_specs=[smem, vmem],
             out_specs=vmem,
             scratch_shapes=[pltpu.VMEM((blocks, BLOCK, LANES), jnp.float32)],
             compiler_params=pltpu.CompilerParams(vmem_limit_bytes=48 * 2**20),
             name="attend",
-        )(rand_pick, global_ids, jnp.zeros((2,), jnp.int32), sent)
+        )(jnp.concatenate([rand_pick.reshape(-1), global_ids]), sent)
     else:
         back = spread_out(
             kernel, sent, rand_pick, global_ids, ways, ranges, blocks, back_shape, groups
@@ -241,17 +266,18 @@
     pool = jnp.concatenate(pool, axis=0)
     picks = lax.dynamic_slice_in_dim(rand_pick, mine * blocks, blocks, 0)
     where = jnp.stack([mine, jnp.int32(ranges)]).astype(jnp.int32)
+    table = jnp.concatenate([picks.reshape(-1), global_ids, where])
     grad_query, totals = pl.pallas_call(
         kernel,
         out_shape=[
             jax.ShapeDtypeStruct((ways, BLOCK, LANES), jnp.bfloat16),
             jax.ShapeDtypeStruct(pool.shape, jnp.float32),
         ],
-        in_specs=[smem, smem, smem, vmem, vmem],
+        in_specs=[smem, vmem, vmem],
         out_specs=[vmem] * 2,
         compiler_params=pltpu.CompilerParams(vmem_limit_bytes=48 * 2**20),
         name="attend",
-    )(picks, global_ids, where, sent, pool)
+    )(table, sent, pool)
     total = totals[:blocks]
     total = total.at[-1].add(moved(totals[blocks], ranges, -1, ways, False))
     total = total.at[0].add(moved(totals[blocks + 1], ranges, 1, ways, False))

time: 50.7 us -> 45.6 us (0.90)
  Pallas kernels: 11.4 us -> 7.02 us
  waiting for transfers between devices: 14.4 us -> 13.7 us
    pallas_call x1, Pallas kernels: 7.39 us -> 3.01 us  [on_device(): pl.pallas_call(kernel, out_shape=jax.ShapeDtypeStruct(back_shape, half_ty...]
    all_to_all x1, waiting for transfers between devices: 14.4 us -> 13.7 us  [exchange(): return lax.all_to_all(block, 'seq', 0, 0, axis_index_groups=groups)]
  transfers between devices with their start and end apart: 1 -> 1, of which waited for: 1 -> 1; matrix products, arithmetic and copies ran while one was open for 0% -> 1% of each run, Pallas kernels for 0% -> 0%
where the time goes in v2:
time: 45.6 us; the launch traced here: 45.3 us
  blocking collectives  15.8 us (35%)
  waiting for transfers between devices  13.7 us (30%)
  starting transfers between devices  7.38 us (16%)
  Pallas kernels  7.02 us (15%)
  local copies, waits for them, and re-layouts  0.74 us (2%)
  between operations  0.64 us (1%)
    all_to_all x1, blocking collectives, exchange(): return lax.all_to_all(block, 'seq', 0, 0, axis_index_groups=groups)  15.8 us
    all_to_all x1, waiting for transfers between devices, exchange(): return lax.all_to_all(block, 'seq', 0, 0, axis_index_groups=groups)  13.7 us
    all_to_all x1, starting transfers between devices, exchange(): return lax.all_to_all(block, 'seq', 0, 0, axis_index_groups=groups)  7.38 us
    pallas_call x1, Pallas kernels, on_device(): pl.pallas_call(kernel, out_shape=jax.ShapeDtypeStruct(back_shape, half_ty...  3.01 us
    pallas_call x1, Pallas kernels, on_device(): pl.pallas_call(pack_kernel, out_shape=jax.ShapeDtypeStruct((HEADS, 2, row...  2.11 us
    pallas_call x1, Pallas kernels, on_device(): pl.pallas_call(unpack_kernel, out_shape=[jax.ShapeDtypeStruct((rows, widt...  1.9 us
  transfers between devices with their start and end apart: 1, of which 1 were waited for; matrix products, arithmetic and copies ran while one was open for 1% of the time, Pallas kernels for 0%

profile of v2, /device:TPU:0, one launch (start us, length us, event | category | flops | bytes accessed | tf_op | source)
XLA Modules:
  0.0 45.3 jit_solution(11257826509475630134)
XLA Ops:
  0.6 2.1 %pack.1 = bf16[8,2,128,128]{3,2,1,0:T(8,128)(2,1)} custom-call(bf16[128,512]{1,0:T(8,128)(2,1)} %q_ref.1, bf16[128,512]{1,0:T(8,128)(2,1)} %k_ref.1, bf16[128,512]{1,0:T(8,128)(2,1)} %v_ref.1, bf16[128,512]{1,0:T(8,128)(2,1)} %g_ref.1), custom_call_target="tpu_custom_call" | custom-call | tf_op jit(solution)/shard_map/pack/pallas_call | solution.py:216
  2.7 0.0 copy-start
  2.7 7.4 %all-to-all-start = ((bf16[8,2,128,128]{3,2,1,0:T(8,128)(2,1)}), bf16[8,2,128,128]{3,2,1,0:T(8,128)(2,1)S(1)}, u32[]{:S(2)}, u32[]{:S(2)}) async-start(bf16[8,2,128,128]{3,2,1,0:T(8,128)(2,1)} %pack.1), calls=%async_computation | async-start | bytes 1048576 | tf_op jit(solution)/shard_map/all_to_all | solution.py:186
  10.1 0.0 copy-done
  10.1 0.1 copy.10
  10.2 0.0 copy-start.1
  10.2 0.1 reshape.12
  10.3 0.6 %copy-done.1 = s32[2]{0:T(128)S(1)} copy-done((s32[2]{0:T(128)S(1)}, s32[2]{0:T(128)}, u32[]{:S(2)}) %copy-start.1) | copy-done | bytes 32
  10.9 0.1 pad_add_fusion.table_ref
  11.0 13.7 %all-to-all-done = bf16[8,2,128,128]{3,2,1,0:T(8,128)(2,1)S(1)} async-done(((bf16[8,2,128,128]{3,2,1,0:T(8,128)(2,1)}), bf16[8,2,128,128]{3,2,1,0:T(8,128)(2,1)S(1)}, u32[]{:S(2)}, u32[]{:S(2)}) %all-to-all-start) | async-done | bytes 524320 | tf_op jit(solution)/shard_map/all_to_all | solution.py:186
  24.6 3.0 %attend.1 = bf16[8,192,128]{2,1,0:T(8,128)(2,1)S(1)} custom-call(s32[50]{0:T(128)S(1)} %pad_add_fusion.table_ref, bf16[8,2,2,64,128]{4,3,2,1,0:T(8,128)(2,1)S(1)} %bitcast.1), custom_call_target="tpu_custom_call" | custom-call | tf_op jit(solution)/shard_map/attend/pallas_call | solution.py:228
  27.6 15.8 %all_to_all.10.in_ref = bf16[8,192,128]{2,1,0:T(8,128)(2,1)} all-to-all(bf16[8,192,128]{2,1,0:T(8,128)(2,1)S(1)} %attend.1), channel_id=1, replica_groups=mesh['doc'=4,'seq'=8] {'seq'}, dimensions={0} | all-to-all | bytes 786432 | tf_op jit(solution)/shard_map/all_to_all | solution.py:186
  43.4 1.9 %unpack.1 = (bf16[128,512]{1,0:T(8,128)(2,1)}, bf16[128,512]{1,0:T(8,128)(2,1)}, bf16[128,512]{1,0:T(8,128)(2,1)}) custom-call(bf16[8,192,128]{2,1,0:T(8,128)(2,1)} %all_to_all.10.in_ref), custom_call_target="tpu_custom_call" | custom-call | tf_op jit(solution)/shard_map/unpack/pallas_call | solution.py:242
Async XLA Ops:
  2.7 7.4 %copy-start = (s32[16,3]{0,1:T(4,128)S(1)}, s32[16,3]{0,1:T(4,128)}, u32[]{:S(2)}) copy-start(s32[16,3]{0,1:T(4,128)} %param.10) | copy-start | bytes 580
  2.7 21.9 %all-to-all-start = ((bf16[8,2,128,128]{3,2,1,0:T(8,128)(2,1)}), bf16[8,2,128,128]{3,2,1,0:T(8,128)(2,1)S(1)}, u32[]{:S(2)}, u32[]{:S(2)}) async-start(bf16[8,2,128,128]{3,2,1,0:T(8,128)(2,1)} %pack.1), calls=%async_computation | async-start | bytes 1048576 | tf_op jit(solution)/shard_map/all_to_all | solution.py:186
  10.2 0.7 %copy-start.1 = (s32[2]{0:T(128)S(1)}, s32[2]{0:T(128)}, u32[]{:S(2)}) copy-start(s32[2]{0:T(128)} %param.11) | copy-start | bytes 28

commit v3 on v2

--- a/solution.py
+++ b/solution.py
@@ -25,28 +25,39 @@
     return pltpu.roll(block, HEAD, 1)
 
 
-def pack_kernel(q_ref, k_ref, v_ref, g_ref, out_ref):
+def pack_kernel(q_ref, k_ref, v_ref, g_ref, *out_refs):
     rows = q_ref.shape[0]
     low = low_lanes((rows, LANES))
-    for pair in range(HEADS // 2):
-        lanes = slice(pair * LANES, (pair + 1) * LANES)
-        for place, (first_ref, second_ref) in enumerate(((k_ref, v_ref), (q_ref, g_ref))):
+    place = lax.rem(lax.axis_index("seq"), HEADS)
+    odd_place = lax.rem(place, 2) == 1
+    for near in range(HEADS // 2):
+        pair = lax.bitwise_xor(place // 2, near)
+        lanes = pl.ds(pl.multiple_of(pair * LANES, LANES), LANES)
+        for kind, (first_ref, second_ref) in enumerate(((k_ref, v_ref), (q_ref, g_ref))):
             first = first_ref[:, lanes].astype(jnp.float32)
             second = second_ref[:, lanes].astype(jnp.float32)
             even = jnp.where(low, first, swap_halves(second))
             odd = jnp.where(low, swap_halves(first), second)
-            for half, tile in enumerate((even, odd)):
-                out_ref[2 * pair + half, place] = tile.astype(jnp.bfloat16)
-
-
-def unpack_kernel(in_ref, gq_ref, gk_ref, gv_ref):
+            same = jnp.where(odd_place, odd, even).astype(jnp.bfloat16)
+            other = jnp.where(odd_place, even, odd).astype(jnp.bfloat16)
+            out_refs[2 * near][kind] = same
+            out_refs[2 * near + 1][kind] = other
+
+
+def unpack_kernel(*refs):
+    in_refs, (gq_ref, gk_ref, gv_ref) = refs[:HEADS], refs[HEADS:]
     rows = gq_ref.shape[0]
     low = low_lanes((rows, LANES))
     low_block = low_lanes((BLOCK, LANES))
-    for pair in range(HEADS // 2):
-        lanes = slice(pair * LANES, (pair + 1) * LANES)
-        even = in_ref[2 * pair].astype(jnp.float32)
-        odd = in_ref[2 * pair + 1].astype(jnp.float32)
+    place = lax.rem(lax.axis_index("seq"), HEADS)
+    odd_place = lax.rem(place, 2) == 1
+    for near in range(HEADS // 2):
+        pair = lax.bitwise_xor(place // 2, near)
+        lanes = pl.ds(pl.multiple_of(pair * LANES, LANES), LANES)
+        same = in_refs[2 * near][...].astype(jnp.float32)
+        other = in_refs[2 * near + 1][...].astype(jnp.float32)
+        even = jnp.where(odd_place, other, same)
+        odd = jnp.where(odd_place, same, other)
         gk = jnp.where(low, even[:rows], swap_halves(odd[:rows]))
         gv = jnp.where(low, swap_halves(even[:rows]), odd[:rows])
         gk_ref[:, lanes] = gk.astype(jnp.bfloat16)
@@ -57,12 +68,15 @@
         gq_ref[BLOCK:, lanes] = second.astype(jnp.bfloat16)
 
 
-def attend_kernel(alone, scale, table_ref, sent_ref, *rest):
+def attend_kernel(alone, scale, table_ref, *rest):
     if alone:
-        out_ref, acc_ref = rest
-        pool_ref = None
+        in_refs, out_refs = rest[:HEADS], rest[HEADS : 2 * HEADS]
+        sent_ref, gq_ref, acc_ref = rest[2 * HEADS :]
+        place = lax.rem(lax.axis_index("seq"), HEADS)
+        for m in range(HEADS):
+            sent_ref[lax.bitwise_xor(place, m)] = in_refs[m][...]
     else:
-        pool_ref, gq_ref, acc_ref = rest
+        sent_ref, pool_ref, gq_ref, acc_ref = rest
     tiles = sent_ref.shape[0]
     blocks = 2 * tiles
     queries = 2 * BLOCK
@@ -154,10 +168,7 @@
         folded = jnp.where(
             low, grad_query[:BLOCK, :LANES], swap_halves(grad_query[BLOCK:, LANES:])
         ).astype(jnp.bfloat16)
-        if alone:
-            out_ref[tile, queries:] = folded
-        else:
-            gq_ref[tile] = folded
+        gq_ref[tile] = folded
         for place, (a, b) in enumerate(pairs):
             part = key_grads[place * BLOCK : (place + 1) * BLOCK]
             if place < 2 + GLOBAL:
@@ -176,14 +187,21 @@
             pairs, keys, sides, _ = ahead.pop(step - 2)
             gather(step - 2, pairs, keys, sides, *weighed.pop(step - 2))
     if alone:
-        for tile in range(tiles):
+        for m in range(HEADS):
+            tile = lax.bitwise_xor(place, m)
             for half in range(2):
                 grads = acc_ref[2 * tile + half].astype(jnp.bfloat16)
-                out_ref[tile, half * BLOCK : (half + 1) * BLOCK] = grads
-
-
-def exchange(block, ways, groups):
-    return lax.all_to_all(block, "seq", 0, 0, axis_index_groups=groups)
+                out_refs[m][half * BLOCK : (half + 1) * BLOCK] = grads
+            out_refs[m][queries:] = gq_ref[tile]
+
+
+def exchange(parts):
+    group = lax.axis_size("seq")
+    arrived = list(parts)
+    for m in reversed(range(1, HEADS)):
+        route = [(i, i ^ m) for i in range(group)]
+        arrived[m] = lax.ppermute(parts[m], "seq", route)
+    return arrived
 
 
 def moved(block, ranges, distance, ways, wrap=True):
@@ -209,49 +227,49 @@
     vmem = pl.BlockSpec(memory_space=pltpu.VMEM)
     smem = pl.BlockSpec(memory_space=pltpu.SMEM)
     half_type = jnp.bfloat16
-    groups = None
-    if not alone:
-        groups = [[r * ways + head for head in range(ways)] for r in range(ranges)]
 
     packed = pl.pallas_call(
         pack_kernel,
-        out_shape=jax.ShapeDtypeStruct((HEADS, 2, rows, LANES), half_type),
+        out_shape=[jax.ShapeDtypeStruct((2, rows, LANES), half_type)] * HEADS,
         in_specs=[vmem] * 4,
-        out_specs=vmem,
+        out_specs=[vmem] * HEADS,
         name="pack",
     )(queries, key_vectors, value_vectors, output_grad)
-    sent = exchange(packed, ways, groups).reshape(ways, 2, 2, BLOCK, LANES)
+    sent = [part.reshape(2, 2, BLOCK, LANES) for part in exchange(packed)]
 
     kernel = functools.partial(attend_kernel, alone, scale)
-    back_shape = (ways, rows + BLOCK, LANES)
     if alone:
         back = pl.pallas_call(
             kernel,
-            out_shape=jax.ShapeDtypeStruct(back_shape, half_type),
-            in_specs=[smem, vmem],
-            out_specs=vmem,
-            scratch_shapes=[pltpu.VMEM((blocks, BLOCK, LANES), jnp.float32)],
+            out_shape=[jax.ShapeDtypeStruct((rows + BLOCK, LANES), half_type)] * HEADS,
+            in_specs=[smem] + [vmem] * HEADS,
+            out_specs=[vmem] * HEADS,
+            scratch_shapes=[
+                pltpu.VMEM((ways, 2, 2, BLOCK, LANES), half_type),
+                pltpu.VMEM((ways, BLOCK, LANES), half_type),
+                pltpu.VMEM((blocks, BLOCK, LANES), jnp.float32),
+            ],
             compiler_params=pltpu.CompilerParams(vmem_limit_bytes=48 * 2**20),
             name="attend",
-        )(jnp.concatenate([rand_pick.reshape(-1), global_ids]), sent)
+        )(jnp.concatenate([rand_pick.reshape(-1), global_ids]), *sent)
     else:
-        back = spread_out(
-            kernel, sent, rand_pick, global_ids, ways, ranges, blocks, back_shape, groups
-        )
-    received = exchange(back, ways, groups)
+        back = spread_out(kernel, sent, rand_pick, global_ids, ways, ranges, blocks)
+    received = exchange(back)
     return pl.pallas_call(
         unpack_kernel,
         out_shape=[jax.ShapeDtypeStruct((rows, width), half_type)] * 3,
-        in_specs=[vmem],
+        in_specs=[vmem] * HEADS,
         out_specs=[vmem] * 3,
         name="unpack",
-    )(received)
-
-
-def spread_out(kernel, sent, rand_pick, global_ids, ways, ranges, blocks, back_shape, groups):
+    )(*received)
+
+
+def spread_out(kernel, sent, rand_pick, global_ids, ways, ranges, blocks):
     vmem = pl.BlockSpec(memory_space=pltpu.VMEM)
     smem = pl.BlockSpec(memory_space=pltpu.SMEM)
     mine = lax.axis_index("seq") // ways
+    order = lax.bitwise_xor(lax.axis_index("seq") % ways, jnp.arange(ways, dtype=jnp.int32))
+    sent = jnp.take(jnp.stack(sent), order, axis=0)
     own = sent[:, 0].reshape(blocks, BLOCK, LANES)
     lags = [(slot + 1) * ranges // 4 for slot in range(RAND)]
     heads = [[r * ways + head for r in range(ranges)] for head in range(ways)]
@@ -292,7 +310,8 @@
         total = total + moved(totals[base + 1 : base + 1 + blocks], ranges, -lag, ways)
         base += blocks + 1
     grads = total.astype(jnp.bfloat16).reshape(ways, 2 * BLOCK, LANES)
-    return jnp.concatenate([grads, grad_query], axis=1).reshape(back_shape)
+    back = jnp.take(jnp.concatenate([grads, grad_query], axis=1), order, axis=0)
+    return [back[m] for m in range(ways)]
 
 
 def solution(mesh):

time: 45.6 us -> 45.1 us (0.989)
  starting transfers between devices: 7.38 us -> 23.6 us
  blocking collectives: 15.8 us -> 0 us
  waiting for transfers between devices: 13.7 us -> 11.2 us
  local copies, waits for them, and re-layouts: 0.74 us -> 2.22 us
    ppermute x0 -> x14, starting transfers between devices: none -> 23.6 us  [exchange(): arrived[m] = lax.ppermute(parts[m], 'seq', route)]
    all_to_all x1 -> x0, blocking collectives: 15.8 us -> none  [exchange(): return lax.all_to_all(block, 'seq', 0, 0, axis_index_groups=groups)]
    all_to_all x1 -> x0, waiting for transfers between devices: 13.7 us -> none  [exchange(): return lax.all_to_all(block, 'seq', 0, 0, axis_index_groups=groups)]
    ppermute x0 -> x14, waiting for transfers between devices: none -> 11.2 us  [exchange(): arrived[m] = lax.ppermute(parts[m], 'seq', route)]
    all_to_all x1 -> x0, starting transfers between devices: 7.38 us -> none  [exchange(): return lax.all_to_all(block, 'seq', 0, 0, axis_index_groups=groups)]
    unnamed x5 -> x23, local copies, waits for them, and re-layouts: 0.66 us -> 2.13 us
  transfers between devices with their start and end apart: 1 -> 14, of which waited for: 1 -> 4; matrix products, arithmetic and copies ran while one was open for 1% -> 1% of each run, Pallas kernels for 0% -> 0%
where the time goes in v3:
time: 45.1 us; the launch traced here: 44.9 us
  starting transfers between devices  23.6 us (52%)
  waiting for transfers between devices  11.2 us (25%)
  Pallas kernels  6.98 us (15%)
  local copies, waits for them, and re-layouts  2.22 us (5%)
  between operations  0.73 us (2%)
    ppermute x14, starting transfers between devices, exchange(): arrived[m] = lax.ppermute(parts[m], 'seq', route)  23.6 us
    ppermute x14, waiting for transfers between devices, exchange(): arrived[m] = lax.ppermute(parts[m], 'seq', route)  11.2 us
    pallas_call x1, Pallas kernels, on_device(): pl.pallas_call(kernel, out_shape=[jax.ShapeDtypeStruct((rows + BLOCK, LAN...  3.08 us
    unnamed x23, local copies, waits for them, and re-layouts  2.13 us
    pallas_call x1, Pallas kernels, on_device(): pl.pallas_call(pack_kernel, out_shape=[jax.ShapeDtypeStruct((2, rows, LAN...  2.02 us
    pallas_call x1, Pallas kernels, on_device(): pl.pallas_call(unpack_kernel, out_shape=[jax.ShapeDtypeStruct((rows, widt...  1.88 us
  transfers between devices with their start and end apart: 14, of which 4 were waited for; matrix products, arithmetic and copies ran while one was open for 1% of the time, Pallas kernels for 0%

profile of v3, /device:TPU:0, one launch (start us, length us, event | category | flops | bytes accessed | tf_op | source)
XLA Modules:
  0.0 44.9 jit_solution(4174229156335229660)
XLA Ops:
  0.6 2.0 %pack.1 = (bf16[2,128,128]{2,1,0:T(8,128)(2,1)}, bf16[2,128,128]{2,1,0:T(8,128)(2,1)}, bf16[2,128,128]{2,1,0:T(8,128)(2,1)}, bf16[2,128,128]{2,1,0:T(8,128)(2,1)...) custom-call(bf16[128,512]{1,0:T(8,128)(2,1)} %q_ref.1, ...), custom_call_target="tpu_custom_call" | custom-call | tf_op jit(solution)/shard_map/pack/pallas_call | solution.py:231
  2.6 2.9 %collective-permute-start = (bf16[2,128,128]{2,1,0:T(8,128)(2,1)}, bf16[2,128,128]{2,1,0:T(8,128)(2,1)S(1)}, u32[]{:S(2)}, u32[]{:S(2)}) collective-permute-start(bf16[2,128,128]{2,1,0:T(8,128)(2,1)} %get-tuple-element.20), channel_id=1, source_target_pairs={{0,1},{1,0},{2,3},{3,2},{4,5},{5,4},{6,7},{7,6},{8,9},{9,8},{10,11... | collective-permute-start | bytes 196616 | tf_op jit(solution)/shard_map/ppermute | solution.py:203
  5.6 1.6 %collective-permute-start.1 = (bf16[2,128,128]{2,1,0:T(8,128)(2,1)}, bf16[2,128,128]{2,1,0:T(8,128)(2,1)S(1)}, u32[]{:S(2)}, u32[]{:S(2)}) collective-permute-start(bf16[2,128,128]{2,1,0:T(8,128)(2,1)} %get-tuple-element.21), channel_id=1, source_target_pairs={{0,2},{1,3},{2,0},{3,1},{4,6},{5,7},{6,4},{7,5},{8,10},{9,11},{10,... | collective-permute-start | bytes 196616 | tf_op jit(solution)/shard_map/ppermute | solution.py:203
  7.2 3.0 %collective-permute-start.3 = (bf16[2,128,128]{2,1,0:T(8,128)(2,1)}, bf16[2,128,128]{2,1,0:T(8,128)(2,1)S(1)}, u32[]{:S(2)}, u32[]{:S(2)}) collective-permute-start(bf16[2,128,128]{2,1,0:T(8,128)(2,1)} %get-tuple-element.23), channel_id=1, source_target_pairs={{0,4},{1,5},{2,6},{3,7},{4,0},{5,1},{6,2},{7,3},{8,12},{9,13},{10,... | collective-permute-start | bytes 196616 | tf_op jit(solution)/shard_map/ppermute | solution.py:203
  10.2 1.3 %collective-permute-start.4 = (bf16[2,128,128]{2,1,0:T(8,128)(2,1)}, bf16[2,128,128]{2,1,0:T(8,128)(2,1)S(1)}, u32[]{:S(2)}, u32[]{:S(2)}) collective-permute-start(bf16[2,128,128]{2,1,0:T(8,128)(2,1)} %get-tuple-element.24), channel_id=1, source_target_pairs={{0,5},{1,4},{2,7},{3,6},{4,1},{5,0},{6,3},{7,2},{8,13},{9,12},{10,... | collective-permute-start | bytes 196616 | tf_op jit(solution)/shard_map/ppermute | solution.py:203
  11.4 0.1 copy.10
  11.5 0.1 reshape.33
  11.6 3.7 %collective-permute-start.5 = (bf16[2,128,128]{2,1,0:T(8,128)(2,1)}, bf16[2,128,128]{2,1,0:T(8,128)(2,1)S(1)}, u32[]{:S(2)}, u32[]{:S(2)}) collective-permute-start(bf16[2,128,128]{2,1,0:T(8,128)(2,1)} %get-tuple-element.25), channel_id=1, source_target_pairs={{0,6},{1,7},{2,4},{3,5},{4,2},{5,3},{6,0},{7,1},{8,14},{9,15},{10,... | collective-permute-start | bytes 196616 | tf_op jit(solution)/shard_map/ppermute | solution.py:203
  15.4 5.1 %collective-permute-done.4 = bf16[2,128,128]{2,1,0:T(8,128)(2,1)S(1)} collective-permute-done((bf16[2,128,128]{2,1,0:T(8,128)(2,1)}, bf16[2,128,128]{2,1,0:T(8,128)(2,1)S(1)}, u32[]{:S(2)}, u32[]{:S(2)}) %collective-permute-start.4) | collective-permute-done | bytes 65568 | tf_op jit(solution)/shard_map/ppermute | solution.py:203
  20.6 2.0 %collective-permute-done.6 = bf16[2,128,128]{2,1,0:T(8,128)(2,1)S(1)} collective-permute-done((bf16[2,128,128]{2,1,0:T(8,128)(2,1)}, bf16[2,128,128]{2,1,0:T(8,128)(2,1)S(1)}, u32[]{:S(2)}, u32[]{:S(2)}) %collective-permute-start.6) | collective-permute-done | bytes 65568 | tf_op jit(solution)/shard_map/ppermute | solution.py:203
  22.6 0.8 %copy-done = bf16[2,128,128]{2,1,0:T(8,128)(2,1)S(1)} copy-done((bf16[2,128,128]{2,1,0:T(8,128)(2,1)S(1)}, bf16[2,128,128]{2,1,0:T(8,128)(2,1)}, u32[]{:S(2)}) %copy-start) | copy-done | bytes 65560
  23.4 3.1 %attend.1 = (bf16[192,128]{1,0:T(8,128)(2,1)S(1)}, bf16[192,128]{1,0:T(8,128)(2,1)S(1)}, bf16[192,128]{1,0:T(8,128)(2,1)S(1)}, bf16[192,128]{1,0:T(8,128)(2,1)S(...) custom-call(s32[50]{0:T(128)S(1)} %pad_add_fusion.table_ref, ...), custom_call_target="tpu_custom_call" | custom-call | tf_op jit(solution)/shard_map/attend/pallas_call | solution.py:242
  26.5 0.6 %copy-done.1 = bf16[192,128]{1,0:T(8,128)(2,1)} copy-done((bf16[192,128]{1,0:T(8,128)(2,1)}, bf16[192,128]{1,0:T(8,128)(2,1)S(1)}, u32[]{:S(2)}) %copy-start.1) | copy-done | bytes 49176
  27.1 0.5 %collective-permute-start.7 = (bf16[192,128]{1,0:T(8,128)(2,1)S(1)}, bf16[192,128]{1,0:T(8,128)(2,1)S(1)}, u32[]{:S(2)}, u32[]{:S(2)}) collective-permute-start(bf16[192,128]{1,0:T(8,128)(2,1)S(1)} %get-tuple-element.28), channel_id=1, source_target_pairs={{0,1},{1,0},{2,3},{3,2},{4,5},{5,4},{6,7},{7,6},{8,9},{9,8},{10,11... | collective-permute-start | bytes 147464 | tf_op jit(solution)/shard_map/ppermute | solution.py:203
  27.7 1.6 %collective-permute-start.8 = (bf16[192,128]{1,0:T(8,128)(2,1)S(1)}, bf16[192,128]{1,0:T(8,128)(2,1)S(1)}, u32[]{:S(2)}, u32[]{:S(2)}) collective-permute-start(bf16[192,128]{1,0:T(8,128)(2,1)S(1)} %get-tuple-element.29), channel_id=1, source_target_pairs={{0,2},{1,3},{2,0},{3,1},{4,6},{5,7},{6,4},{7,5},{8,10},{9,11},{10,... | collective-permute-start | bytes 147464 | tf_op jit(solution)/shard_map/ppermute | solution.py:203
  29.3 1.3 %collective-permute-start.9 = (bf16[192,128]{1,0:T(8,128)(2,1)S(1)}, bf16[192,128]{1,0:T(8,128)(2,1)S(1)}, u32[]{:S(2)}, u32[]{:S(2)}) collective-permute-start(bf16[192,128]{1,0:T(8,128)(2,1)S(1)} %get-tuple-element.30), channel_id=1, source_target_pairs={{0,3},{1,2},{2,1},{3,0},{4,7},{5,6},{6,5},{7,4},{8,11},{9,10},{10,... | collective-permute-start | bytes 147464 | tf_op jit(solution)/shard_map/ppermute | solution.py:203
  30.6 2.5 %collective-permute-start.10 = (bf16[192,128]{1,0:T(8,128)(2,1)S(1)}, bf16[192,128]{1,0:T(8,128)(2,1)S(1)}, u32[]{:S(2)}, u32[]{:S(2)}) collective-permute-start(bf16[192,128]{1,0:T(8,128)(2,1)S(1)} %get-tuple-element.31), channel_id=1, source_target_pairs={{0,4},{1,5},{2,6},{3,7},{4,0},{5,1},{6,2},{7,3},{8,12},{9,13},{10,... | collective-permute-start | bytes 147464 | tf_op jit(solution)/shard_map/ppermute | solution.py:203
  33.1 0.4 collective-permute-start.11
  33.5 2.0 %collective-permute-start.12 = (bf16[192,128]{1,0:T(8,128)(2,1)S(1)}, bf16[192,128]{1,0:T(8,128)(2,1)S(1)}, u32[]{:S(2)}, u32[]{:S(2)}) collective-permute-start(bf16[192,128]{1,0:T(8,128)(2,1)S(1)} %get-tuple-element.33), channel_id=1, source_target_pairs={{0,6},{1,7},{2,4},{3,5},{4,2},{5,3},{6,0},{7,1},{8,14},{9,15},{10,... | collective-permute-start | bytes 147464 | tf_op jit(solution)/shard_map/ppermute | solution.py:203
  35.5 2.8 %collective-permute-start.13 = (bf16[192,128]{1,0:T(8,128)(2,1)S(1)}, bf16[192,128]{1,0:T(8,128)(2,1)S(1)}, u32[]{:S(2)}, u32[]{:S(2)}) collective-permute-start(bf16[192,128]{1,0:T(8,128)(2,1)S(1)} %get-tuple-element.34), channel_id=1, source_target_pairs={{0,7},{1,6},{2,5},{3,4},{4,3},{5,2},{6,1},{7,0},{8,15},{9,14},{10,... | collective-permute-start | bytes 147464 | tf_op jit(solution)/shard_map/ppermute | solution.py:203
  38.3 2.4 %collective-permute-done.11.refs_5_ = bf16[192,128]{1,0:T(8,128)(2,1)S(1)} collective-permute-done((bf16[192,128]{1,0:T(8,128)(2,1)S(1)}, bf16[192,128]{1,0:T(8,128)(2,1)S(1)}, u32[]{:S(2)}, u32[]{:S(2)}) %collective-permute-start.11) | collective-permute-done | bytes 49184 | tf_op jit(solution)/shard_map/ppermute | solution.py:203
  40.7 1.7 %collective-permute-done.13.refs_7_ = bf16[192,128]{1,0:T(8,128)(2,1)S(1)} collective-permute-done((bf16[192,128]{1,0:T(8,128)(2,1)S(1)}, bf16[192,128]{1,0:T(8,128)(2,1)S(1)}, u32[]{:S(2)}, u32[]{:S(2)}) %collective-permute-start.13) | collective-permute-done | bytes 49184 | tf_op jit(solution)/shard_map/ppermute | solution.py:203
  42.4 0.6 %copy-done.8 = bf16[192,128]{1,0:T(8,128)(2,1)} copy-done((bf16[192,128]{1,0:T(8,128)(2,1)}, bf16[192,128]{1,0:T(8,128)(2,1)S(1)}, u32[]{:S(2)}) %copy-start.8) | copy-done | bytes 49176
  43.0 1.9 %unpack.1 = (bf16[128,512]{1,0:T(8,128)(2,1)}, bf16[128,512]{1,0:T(8,128)(2,1)}, bf16[128,512]{1,0:T(8,128)(2,1)}) custom-call(bf16[192,128]{1,0:T(8,128)(2,1)} %copy-done.1, bf16[192,128]{1,0:T(8,128)(2,1)} %copy-done.2, bf16[192,128]{1,0:T(8,128)(2,1)} %copy-done.3, bf16[192,128]{1,0:T(8,128)(2,1)} %copy-done.4, bf16[192,128]{1,0:T(8,128)(2,1)} %copy-done.5, ...), custom_call_target="tpu_custom_call" | custom-call | tf_op jit(solution)/shard_map/unpack/pallas_call | solution.py:258
  (32 shorter events, 0.2 us)
Async XLA Ops:
  2.6 9.0 %collective-permute-start = (bf16[2,128,128]{2,1,0:T(8,128)(2,1)}, bf16[2,128,128]{2,1,0:T(8,128)(2,1)S(1)}, u32[]{:S(2)}, u32[]{:S(2)}) collective-permute-start(bf16[2,128,128]{2,1,0:T(8,128)(2,1)} %get-tuple-element.20), channel_id=1, source_target_pairs={{0,1},{1,0},{2,3},{3,2},{4,5},{5,4},{6,7},{7,6},{8,9},{9,8},{10,11... | collective-permute-start | bytes 196616 | tf_op jit(solution)/shard_map/ppermute | solution.py:203
  5.6 9.7 %collective-permute-start.1 = (bf16[2,128,128]{2,1,0:T(8,128)(2,1)}, bf16[2,128,128]{2,1,0:T(8,128)(2,1)S(1)}, u32[]{:S(2)}, u32[]{:S(2)}) collective-permute-start(bf16[2,128,128]{2,1,0:T(8,128)(2,1)} %get-tuple-element.21), channel_id=1, source_target_pairs={{0,2},{1,3},{2,0},{3,1},{4,6},{5,7},{6,4},{7,5},{8,10},{9,11},{10,... | collective-permute-start | bytes 196616 | tf_op jit(solution)/shard_map/ppermute | solution.py:203
  7.2 4.3 %copy-start.9 = (s32[16,3]{0,1:T(4,128)S(1)}, s32[16,3]{0,1:T(4,128)}, u32[]{:S(2)}) copy-start(s32[16,3]{0,1:T(4,128)} %param.10) | copy-start | bytes 580
  7.2 8.3 %collective-permute-start.2 = (bf16[2,128,128]{2,1,0:T(8,128)(2,1)}, bf16[2,128,128]{2,1,0:T(8,128)(2,1)S(1)}, u32[]{:S(2)}, u32[]{:S(2)}) collective-permute-start(bf16[2,128,128]{2,1,0:T(8,128)(2,1)} %get-tuple-element.22), channel_id=1, source_target_pairs={{0,3},{1,2},{2,1},{3,0},{4,7},{5,6},{6,5},{7,4},{8,11},{9,10},{10,... | collective-permute-start | bytes 196616 | tf_op jit(solution)/shard_map/ppermute | solution.py:203
  7.2 8.3 %collective-permute-start.3 = (bf16[2,128,128]{2,1,0:T(8,128)(2,1)}, bf16[2,128,128]{2,1,0:T(8,128)(2,1)S(1)}, u32[]{:S(2)}, u32[]{:S(2)}) collective-permute-start(bf16[2,128,128]{2,1,0:T(8,128)(2,1)} %get-tuple-element.23), channel_id=1, source_target_pairs={{0,4},{1,5},{2,6},{3,7},{4,0},{5,1},{6,2},{7,3},{8,12},{9,13},{10,... | collective-permute-start | bytes 196616 | tf_op jit(solution)/shard_map/ppermute | solution.py:203
  10.2 10.4 %collective-permute-start.4 = (bf16[2,128,128]{2,1,0:T(8,128)(2,1)}, bf16[2,128,128]{2,1,0:T(8,128)(2,1)S(1)}, u32[]{:S(2)}, u32[]{:S(2)}) collective-permute-start(bf16[2,128,128]{2,1,0:T(8,128)(2,1)} %get-tuple-element.24), channel_id=1, source_target_pairs={{0,5},{1,4},{2,7},{3,6},{4,1},{5,0},{6,3},{7,2},{8,13},{9,12},{10,... | collective-permute-start | bytes 196616 | tf_op jit(solution)/shard_map/ppermute | solution.py:203
  11.6 3.7 %copy-start.10 = (s32[2]{0:T(128)S(1)}, s32[2]{0:T(128)}, u32[]{:S(2)}) copy-start(s32[2]{0:T(128)} %param.11) | copy-start | bytes 28
  11.6 8.9 %collective-permute-start.5 = (bf16[2,128,128]{2,1,0:T(8,128)(2,1)}, bf16[2,128,128]{2,1,0:T(8,128)(2,1)S(1)}, u32[]{:S(2)}, u32[]{:S(2)}) collective-permute-start(bf16[2,128,128]{2,1,0:T(8,128)(2,1)} %get-tuple-element.25), channel_id=1, source_target_pairs={{0,6},{1,7},{2,4},{3,5},{4,2},{5,3},{6,0},{7,1},{8,14},{9,15},{10,... | collective-permute-start | bytes 196616 | tf_op jit(solution)/shard_map/ppermute | solution.py:203
  15.3 7.3 %collective-permute-start.6 = (bf16[2,128,128]{2,1,0:T(8,128)(2,1)}, bf16[2,128,128]{2,1,0:T(8,128)(2,1)S(1)}, u32[]{:S(2)}, u32[]{:S(2)}) collective-permute-start(bf16[2,128,128]{2,1,0:T(8,128)(2,1)} %get-tuple-element.26), channel_id=1, source_target_pairs={{0,7},{1,6},{2,5},{3,4},{4,3},{5,2},{6,1},{7,0},{8,15},{9,14},{10,... | collective-permute-start | bytes 196616 | tf_op jit(solution)/shard_map/ppermute | solution.py:203
  22.6 0.8 %copy-start = (bf16[2,128,128]{2,1,0:T(8,128)(2,1)S(1)}, bf16[2,128,128]{2,1,0:T(8,128)(2,1)}, u32[]{:S(2)}) copy-start(bf16[2,128,128]{2,1,0:T(8,128)(2,1)} %get-tuple-element.19) | copy-start | bytes 196612
  27.1 6.4 %collective-permute-start.7 = (bf16[192,128]{1,0:T(8,128)(2,1)S(1)}, bf16[192,128]{1,0:T(8,128)(2,1)S(1)}, u32[]{:S(2)}, u32[]{:S(2)}) collective-permute-start(bf16[192,128]{1,0:T(8,128)(2,1)S(1)} %get-tuple-element.28), channel_id=1, source_target_pairs={{0,1},{1,0},{2,3},{3,2},{4,5},{5,4},{6,7},{7,6},{8,9},{9,8},{10,11... | collective-permute-start | bytes 147464 | tf_op jit(solution)/shard_map/ppermute | solution.py:203
  27.7 7.8 %collective-permute-start.8 = (bf16[192,128]{1,0:T(8,128)(2,1)S(1)}, bf16[192,128]{1,0:T(8,128)(2,1)S(1)}, u32[]{:S(2)}, u32[]{:S(2)}) collective-permute-start(bf16[192,128]{1,0:T(8,128)(2,1)S(1)} %get-tuple-element.29), channel_id=1, source_target_pairs={{0,2},{1,3},{2,0},{3,1},{4,6},{5,7},{6,4},{7,5},{8,10},{9,11},{10,... | collective-permute-start | bytes 147464 | tf_op jit(solution)/shard_map/ppermute | solution.py:203
  29.3 9.0 %collective-permute-start.9 = (bf16[192,128]{1,0:T(8,128)(2,1)S(1)}, bf16[192,128]{1,0:T(8,128)(2,1)S(1)}, u32[]{:S(2)}, u32[]{:S(2)}) collective-permute-start(bf16[192,128]{1,0:T(8,128)(2,1)S(1)} %get-tuple-element.30), channel_id=1, source_target_pairs={{0,3},{1,2},{2,1},{3,0},{4,7},{5,6},{6,5},{7,4},{8,11},{9,10},{10,... | collective-permute-start | bytes 147464 | tf_op jit(solution)/shard_map/ppermute | solution.py:203
  30.6 7.7 %collective-permute-start.10 = (bf16[192,128]{1,0:T(8,128)(2,1)S(1)}, bf16[192,128]{1,0:T(8,128)(2,1)S(1)}, u32[]{:S(2)}, u32[]{:S(2)}) collective-permute-start(bf16[192,128]{1,0:T(8,128)(2,1)S(1)} %get-tuple-element.31), channel_id=1, source_target_pairs={{0,4},{1,5},{2,6},{3,7},{4,0},{5,1},{6,2},{7,3},{8,12},{9,13},{10,... | collective-permute-start | bytes 147464 | tf_op jit(solution)/shard_map/ppermute | solution.py:203
  33.1 7.6 %collective-permute-start.11 = (bf16[192,128]{1,0:T(8,128)(2,1)S(1)}, bf16[192,128]{1,0:T(8,128)(2,1)S(1)}, u32[]{:S(2)}, u32[]{:S(2)}) collective-permute-start(bf16[192,128]{1,0:T(8,128)(2,1)S(1)} %get-tuple-element.32), channel_id=1, source_target_pairs={{0,5},{1,4},{2,7},{3,6},{4,1},{5,0},{6,3},{7,2},{8,13},{9,12},{10,... | collective-permute-start | bytes 147464 | tf_op jit(solution)/shard_map/ppermute | solution.py:203
  33.5 8.9 %copy-start.2 = (bf16[192,128]{1,0:T(8,128)(2,1)}, bf16[192,128]{1,0:T(8,128)(2,1)S(1)}, u32[]{:S(2)}) copy-start(bf16[192,128]{1,0:T(8,128)(2,1)S(1)} %collective-permute-done.7.refs_1_) | copy-start | bytes 147460
  33.5 7.2 %collective-permute-start.12 = (bf16[192,128]{1,0:T(8,128)(2,1)S(1)}, bf16[192,128]{1,0:T(8,128)(2,1)S(1)}, u32[]{:S(2)}, u32[]{:S(2)}) collective-permute-start(bf16[192,128]{1,0:T(8,128)(2,1)S(1)} %get-tuple-element.33), channel_id=1, source_target_pairs={{0,6},{1,7},{2,4},{3,5},{4,2},{5,3},{6,0},{7,1},{8,14},{9,15},{10,... | collective-permute-start | bytes 147464 | tf_op jit(solution)/shard_map/ppermute | solution.py:203
  35.5 6.9 %copy-start.3 = (bf16[192,128]{1,0:T(8,128)(2,1)}, bf16[192,128]{1,0:T(8,128)(2,1)S(1)}, u32[]{:S(2)}) copy-start(bf16[192,128]{1,0:T(8,128)(2,1)S(1)} %collective-permute-done.8.refs_2_) | copy-start | bytes 147460
  35.5 6.9 %collective-permute-start.13 = (bf16[192,128]{1,0:T(8,128)(2,1)S(1)}, bf16[192,128]{1,0:T(8,128)(2,1)S(1)}, u32[]{:S(2)}, u32[]{:S(2)}) collective-permute-start(bf16[192,128]{1,0:T(8,128)(2,1)S(1)} %get-tuple-element.34), channel_id=1, source_target_pairs={{0,7},{1,6},{2,5},{3,4},{4,3},{5,2},{6,1},{7,0},{8,15},{9,14},{10,... | collective-permute-start | bytes 147464 | tf_op jit(solution)/shard_map/ppermute | solution.py:203
  38.3 4.1 %copy-start.4 = (bf16[192,128]{1,0:T(8,128)(2,1)}, bf16[192,128]{1,0:T(8,128)(2,1)S(1)}, u32[]{:S(2)}) copy-start(bf16[192,128]{1,0:T(8,128)(2,1)S(1)} %collective-permute-done.9.refs_3_) | copy-start | bytes 147460
  38.3 4.1 %copy-start.5 = (bf16[192,128]{1,0:T(8,128)(2,1)}, bf16[192,128]{1,0:T(8,128)(2,1)S(1)}, u32[]{:S(2)}) copy-start(bf16[192,128]{1,0:T(8,128)(2,1)S(1)} %collective-permute-done.10.refs_4_) | copy-start | bytes 147460
  40.7 1.7 %copy-start.6 = (bf16[192,128]{1,0:T(8,128)(2,1)}, bf16[192,128]{1,0:T(8,128)(2,1)S(1)}, u32[]{:S(2)}) copy-start(bf16[192,128]{1,0:T(8,128)(2,1)S(1)} %collective-permute-done.11.refs_5_) | copy-start | bytes 147460
  40.7 1.7 %copy-start.7 = (bf16[192,128]{1,0:T(8,128)(2,1)}, bf16[192,128]{1,0:T(8,128)(2,1)S(1)}, u32[]{:S(2)}) copy-start(bf16[192,128]{1,0:T(8,128)(2,1)S(1)} %collective-permute-done.12.refs_6_) | copy-start | bytes 147460
  42.4 0.6 %copy-start.8 = (bf16[192,128]{1,0:T(8,128)(2,1)}, bf16[192,128]{1,0:T(8,128)(2,1)S(1)}, u32[]{:S(2)}) copy-start(bf16[192,128]{1,0:T(8,128)(2,1)S(1)} %collective-permute-done.13.refs_7_) | copy-start | bytes 147460
  (1 other events, 0.6 us)

commit v4 on v3

--- a/solution.py
+++ b/solution.py
@@ -14,6 +14,7 @@
 GLOBAL = 2
 HEAD = 64
 LANES = 2 * HEAD
+PARTNERS = (0, 4, 6, 5, 7, 3, 2, 1)
 MASKED = -1e30
 
 
@@ -45,7 +46,8 @@
 
 
 def unpack_kernel(*refs):
-    in_refs, (gq_ref, gk_ref, gv_ref) = refs[:HEADS], refs[HEADS:]
+    in_refs = dict(zip(PARTNERS, refs[:HEADS]))
+    gq_ref, gk_ref, gv_ref = refs[HEADS:]
     rows = gq_ref.shape[0]
     low = low_lanes((rows, LANES))
     low_block = low_lanes((BLOCK, LANES))
@@ -70,7 +72,8 @@
 
 def attend_kernel(alone, scale, table_ref, *rest):
     if alone:
-        in_refs, out_refs = rest[:HEADS], rest[HEADS : 2 * HEADS]
+        in_refs = dict(zip(PARTNERS, rest[:HEADS]))
+        out_refs = rest[HEADS : 2 * HEADS]
         sent_ref, gq_ref, acc_ref = rest[2 * HEADS :]
         place = lax.rem(lax.axis_index("seq"), HEADS)
         for m in range(HEADS):
@@ -198,7 +201,7 @@
 def exchange(parts):
     group = lax.axis_size("seq")
     arrived = list(parts)
-    for m in reversed(range(1, HEADS)):
+    for m in PARTNERS[1:]:
         route = [(i, i ^ m) for i in range(group)]
         arrived[m] = lax.ppermute(parts[m], "seq", route)
     return arrived
@@ -233,6 +236,7 @@
         out_shape=[jax.ShapeDtypeStruct((2, rows, LANES), half_type)] * HEADS,
         in_specs=[vmem] * 4,
         out_specs=[vmem] * HEADS,
+        compiler_params=pltpu.CompilerParams(vmem_limit_bytes=8 * 2**20),
         name="pack",
     )(queries, key_vectors, value_vectors, output_grad)
     sent = [part.reshape(2, 2, BLOCK, LANES) for part in exchange(packed)]
@@ -249,9 +253,9 @@
                 pltpu.VMEM((ways, BLOCK, LANES), half_type),
                 pltpu.VMEM((blocks, BLOCK, LANES), jnp.float32),
             ],
-            compiler_params=pltpu.CompilerParams(vmem_limit_bytes=48 * 2**20),
+            compiler_params=pltpu.CompilerParams(vmem_limit_bytes=24 * 2**20),
             name="attend",
-        )(jnp.concatenate([rand_pick.reshape(-1), global_ids]), *sent)
+        )(jnp.concatenate([rand_pick.reshape(-1), global_ids]), *[sent[m] for m in PARTNERS])
     else:
         back = spread_out(kernel, sent, rand_pick, global_ids, ways, ranges, blocks)
     received = exchange(back)
@@ -260,8 +264,9 @@
         out_shape=[jax.ShapeDtypeStruct((rows, width), half_type)] * 3,
         in_specs=[vmem] * HEADS,
         out_specs=[vmem] * 3,
+        compiler_params=pltpu.CompilerParams(vmem_limit_bytes=8 * 2**20),
         name="unpack",
-    )(*received)
+    )(*[received[m] for m in PARTNERS])
 
 
 def spread_out(kernel, sent, rand_pick, global_ids, ways, ranges, blocks):
@@ -293,7 +298,7 @@
         ],
         in_specs=[smem, vmem, vmem],
         out_specs=[vmem] * 2,
-        compiler_params=pltpu.CompilerParams(vmem_limit_bytes=48 * 2**20),
+        compiler_params=pltpu.CompilerParams(vmem_limit_bytes=24 * 2**20),
         name="attend",
     )(table, sent, pool)
     total = totals[:blocks]

time: 45.1 us -> 40.4 us (0.90)
  waiting for transfers between devices: 11.2 us -> 6.08 us
  Pallas kernels: 6.98 us -> 4.24 us
  starting transfers between devices: 23.6 us -> 25.3 us
  local copies, waits for them, and re-layouts: 2.22 us -> 3.79 us
    ppermute x14, waiting for transfers between devices: 11.2 us -> 6.08 us  [exchange(): arrived[m] = lax.ppermute(parts[m], 'seq', route)]
    pallas_call x1, Pallas kernels: 2.02 us -> 0.24 us  [on_device(): pl.pallas_call(pack_kernel, out_shape=[jax.ShapeDtypeStruct((2, rows, LAN...]
    ppermute x14, starting transfers between devices: 23.6 us -> 25.3 us  [exchange(): arrived[m] = lax.ppermute(parts[m], 'seq', route)]
    unnamed x23 -> x13, local copies, waits for them, and re-layouts: 2.13 us -> 3.7 us
    pallas_call x1, Pallas kernels: 1.88 us -> 0.92 us  [on_device(): pl.pallas_call(unpack_kernel, out_shape=[jax.ShapeDtypeStruct((rows, widt...]
  transfers between devices with their start and end apart: 14 -> 14, of which waited for: 4 -> 8; matrix products, arithmetic and copies ran while one was open for 1% -> 1% of each run, Pallas kernels for 0% -> 0%
where the time goes in v4:
time: 40.4 us; the launch traced here: 40.2 us
  starting transfers between devices  25.3 us (63%)
  waiting for transfers between devices  6.08 us (15%)
  Pallas kernels  4.24 us (10%)
  local copies, waits for them, and re-layouts  3.79 us (9%)
  between operations  0.69 us (2%)
    ppermute x14, starting transfers between devices, exchange(): arrived[m] = lax.ppermute(parts[m], 'seq', route)  25.3 us
    ppermute x14, waiting for transfers between devices, exchange(): arrived[m] = lax.ppermute(parts[m], 'seq', route)  6.08 us
    unnamed x13, local copies, waits for them, and re-layouts  3.7 us
    pallas_call x1, Pallas kernels, on_device(): pl.pallas_call(kernel, out_shape=[jax.ShapeDtypeStruct((rows + BLOCK, LAN...  3.07 us
    pallas_call x1, Pallas kernels, on_device(): pl.pallas_call(unpack_kernel, out_shape=[jax.ShapeDtypeStruct((rows, widt...  0.92 us
  transfers between devices with their start and end apart: 14, of which 8 were waited for; matrix products, arithmetic and copies ran while one was open for 1% of the time, Pallas kernels for 0%

profile of v4, /device:TPU:0, one launch (start us, length us, event | category | flops | bytes accessed | tf_op | source)
XLA Modules:
  0.0 40.2 jit_solution(16015735928880474848)
XLA Ops:
  0.6 0.9 %copy-done = bf16[128,512]{1,0:T(8,128)(2,1)S(1)} copy-done((bf16[128,512]{1,0:T(8,128)(2,1)S(1)}, bf16[128,512]{1,0:T(8,128)(2,1)}, u32[]{:S(2)}) %copy-start) | copy-done | bytes 131096
  1.5 0.9 %copy-done.1 = bf16[128,512]{1,0:T(8,128)(2,1)S(1)} copy-done((bf16[128,512]{1,0:T(8,128)(2,1)S(1)}, bf16[128,512]{1,0:T(8,128)(2,1)}, u32[]{:S(2)}) %copy-start.1) | copy-done | bytes 131096
  2.4 0.9 %copy-done.2 = bf16[128,512]{1,0:T(8,128)(2,1)S(1)} copy-done((bf16[128,512]{1,0:T(8,128)(2,1)S(1)}, bf16[128,512]{1,0:T(8,128)(2,1)}, u32[]{:S(2)}) %copy-start.2) | copy-done | bytes 131096
  3.3 0.9 %copy-done.3 = bf16[128,512]{1,0:T(8,128)(2,1)S(1)} copy-done((bf16[128,512]{1,0:T(8,128)(2,1)S(1)}, bf16[128,512]{1,0:T(8,128)(2,1)}, u32[]{:S(2)}) %copy-start.3) | copy-done | bytes 131096
  4.5 4.1 %collective-permute-start = (bf16[2,128,128]{2,1,0:T(8,128)(2,1)S(1)}, bf16[2,128,128]{2,1,0:T(8,128)(2,1)S(1)}, u32[]{:S(2)}, u32[]{:S(2)}) collective-permute-start(bf16[2,128,128]{2,1,0:T(8,128)(2,1)S(1)} %get-tuple-element.20), channel_id=1, source_target_pairs={{0,4},{1,5},{2,6},{3,7},{4,0},{5,1},{6,2},{7,3},{8,12},{9,13},{10,... | collective-permute-start | bytes 196616 | tf_op jit(solution)/shard_map/ppermute | solution.py:206
  8.6 1.3 %collective-permute-start.1 = (bf16[2,128,128]{2,1,0:T(8,128)(2,1)S(1)}, bf16[2,128,128]{2,1,0:T(8,128)(2,1)S(1)}, u32[]{:S(2)}, u32[]{:S(2)}) collective-permute-start(bf16[2,128,128]{2,1,0:T(8,128)(2,1)S(1)} %get-tuple-element.21), channel_id=1, source_target_pairs={{0,6},{1,7},{2,4},{3,5},{4,2},{5,3},{6,0},{7,1},{8,14},{9,15},{10,... | collective-permute-start | bytes 196616 | tf_op jit(solution)/shard_map/ppermute | solution.py:206
  10.0 2.6 %collective-permute-start.2 = (bf16[2,128,128]{2,1,0:T(8,128)(2,1)S(1)}, bf16[2,128,128]{2,1,0:T(8,128)(2,1)S(1)}, u32[]{:S(2)}, u32[]{:S(2)}) collective-permute-start(bf16[2,128,128]{2,1,0:T(8,128)(2,1)S(1)} %get-tuple-element.22), channel_id=1, source_target_pairs={{0,5},{1,4},{2,7},{3,6},{4,1},{5,0},{6,3},{7,2},{8,13},{9,12},{10,... | collective-permute-start | bytes 196616 | tf_op jit(solution)/shard_map/ppermute | solution.py:206
  12.6 0.9 %collective-permute-start.3 = (bf16[2,128,128]{2,1,0:T(8,128)(2,1)S(1)}, bf16[2,128,128]{2,1,0:T(8,128)(2,1)S(1)}, u32[]{:S(2)}, u32[]{:S(2)}) collective-permute-start(bf16[2,128,128]{2,1,0:T(8,128)(2,1)S(1)} %get-tuple-element.23), channel_id=1, source_target_pairs={{0,7},{1,6},{2,5},{3,4},{4,3},{5,2},{6,1},{7,0},{8,15},{9,14},{10,... | collective-permute-start | bytes 196616 | tf_op jit(solution)/shard_map/ppermute | solution.py:206
  13.4 1.8 %collective-permute-start.4 = (bf16[2,128,128]{2,1,0:T(8,128)(2,1)S(1)}, bf16[2,128,128]{2,1,0:T(8,128)(2,1)S(1)}, u32[]{:S(2)}, u32[]{:S(2)}) collective-permute-start(bf16[2,128,128]{2,1,0:T(8,128)(2,1)S(1)} %get-tuple-element.24), channel_id=1, source_target_pairs={{0,3},{1,2},{2,1},{3,0},{4,7},{5,6},{6,5},{7,4},{8,11},{9,10},{10,... | collective-permute-start | bytes 196616 | tf_op jit(solution)/shard_map/ppermute | solution.py:206
  15.5 1.4 %collective-permute-start.5 = (bf16[2,128,128]{2,1,0:T(8,128)(2,1)S(1)}, bf16[2,128,128]{2,1,0:T(8,128)(2,1)S(1)}, u32[]{:S(2)}, u32[]{:S(2)}) collective-permute-start(bf16[2,128,128]{2,1,0:T(8,128)(2,1)S(1)} %get-tuple-element.25), channel_id=1, source_target_pairs={{0,2},{1,3},{2,0},{3,1},{4,6},{5,7},{6,4},{7,5},{8,10},{9,11},{10,... | collective-permute-start | bytes 196616 | tf_op jit(solution)/shard_map/ppermute | solution.py:206
  16.8 2.0 %collective-permute-start.6 = (bf16[2,128,128]{2,1,0:T(8,128)(2,1)S(1)}, bf16[2,128,128]{2,1,0:T(8,128)(2,1)S(1)}, u32[]{:S(2)}, u32[]{:S(2)}) collective-permute-start(bf16[2,128,128]{2,1,0:T(8,128)(2,1)S(1)} %get-tuple-element.26), channel_id=1, source_target_pairs={{0,1},{1,0},{2,3},{3,2},{4,5},{5,4},{6,7},{7,6},{8,9},{9,8},{10,11... | collective-permute-start | bytes 196616 | tf_op jit(solution)/shard_map/ppermute | solution.py:206
  18.9 1.8 %collective-permute-done.2 = bf16[2,128,128]{2,1,0:T(8,128)(2,1)S(1)} collective-permute-done((bf16[2,128,128]{2,1,0:T(8,128)(2,1)S(1)}, bf16[2,128,128]{2,1,0:T(8,128)(2,1)S(1)}, u32[]{:S(2)}, u32[]{:S(2)}) %collective-permute-start.2) | collective-permute-done | bytes 65568 | tf_op jit(solution)/shard_map/ppermute | solution.py:206
  20.7 0.5 %collective-permute-done.4 = bf16[2,128,128]{2,1,0:T(8,128)(2,1)S(1)} collective-permute-done((bf16[2,128,128]{2,1,0:T(8,128)(2,1)S(1)}, bf16[2,128,128]{2,1,0:T(8,128)(2,1)S(1)}, u32[]{:S(2)}, u32[]{:S(2)}) %collective-permute-start.4) | collective-permute-done | bytes 65568 | tf_op jit(solution)/shard_map/ppermute | solution.py:206
  21.5 0.6 %collective-permute-done.6 = bf16[2,128,128]{2,1,0:T(8,128)(2,1)S(1)} collective-permute-done((bf16[2,128,128]{2,1,0:T(8,128)(2,1)S(1)}, bf16[2,128,128]{2,1,0:T(8,128)(2,1)S(1)}, u32[]{:S(2)}, u32[]{:S(2)}) %collective-permute-start.6) | collective-permute-done | bytes 65568 | tf_op jit(solution)/shard_map/ppermute | solution.py:206
  22.1 3.1 %attend.1 = (bf16[192,128]{1,0:T(8,128)(2,1)S(1)}, bf16[192,128]{1,0:T(8,128)(2,1)S(1)}, bf16[192,128]{1,0:T(8,128)(2,1)S(1)}, bf16[192,128]{1,0:T(8,128)(2,1)S(...) custom-call(s32[50]{0:T(128)S(1)} %pad_add_fusion.table_ref, ...), custom_call_target="tpu_custom_call" | custom-call | tf_op jit(solution)/shard_map/attend/pallas_call | solution.py:246
  25.2 3.2 %collective-permute-start.7 = (bf16[192,128]{1,0:T(8,128)(2,1)S(1)}, bf16[192,128]{1,0:T(8,128)(2,1)S(1)}, u32[]{:S(2)}, u32[]{:S(2)}) collective-permute-start(bf16[192,128]{1,0:T(8,128)(2,1)S(1)} %get-tuple-element.28), channel_id=1, source_target_pairs={{0,4},{1,5},{2,6},{3,7},{4,0},{5,1},{6,2},{7,3},{8,12},{9,13},{10,... | collective-permute-start | bytes 147464 | tf_op jit(solution)/shard_map/ppermute | solution.py:206
  28.9 1.8 %collective-permute-start.9 = (bf16[192,128]{1,0:T(8,128)(2,1)S(1)}, bf16[192,128]{1,0:T(8,128)(2,1)S(1)}, u32[]{:S(2)}, u32[]{:S(2)}) collective-permute-start(bf16[192,128]{1,0:T(8,128)(2,1)S(1)} %get-tuple-element.30), channel_id=1, source_target_pairs={{0,5},{1,4},{2,7},{3,6},{4,1},{5,0},{6,3},{7,2},{8,13},{9,12},{10,... | collective-permute-start | bytes 147464 | tf_op jit(solution)/shard_map/ppermute | solution.py:206
  30.7 2.3 %collective-permute-start.10 = (bf16[192,128]{1,0:T(8,128)(2,1)S(1)}, bf16[192,128]{1,0:T(8,128)(2,1)S(1)}, u32[]{:S(2)}, u32[]{:S(2)}) collective-permute-start(bf16[192,128]{1,0:T(8,128)(2,1)S(1)} %get-tuple-element.31), channel_id=1, source_target_pairs={{0,7},{1,6},{2,5},{3,4},{4,3},{5,2},{6,1},{7,0},{8,15},{9,14},{10,... | collective-permute-start | bytes 147464 | tf_op jit(solution)/shard_map/ppermute | solution.py:206
  33.0 0.9 %collective-permute-start.11 = (bf16[192,128]{1,0:T(8,128)(2,1)S(1)}, bf16[192,128]{1,0:T(8,128)(2,1)S(1)}, u32[]{:S(2)}, u32[]{:S(2)}) collective-permute-start(bf16[192,128]{1,0:T(8,128)(2,1)S(1)} %get-tuple-element.32), channel_id=1, source_target_pairs={{0,3},{1,2},{2,1},{3,0},{4,7},{5,6},{6,5},{7,4},{8,11},{9,10},{10,... | collective-permute-start | bytes 147464 | tf_op jit(solution)/shard_map/ppermute | solution.py:206
  33.9 1.3 %collective-permute-start.12 = (bf16[192,128]{1,0:T(8,128)(2,1)S(1)}, bf16[192,128]{1,0:T(8,128)(2,1)S(1)}, u32[]{:S(2)}, u32[]{:S(2)}) collective-permute-start(bf16[192,128]{1,0:T(8,128)(2,1)S(1)} %get-tuple-element.33), channel_id=1, source_target_pairs={{0,2},{1,3},{2,0},{3,1},{4,6},{5,7},{6,4},{7,5},{8,10},{9,11},{10,... | collective-permute-start | bytes 147464 | tf_op jit(solution)/shard_map/ppermute | solution.py:206
  35.2 1.3 %collective-permute-start.13 = (bf16[192,128]{1,0:T(8,128)(2,1)S(1)}, bf16[192,128]{1,0:T(8,128)(2,1)S(1)}, u32[]{:S(2)}, u32[]{:S(2)}) collective-permute-start(bf16[192,128]{1,0:T(8,128)(2,1)S(1)} %get-tuple-element.34), channel_id=1, source_target_pairs={{0,1},{1,0},{2,3},{3,2},{4,5},{5,4},{6,7},{7,6},{8,9},{9,8},{10,11... | collective-permute-start | bytes 147464 | tf_op jit(solution)/shard_map/ppermute | solution.py:206
  36.8 1.2 %collective-permute-done.10.refs_4_ = bf16[192,128]{1,0:T(8,128)(2,1)S(1)} collective-permute-done((bf16[192,128]{1,0:T(8,128)(2,1)S(1)}, bf16[192,128]{1,0:T(8,128)(2,1)S(1)}, u32[]{:S(2)}, u32[]{:S(2)}) %collective-permute-start.10) | collective-permute-done | bytes 49184 | tf_op jit(solution)/shard_map/ppermute | solution.py:206
  38.2 1.1 %collective-permute-done.13.refs_7_ = bf16[192,128]{1,0:T(8,128)(2,1)S(1)} collective-permute-done((bf16[192,128]{1,0:T(8,128)(2,1)S(1)}, bf16[192,128]{1,0:T(8,128)(2,1)S(1)}, u32[]{:S(2)}, u32[]{:S(2)}) %collective-permute-start.13) | collective-permute-done | bytes 49184 | tf_op jit(solution)/shard_map/ppermute | solution.py:206
  39.3 0.9 %unpack.1 = (bf16[128,512]{1,0:T(8,128)(2,1)}, bf16[128,512]{1,0:T(8,128)(2,1)}, bf16[128,512]{1,0:T(8,128)(2,1)}) custom-call(bf16[192,128]{1,0:T(8,128)(2,1)S(1)} %get-tuple-element.27.refs_0_, bf16[192,128]{1,0:T(8,128)(2,1)S(1)} %collective-permute-done.7.refs_1_, bf16[192,128]{1,0:T(8,128)(2,1)S(1)} %collective-permute-done.8.refs_2_, ...), custom_call_target="tpu_custom_call" | custom-call | tf_op jit(solution)/shard_map/unpack/pallas_call | solution.py:262
  (22 shorter events, 1.9 us)
Async XLA Ops:
  0.6 0.9 %copy-start = (bf16[128,512]{1,0:T(8,128)(2,1)S(1)}, bf16[128,512]{1,0:T(8,128)(2,1)}, u32[]{:S(2)}) copy-start(bf16[128,512]{1,0:T(8,128)(2,1)} %q_ref.1) | copy-start | bytes 393220
  1.5 0.9 %copy-start.1 = (bf16[128,512]{1,0:T(8,128)(2,1)S(1)}, bf16[128,512]{1,0:T(8,128)(2,1)}, u32[]{:S(2)}) copy-start(bf16[128,512]{1,0:T(8,128)(2,1)} %k_ref.1) | copy-start | bytes 393220
  2.4 0.9 %copy-start.2 = (bf16[128,512]{1,0:T(8,128)(2,1)S(1)}, bf16[128,512]{1,0:T(8,128)(2,1)}, u32[]{:S(2)}) copy-start(bf16[128,512]{1,0:T(8,128)(2,1)} %v_ref.1) | copy-start | bytes 393220
  3.3 0.9 %copy-start.3 = (bf16[128,512]{1,0:T(8,128)(2,1)S(1)}, bf16[128,512]{1,0:T(8,128)(2,1)}, u32[]{:S(2)}) copy-start(bf16[128,512]{1,0:T(8,128)(2,1)} %g_ref.1) | copy-start | bytes 393220
  4.5 10.9 %collective-permute-start = (bf16[2,128,128]{2,1,0:T(8,128)(2,1)S(1)}, bf16[2,128,128]{2,1,0:T(8,128)(2,1)S(1)}, u32[]{:S(2)}, u32[]{:S(2)}) collective-permute-start(bf16[2,128,128]{2,1,0:T(8,128)(2,1)S(1)} %get-tuple-element.20), channel_id=1, source_target_pairs={{0,4},{1,5},{2,6},{3,7},{4,0},{5,1},{6,2},{7,3},{8,12},{9,13},{10,... | collective-permute-start | bytes 196616 | tf_op jit(solution)/shard_map/ppermute | solution.py:206
  8.6 8.2 %collective-permute-start.1 = (bf16[2,128,128]{2,1,0:T(8,128)(2,1)S(1)}, bf16[2,128,128]{2,1,0:T(8,128)(2,1)S(1)}, u32[]{:S(2)}, u32[]{:S(2)}) collective-permute-start(bf16[2,128,128]{2,1,0:T(8,128)(2,1)S(1)} %get-tuple-element.21), channel_id=1, source_target_pairs={{0,6},{1,7},{2,4},{3,5},{4,2},{5,3},{6,0},{7,1},{8,14},{9,15},{10,... | collective-permute-start | bytes 196616 | tf_op jit(solution)/shard_map/ppermute | solution.py:206
  9.9 5.3 %copy-start.4 = (s32[16,3]{0,1:T(4,128)S(1)}, s32[16,3]{0,1:T(4,128)}, u32[]{:S(2)}) copy-start(s32[16,3]{0,1:T(4,128)} %param.10) | copy-start | bytes 580
  10.0 10.7 %collective-permute-start.2 = (bf16[2,128,128]{2,1,0:T(8,128)(2,1)S(1)}, bf16[2,128,128]{2,1,0:T(8,128)(2,1)S(1)}, u32[]{:S(2)}, u32[]{:S(2)}) collective-permute-start(bf16[2,128,128]{2,1,0:T(8,128)(2,1)S(1)} %get-tuple-element.22), channel_id=1, source_target_pairs={{0,5},{1,4},{2,7},{3,6},{4,1},{5,0},{6,3},{7,2},{8,13},{9,12},{10,... | collective-permute-start | bytes 196616 | tf_op jit(solution)/shard_map/ppermute | solution.py:206
  12.6 8.1 %collective-permute-start.3 = (bf16[2,128,128]{2,1,0:T(8,128)(2,1)S(1)}, bf16[2,128,128]{2,1,0:T(8,128)(2,1)S(1)}, u32[]{:S(2)}, u32[]{:S(2)}) collective-permute-start(bf16[2,128,128]{2,1,0:T(8,128)(2,1)S(1)} %get-tuple-element.23), channel_id=1, source_target_pairs={{0,7},{1,6},{2,5},{3,4},{4,3},{5,2},{6,1},{7,0},{8,15},{9,14},{10,... | collective-permute-start | bytes 196616 | tf_op jit(solution)/shard_map/ppermute | solution.py:206
  13.4 7.8 %collective-permute-start.4 = (bf16[2,128,128]{2,1,0:T(8,128)(2,1)S(1)}, bf16[2,128,128]{2,1,0:T(8,128)(2,1)S(1)}, u32[]{:S(2)}, u32[]{:S(2)}) collective-permute-start(bf16[2,128,128]{2,1,0:T(8,128)(2,1)S(1)} %get-tuple-element.24), channel_id=1, source_target_pairs={{0,3},{1,2},{2,1},{3,0},{4,7},{5,6},{6,5},{7,4},{8,11},{9,10},{10,... | collective-permute-start | bytes 196616 | tf_op jit(solution)/shard_map/ppermute | solution.py:206
  15.5 3.3 %copy-start.5 = (s32[2]{0:T(128)S(1)}, s32[2]{0:T(128)}, u32[]{:S(2)}) copy-start(s32[2]{0:T(128)} %param.11) | copy-start | bytes 28
  15.5 6.1 %collective-permute-start.5 = (bf16[2,128,128]{2,1,0:T(8,128)(2,1)S(1)}, bf16[2,128,128]{2,1,0:T(8,128)(2,1)S(1)}, u32[]{:S(2)}, u32[]{:S(2)}) collective-permute-start(bf16[2,128,128]{2,1,0:T(8,128)(2,1)S(1)} %get-tuple-element.25), channel_id=1, source_target_pairs={{0,2},{1,3},{2,0},{3,1},{4,6},{5,7},{6,4},{7,5},{8,10},{9,11},{10,... | collective-permute-start | bytes 196616 | tf_op jit(solution)/shard_map/ppermute | solution.py:206
  16.8 5.3 %collective-permute-start.6 = (bf16[2,128,128]{2,1,0:T(8,128)(2,1)S(1)}, bf16[2,128,128]{2,1,0:T(8,128)(2,1)S(1)}, u32[]{:S(2)}, u32[]{:S(2)}) collective-permute-start(bf16[2,128,128]{2,1,0:T(8,128)(2,1)S(1)} %get-tuple-element.26), channel_id=1, source_target_pairs={{0,1},{1,0},{2,3},{3,2},{4,5},{5,4},{6,7},{7,6},{8,9},{9,8},{10,11... | collective-permute-start | bytes 196616 | tf_op jit(solution)/shard_map/ppermute | solution.py:206
  25.2 8.7 %collective-permute-start.7 = (bf16[192,128]{1,0:T(8,128)(2,1)S(1)}, bf16[192,128]{1,0:T(8,128)(2,1)S(1)}, u32[]{:S(2)}, u32[]{:S(2)}) collective-permute-start(bf16[192,128]{1,0:T(8,128)(2,1)S(1)} %get-tuple-element.28), channel_id=1, source_target_pairs={{0,4},{1,5},{2,6},{3,7},{4,0},{5,1},{6,2},{7,3},{8,12},{9,13},{10,... | collective-permute-start | bytes 147464 | tf_op jit(solution)/shard_map/ppermute | solution.py:206
  28.4 6.8 %collective-permute-start.8 = (bf16[192,128]{1,0:T(8,128)(2,1)S(1)}, bf16[192,128]{1,0:T(8,128)(2,1)S(1)}, u32[]{:S(2)}, u32[]{:S(2)}) collective-permute-start(bf16[192,128]{1,0:T(8,128)(2,1)S(1)} %get-tuple-element.29), channel_id=1, source_target_pairs={{0,6},{1,7},{2,4},{3,5},{4,2},{5,3},{6,0},{7,1},{8,14},{9,15},{10,... | collective-permute-start | bytes 147464 | tf_op jit(solution)/shard_map/ppermute | solution.py:206
  28.9 7.8 %collective-permute-start.9 = (bf16[192,128]{1,0:T(8,128)(2,1)S(1)}, bf16[192,128]{1,0:T(8,128)(2,1)S(1)}, u32[]{:S(2)}, u32[]{:S(2)}) collective-permute-start(bf16[192,128]{1,0:T(8,128)(2,1)S(1)} %get-tuple-element.30), channel_id=1, source_target_pairs={{0,5},{1,4},{2,7},{3,6},{4,1},{5,0},{6,3},{7,2},{8,13},{9,12},{10,... | collective-permute-start | bytes 147464 | tf_op jit(solution)/shard_map/ppermute | solution.py:206
  30.7 7.2 %collective-permute-start.10 = (bf16[192,128]{1,0:T(8,128)(2,1)S(1)}, bf16[192,128]{1,0:T(8,128)(2,1)S(1)}, u32[]{:S(2)}, u32[]{:S(2)}) collective-permute-start(bf16[192,128]{1,0:T(8,128)(2,1)S(1)} %get-tuple-element.31), channel_id=1, source_target_pairs={{0,7},{1,6},{2,5},{3,4},{4,3},{5,2},{6,1},{7,0},{8,15},{9,14},{10,... | collective-permute-start | bytes 147464 | tf_op jit(solution)/shard_map/ppermute | solution.py:206
  33.0 5.2 %collective-permute-start.11 = (bf16[192,128]{1,0:T(8,128)(2,1)S(1)}, bf16[192,128]{1,0:T(8,128)(2,1)S(1)}, u32[]{:S(2)}, u32[]{:S(2)}) collective-permute-start(bf16[192,128]{1,0:T(8,128)(2,1)S(1)} %get-tuple-element.32), channel_id=1, source_target_pairs={{0,3},{1,2},{2,1},{3,0},{4,7},{5,6},{6,5},{7,4},{8,11},{9,10},{10,... | collective-permute-start | bytes 147464 | tf_op jit(solution)/shard_map/ppermute | solution.py:206
  33.9 4.3 %collective-permute-start.12 = (bf16[192,128]{1,0:T(8,128)(2,1)S(1)}, bf16[192,128]{1,0:T(8,128)(2,1)S(1)}, u32[]{:S(2)}, u32[]{:S(2)}) collective-permute-start(bf16[192,128]{1,0:T(8,128)(2,1)S(1)} %get-tuple-element.33), channel_id=1, source_target_pairs={{0,2},{1,3},{2,0},{3,1},{4,6},{5,7},{6,4},{7,5},{8,10},{9,11},{10,... | collective-permute-start | bytes 147464 | tf_op jit(solution)/shard_map/ppermute | solution.py:206
  35.2 4.1 %collective-permute-start.13 = (bf16[192,128]{1,0:T(8,128)(2,1)S(1)}, bf16[192,128]{1,0:T(8,128)(2,1)S(1)}, u32[]{:S(2)}, u32[]{:S(2)}) collective-permute-start(bf16[192,128]{1,0:T(8,128)(2,1)S(1)} %get-tuple-element.34), channel_id=1, source_target_pairs={{0,1},{1,0},{2,3},{3,2},{4,5},{5,4},{6,7},{7,6},{8,9},{9,8},{10,11... | collective-permute-start | bytes 147464 | tf_op jit(solution)/shard_map/ppermute | solution.py:206

commit v5 on v4

--- a/solution.py
+++ b/solution.py
@@ -26,11 +26,18 @@
     return pltpu.roll(block, HEAD, 1)
 
 
-def pack_kernel(q_ref, k_ref, v_ref, g_ref, *out_refs):
-    rows = q_ref.shape[0]
+def pack_kernel(*refs):
+    out_refs, held_ref, sems = refs[4 : 4 + HEADS], refs[-2], refs[-1]
+    copies = [pltpu.make_async_copy(refs[i], held_ref.at[i], sems.at[i]) for i in range(4)]
+    for copy in copies:
+        copy.start()
+    q_ref, k_ref, v_ref, g_ref = [held_ref.at[i] for i in range(4)]
+    rows = held_ref.shape[1]
     low = low_lanes((rows, LANES))
     place = lax.rem(lax.axis_index("seq"), HEADS)
     odd_place = lax.rem(place, 2) == 1
+    for copy in copies:
+        copy.wait()
     for near in range(HEADS // 2):
         pair = lax.bitwise_xor(place // 2, near)
         lanes = pl.ds(pl.multiple_of(pair * LANES, LANES), LANES)
@@ -234,8 +241,12 @@
     packed = pl.pallas_call(
         pack_kernel,
         out_shape=[jax.ShapeDtypeStruct((2, rows, LANES), half_type)] * HEADS,
-        in_specs=[vmem] * 4,
+        in_specs=[pl.BlockSpec(memory_space=pltpu.HBM)] * 4,
         out_specs=[vmem] * HEADS,
+        scratch_shapes=[
+            pltpu.VMEM((4, rows, width), half_type),
+            pltpu.SemaphoreType.DMA((4,)),
+        ],
         compiler_params=pltpu.CompilerParams(vmem_limit_bytes=8 * 2**20),
         name="pack",
     )(queries, key_vectors, value_vectors, output_grad)

time: 40.4 us -> 41.1 us (1.017)
  Pallas kernels: 4.24 us -> 4.92 us
    pallas_call x1, Pallas kernels: 0.24 us -> 0.92 us  [on_device(): pl.pallas_call(pack_kernel, out_shape=[jax.ShapeDtypeStruct((2, rows, LAN...]
where the time goes in v5:
time: 41.1 us; the launch traced here: 40.9 us
  starting transfers between devices  25.3 us (62%)
  waiting for transfers between devices  6.08 us (15%)
  Pallas kernels  4.92 us (12%)
  local copies, waits for them, and re-layouts  3.79 us (9%)
  between operations  0.69 us (2%)
    ppermute x14, starting transfers between devices, exchange(): arrived[m] = lax.ppermute(parts[m], 'seq', route)  25.3 us
    ppermute x14, waiting for transfers between devices, exchange(): arrived[m] = lax.ppermute(parts[m], 'seq', route)  6.08 us
    unnamed x13, local copies, waits for them, and re-layouts  3.7 us
    pallas_call x1, Pallas kernels, on_device(): pl.pallas_call(kernel, out_shape=[jax.ShapeDtypeStruct((rows + BLOCK, LAN...  3.07 us
    pallas_call x1, Pallas kernels, on_device(): pl.pallas_call(unpack_kernel, out_shape=[jax.ShapeDtypeStruct((rows, widt...  0.92 us
    pallas_call x1, Pallas kernels, on_device(): pl.pallas_call(pack_kernel, out_shape=[jax.ShapeDtypeStruct((2, rows, LAN...  0.92 us
  transfers between devices with their start and end apart: 14, of which 8 were waited for; matrix products, arithmetic and copies ran while one was open for 1% of the time, Pallas kernels for 0%

profile of v5, /device:TPU:0, one launch (start us, length us, event | category | flops | bytes accessed | tf_op | source)
XLA Modules:
  0.0 40.9 jit_solution(5780811751684556982)
XLA Ops:
  0.6 0.9 %copy-done = bf16[128,512]{1,0:T(8,128)(2,1)S(1)} copy-done((bf16[128,512]{1,0:T(8,128)(2,1)S(1)}, bf16[128,512]{1,0:T(8,128)(2,1)}, u32[]{:S(2)}) %copy-start) | copy-done | bytes 131096
  1.5 0.9 %copy-done.1 = bf16[128,512]{1,0:T(8,128)(2,1)S(1)} copy-done((bf16[128,512]{1,0:T(8,128)(2,1)S(1)}, bf16[128,512]{1,0:T(8,128)(2,1)}, u32[]{:S(2)}) %copy-start.1) | copy-done | bytes 131096
  2.4 0.9 %copy-done.2 = bf16[128,512]{1,0:T(8,128)(2,1)S(1)} copy-done((bf16[128,512]{1,0:T(8,128)(2,1)S(1)}, bf16[128,512]{1,0:T(8,128)(2,1)}, u32[]{:S(2)}) %copy-start.2) | copy-done | bytes 131096
  3.3 0.9 %copy-done.3 = bf16[128,512]{1,0:T(8,128)(2,1)S(1)} copy-done((bf16[128,512]{1,0:T(8,128)(2,1)S(1)}, bf16[128,512]{1,0:T(8,128)(2,1)}, u32[]{:S(2)}) %copy-start.3) | copy-done | bytes 131096
  4.3 0.9 %pack.1 = (bf16[2,128,128]{2,1,0:T(8,128)(2,1)S(1)}, bf16[2,128,128]{2,1,0:T(8,128)(2,1)S(1)}, bf16[2,128,128]{2,1,0:T(8,128)(2,1)S(1)}, bf16[2,128,128]{2,1,0:T...) custom-call(bf16[128,512]{1,0:T(8,128)(2,1)S(1)} %copy-done, ...), custom_call_target="tpu_custom_call" | custom-call | tf_op jit(solution)/shard_map/pack/pallas_call | solution.py:241
  5.2 4.1 %collective-permute-start = (bf16[2,128,128]{2,1,0:T(8,128)(2,1)S(1)}, bf16[2,128,128]{2,1,0:T(8,128)(2,1)S(1)}, u32[]{:S(2)}, u32[]{:S(2)}) collective-permute-start(bf16[2,128,128]{2,1,0:T(8,128)(2,1)S(1)} %get-tuple-element.20), channel_id=1, source_target_pairs={{0,4},{1,5},{2,6},{3,7},{4,0},{5,1},{6,2},{7,3},{8,12},{9,13},{10,... | collective-permute-start | bytes 196616 | tf_op jit(solution)/shard_map/ppermute | solution.py:213
  9.3 1.4 %collective-permute-start.1 = (bf16[2,128,128]{2,1,0:T(8,128)(2,1)S(1)}, bf16[2,128,128]{2,1,0:T(8,128)(2,1)S(1)}, u32[]{:S(2)}, u32[]{:S(2)}) collective-permute-start(bf16[2,128,128]{2,1,0:T(8,128)(2,1)S(1)} %get-tuple-element.21), channel_id=1, source_target_pairs={{0,6},{1,7},{2,4},{3,5},{4,2},{5,3},{6,0},{7,1},{8,14},{9,15},{10,... | collective-permute-start | bytes 196616 | tf_op jit(solution)/shard_map/ppermute | solution.py:213
  10.6 2.6 %collective-permute-start.2 = (bf16[2,128,128]{2,1,0:T(8,128)(2,1)S(1)}, bf16[2,128,128]{2,1,0:T(8,128)(2,1)S(1)}, u32[]{:S(2)}, u32[]{:S(2)}) collective-permute-start(bf16[2,128,128]{2,1,0:T(8,128)(2,1)S(1)} %get-tuple-element.22), channel_id=1, source_target_pairs={{0,5},{1,4},{2,7},{3,6},{4,1},{5,0},{6,3},{7,2},{8,13},{9,12},{10,... | collective-permute-start | bytes 196616 | tf_op jit(solution)/shard_map/ppermute | solution.py:213
  13.2 0.9 %collective-permute-start.3 = (bf16[2,128,128]{2,1,0:T(8,128)(2,1)S(1)}, bf16[2,128,128]{2,1,0:T(8,128)(2,1)S(1)}, u32[]{:S(2)}, u32[]{:S(2)}) collective-permute-start(bf16[2,128,128]{2,1,0:T(8,128)(2,1)S(1)} %get-tuple-element.23), channel_id=1, source_target_pairs={{0,7},{1,6},{2,5},{3,4},{4,3},{5,2},{6,1},{7,0},{8,15},{9,14},{10,... | collective-permute-start | bytes 196616 | tf_op jit(solution)/shard_map/ppermute | solution.py:213
  14.1 1.8 %collective-permute-start.4 = (bf16[2,128,128]{2,1,0:T(8,128)(2,1)S(1)}, bf16[2,128,128]{2,1,0:T(8,128)(2,1)S(1)}, u32[]{:S(2)}, u32[]{:S(2)}) collective-permute-start(bf16[2,128,128]{2,1,0:T(8,128)(2,1)S(1)} %get-tuple-element.24), channel_id=1, source_target_pairs={{0,3},{1,2},{2,1},{3,0},{4,7},{5,6},{6,5},{7,4},{8,11},{9,10},{10,... | collective-permute-start | bytes 196616 | tf_op jit(solution)/shard_map/ppermute | solution.py:213
  16.1 1.4 %collective-permute-start.5 = (bf16[2,128,128]{2,1,0:T(8,128)(2,1)S(1)}, bf16[2,128,128]{2,1,0:T(8,128)(2,1)S(1)}, u32[]{:S(2)}, u32[]{:S(2)}) collective-permute-start(bf16[2,128,128]{2,1,0:T(8,128)(2,1)S(1)} %get-tuple-element.25), channel_id=1, source_target_pairs={{0,2},{1,3},{2,0},{3,1},{4,6},{5,7},{6,4},{7,5},{8,10},{9,11},{10,... | collective-permute-start | bytes 196616 | tf_op jit(solution)/shard_map/ppermute | solution.py:213
  17.5 2.0 %collective-permute-start.6 = (bf16[2,128,128]{2,1,0:T(8,128)(2,1)S(1)}, bf16[2,128,128]{2,1,0:T(8,128)(2,1)S(1)}, u32[]{:S(2)}, u32[]{:S(2)}) collective-permute-start(bf16[2,128,128]{2,1,0:T(8,128)(2,1)S(1)} %get-tuple-element.26), channel_id=1, source_target_pairs={{0,1},{1,0},{2,3},{3,2},{4,5},{5,4},{6,7},{7,6},{8,9},{9,8},{10,11... | collective-permute-start | bytes 196616 | tf_op jit(solution)/shard_map/ppermute | solution.py:213
  19.5 1.8 %collective-permute-done.2 = bf16[2,128,128]{2,1,0:T(8,128)(2,1)S(1)} collective-permute-done((bf16[2,128,128]{2,1,0:T(8,128)(2,1)S(1)}, bf16[2,128,128]{2,1,0:T(8,128)(2,1)S(1)}, u32[]{:S(2)}, u32[]{:S(2)}) %collective-permute-start.2) | collective-permute-done | bytes 65568 | tf_op jit(solution)/shard_map/ppermute | solution.py:213
  22.2 0.6 %collective-permute-done.6 = bf16[2,128,128]{2,1,0:T(8,128)(2,1)S(1)} collective-permute-done((bf16[2,128,128]{2,1,0:T(8,128)(2,1)S(1)}, bf16[2,128,128]{2,1,0:T(8,128)(2,1)S(1)}, u32[]{:S(2)}, u32[]{:S(2)}) %collective-permute-start.6) | collective-permute-done | bytes 65568 | tf_op jit(solution)/shard_map/ppermute | solution.py:213
  22.8 3.1 %attend.1 = (bf16[192,128]{1,0:T(8,128)(2,1)S(1)}, bf16[192,128]{1,0:T(8,128)(2,1)S(1)}, bf16[192,128]{1,0:T(8,128)(2,1)S(1)}, bf16[192,128]{1,0:T(8,128)(2,1)S(...) custom-call(s32[50]{0:T(128)S(1)} %pad_add_fusion.table_ref, ...), custom_call_target="tpu_custom_call" | custom-call | tf_op jit(solution)/shard_map/attend/pallas_call | solution.py:257
  25.9 3.2 %collective-permute-start.7 = (bf16[192,128]{1,0:T(8,128)(2,1)S(1)}, bf16[192,128]{1,0:T(8,128)(2,1)S(1)}, u32[]{:S(2)}, u32[]{:S(2)}) collective-permute-start(bf16[192,128]{1,0:T(8,128)(2,1)S(1)} %get-tuple-element.28), channel_id=1, source_target_pairs={{0,4},{1,5},{2,6},{3,7},{4,0},{5,1},{6,2},{7,3},{8,12},{9,13},{10,... | collective-permute-start | bytes 147464 | tf_op jit(solution)/shard_map/ppermute | solution.py:213
  29.6 1.8 %collective-permute-start.9 = (bf16[192,128]{1,0:T(8,128)(2,1)S(1)}, bf16[192,128]{1,0:T(8,128)(2,1)S(1)}, u32[]{:S(2)}, u32[]{:S(2)}) collective-permute-start(bf16[192,128]{1,0:T(8,128)(2,1)S(1)} %get-tuple-element.30), channel_id=1, source_target_pairs={{0,5},{1,4},{2,7},{3,6},{4,1},{5,0},{6,3},{7,2},{8,13},{9,12},{10,... | collective-permute-start | bytes 147464 | tf_op jit(solution)/shard_map/ppermute | solution.py:213
  31.4 2.3 %collective-permute-start.10 = (bf16[192,128]{1,0:T(8,128)(2,1)S(1)}, bf16[192,128]{1,0:T(8,128)(2,1)S(1)}, u32[]{:S(2)}, u32[]{:S(2)}) collective-permute-start(bf16[192,128]{1,0:T(8,128)(2,1)S(1)} %get-tuple-element.31), channel_id=1, source_target_pairs={{0,7},{1,6},{2,5},{3,4},{4,3},{5,2},{6,1},{7,0},{8,15},{9,14},{10,... | collective-permute-start | bytes 147464 | tf_op jit(solution)/shard_map/ppermute | solution.py:213
  33.7 0.9 %collective-permute-start.11 = (bf16[192,128]{1,0:T(8,128)(2,1)S(1)}, bf16[192,128]{1,0:T(8,128)(2,1)S(1)}, u32[]{:S(2)}, u32[]{:S(2)}) collective-permute-start(bf16[192,128]{1,0:T(8,128)(2,1)S(1)} %get-tuple-element.32), channel_id=1, source_target_pairs={{0,3},{1,2},{2,1},{3,0},{4,7},{5,6},{6,5},{7,4},{8,11},{9,10},{10,... | collective-permute-start | bytes 147464 | tf_op jit(solution)/shard_map/ppermute | solution.py:213
  34.6 1.2 %collective-permute-start.12 = (bf16[192,128]{1,0:T(8,128)(2,1)S(1)}, bf16[192,128]{1,0:T(8,128)(2,1)S(1)}, u32[]{:S(2)}, u32[]{:S(2)}) collective-permute-start(bf16[192,128]{1,0:T(8,128)(2,1)S(1)} %get-tuple-element.33), channel_id=1, source_target_pairs={{0,2},{1,3},{2,0},{3,1},{4,6},{5,7},{6,4},{7,5},{8,10},{9,11},{10,... | collective-permute-start | bytes 147464 | tf_op jit(solution)/shard_map/ppermute | solution.py:213
  35.9 1.3 %collective-permute-start.13 = (bf16[192,128]{1,0:T(8,128)(2,1)S(1)}, bf16[192,128]{1,0:T(8,128)(2,1)S(1)}, u32[]{:S(2)}, u32[]{:S(2)}) collective-permute-start(bf16[192,128]{1,0:T(8,128)(2,1)S(1)} %get-tuple-element.34), channel_id=1, source_target_pairs={{0,1},{1,0},{2,3},{3,2},{4,5},{5,4},{6,7},{7,6},{8,9},{9,8},{10,11... | collective-permute-start | bytes 147464 | tf_op jit(solution)/shard_map/ppermute | solution.py:213
  37.4 1.2 %collective-permute-done.10.refs_4_ = bf16[192,128]{1,0:T(8,128)(2,1)S(1)} collective-permute-done((bf16[192,128]{1,0:T(8,128)(2,1)S(1)}, bf16[192,128]{1,0:T(8,128)(2,1)S(1)}, u32[]{:S(2)}, u32[]{:S(2)}) %collective-permute-start.10) | collective-permute-done | bytes 49184 | tf_op jit(solution)/shard_map/ppermute | solution.py:213
  38.9 1.1 %collective-permute-done.13.refs_7_ = bf16[192,128]{1,0:T(8,128)(2,1)S(1)} collective-permute-done((bf16[192,128]{1,0:T(8,128)(2,1)S(1)}, bf16[192,128]{1,0:T(8,128)(2,1)S(1)}, u32[]{:S(2)}, u32[]{:S(2)}) %collective-permute-start.13) | collective-permute-done | bytes 49184 | tf_op jit(solution)/shard_map/ppermute | solution.py:213
  40.0 0.9 %unpack.1 = (bf16[128,512]{1,0:T(8,128)(2,1)}, bf16[128,512]{1,0:T(8,128)(2,1)}, bf16[128,512]{1,0:T(8,128)(2,1)}) custom-call(bf16[192,128]{1,0:T(8,128)(2,1)S(1)} %get-tuple-element.27.refs_0_, bf16[192,128]{1,0:T(8,128)(2,1)S(1)} %collective-permute-done.7.refs_1_, bf16[192,128]{1,0:T(8,128)(2,1)S(1)} %collective-permute-done.8.refs_2_, ...), custom_call_target="tpu_custom_call" | custom-call | tf_op jit(solution)/shard_map/unpack/pallas_call | solution.py:273
  (22 shorter events, 2.2 us)
Async XLA Ops:
  0.6 0.9 %copy-start = (bf16[128,512]{1,0:T(8,128)(2,1)S(1)}, bf16[128,512]{1,0:T(8,128)(2,1)}, u32[]{:S(2)}) copy-start(bf16[128,512]{1,0:T(8,128)(2,1)} %refs_0_.1) | copy-start | bytes 393220
  1.5 0.9 %copy-start.1 = (bf16[128,512]{1,0:T(8,128)(2,1)S(1)}, bf16[128,512]{1,0:T(8,128)(2,1)}, u32[]{:S(2)}) copy-start(bf16[128,512]{1,0:T(8,128)(2,1)} %refs_1_.1) | copy-start | bytes 393220
  2.4 0.9 %copy-start.2 = (bf16[128,512]{1,0:T(8,128)(2,1)S(1)}, bf16[128,512]{1,0:T(8,128)(2,1)}, u32[]{:S(2)}) copy-start(bf16[128,512]{1,0:T(8,128)(2,1)} %refs_2_.1) | copy-start | bytes 393220
  3.3 0.9 %copy-start.3 = (bf16[128,512]{1,0:T(8,128)(2,1)S(1)}, bf16[128,512]{1,0:T(8,128)(2,1)}, u32[]{:S(2)}) copy-start(bf16[128,512]{1,0:T(8,128)(2,1)} %refs_3_.1) | copy-start | bytes 393220
  5.2 10.9 %collective-permute-start = (bf16[2,128,128]{2,1,0:T(8,128)(2,1)S(1)}, bf16[2,128,128]{2,1,0:T(8,128)(2,1)S(1)}, u32[]{:S(2)}, u32[]{:S(2)}) collective-permute-start(bf16[2,128,128]{2,1,0:T(8,128)(2,1)S(1)} %get-tuple-element.20), channel_id=1, source_target_pairs={{0,4},{1,5},{2,6},{3,7},{4,0},{5,1},{6,2},{7,3},{8,12},{9,13},{10,... | collective-permute-start | bytes 196616 | tf_op jit(solution)/shard_map/ppermute | solution.py:213
  9.3 8.2 %collective-permute-start.1 = (bf16[2,128,128]{2,1,0:T(8,128)(2,1)S(1)}, bf16[2,128,128]{2,1,0:T(8,128)(2,1)S(1)}, u32[]{:S(2)}, u32[]{:S(2)}) collective-permute-start(bf16[2,128,128]{2,1,0:T(8,128)(2,1)S(1)} %get-tuple-element.21), channel_id=1, source_target_pairs={{0,6},{1,7},{2,4},{3,5},{4,2},{5,3},{6,0},{7,1},{8,14},{9,15},{10,... | collective-permute-start | bytes 196616 | tf_op jit(solution)/shard_map/ppermute | solution.py:213
  10.6 5.3 %copy-start.4 = (s32[16,3]{0,1:T(4,128)S(1)}, s32[16,3]{0,1:T(4,128)}, u32[]{:S(2)}) copy-start(s32[16,3]{0,1:T(4,128)} %param.10) | copy-start | bytes 580
  10.6 10.7 %collective-permute-start.2 = (bf16[2,128,128]{2,1,0:T(8,128)(2,1)S(1)}, bf16[2,128,128]{2,1,0:T(8,128)(2,1)S(1)}, u32[]{:S(2)}, u32[]{:S(2)}) collective-permute-start(bf16[2,128,128]{2,1,0:T(8,128)(2,1)S(1)} %get-tuple-element.22), channel_id=1, source_target_pairs={{0,5},{1,4},{2,7},{3,6},{4,1},{5,0},{6,3},{7,2},{8,13},{9,12},{10,... | collective-permute-start | bytes 196616 | tf_op jit(solution)/shard_map/ppermute | solution.py:213
  13.2 8.1 %collective-permute-start.3 = (bf16[2,128,128]{2,1,0:T(8,128)(2,1)S(1)}, bf16[2,128,128]{2,1,0:T(8,128)(2,1)S(1)}, u32[]{:S(2)}, u32[]{:S(2)}) collective-permute-start(bf16[2,128,128]{2,1,0:T(8,128)(2,1)S(1)} %get-tuple-element.23), channel_id=1, source_target_pairs={{0,7},{1,6},{2,5},{3,4},{4,3},{5,2},{6,1},{7,0},{8,15},{9,14},{10,... | collective-permute-start | bytes 196616 | tf_op jit(solution)/shard_map/ppermute | solution.py:213
  14.1 7.8 %collective-permute-start.4 = (bf16[2,128,128]{2,1,0:T(8,128)(2,1)S(1)}, bf16[2,128,128]{2,1,0:T(8,128)(2,1)S(1)}, u32[]{:S(2)}, u32[]{:S(2)}) collective-permute-start(bf16[2,128,128]{2,1,0:T(8,128)(2,1)S(1)} %get-tuple-element.24), channel_id=1, source_target_pairs={{0,3},{1,2},{2,1},{3,0},{4,7},{5,6},{6,5},{7,4},{8,11},{9,10},{10,... | collective-permute-start | bytes 196616 | tf_op jit(solution)/shard_map/ppermute | solution.py:213
  16.1 3.3 %copy-start.5 = (s32[2]{0:T(128)S(1)}, s32[2]{0:T(128)}, u32[]{:S(2)}) copy-start(s32[2]{0:T(128)} %param.11) | copy-start | bytes 28
  16.1 6.1 %collective-permute-start.5 = (bf16[2,128,128]{2,1,0:T(8,128)(2,1)S(1)}, bf16[2,128,128]{2,1,0:T(8,128)(2,1)S(1)}, u32[]{:S(2)}, u32[]{:S(2)}) collective-permute-start(bf16[2,128,128]{2,1,0:T(8,128)(2,1)S(1)} %get-tuple-element.25), channel_id=1, source_target_pairs={{0,2},{1,3},{2,0},{3,1},{4,6},{5,7},{6,4},{7,5},{8,10},{9,11},{10,... | collective-permute-start | bytes 196616 | tf_op jit(solution)/shard_map/ppermute | solution.py:213
  17.5 5.3 %collective-permute-start.6 = (bf16[2,128,128]{2,1,0:T(8,128)(2,1)S(1)}, bf16[2,128,128]{2,1,0:T(8,128)(2,1)S(1)}, u32[]{:S(2)}, u32[]{:S(2)}) collective-permute-start(bf16[2,128,128]{2,1,0:T(8,128)(2,1)S(1)} %get-tuple-element.26), channel_id=1, source_target_pairs={{0,1},{1,0},{2,3},{3,2},{4,5},{5,4},{6,7},{7,6},{8,9},{9,8},{10,11... | collective-permute-start | bytes 196616 | tf_op jit(solution)/shard_map/ppermute | solution.py:213
  25.9 8.7 %collective-permute-start.7 = (bf16[192,128]{1,0:T(8,128)(2,1)S(1)}, bf16[192,128]{1,0:T(8,128)(2,1)S(1)}, u32[]{:S(2)}, u32[]{:S(2)}) collective-permute-start(bf16[192,128]{1,0:T(8,128)(2,1)S(1)} %get-tuple-element.28), channel_id=1, source_target_pairs={{0,4},{1,5},{2,6},{3,7},{4,0},{5,1},{6,2},{7,3},{8,12},{9,13},{10,... | collective-permute-start | bytes 147464 | tf_op jit(solution)/shard_map/ppermute | solution.py:213
  29.1 6.8 %collective-permute-start.8 = (bf16[192,128]{1,0:T(8,128)(2,1)S(1)}, bf16[192,128]{1,0:T(8,128)(2,1)S(1)}, u32[]{:S(2)}, u32[]{:S(2)}) collective-permute-start(bf16[192,128]{1,0:T(8,128)(2,1)S(1)} %get-tuple-element.29), channel_id=1, source_target_pairs={{0,6},{1,7},{2,4},{3,5},{4,2},{5,3},{6,0},{7,1},{8,14},{9,15},{10,... | collective-permute-start | bytes 147464 | tf_op jit(solution)/shard_map/ppermute | solution.py:213
  29.6 7.8 %collective-permute-start.9 = (bf16[192,128]{1,0:T(8,128)(2,1)S(1)}, bf16[192,128]{1,0:T(8,128)(2,1)S(1)}, u32[]{:S(2)}, u32[]{:S(2)}) collective-permute-start(bf16[192,128]{1,0:T(8,128)(2,1)S(1)} %get-tuple-element.30), channel_id=1, source_target_pairs={{0,5},{1,4},{2,7},{3,6},{4,1},{5,0},{6,3},{7,2},{8,13},{9,12},{10,... | collective-permute-start | bytes 147464 | tf_op jit(solution)/shard_map/ppermute | solution.py:213
  31.4 7.2 %collective-permute-start.10 = (bf16[192,128]{1,0:T(8,128)(2,1)S(1)}, bf16[192,128]{1,0:T(8,128)(2,1)S(1)}, u32[]{:S(2)}, u32[]{:S(2)}) collective-permute-start(bf16[192,128]{1,0:T(8,128)(2,1)S(1)} %get-tuple-element.31), channel_id=1, source_target_pairs={{0,7},{1,6},{2,5},{3,4},{4,3},{5,2},{6,1},{7,0},{8,15},{9,14},{10,... | collective-permute-start | bytes 147464 | tf_op jit(solution)/shard_map/ppermute | solution.py:213
  33.7 5.2 %collective-permute-start.11 = (bf16[192,128]{1,0:T(8,128)(2,1)S(1)}, bf16[192,128]{1,0:T(8,128)(2,1)S(1)}, u32[]{:S(2)}, u32[]{:S(2)}) collective-permute-start(bf16[192,128]{1,0:T(8,128)(2,1)S(1)} %get-tuple-element.32), channel_id=1, source_target_pairs={{0,3},{1,2},{2,1},{3,0},{4,7},{5,6},{6,5},{7,4},{8,11},{9,10},{10,... | collective-permute-start | bytes 147464 | tf_op jit(solution)/shard_map/ppermute | solution.py:213
  34.6 4.3 %collective-permute-start.12 = (bf16[192,128]{1,0:T(8,128)(2,1)S(1)}, bf16[192,128]{1,0:T(8,128)(2,1)S(1)}, u32[]{:S(2)}, u32[]{:S(2)}) collective-permute-start(bf16[192,128]{1,0:T(8,128)(2,1)S(1)} %get-tuple-element.33), channel_id=1, source_target_pairs={{0,2},{1,3},{2,0},{3,1},{4,6},{5,7},{6,4},{7,5},{8,10},{9,11},{10,... | collective-permute-start | bytes 147464 | tf_op jit(solution)/shard_map/ppermute | solution.py:213
  35.9 4.1 %collective-permute-start.13 = (bf16[192,128]{1,0:T(8,128)(2,1)S(1)}, bf16[192,128]{1,0:T(8,128)(2,1)S(1)}, u32[]{:S(2)}, u32[]{:S(2)}) collective-permute-start(bf16[192,128]{1,0:T(8,128)(2,1)S(1)} %get-tuple-element.34), channel_id=1, source_target_pairs={{0,1},{1,0},{2,3},{3,2},{4,5},{5,4},{6,7},{7,6},{8,9},{9,8},{10,11... | collective-permute-start | bytes 147464 | tf_op jit(solution)/shard_map/ppermute | solution.py:213

commit v6 on v4

--- a/solution.py
+++ b/solution.py
@@ -15,6 +15,7 @@
 HEAD = 64
 LANES = 2 * HEAD
 PARTNERS = (0, 4, 6, 5, 7, 3, 2, 1)
+NEAR = (2, 3, 1, 0)
 MASKED = -1e30
 
 
@@ -26,23 +27,43 @@
     return pltpu.roll(block, HEAD, 1)
 
 
-def pack_kernel(q_ref, k_ref, v_ref, g_ref, *out_refs):
-    rows = q_ref.shape[0]
+def pack_kernel(*refs):
+    in_refs, out_refs = refs[:4], refs[4 : 4 + HEADS]
+    held_ref, packed_ref, in_sems, out_sems = refs[4 + HEADS :]
+    rows = held_ref.shape[2]
     low = low_lanes((rows, LANES))
     place = lax.rem(lax.axis_index("seq"), HEADS)
     odd_place = lax.rem(place, 2) == 1
-    for near in range(HEADS // 2):
+    arriving = {}
+    for near in NEAR:
         pair = lax.bitwise_xor(place // 2, near)
         lanes = pl.ds(pl.multiple_of(pair * LANES, LANES), LANES)
-        for kind, (first_ref, second_ref) in enumerate(((k_ref, v_ref), (q_ref, g_ref))):
-            first = first_ref[:, lanes].astype(jnp.float32)
-            second = second_ref[:, lanes].astype(jnp.float32)
+        for kind, ref in enumerate(in_refs):
+            arriving[near, kind] = pltpu.make_async_copy(
+                ref.at[:, lanes], held_ref.at[near, kind], in_sems.at[near, kind]
+            )
+            arriving[near, kind].start()
+    leaving = []
+    for near in NEAR:
+        for kind in range(4):
+            arriving[near, kind].wait()
+        q, k, v, g = [held_ref[near, kind].astype(jnp.float32) for kind in range(4)]
+        for kind, (first, second) in enumerate(((k, v), (q, g))):
             even = jnp.where(low, first, swap_halves(second))
             odd = jnp.where(low, swap_halves(first), second)
             same = jnp.where(odd_place, odd, even).astype(jnp.bfloat16)
             other = jnp.where(odd_place, even, odd).astype(jnp.bfloat16)
-            out_refs[2 * near][kind] = same
-            out_refs[2 * near + 1][kind] = other
+            packed_ref[2 * near, kind] = same
+            packed_ref[2 * near + 1, kind] = other
+        for m in (2 * near, 2 * near + 1):
+            leaving.append(pltpu.make_async_copy(packed_ref.at[m], out_refs[m], out_sems.at[m]))
+            leaving[-1].start()
+    for copy in leaving:
+        copy.wait()
+
+
+def keep_kernel(in_ref, out_ref):
+    out_ref[...] = in_ref[...]
 
 
 def unpack_kernel(*refs):
@@ -231,14 +252,28 @@
     smem = pl.BlockSpec(memory_space=pltpu.SMEM)
     half_type = jnp.bfloat16
 
-    packed = pl.pallas_call(
+    anywhere = pl.BlockSpec(memory_space=pl.ANY)
+    packed = list(pl.pallas_call(
         pack_kernel,
         out_shape=[jax.ShapeDtypeStruct((2, rows, LANES), half_type)] * HEADS,
-        in_specs=[vmem] * 4,
-        out_specs=[vmem] * HEADS,
+        in_specs=[anywhere] * 4,
+        out_specs=[anywhere] * HEADS,
+        scratch_shapes=[
+            pltpu.VMEM((HEADS // 2, 4, rows, LANES), half_type),
+            pltpu.VMEM((HEADS, 2, rows, LANES), half_type),
+            pltpu.SemaphoreType.DMA((HEADS // 2, 4)),
+            pltpu.SemaphoreType.DMA((HEADS,)),
+        ],
+        name="pack",
+    )(queries, key_vectors, value_vectors, output_grad))
+    packed[0] = pl.pallas_call(
+        keep_kernel,
+        out_shape=jax.ShapeDtypeStruct((2, rows, LANES), half_type),
+        in_specs=[vmem],
+        out_specs=vmem,
         compiler_params=pltpu.CompilerParams(vmem_limit_bytes=8 * 2**20),
-        name="pack",
-    )(queries, key_vectors, value_vectors, output_grad)
+        name="keep",
+    )(packed[0])
     sent = [part.reshape(2, 2, BLOCK, LANES) for part in exchange(packed)]
 
     kernel = functools.partial(attend_kernel, alone, scale)

time: 40.4 us -> 39 us (0.965)
  local copies, waits for them, and re-layouts: 3.79 us -> 1.83 us
  Pallas kernels: 4.24 us -> 6.15 us
  starting transfers between devices: 25.3 us -> 23.8 us
    unnamed x13 -> x11, local copies, waits for them, and re-layouts: 3.7 us -> 1.75 us
    pallas_call x1, Pallas kernels: 0.24 us -> 2.14 us  [on_device(): pl.pallas_call(pack_kernel, out_shape=[jax.ShapeDtypeStruct((2, rows, LAN...]
    ppermute x14, starting transfers between devices: 25.3 us -> 23.8 us  [exchange(): arrived[m] = lax.ppermute(parts[m], 'seq', route)]
where the time goes in v6:
time: 39 us; the launch traced here: 38.7 us
  starting transfers between devices  23.8 us (61%)
  waiting for transfers between devices  6.16 us (16%)
  Pallas kernels  6.15 us (16%)
  local copies, waits for them, and re-layouts  1.83 us (5%)
  between operations  0.69 us (2%)
    ppermute x14, starting transfers between devices, exchange(): arrived[m] = lax.ppermute(parts[m], 'seq', route)  23.8 us
    ppermute x14, waiting for transfers between devices, exchange(): arrived[m] = lax.ppermute(parts[m], 'seq', route)  6.16 us
    pallas_call x1, Pallas kernels, on_device(): pl.pallas_call(kernel, out_shape=[jax.ShapeDtypeStruct((rows + BLOCK, LAN...  3.08 us
    pallas_call x1, Pallas kernels, on_device(): pl.pallas_call(pack_kernel, out_shape=[jax.ShapeDtypeStruct((2, rows, LAN...  2.14 us
    unnamed x11, local copies, waits for them, and re-layouts  1.75 us
    pallas_call x1, Pallas kernels, on_device(): pl.pallas_call(unpack_kernel, out_shape=[jax.ShapeDtypeStruct((rows, widt...  0.92 us
  transfers between devices with their start and end apart: 14, of which 8 were waited for; matrix products, arithmetic and copies ran while one was open for 1% of the time, Pallas kernels for 0%

profile of v6, /device:TPU:0, one launch (start us, length us, event | category | flops | bytes accessed | tf_op | source)
XLA Modules:
  0.0 38.7 jit_solution(8980555320356163110)
XLA Ops:
  0.6 2.1 %pack.1 = (bf16[2,128,128]{2,1,0:T(8,128)(2,1)}, bf16[2,128,128]{2,1,0:T(8,128)(2,1)}, bf16[2,128,128]{2,1,0:T(8,128)(2,1)}, bf16[2,128,128]{2,1,0:T(8,128)(2,1)...) custom-call(bf16[128,512]{1,0:T(8,128)(2,1)} %refs_0_.1, ...), custom_call_target="tpu_custom_call" | custom-call | tf_op jit(solution)/shard_map/pack/pallas_call | solution.py:256
  2.8 4.1 %collective-permute-start = (bf16[2,128,128]{2,1,0:T(8,128)(2,1)}, bf16[2,128,128]{2,1,0:T(8,128)(2,1)S(1)}, u32[]{:S(2)}, u32[]{:S(2)}) collective-permute-start(bf16[2,128,128]{2,1,0:T(8,128)(2,1)} %get-tuple-element.20), channel_id=1, source_target_pairs={{0,4},{1,5},{2,6},{3,7},{4,0},{5,1},{6,2},{7,3},{8,12},{9,13},{10,... | collective-permute-start | bytes 196616 | tf_op jit(solution)/shard_map/ppermute | solution.py:227
  6.9 1.3 %collective-permute-start.1 = (bf16[2,128,128]{2,1,0:T(8,128)(2,1)}, bf16[2,128,128]{2,1,0:T(8,128)(2,1)S(1)}, u32[]{:S(2)}, u32[]{:S(2)}) collective-permute-start(bf16[2,128,128]{2,1,0:T(8,128)(2,1)} %get-tuple-element.21), channel_id=1, source_target_pairs={{0,6},{1,7},{2,4},{3,5},{4,2},{5,3},{6,0},{7,1},{8,14},{9,15},{10,... | collective-permute-start | bytes 196616 | tf_op jit(solution)/shard_map/ppermute | solution.py:227
  8.2 2.6 %collective-permute-start.2 = (bf16[2,128,128]{2,1,0:T(8,128)(2,1)}, bf16[2,128,128]{2,1,0:T(8,128)(2,1)S(1)}, u32[]{:S(2)}, u32[]{:S(2)}) collective-permute-start(bf16[2,128,128]{2,1,0:T(8,128)(2,1)} %get-tuple-element.22), channel_id=1, source_target_pairs={{0,5},{1,4},{2,7},{3,6},{4,1},{5,0},{6,3},{7,2},{8,13},{9,12},{10,... | collective-permute-start | bytes 196616 | tf_op jit(solution)/shard_map/ppermute | solution.py:227
  10.9 0.9 %collective-permute-start.3 = (bf16[2,128,128]{2,1,0:T(8,128)(2,1)}, bf16[2,128,128]{2,1,0:T(8,128)(2,1)S(1)}, u32[]{:S(2)}, u32[]{:S(2)}) collective-permute-start(bf16[2,128,128]{2,1,0:T(8,128)(2,1)} %get-tuple-element.23), channel_id=1, source_target_pairs={{0,7},{1,6},{2,5},{3,4},{4,3},{5,2},{6,1},{7,0},{8,15},{9,14},{10,... | collective-permute-start | bytes 196616 | tf_op jit(solution)/shard_map/ppermute | solution.py:227
  11.7 1.8 %collective-permute-start.4 = (bf16[2,128,128]{2,1,0:T(8,128)(2,1)}, bf16[2,128,128]{2,1,0:T(8,128)(2,1)S(1)}, u32[]{:S(2)}, u32[]{:S(2)}) collective-permute-start(bf16[2,128,128]{2,1,0:T(8,128)(2,1)} %get-tuple-element.24), channel_id=1, source_target_pairs={{0,3},{1,2},{2,1},{3,0},{4,7},{5,6},{6,5},{7,4},{8,11},{9,10},{10,... | collective-permute-start | bytes 196616 | tf_op jit(solution)/shard_map/ppermute | solution.py:227
  13.7 0.8 %copy-done = bf16[2,128,128]{2,1,0:T(8,128)(2,1)S(1)} copy-done((bf16[2,128,128]{2,1,0:T(8,128)(2,1)S(1)}, bf16[2,128,128]{2,1,0:T(8,128)(2,1)}, u32[]{:S(2)}) %copy-start) | copy-done | bytes 65560
  14.6 0.8 %copy-done.3 = bf16[2,128,128]{2,1,0:T(8,128)(2,1)S(1)} copy-done((bf16[2,128,128]{2,1,0:T(8,128)(2,1)S(1)}, bf16[2,128,128]{2,1,0:T(8,128)(2,1)}, u32[]{:S(2)}) %copy-start.3) | copy-done | bytes 65560
  15.4 1.1 %collective-permute-start.5 = (bf16[2,128,128]{2,1,0:T(8,128)(2,1)S(1)}, bf16[2,128,128]{2,1,0:T(8,128)(2,1)S(1)}, u32[]{:S(2)}, u32[]{:S(2)}) collective-permute-start(bf16[2,128,128]{2,1,0:T(8,128)(2,1)S(1)} %copy-done.3), channel_id=1, source_target_pairs={{0,2},{1,3},{2,0},{3,1},{4,6},{5,7},{6,4},{7,5},{8,10},{9,11},{10,... | collective-permute-start | bytes 196616 | tf_op jit(solution)/shard_map/ppermute | solution.py:227
  16.5 0.8 %collective-permute-start.6 = (bf16[2,128,128]{2,1,0:T(8,128)(2,1)S(1)}, bf16[2,128,128]{2,1,0:T(8,128)(2,1)S(1)}, u32[]{:S(2)}, u32[]{:S(2)}) collective-permute-start(bf16[2,128,128]{2,1,0:T(8,128)(2,1)S(1)} %copy-done.2), channel_id=1, source_target_pairs={{0,1},{1,0},{2,3},{3,2},{4,5},{5,4},{6,7},{7,6},{8,9},{9,8},{10,11... | collective-permute-start | bytes 196616 | tf_op jit(solution)/shard_map/ppermute | solution.py:227
  17.5 1.7 %collective-permute-done.2 = bf16[2,128,128]{2,1,0:T(8,128)(2,1)S(1)} collective-permute-done((bf16[2,128,128]{2,1,0:T(8,128)(2,1)}, bf16[2,128,128]{2,1,0:T(8,128)(2,1)S(1)}, u32[]{:S(2)}, u32[]{:S(2)}) %collective-permute-start.2) | collective-permute-done | bytes 65568 | tf_op jit(solution)/shard_map/ppermute | solution.py:227
  19.2 0.7 %collective-permute-done.4 = bf16[2,128,128]{2,1,0:T(8,128)(2,1)S(1)} collective-permute-done((bf16[2,128,128]{2,1,0:T(8,128)(2,1)}, bf16[2,128,128]{2,1,0:T(8,128)(2,1)S(1)}, u32[]{:S(2)}, u32[]{:S(2)}) %collective-permute-start.4) | collective-permute-done | bytes 65568 | tf_op jit(solution)/shard_map/ppermute | solution.py:227
  20.0 0.8 %collective-permute-done.6 = bf16[2,128,128]{2,1,0:T(8,128)(2,1)S(1)} collective-permute-done((bf16[2,128,128]{2,1,0:T(8,128)(2,1)S(1)}, bf16[2,128,128]{2,1,0:T(8,128)(2,1)S(1)}, u32[]{:S(2)}, u32[]{:S(2)}) %collective-permute-start.6) | collective-permute-done | bytes 65568 | tf_op jit(solution)/shard_map/ppermute | solution.py:227
  20.8 3.1 %attend.1 = (bf16[192,128]{1,0:T(8,128)(2,1)S(1)}, bf16[192,128]{1,0:T(8,128)(2,1)S(1)}, bf16[192,128]{1,0:T(8,128)(2,1)S(1)}, bf16[192,128]{1,0:T(8,128)(2,1)S(...) custom-call(s32[50]{0:T(128)S(1)} %pad_add_fusion.table_ref, ...), custom_call_target="tpu_custom_call" | custom-call | tf_op jit(solution)/shard_map/attend/pallas_call | solution.py:281
  23.9 3.0 %collective-permute-start.7 = (bf16[192,128]{1,0:T(8,128)(2,1)S(1)}, bf16[192,128]{1,0:T(8,128)(2,1)S(1)}, u32[]{:S(2)}, u32[]{:S(2)}) collective-permute-start(bf16[192,128]{1,0:T(8,128)(2,1)S(1)} %get-tuple-element.28), channel_id=1, source_target_pairs={{0,4},{1,5},{2,6},{3,7},{4,0},{5,1},{6,2},{7,3},{8,12},{9,13},{10,... | collective-permute-start | bytes 147464 | tf_op jit(solution)/shard_map/ppermute | solution.py:227
  26.9 0.7 %collective-permute-start.8 = (bf16[192,128]{1,0:T(8,128)(2,1)S(1)}, bf16[192,128]{1,0:T(8,128)(2,1)S(1)}, u32[]{:S(2)}, u32[]{:S(2)}) collective-permute-start(bf16[192,128]{1,0:T(8,128)(2,1)S(1)} %get-tuple-element.29), channel_id=1, source_target_pairs={{0,6},{1,7},{2,4},{3,5},{4,2},{5,3},{6,0},{7,1},{8,14},{9,15},{10,... | collective-permute-start | bytes 147464 | tf_op jit(solution)/shard_map/ppermute | solution.py:227
  27.6 1.6 %collective-permute-start.9 = (bf16[192,128]{1,0:T(8,128)(2,1)S(1)}, bf16[192,128]{1,0:T(8,128)(2,1)S(1)}, u32[]{:S(2)}, u32[]{:S(2)}) collective-permute-start(bf16[192,128]{1,0:T(8,128)(2,1)S(1)} %get-tuple-element.30), channel_id=1, source_target_pairs={{0,5},{1,4},{2,7},{3,6},{4,1},{5,0},{6,3},{7,2},{8,13},{9,12},{10,... | collective-permute-start | bytes 147464 | tf_op jit(solution)/shard_map/ppermute | solution.py:227
  29.2 2.3 %collective-permute-start.10 = (bf16[192,128]{1,0:T(8,128)(2,1)S(1)}, bf16[192,128]{1,0:T(8,128)(2,1)S(1)}, u32[]{:S(2)}, u32[]{:S(2)}) collective-permute-start(bf16[192,128]{1,0:T(8,128)(2,1)S(1)} %get-tuple-element.31), channel_id=1, source_target_pairs={{0,7},{1,6},{2,5},{3,4},{4,3},{5,2},{6,1},{7,0},{8,15},{9,14},{10,... | collective-permute-start | bytes 147464 | tf_op jit(solution)/shard_map/ppermute | solution.py:227
  31.5 1.0 %collective-permute-start.11 = (bf16[192,128]{1,0:T(8,128)(2,1)S(1)}, bf16[192,128]{1,0:T(8,128)(2,1)S(1)}, u32[]{:S(2)}, u32[]{:S(2)}) collective-permute-start(bf16[192,128]{1,0:T(8,128)(2,1)S(1)} %get-tuple-element.32), channel_id=1, source_target_pairs={{0,3},{1,2},{2,1},{3,0},{4,7},{5,6},{6,5},{7,4},{8,11},{9,10},{10,... | collective-permute-start | bytes 147464 | tf_op jit(solution)/shard_map/ppermute | solution.py:227
  32.5 1.1 %collective-permute-start.12 = (bf16[192,128]{1,0:T(8,128)(2,1)S(1)}, bf16[192,128]{1,0:T(8,128)(2,1)S(1)}, u32[]{:S(2)}, u32[]{:S(2)}) collective-permute-start(bf16[192,128]{1,0:T(8,128)(2,1)S(1)} %get-tuple-element.33), channel_id=1, source_target_pairs={{0,2},{1,3},{2,0},{3,1},{4,6},{5,7},{6,4},{7,5},{8,10},{9,11},{10,... | collective-permute-start | bytes 147464 | tf_op jit(solution)/shard_map/ppermute | solution.py:227
  33.7 1.3 %collective-permute-start.13 = (bf16[192,128]{1,0:T(8,128)(2,1)S(1)}, bf16[192,128]{1,0:T(8,128)(2,1)S(1)}, u32[]{:S(2)}, u32[]{:S(2)}) collective-permute-start(bf16[192,128]{1,0:T(8,128)(2,1)S(1)} %get-tuple-element.34), channel_id=1, source_target_pairs={{0,1},{1,0},{2,3},{3,2},{4,5},{5,4},{6,7},{7,6},{8,9},{9,8},{10,11... | collective-permute-start | bytes 147464 | tf_op jit(solution)/shard_map/ppermute | solution.py:227
  35.3 1.1 %collective-permute-done.10.refs_4_ = bf16[192,128]{1,0:T(8,128)(2,1)S(1)} collective-permute-done((bf16[192,128]{1,0:T(8,128)(2,1)S(1)}, bf16[192,128]{1,0:T(8,128)(2,1)S(1)}, u32[]{:S(2)}, u32[]{:S(2)}) %collective-permute-start.10) | collective-permute-done | bytes 49184 | tf_op jit(solution)/shard_map/ppermute | solution.py:227
  36.8 1.0 %collective-permute-done.13.refs_7_ = bf16[192,128]{1,0:T(8,128)(2,1)S(1)} collective-permute-done((bf16[192,128]{1,0:T(8,128)(2,1)S(1)}, bf16[192,128]{1,0:T(8,128)(2,1)S(1)}, u32[]{:S(2)}, u32[]{:S(2)}) %collective-permute-start.13) | collective-permute-done | bytes 49184 | tf_op jit(solution)/shard_map/ppermute | solution.py:227
  37.8 0.9 %unpack.1 = (bf16[128,512]{1,0:T(8,128)(2,1)}, bf16[128,512]{1,0:T(8,128)(2,1)}, bf16[128,512]{1,0:T(8,128)(2,1)}) custom-call(bf16[192,128]{1,0:T(8,128)(2,1)S(1)} %get-tuple-element.27.refs_0_, bf16[192,128]{1,0:T(8,128)(2,1)S(1)} %collective-permute-done.7.refs_1_, bf16[192,128]{1,0:T(8,128)(2,1)S(1)} %collective-permute-done.8.refs_2_, ...), custom_call_target="tpu_custom_call" | custom-call | tf_op jit(solution)/shard_map/unpack/pallas_call | solution.py:297
  (21 shorter events, 1.1 us)
Async XLA Ops:
  2.8 11.8 %collective-permute-start = (bf16[2,128,128]{2,1,0:T(8,128)(2,1)}, bf16[2,128,128]{2,1,0:T(8,128)(2,1)S(1)}, u32[]{:S(2)}, u32[]{:S(2)}) collective-permute-start(bf16[2,128,128]{2,1,0:T(8,128)(2,1)} %get-tuple-element.20), channel_id=1, source_target_pairs={{0,4},{1,5},{2,6},{3,7},{4,0},{5,1},{6,2},{7,3},{8,12},{9,13},{10,... | collective-permute-start | bytes 196616 | tf_op jit(solution)/shard_map/ppermute | solution.py:227
  6.9 9.7 %collective-permute-start.1 = (bf16[2,128,128]{2,1,0:T(8,128)(2,1)}, bf16[2,128,128]{2,1,0:T(8,128)(2,1)S(1)}, u32[]{:S(2)}, u32[]{:S(2)}) collective-permute-start(bf16[2,128,128]{2,1,0:T(8,128)(2,1)} %get-tuple-element.21), channel_id=1, source_target_pairs={{0,6},{1,7},{2,4},{3,5},{4,2},{5,3},{6,0},{7,1},{8,14},{9,15},{10,... | collective-permute-start | bytes 196616 | tf_op jit(solution)/shard_map/ppermute | solution.py:227
  8.2 5.3 %copy-start.1 = (s32[16,3]{0,1:T(4,128)S(1)}, s32[16,3]{0,1:T(4,128)}, u32[]{:S(2)}) copy-start(s32[16,3]{0,1:T(4,128)} %param.10) | copy-start | bytes 580
  8.2 11.0 %collective-permute-start.2 = (bf16[2,128,128]{2,1,0:T(8,128)(2,1)}, bf16[2,128,128]{2,1,0:T(8,128)(2,1)S(1)}, u32[]{:S(2)}, u32[]{:S(2)}) collective-permute-start(bf16[2,128,128]{2,1,0:T(8,128)(2,1)} %get-tuple-element.22), channel_id=1, source_target_pairs={{0,5},{1,4},{2,7},{3,6},{4,1},{5,0},{6,3},{7,2},{8,13},{9,12},{10,... | collective-permute-start | bytes 196616 | tf_op jit(solution)/shard_map/ppermute | solution.py:227
  10.9 8.4 %collective-permute-start.3 = (bf16[2,128,128]{2,1,0:T(8,128)(2,1)}, bf16[2,128,128]{2,1,0:T(8,128)(2,1)S(1)}, u32[]{:S(2)}, u32[]{:S(2)}) collective-permute-start(bf16[2,128,128]{2,1,0:T(8,128)(2,1)} %get-tuple-element.23), channel_id=1, source_target_pairs={{0,7},{1,6},{2,5},{3,4},{4,3},{5,2},{6,1},{7,0},{8,15},{9,14},{10,... | collective-permute-start | bytes 196616 | tf_op jit(solution)/shard_map/ppermute | solution.py:227
  11.7 8.1 %collective-permute-start.4 = (bf16[2,128,128]{2,1,0:T(8,128)(2,1)}, bf16[2,128,128]{2,1,0:T(8,128)(2,1)S(1)}, u32[]{:S(2)}, u32[]{:S(2)}) collective-permute-start(bf16[2,128,128]{2,1,0:T(8,128)(2,1)} %get-tuple-element.24), channel_id=1, source_target_pairs={{0,3},{1,2},{2,1},{3,0},{4,7},{5,6},{6,5},{7,4},{8,11},{9,10},{10,... | collective-permute-start | bytes 196616 | tf_op jit(solution)/shard_map/ppermute | solution.py:227
  13.7 0.8 %copy-start = (bf16[2,128,128]{2,1,0:T(8,128)(2,1)S(1)}, bf16[2,128,128]{2,1,0:T(8,128)(2,1)}, u32[]{:S(2)}) copy-start(bf16[2,128,128]{2,1,0:T(8,128)(2,1)} %get-tuple-element.19.in_ref) | copy-start | bytes 196612
  14.6 0.8 %copy-start.3 = (bf16[2,128,128]{2,1,0:T(8,128)(2,1)S(1)}, bf16[2,128,128]{2,1,0:T(8,128)(2,1)}, u32[]{:S(2)}) copy-start(bf16[2,128,128]{2,1,0:T(8,128)(2,1)} %get-tuple-element.25) | copy-start | bytes 196612
  14.6 2.0 %copy-start.2 = (bf16[2,128,128]{2,1,0:T(8,128)(2,1)S(1)}, bf16[2,128,128]{2,1,0:T(8,128)(2,1)}, u32[]{:S(2)}) copy-start(bf16[2,128,128]{2,1,0:T(8,128)(2,1)} %get-tuple-element.26) | copy-start | bytes 196612
  15.4 2.0 %copy-start.4 = (s32[2]{0:T(128)S(1)}, s32[2]{0:T(128)}, u32[]{:S(2)}) copy-start(s32[2]{0:T(128)} %param.11) | copy-start | bytes 28
  15.4 4.6 %collective-permute-start.5 = (bf16[2,128,128]{2,1,0:T(8,128)(2,1)S(1)}, bf16[2,128,128]{2,1,0:T(8,128)(2,1)S(1)}, u32[]{:S(2)}, u32[]{:S(2)}) collective-permute-start(bf16[2,128,128]{2,1,0:T(8,128)(2,1)S(1)} %copy-done.3), channel_id=1, source_target_pairs={{0,2},{1,3},{2,0},{3,1},{4,6},{5,7},{6,4},{7,5},{8,10},{9,11},{10,... | collective-permute-start | bytes 196616 | tf_op jit(solution)/shard_map/ppermute | solution.py:227
  16.5 4.3 %collective-permute-start.6 = (bf16[2,128,128]{2,1,0:T(8,128)(2,1)S(1)}, bf16[2,128,128]{2,1,0:T(8,128)(2,1)S(1)}, u32[]{:S(2)}, u32[]{:S(2)}) collective-permute-start(bf16[2,128,128]{2,1,0:T(8,128)(2,1)S(1)} %copy-done.2), channel_id=1, source_target_pairs={{0,1},{1,0},{2,3},{3,2},{4,5},{5,4},{6,7},{7,6},{8,9},{9,8},{10,11... | collective-permute-start | bytes 196616 | tf_op jit(solution)/shard_map/ppermute | solution.py:227
  23.9 8.6 %collective-permute-start.7 = (bf16[192,128]{1,0:T(8,128)(2,1)S(1)}, bf16[192,128]{1,0:T(8,128)(2,1)S(1)}, u32[]{:S(2)}, u32[]{:S(2)}) collective-permute-start(bf16[192,128]{1,0:T(8,128)(2,1)S(1)} %get-tuple-element.28), channel_id=1, source_target_pairs={{0,4},{1,5},{2,6},{3,7},{4,0},{5,1},{6,2},{7,3},{8,12},{9,13},{10,... | collective-permute-start | bytes 147464 | tf_op jit(solution)/shard_map/ppermute | solution.py:227
  26.9 6.8 %collective-permute-start.8 = (bf16[192,128]{1,0:T(8,128)(2,1)S(1)}, bf16[192,128]{1,0:T(8,128)(2,1)S(1)}, u32[]{:S(2)}, u32[]{:S(2)}) collective-permute-start(bf16[192,128]{1,0:T(8,128)(2,1)S(1)} %get-tuple-element.29), channel_id=1, source_target_pairs={{0,6},{1,7},{2,4},{3,5},{4,2},{5,3},{6,0},{7,1},{8,14},{9,15},{10,... | collective-permute-start | bytes 147464 | tf_op jit(solution)/shard_map/ppermute | solution.py:227
  27.6 7.7 %collective-permute-start.9 = (bf16[192,128]{1,0:T(8,128)(2,1)S(1)}, bf16[192,128]{1,0:T(8,128)(2,1)S(1)}, u32[]{:S(2)}, u32[]{:S(2)}) collective-permute-start(bf16[192,128]{1,0:T(8,128)(2,1)S(1)} %get-tuple-element.30), channel_id=1, source_target_pairs={{0,5},{1,4},{2,7},{3,6},{4,1},{5,0},{6,3},{7,2},{8,13},{9,12},{10,... | collective-permute-start | bytes 147464 | tf_op jit(solution)/shard_map/ppermute | solution.py:227
  29.2 7.2 %collective-permute-start.10 = (bf16[192,128]{1,0:T(8,128)(2,1)S(1)}, bf16[192,128]{1,0:T(8,128)(2,1)S(1)}, u32[]{:S(2)}, u32[]{:S(2)}) collective-permute-start(bf16[192,128]{1,0:T(8,128)(2,1)S(1)} %get-tuple-element.31), channel_id=1, source_target_pairs={{0,7},{1,6},{2,5},{3,4},{4,3},{5,2},{6,1},{7,0},{8,15},{9,14},{10,... | collective-permute-start | bytes 147464 | tf_op jit(solution)/shard_map/ppermute | solution.py:227
  31.5 5.2 %collective-permute-start.11 = (bf16[192,128]{1,0:T(8,128)(2,1)S(1)}, bf16[192,128]{1,0:T(8,128)(2,1)S(1)}, u32[]{:S(2)}, u32[]{:S(2)}) collective-permute-start(bf16[192,128]{1,0:T(8,128)(2,1)S(1)} %get-tuple-element.32), channel_id=1, source_target_pairs={{0,3},{1,2},{2,1},{3,0},{4,7},{5,6},{6,5},{7,4},{8,11},{9,10},{10,... | collective-permute-start | bytes 147464 | tf_op jit(solution)/shard_map/ppermute | solution.py:227
  32.5 4.2 %collective-permute-start.12 = (bf16[192,128]{1,0:T(8,128)(2,1)S(1)}, bf16[192,128]{1,0:T(8,128)(2,1)S(1)}, u32[]{:S(2)}, u32[]{:S(2)}) collective-permute-start(bf16[192,128]{1,0:T(8,128)(2,1)S(1)} %get-tuple-element.33), channel_id=1, source_target_pairs={{0,2},{1,3},{2,0},{3,1},{4,6},{5,7},{6,4},{7,5},{8,10},{9,11},{10,... | collective-permute-start | bytes 147464 | tf_op jit(solution)/shard_map/ppermute | solution.py:227
  33.7 4.1 %collective-permute-start.13 = (bf16[192,128]{1,0:T(8,128)(2,1)S(1)}, bf16[192,128]{1,0:T(8,128)(2,1)S(1)}, u32[]{:S(2)}, u32[]{:S(2)}) collective-permute-start(bf16[192,128]{1,0:T(8,128)(2,1)S(1)} %get-tuple-element.34), channel_id=1, source_target_pairs={{0,1},{1,0},{2,3},{3,2},{4,5},{5,4},{6,7},{7,6},{8,9},{9,8},{10,11... | collective-permute-start | bytes 147464 | tf_op jit(solution)/shard_map/ppermute | solution.py:227

commit v7 on v6

--- a/solution.py
+++ b/solution.py
@@ -16,6 +16,7 @@
 LANES = 2 * HEAD
 PARTNERS = (0, 4, 6, 5, 7, 3, 2, 1)
 NEAR = (2, 3, 1, 0)
+PACK_GRANT = 427 * 2**17
 MASKED = -1e30
 
 
@@ -29,7 +30,7 @@
 
 def pack_kernel(*refs):
     in_refs, out_refs = refs[:4], refs[4 : 4 + HEADS]
-    held_ref, packed_ref, in_sems, out_sems = refs[4 + HEADS :]
+    held_ref, in_sems = refs[4 + HEADS :]
     rows = held_ref.shape[2]
     low = low_lanes((rows, LANES))
     place = lax.rem(lax.axis_index("seq"), HEADS)
@@ -43,7 +44,6 @@
                 ref.at[:, lanes], held_ref.at[near, kind], in_sems.at[near, kind]
             )
             arriving[near, kind].start()
-    leaving = []
     for near in NEAR:
         for kind in range(4):
             arriving[near, kind].wait()
@@ -53,17 +53,8 @@
             odd = jnp.where(low, swap_halves(first), second)
             same = jnp.where(odd_place, odd, even).astype(jnp.bfloat16)
             other = jnp.where(odd_place, even, odd).astype(jnp.bfloat16)
-            packed_ref[2 * near, kind] = same
-            packed_ref[2 * near + 1, kind] = other
-        for m in (2 * near, 2 * near + 1):
-            leaving.append(pltpu.make_async_copy(packed_ref.at[m], out_refs[m], out_sems.at[m]))
-            leaving[-1].start()
-    for copy in leaving:
-        copy.wait()
-
-
-def keep_kernel(in_ref, out_ref):
-    out_ref[...] = in_ref[...]
+            out_refs[2 * near][kind] = same
+            out_refs[2 * near + 1][kind] = other
 
 
 def unpack_kernel(*refs):
@@ -253,27 +244,18 @@
     half_type = jnp.bfloat16
 
     anywhere = pl.BlockSpec(memory_space=pl.ANY)
-    packed = list(pl.pallas_call(
+    packed = pl.pallas_call(
         pack_kernel,
         out_shape=[jax.ShapeDtypeStruct((2, rows, LANES), half_type)] * HEADS,
         in_specs=[anywhere] * 4,
-        out_specs=[anywhere] * HEADS,
+        out_specs=[vmem] * HEADS,
         scratch_shapes=[
             pltpu.VMEM((HEADS // 2, 4, rows, LANES), half_type),
-            pltpu.VMEM((HEADS, 2, rows, LANES), half_type),
             pltpu.SemaphoreType.DMA((HEADS // 2, 4)),
-            pltpu.SemaphoreType.DMA((HEADS,)),
         ],
+        compiler_params=pltpu.CompilerParams(vmem_limit_bytes=PACK_GRANT),
         name="pack",
-    )(queries, key_vectors, value_vectors, output_grad))
-    packed[0] = pl.pallas_call(
-        keep_kernel,
-        out_shape=jax.ShapeDtypeStruct((2, rows, LANES), half_type),
-        in_specs=[vmem],
-        out_specs=vmem,
-        compiler_params=pltpu.CompilerParams(vmem_limit_bytes=8 * 2**20),
-        name="keep",
-    )(packed[0])
+    )(queries, key_vectors, value_vectors, output_grad)
     sent = [part.reshape(2, 2, BLOCK, LANES) for part in exchange(packed)]
 
     kernel = functools.partial(attend_kernel, alone, scale)

time: 39 us -> 38 us (0.974)
  local copies, waits for them, and re-layouts: 1.83 us -> 0.18 us
  starting transfers between devices: 23.8 us -> 25.3 us
  Pallas kernels: 6.15 us -> 5.42 us
    unnamed x11 -> x5, local copies, waits for them, and re-layouts: 1.75 us -> 0.09 us
    ppermute x14, starting transfers between devices: 23.8 us -> 25.3 us  [exchange(): arrived[m] = lax.ppermute(parts[m], 'seq', route)]
    pallas_call x1, Pallas kernels: 2.14 us -> 1.42 us  [on_device(): pl.pallas_call(pack_kernel, out_shape=[jax.ShapeDtypeStruct((2, rows, LAN...]
where the time goes in v7:
time: 38 us; the launch traced here: 37.8 us
  starting transfers between devices  25.3 us (67%)
  waiting for transfers between devices  6.09 us (16%)
  Pallas kernels  5.42 us (14%)
  between operations  0.68 us (2%)
    ppermute x14, starting transfers between devices, exchange(): arrived[m] = lax.ppermute(parts[m], 'seq', route)  25.3 us
    ppermute x14, waiting for transfers between devices, exchange(): arrived[m] = lax.ppermute(parts[m], 'seq', route)  6.09 us
    pallas_call x1, Pallas kernels, on_device(): pl.pallas_call(kernel, out_shape=[jax.ShapeDtypeStruct((rows + BLOCK, LAN...  3.08 us
    pallas_call x1, Pallas kernels, on_device(): pl.pallas_call(pack_kernel, out_shape=[jax.ShapeDtypeStruct((2, rows, LAN...  1.42 us
    pallas_call x1, Pallas kernels, on_device(): pl.pallas_call(unpack_kernel, out_shape=[jax.ShapeDtypeStruct((rows, widt...  0.92 us
  transfers between devices with their start and end apart: 14, of which 8 were waited for; matrix products, arithmetic and copies ran while one was open for 1% of the time, Pallas kernels for 0%

profile of v7, /device:TPU:0, one launch (start us, length us, event | category | flops | bytes accessed | tf_op | source)
XLA Modules:
  0.0 37.8 jit_solution(17835275591312175022)
XLA Ops:
  0.6 1.4 %pack.1 = (bf16[2,128,128]{2,1,0:T(8,128)(2,1)S(1)}, bf16[2,128,128]{2,1,0:T(8,128)(2,1)S(1)}, bf16[2,128,128]{2,1,0:T(8,128)(2,1)S(1)}, bf16[2,128,128]{2,1,0:T...) custom-call(bf16[128,512]{1,0:T(8,128)(2,1)} %refs_0_.1, ...), custom_call_target="tpu_custom_call" | custom-call | tf_op jit(solution)/shard_map/pack/pallas_call | solution.py:247
  2.1 4.1 %collective-permute-start = (bf16[2,128,128]{2,1,0:T(8,128)(2,1)S(1)}, bf16[2,128,128]{2,1,0:T(8,128)(2,1)S(1)}, u32[]{:S(2)}, u32[]{:S(2)}) collective-permute-start(bf16[2,128,128]{2,1,0:T(8,128)(2,1)S(1)} %get-tuple-element.20), channel_id=1, source_target_pairs={{0,4},{1,5},{2,6},{3,7},{4,0},{5,1},{6,2},{7,3},{8,12},{9,13},{10,... | collective-permute-start | bytes 196616 | tf_op jit(solution)/shard_map/ppermute | solution.py:218
  6.2 1.3 %collective-permute-start.1 = (bf16[2,128,128]{2,1,0:T(8,128)(2,1)S(1)}, bf16[2,128,128]{2,1,0:T(8,128)(2,1)S(1)}, u32[]{:S(2)}, u32[]{:S(2)}) collective-permute-start(bf16[2,128,128]{2,1,0:T(8,128)(2,1)S(1)} %get-tuple-element.21), channel_id=1, source_target_pairs={{0,6},{1,7},{2,4},{3,5},{4,2},{5,3},{6,0},{7,1},{8,14},{9,15},{10,... | collective-permute-start | bytes 196616 | tf_op jit(solution)/shard_map/ppermute | solution.py:218
  7.5 2.6 %collective-permute-start.2 = (bf16[2,128,128]{2,1,0:T(8,128)(2,1)S(1)}, bf16[2,128,128]{2,1,0:T(8,128)(2,1)S(1)}, u32[]{:S(2)}, u32[]{:S(2)}) collective-permute-start(bf16[2,128,128]{2,1,0:T(8,128)(2,1)S(1)} %get-tuple-element.22), channel_id=1, source_target_pairs={{0,5},{1,4},{2,7},{3,6},{4,1},{5,0},{6,3},{7,2},{8,13},{9,12},{10,... | collective-permute-start | bytes 196616 | tf_op jit(solution)/shard_map/ppermute | solution.py:218
  10.1 0.9 %collective-permute-start.3 = (bf16[2,128,128]{2,1,0:T(8,128)(2,1)S(1)}, bf16[2,128,128]{2,1,0:T(8,128)(2,1)S(1)}, u32[]{:S(2)}, u32[]{:S(2)}) collective-permute-start(bf16[2,128,128]{2,1,0:T(8,128)(2,1)S(1)} %get-tuple-element.23), channel_id=1, source_target_pairs={{0,7},{1,6},{2,5},{3,4},{4,3},{5,2},{6,1},{7,0},{8,15},{9,14},{10,... | collective-permute-start | bytes 196616 | tf_op jit(solution)/shard_map/ppermute | solution.py:218
  11.0 1.8 %collective-permute-start.4 = (bf16[2,128,128]{2,1,0:T(8,128)(2,1)S(1)}, bf16[2,128,128]{2,1,0:T(8,128)(2,1)S(1)}, u32[]{:S(2)}, u32[]{:S(2)}) collective-permute-start(bf16[2,128,128]{2,1,0:T(8,128)(2,1)S(1)} %get-tuple-element.24), channel_id=1, source_target_pairs={{0,3},{1,2},{2,1},{3,0},{4,7},{5,6},{6,5},{7,4},{8,11},{9,10},{10,... | collective-permute-start | bytes 196616 | tf_op jit(solution)/shard_map/ppermute | solution.py:218
  13.0 1.4 %collective-permute-start.5 = (bf16[2,128,128]{2,1,0:T(8,128)(2,1)S(1)}, bf16[2,128,128]{2,1,0:T(8,128)(2,1)S(1)}, u32[]{:S(2)}, u32[]{:S(2)}) collective-permute-start(bf16[2,128,128]{2,1,0:T(8,128)(2,1)S(1)} %get-tuple-element.25), channel_id=1, source_target_pairs={{0,2},{1,3},{2,0},{3,1},{4,6},{5,7},{6,4},{7,5},{8,10},{9,11},{10,... | collective-permute-start | bytes 196616 | tf_op jit(solution)/shard_map/ppermute | solution.py:218
  14.4 2.0 %collective-permute-start.6 = (bf16[2,128,128]{2,1,0:T(8,128)(2,1)S(1)}, bf16[2,128,128]{2,1,0:T(8,128)(2,1)S(1)}, u32[]{:S(2)}, u32[]{:S(2)}) collective-permute-start(bf16[2,128,128]{2,1,0:T(8,128)(2,1)S(1)} %get-tuple-element.26), channel_id=1, source_target_pairs={{0,1},{1,0},{2,3},{3,2},{4,5},{5,4},{6,7},{7,6},{8,9},{9,8},{10,11... | collective-permute-start | bytes 196616 | tf_op jit(solution)/shard_map/ppermute | solution.py:218
  16.4 1.8 %collective-permute-done.2 = bf16[2,128,128]{2,1,0:T(8,128)(2,1)S(1)} collective-permute-done((bf16[2,128,128]{2,1,0:T(8,128)(2,1)S(1)}, bf16[2,128,128]{2,1,0:T(8,128)(2,1)S(1)}, u32[]{:S(2)}, u32[]{:S(2)}) %collective-permute-start.2) | collective-permute-done | bytes 65568 | tf_op jit(solution)/shard_map/ppermute | solution.py:218
  18.2 0.5 %collective-permute-done.4 = bf16[2,128,128]{2,1,0:T(8,128)(2,1)S(1)} collective-permute-done((bf16[2,128,128]{2,1,0:T(8,128)(2,1)S(1)}, bf16[2,128,128]{2,1,0:T(8,128)(2,1)S(1)}, u32[]{:S(2)}, u32[]{:S(2)}) %collective-permute-start.4) | collective-permute-done | bytes 65568 | tf_op jit(solution)/shard_map/ppermute | solution.py:218
  18.8 0.3 collective-permute-done.5
  19.1 0.6 %collective-permute-done.6 = bf16[2,128,128]{2,1,0:T(8,128)(2,1)S(1)} collective-permute-done((bf16[2,128,128]{2,1,0:T(8,128)(2,1)S(1)}, bf16[2,128,128]{2,1,0:T(8,128)(2,1)S(1)}, u32[]{:S(2)}, u32[]{:S(2)}) %collective-permute-start.6) | collective-permute-done | bytes 65568 | tf_op jit(solution)/shard_map/ppermute | solution.py:218
  19.7 3.1 %attend.1 = (bf16[192,128]{1,0:T(8,128)(2,1)S(1)}, bf16[192,128]{1,0:T(8,128)(2,1)S(1)}, bf16[192,128]{1,0:T(8,128)(2,1)S(1)}, bf16[192,128]{1,0:T(8,128)(2,1)S(...) custom-call(s32[50]{0:T(128)S(1)} %pad_add_fusion.table_ref, ...), custom_call_target="tpu_custom_call" | custom-call | tf_op jit(solution)/shard_map/attend/pallas_call | solution.py:263
  22.8 3.2 %collective-permute-start.7 = (bf16[192,128]{1,0:T(8,128)(2,1)S(1)}, bf16[192,128]{1,0:T(8,128)(2,1)S(1)}, u32[]{:S(2)}, u32[]{:S(2)}) collective-permute-start(bf16[192,128]{1,0:T(8,128)(2,1)S(1)} %get-tuple-element.28), channel_id=1, source_target_pairs={{0,4},{1,5},{2,6},{3,7},{4,0},{5,1},{6,2},{7,3},{8,12},{9,13},{10,... | collective-permute-start | bytes 147464 | tf_op jit(solution)/shard_map/ppermute | solution.py:218
  26.0 0.5 %collective-permute-start.8 = (bf16[192,128]{1,0:T(8,128)(2,1)S(1)}, bf16[192,128]{1,0:T(8,128)(2,1)S(1)}, u32[]{:S(2)}, u32[]{:S(2)}) collective-permute-start(bf16[192,128]{1,0:T(8,128)(2,1)S(1)} %get-tuple-element.29), channel_id=1, source_target_pairs={{0,6},{1,7},{2,4},{3,5},{4,2},{5,3},{6,0},{7,1},{8,14},{9,15},{10,... | collective-permute-start | bytes 147464 | tf_op jit(solution)/shard_map/ppermute | solution.py:218
  26.5 1.8 %collective-permute-start.9 = (bf16[192,128]{1,0:T(8,128)(2,1)S(1)}, bf16[192,128]{1,0:T(8,128)(2,1)S(1)}, u32[]{:S(2)}, u32[]{:S(2)}) collective-permute-start(bf16[192,128]{1,0:T(8,128)(2,1)S(1)} %get-tuple-element.30), channel_id=1, source_target_pairs={{0,5},{1,4},{2,7},{3,6},{4,1},{5,0},{6,3},{7,2},{8,13},{9,12},{10,... | collective-permute-start | bytes 147464 | tf_op jit(solution)/shard_map/ppermute | solution.py:218
  28.3 2.3 %collective-permute-start.10 = (bf16[192,128]{1,0:T(8,128)(2,1)S(1)}, bf16[192,128]{1,0:T(8,128)(2,1)S(1)}, u32[]{:S(2)}, u32[]{:S(2)}) collective-permute-start(bf16[192,128]{1,0:T(8,128)(2,1)S(1)} %get-tuple-element.31), channel_id=1, source_target_pairs={{0,7},{1,6},{2,5},{3,4},{4,3},{5,2},{6,1},{7,0},{8,15},{9,14},{10,... | collective-permute-start | bytes 147464 | tf_op jit(solution)/shard_map/ppermute | solution.py:218
  30.6 0.9 %collective-permute-start.11 = (bf16[192,128]{1,0:T(8,128)(2,1)S(1)}, bf16[192,128]{1,0:T(8,128)(2,1)S(1)}, u32[]{:S(2)}, u32[]{:S(2)}) collective-permute-start(bf16[192,128]{1,0:T(8,128)(2,1)S(1)} %get-tuple-element.32), channel_id=1, source_target_pairs={{0,3},{1,2},{2,1},{3,0},{4,7},{5,6},{6,5},{7,4},{8,11},{9,10},{10,... | collective-permute-start | bytes 147464 | tf_op jit(solution)/shard_map/ppermute | solution.py:218
  31.5 1.3 %collective-permute-start.12 = (bf16[192,128]{1,0:T(8,128)(2,1)S(1)}, bf16[192,128]{1,0:T(8,128)(2,1)S(1)}, u32[]{:S(2)}, u32[]{:S(2)}) collective-permute-start(bf16[192,128]{1,0:T(8,128)(2,1)S(1)} %get-tuple-element.33), channel_id=1, source_target_pairs={{0,2},{1,3},{2,0},{3,1},{4,6},{5,7},{6,4},{7,5},{8,10},{9,11},{10,... | collective-permute-start | bytes 147464 | tf_op jit(solution)/shard_map/ppermute | solution.py:218
  32.8 1.3 %collective-permute-start.13 = (bf16[192,128]{1,0:T(8,128)(2,1)S(1)}, bf16[192,128]{1,0:T(8,128)(2,1)S(1)}, u32[]{:S(2)}, u32[]{:S(2)}) collective-permute-start(bf16[192,128]{1,0:T(8,128)(2,1)S(1)} %get-tuple-element.34), channel_id=1, source_target_pairs={{0,1},{1,0},{2,3},{3,2},{4,5},{5,4},{6,7},{7,6},{8,9},{9,8},{10,11... | collective-permute-start | bytes 147464 | tf_op jit(solution)/shard_map/ppermute | solution.py:218
  34.3 1.2 %collective-permute-done.10.refs_4_ = bf16[192,128]{1,0:T(8,128)(2,1)S(1)} collective-permute-done((bf16[192,128]{1,0:T(8,128)(2,1)S(1)}, bf16[192,128]{1,0:T(8,128)(2,1)S(1)}, u32[]{:S(2)}, u32[]{:S(2)}) %collective-permute-start.10) | collective-permute-done | bytes 49184 | tf_op jit(solution)/shard_map/ppermute | solution.py:218
  35.5 0.3 collective-permute-done.11.refs_5_
  35.8 1.1 %collective-permute-done.13.refs_7_ = bf16[192,128]{1,0:T(8,128)(2,1)S(1)} collective-permute-done((bf16[192,128]{1,0:T(8,128)(2,1)S(1)}, bf16[192,128]{1,0:T(8,128)(2,1)S(1)}, u32[]{:S(2)}, u32[]{:S(2)}) %collective-permute-start.13) | collective-permute-done | bytes 49184 | tf_op jit(solution)/shard_map/ppermute | solution.py:218
  36.8 0.9 %unpack.1 = (bf16[128,512]{1,0:T(8,128)(2,1)}, bf16[128,512]{1,0:T(8,128)(2,1)}, bf16[128,512]{1,0:T(8,128)(2,1)}) custom-call(bf16[192,128]{1,0:T(8,128)(2,1)S(1)} %get-tuple-element.27.refs_0_, bf16[192,128]{1,0:T(8,128)(2,1)S(1)} %collective-permute-done.7.refs_1_, bf16[192,128]{1,0:T(8,128)(2,1)S(1)} %collective-permute-done.8.refs_2_, ...), custom_call_target="tpu_custom_call" | custom-call | tf_op jit(solution)/shard_map/unpack/pallas_call | solution.py:279
  (14 shorter events, 0.5 us)
Async XLA Ops:
  2.1 10.9 %collective-permute-start = (bf16[2,128,128]{2,1,0:T(8,128)(2,1)S(1)}, bf16[2,128,128]{2,1,0:T(8,128)(2,1)S(1)}, u32[]{:S(2)}, u32[]{:S(2)}) collective-permute-start(bf16[2,128,128]{2,1,0:T(8,128)(2,1)S(1)} %get-tuple-element.20), channel_id=1, source_target_pairs={{0,4},{1,5},{2,6},{3,7},{4,0},{5,1},{6,2},{7,3},{8,12},{9,13},{10,... | collective-permute-start | bytes 196616 | tf_op jit(solution)/shard_map/ppermute | solution.py:218
  6.2 8.2 %collective-permute-start.1 = (bf16[2,128,128]{2,1,0:T(8,128)(2,1)S(1)}, bf16[2,128,128]{2,1,0:T(8,128)(2,1)S(1)}, u32[]{:S(2)}, u32[]{:S(2)}) collective-permute-start(bf16[2,128,128]{2,1,0:T(8,128)(2,1)S(1)} %get-tuple-element.21), channel_id=1, source_target_pairs={{0,6},{1,7},{2,4},{3,5},{4,2},{5,3},{6,0},{7,1},{8,14},{9,15},{10,... | collective-permute-start | bytes 196616 | tf_op jit(solution)/shard_map/ppermute | solution.py:218
  7.5 5.3 %copy-start = (s32[16,3]{0,1:T(4,128)S(1)}, s32[16,3]{0,1:T(4,128)}, u32[]{:S(2)}) copy-start(s32[16,3]{0,1:T(4,128)} %param.10) | copy-start | bytes 580
  7.5 10.7 %collective-permute-start.2 = (bf16[2,128,128]{2,1,0:T(8,128)(2,1)S(1)}, bf16[2,128,128]{2,1,0:T(8,128)(2,1)S(1)}, u32[]{:S(2)}, u32[]{:S(2)}) collective-permute-start(bf16[2,128,128]{2,1,0:T(8,128)(2,1)S(1)} %get-tuple-element.22), channel_id=1, source_target_pairs={{0,5},{1,4},{2,7},{3,6},{4,1},{5,0},{6,3},{7,2},{8,13},{9,12},{10,... | collective-permute-start | bytes 196616 | tf_op jit(solution)/shard_map/ppermute | solution.py:218
  10.1 8.1 %collective-permute-start.3 = (bf16[2,128,128]{2,1,0:T(8,128)(2,1)S(1)}, bf16[2,128,128]{2,1,0:T(8,128)(2,1)S(1)}, u32[]{:S(2)}, u32[]{:S(2)}) collective-permute-start(bf16[2,128,128]{2,1,0:T(8,128)(2,1)S(1)} %get-tuple-element.23), channel_id=1, source_target_pairs={{0,7},{1,6},{2,5},{3,4},{4,3},{5,2},{6,1},{7,0},{8,15},{9,14},{10,... | collective-permute-start | bytes 196616 | tf_op jit(solution)/shard_map/ppermute | solution.py:218
  11.0 7.8 %collective-permute-start.4 = (bf16[2,128,128]{2,1,0:T(8,128)(2,1)S(1)}, bf16[2,128,128]{2,1,0:T(8,128)(2,1)S(1)}, u32[]{:S(2)}, u32[]{:S(2)}) collective-permute-start(bf16[2,128,128]{2,1,0:T(8,128)(2,1)S(1)} %get-tuple-element.24), channel_id=1, source_target_pairs={{0,3},{1,2},{2,1},{3,0},{4,7},{5,6},{6,5},{7,4},{8,11},{9,10},{10,... | collective-permute-start | bytes 196616 | tf_op jit(solution)/shard_map/ppermute | solution.py:218
  13.0 3.3 %copy-start.1 = (s32[2]{0:T(128)S(1)}, s32[2]{0:T(128)}, u32[]{:S(2)}) copy-start(s32[2]{0:T(128)} %param.11) | copy-start | bytes 28
  13.0 6.1 %collective-permute-start.5 = (bf16[2,128,128]{2,1,0:T(8,128)(2,1)S(1)}, bf16[2,128,128]{2,1,0:T(8,128)(2,1)S(1)}, u32[]{:S(2)}, u32[]{:S(2)}) collective-permute-start(bf16[2,128,128]{2,1,0:T(8,128)(2,1)S(1)} %get-tuple-element.25), channel_id=1, source_target_pairs={{0,2},{1,3},{2,0},{3,1},{4,6},{5,7},{6,4},{7,5},{8,10},{9,11},{10,... | collective-permute-start | bytes 196616 | tf_op jit(solution)/shard_map/ppermute | solution.py:218
  14.4 5.3 %collective-permute-start.6 = (bf16[2,128,128]{2,1,0:T(8,128)(2,1)S(1)}, bf16[2,128,128]{2,1,0:T(8,128)(2,1)S(1)}, u32[]{:S(2)}, u32[]{:S(2)}) collective-permute-start(bf16[2,128,128]{2,1,0:T(8,128)(2,1)S(1)} %get-tuple-element.26), channel_id=1, source_target_pairs={{0,1},{1,0},{2,3},{3,2},{4,5},{5,4},{6,7},{7,6},{8,9},{9,8},{10,11... | collective-permute-start | bytes 196616 | tf_op jit(solution)/shard_map/ppermute | solution.py:218
  22.8 8.7 %collective-permute-start.7 = (bf16[192,128]{1,0:T(8,128)(2,1)S(1)}, bf16[192,128]{1,0:T(8,128)(2,1)S(1)}, u32[]{:S(2)}, u32[]{:S(2)}) collective-permute-start(bf16[192,128]{1,0:T(8,128)(2,1)S(1)} %get-tuple-element.28), channel_id=1, source_target_pairs={{0,4},{1,5},{2,6},{3,7},{4,0},{5,1},{6,2},{7,3},{8,12},{9,13},{10,... | collective-permute-start | bytes 147464 | tf_op jit(solution)/shard_map/ppermute | solution.py:218
  26.0 6.8 %collective-permute-start.8 = (bf16[192,128]{1,0:T(8,128)(2,1)S(1)}, bf16[192,128]{1,0:T(8,128)(2,1)S(1)}, u32[]{:S(2)}, u32[]{:S(2)}) collective-permute-start(bf16[192,128]{1,0:T(8,128)(2,1)S(1)} %get-tuple-element.29), channel_id=1, source_target_pairs={{0,6},{1,7},{2,4},{3,5},{4,2},{5,3},{6,0},{7,1},{8,14},{9,15},{10,... | collective-permute-start | bytes 147464 | tf_op jit(solution)/shard_map/ppermute | solution.py:218
  26.5 7.8 %collective-permute-start.9 = (bf16[192,128]{1,0:T(8,128)(2,1)S(1)}, bf16[192,128]{1,0:T(8,128)(2,1)S(1)}, u32[]{:S(2)}, u32[]{:S(2)}) collective-permute-start(bf16[192,128]{1,0:T(8,128)(2,1)S(1)} %get-tuple-element.30), channel_id=1, source_target_pairs={{0,5},{1,4},{2,7},{3,6},{4,1},{5,0},{6,3},{7,2},{8,13},{9,12},{10,... | collective-permute-start | bytes 147464 | tf_op jit(solution)/shard_map/ppermute | solution.py:218
  28.3 7.2 %collective-permute-start.10 = (bf16[192,128]{1,0:T(8,128)(2,1)S(1)}, bf16[192,128]{1,0:T(8,128)(2,1)S(1)}, u32[]{:S(2)}, u32[]{:S(2)}) collective-permute-start(bf16[192,128]{1,0:T(8,128)(2,1)S(1)} %get-tuple-element.31), channel_id=1, source_target_pairs={{0,7},{1,6},{2,5},{3,4},{4,3},{5,2},{6,1},{7,0},{8,15},{9,14},{10,... | collective-permute-start | bytes 147464 | tf_op jit(solution)/shard_map/ppermute | solution.py:218
  30.6 5.2 %collective-permute-start.11 = (bf16[192,128]{1,0:T(8,128)(2,1)S(1)}, bf16[192,128]{1,0:T(8,128)(2,1)S(1)}, u32[]{:S(2)}, u32[]{:S(2)}) collective-permute-start(bf16[192,128]{1,0:T(8,128)(2,1)S(1)} %get-tuple-element.32), channel_id=1, source_target_pairs={{0,3},{1,2},{2,1},{3,0},{4,7},{5,6},{6,5},{7,4},{8,11},{9,10},{10,... | collective-permute-start | bytes 147464 | tf_op jit(solution)/shard_map/ppermute | solution.py:218
  31.5 4.3 %collective-permute-start.12 = (bf16[192,128]{1,0:T(8,128)(2,1)S(1)}, bf16[192,128]{1,0:T(8,128)(2,1)S(1)}, u32[]{:S(2)}, u32[]{:S(2)}) collective-permute-start(bf16[192,128]{1,0:T(8,128)(2,1)S(1)} %get-tuple-element.33), channel_id=1, source_target_pairs={{0,2},{1,3},{2,0},{3,1},{4,6},{5,7},{6,4},{7,5},{8,10},{9,11},{10,... | collective-permute-start | bytes 147464 | tf_op jit(solution)/shard_map/ppermute | solution.py:218
  32.8 4.1 %collective-permute-start.13 = (bf16[192,128]{1,0:T(8,128)(2,1)S(1)}, bf16[192,128]{1,0:T(8,128)(2,1)S(1)}, u32[]{:S(2)}, u32[]{:S(2)}) collective-permute-start(bf16[192,128]{1,0:T(8,128)(2,1)S(1)} %get-tuple-element.34), channel_id=1, source_target_pairs={{0,1},{1,0},{2,3},{3,2},{4,5},{5,4},{6,7},{7,6},{8,9},{9,8},{10,11... | collective-permute-start | bytes 147464 | tf_op jit(solution)/shard_map/ppermute | solution.py:218

commit v8 on v7

--- a/solution.py
+++ b/solution.py
@@ -14,7 +14,8 @@
 GLOBAL = 2
 HEAD = 64
 LANES = 2 * HEAD
-PARTNERS = (0, 4, 6, 5, 7, 3, 2, 1)
+PARTNERS_IN = (0, 4, 6, 3, 7, 5, 2, 1)
+PARTNERS_BACK = (0, 6, 5, 7, 3, 4, 2, 1)
 NEAR = (2, 3, 1, 0)
 PACK_GRANT = 427 * 2**17
 MASKED = -1e30
@@ -58,7 +59,7 @@
 
 
 def unpack_kernel(*refs):
-    in_refs = dict(zip(PARTNERS, refs[:HEADS]))
+    in_refs = dict(zip(PARTNERS_BACK, refs[:HEADS]))
     gq_ref, gk_ref, gv_ref = refs[HEADS:]
     rows = gq_ref.shape[0]
     low = low_lanes((rows, LANES))
@@ -84,7 +85,7 @@
 
 def attend_kernel(alone, scale, table_ref, *rest):
     if alone:
-        in_refs = dict(zip(PARTNERS, rest[:HEADS]))
+        in_refs = dict(zip(PARTNERS_IN, rest[:HEADS]))
         out_refs = rest[HEADS : 2 * HEADS]
         sent_ref, gq_ref, acc_ref = rest[2 * HEADS :]
         place = lax.rem(lax.axis_index("seq"), HEADS)
@@ -210,10 +211,10 @@
             out_refs[m][queries:] = gq_ref[tile]
 
 
-def exchange(parts):
+def exchange(parts, partners):
     group = lax.axis_size("seq")
     arrived = list(parts)
-    for m in PARTNERS[1:]:
+    for m in partners[1:]:
         route = [(i, i ^ m) for i in range(group)]
         arrived[m] = lax.ppermute(parts[m], "seq", route)
     return arrived
@@ -256,7 +257,7 @@
         compiler_params=pltpu.CompilerParams(vmem_limit_bytes=PACK_GRANT),
         name="pack",
     )(queries, key_vectors, value_vectors, output_grad)
-    sent = [part.reshape(2, 2, BLOCK, LANES) for part in exchange(packed)]
+    sent = [part.reshape(2, 2, BLOCK, LANES) for part in exchange(packed, PARTNERS_IN)]
 
     kernel = functools.partial(attend_kernel, alone, scale)
     if alone:
@@ -272,10 +273,10 @@
             ],
             compiler_params=pltpu.CompilerParams(vmem_limit_bytes=24 * 2**20),
             name="attend",
-        )(jnp.concatenate([rand_pick.reshape(-1), global_ids]), *[sent[m] for m in PARTNERS])
+        )(jnp.concatenate([rand_pick.reshape(-1), global_ids]), *[sent[m] for m in PARTNERS_IN])
     else:
         back = spread_out(kernel, sent, rand_pick, global_ids, ways, ranges, blocks)
-    received = exchange(back)
+    received = exchange(back, PARTNERS_BACK)
     return pl.pallas_call(
         unpack_kernel,
         out_shape=[jax.ShapeDtypeStruct((rows, width), half_type)] * 3,
@@ -283,7 +284,7 @@
         out_specs=[vmem] * 3,
         compiler_params=pltpu.CompilerParams(vmem_limit_bytes=8 * 2**20),
         name="unpack",
-    )(*[received[m] for m in PARTNERS])
+    )(*[received[m] for m in PARTNERS_BACK])
 
 
 def spread_out(kernel, sent, rand_pick, global_ids, ways, ranges, blocks):

time: 38 us -> 37.8 us (level)
  starting transfers between devices: 25.3 us -> 22.8 us
  waiting for transfers between devices: 6.09 us -> 8.42 us
    ppermute x14, starting transfers between devices: 25.3 us -> 22.8 us  [exchange(): arrived[m] = lax.ppermute(parts[m], 'seq', route)]
    ppermute x14, waiting for transfers between devices: 6.09 us -> 8.42 us  [exchange(): arrived[m] = lax.ppermute(parts[m], 'seq', route)]
where the time goes in v8:
time: 37.8 us; the launch traced here: 37.6 us
  starting transfers between devices  22.8 us (60%)
  waiting for transfers between devices  8.42 us (22%)
  Pallas kernels  5.42 us (14%)
  between operations  0.68 us (2%)
    ppermute x14, starting transfers between devices, exchange(): arrived[m] = lax.ppermute(parts[m], 'seq', route)  22.8 us
    ppermute x14, waiting for transfers between devices, exchange(): arrived[m] = lax.ppermute(parts[m], 'seq', route)  8.42 us
    pallas_call x1, Pallas kernels, on_device(): pl.pallas_call(kernel, out_shape=[jax.ShapeDtypeStruct((rows + BLOCK, LAN...  3.08 us
    pallas_call x1, Pallas kernels, on_device(): pl.pallas_call(pack_kernel, out_shape=[jax.ShapeDtypeStruct((2, rows, LAN...  1.42 us
    pallas_call x1, Pallas kernels, on_device(): pl.pallas_call(unpack_kernel, out_shape=[jax.ShapeDtypeStruct((rows, widt...  0.92 us
  transfers between devices with their start and end apart: 14, of which 8 were waited for; matrix products, arithmetic and copies ran while one was open for 1% of the time, Pallas kernels for 0%

profile of v8, /device:TPU:0, one launch (start us, length us, event | category | flops | bytes accessed | tf_op | source)
XLA Modules:
  0.0 37.6 jit_solution(9110244653700336292)
XLA Ops:
  0.6 1.4 %pack.1 = (bf16[2,128,128]{2,1,0:T(8,128)(2,1)S(1)}, bf16[2,128,128]{2,1,0:T(8,128)(2,1)S(1)}, bf16[2,128,128]{2,1,0:T(8,128)(2,1)S(1)}, bf16[2,128,128]{2,1,0:T...) custom-call(bf16[128,512]{1,0:T(8,128)(2,1)} %refs_0_.1, ...), custom_call_target="tpu_custom_call" | custom-call | tf_op jit(solution)/shard_map/pack/pallas_call | solution.py:248
  2.1 4.1 %collective-permute-start = (bf16[2,128,128]{2,1,0:T(8,128)(2,1)S(1)}, bf16[2,128,128]{2,1,0:T(8,128)(2,1)S(1)}, u32[]{:S(2)}, u32[]{:S(2)}) collective-permute-start(bf16[2,128,128]{2,1,0:T(8,128)(2,1)S(1)} %get-tuple-element.20), channel_id=1, source_target_pairs={{0,4},{1,5},{2,6},{3,7},{4,0},{5,1},{6,2},{7,3},{8,12},{9,13},{10,... | collective-permute-start | bytes 196616 | tf_op jit(solution)/shard_map/ppermute | solution.py:219
  6.2 1.3 %collective-permute-start.1 = (bf16[2,128,128]{2,1,0:T(8,128)(2,1)S(1)}, bf16[2,128,128]{2,1,0:T(8,128)(2,1)S(1)}, u32[]{:S(2)}, u32[]{:S(2)}) collective-permute-start(bf16[2,128,128]{2,1,0:T(8,128)(2,1)S(1)} %get-tuple-element.21), channel_id=1, source_target_pairs={{0,6},{1,7},{2,4},{3,5},{4,2},{5,3},{6,0},{7,1},{8,14},{9,15},{10,... | collective-permute-start | bytes 196616 | tf_op jit(solution)/shard_map/ppermute | solution.py:219
  7.5 1.2 %collective-permute-start.2 = (bf16[2,128,128]{2,1,0:T(8,128)(2,1)S(1)}, bf16[2,128,128]{2,1,0:T(8,128)(2,1)S(1)}, u32[]{:S(2)}, u32[]{:S(2)}) collective-permute-start(bf16[2,128,128]{2,1,0:T(8,128)(2,1)S(1)} %get-tuple-element.22), channel_id=1, source_target_pairs={{0,3},{1,2},{2,1},{3,0},{4,7},{5,6},{6,5},{7,4},{8,11},{9,10},{10,... | collective-permute-start | bytes 196616 | tf_op jit(solution)/shard_map/ppermute | solution.py:219
  8.7 2.9 %collective-permute-start.3 = (bf16[2,128,128]{2,1,0:T(8,128)(2,1)S(1)}, bf16[2,128,128]{2,1,0:T(8,128)(2,1)S(1)}, u32[]{:S(2)}, u32[]{:S(2)}) collective-permute-start(bf16[2,128,128]{2,1,0:T(8,128)(2,1)S(1)} %get-tuple-element.23), channel_id=1, source_target_pairs={{0,7},{1,6},{2,5},{3,4},{4,3},{5,2},{6,1},{7,0},{8,15},{9,14},{10,... | collective-permute-start | bytes 196616 | tf_op jit(solution)/shard_map/ppermute | solution.py:219
  11.6 1.3 %collective-permute-start.4 = (bf16[2,128,128]{2,1,0:T(8,128)(2,1)S(1)}, bf16[2,128,128]{2,1,0:T(8,128)(2,1)S(1)}, u32[]{:S(2)}, u32[]{:S(2)}) collective-permute-start(bf16[2,128,128]{2,1,0:T(8,128)(2,1)S(1)} %get-tuple-element.24), channel_id=1, source_target_pairs={{0,5},{1,4},{2,7},{3,6},{4,1},{5,0},{6,3},{7,2},{8,13},{9,12},{10,... | collective-permute-start | bytes 196616 | tf_op jit(solution)/shard_map/ppermute | solution.py:219
  13.0 1.2 %collective-permute-start.5 = (bf16[2,128,128]{2,1,0:T(8,128)(2,1)S(1)}, bf16[2,128,128]{2,1,0:T(8,128)(2,1)S(1)}, u32[]{:S(2)}, u32[]{:S(2)}) collective-permute-start(bf16[2,128,128]{2,1,0:T(8,128)(2,1)S(1)} %get-tuple-element.25), channel_id=1, source_target_pairs={{0,2},{1,3},{2,0},{3,1},{4,6},{5,7},{6,4},{7,5},{8,10},{9,11},{10,... | collective-permute-start | bytes 196616 | tf_op jit(solution)/shard_map/ppermute | solution.py:219
  14.2 0.5 %collective-permute-start.6 = (bf16[2,128,128]{2,1,0:T(8,128)(2,1)S(1)}, bf16[2,128,128]{2,1,0:T(8,128)(2,1)S(1)}, u32[]{:S(2)}, u32[]{:S(2)}) collective-permute-start(bf16[2,128,128]{2,1,0:T(8,128)(2,1)S(1)} %get-tuple-element.26), channel_id=1, source_target_pairs={{0,1},{1,0},{2,3},{3,2},{4,5},{5,4},{6,7},{7,6},{8,9},{9,8},{10,11... | collective-permute-start | bytes 196616 | tf_op jit(solution)/shard_map/ppermute | solution.py:219
  14.8 1.2 %collective-permute-done.3 = bf16[2,128,128]{2,1,0:T(8,128)(2,1)S(1)} collective-permute-done((bf16[2,128,128]{2,1,0:T(8,128)(2,1)S(1)}, bf16[2,128,128]{2,1,0:T(8,128)(2,1)S(1)}, u32[]{:S(2)}, u32[]{:S(2)}) %collective-permute-start.3) | collective-permute-done | bytes 65568 | tf_op jit(solution)/shard_map/ppermute | solution.py:219
  16.1 3.5 %collective-permute-done.4 = bf16[2,128,128]{2,1,0:T(8,128)(2,1)S(1)} collective-permute-done((bf16[2,128,128]{2,1,0:T(8,128)(2,1)S(1)}, bf16[2,128,128]{2,1,0:T(8,128)(2,1)S(1)}, u32[]{:S(2)}, u32[]{:S(2)}) %collective-permute-start.4) | collective-permute-done | bytes 65568 | tf_op jit(solution)/shard_map/ppermute | solution.py:219
  19.9 3.1 %attend.1 = (bf16[192,128]{1,0:T(8,128)(2,1)S(1)}, bf16[192,128]{1,0:T(8,128)(2,1)S(1)}, bf16[192,128]{1,0:T(8,128)(2,1)S(1)}, bf16[192,128]{1,0:T(8,128)(2,1)S(...) custom-call(s32[50]{0:T(128)S(1)} %pad_add_fusion.table_ref, ...), custom_call_target="tpu_custom_call" | custom-call | tf_op jit(solution)/shard_map/attend/pallas_call | solution.py:264
  23.0 3.0 %collective-permute-start.7 = (bf16[192,128]{1,0:T(8,128)(2,1)S(1)}, bf16[192,128]{1,0:T(8,128)(2,1)S(1)}, u32[]{:S(2)}, u32[]{:S(2)}) collective-permute-start(bf16[192,128]{1,0:T(8,128)(2,1)S(1)} %get-tuple-element.28), channel_id=1, source_target_pairs={{0,6},{1,7},{2,4},{3,5},{4,2},{5,3},{6,0},{7,1},{8,14},{9,15},{10,... | collective-permute-start | bytes 147464 | tf_op jit(solution)/shard_map/ppermute | solution.py:219
  26.0 0.8 %collective-permute-start.8 = (bf16[192,128]{1,0:T(8,128)(2,1)S(1)}, bf16[192,128]{1,0:T(8,128)(2,1)S(1)}, u32[]{:S(2)}, u32[]{:S(2)}) collective-permute-start(bf16[192,128]{1,0:T(8,128)(2,1)S(1)} %get-tuple-element.29), channel_id=1, source_target_pairs={{0,5},{1,4},{2,7},{3,6},{4,1},{5,0},{6,3},{7,2},{8,13},{9,12},{10,... | collective-permute-start | bytes 147464 | tf_op jit(solution)/shard_map/ppermute | solution.py:219
  26.8 2.8 %collective-permute-start.9 = (bf16[192,128]{1,0:T(8,128)(2,1)S(1)}, bf16[192,128]{1,0:T(8,128)(2,1)S(1)}, u32[]{:S(2)}, u32[]{:S(2)}) collective-permute-start(bf16[192,128]{1,0:T(8,128)(2,1)S(1)} %get-tuple-element.30), channel_id=1, source_target_pairs={{0,7},{1,6},{2,5},{3,4},{4,3},{5,2},{6,1},{7,0},{8,15},{9,14},{10,... | collective-permute-start | bytes 147464 | tf_op jit(solution)/shard_map/ppermute | solution.py:219
  29.6 0.7 %collective-permute-start.10 = (bf16[192,128]{1,0:T(8,128)(2,1)S(1)}, bf16[192,128]{1,0:T(8,128)(2,1)S(1)}, u32[]{:S(2)}, u32[]{:S(2)}) collective-permute-start(bf16[192,128]{1,0:T(8,128)(2,1)S(1)} %get-tuple-element.31), channel_id=1, source_target_pairs={{0,3},{1,2},{2,1},{3,0},{4,7},{5,6},{6,5},{7,4},{8,11},{9,10},{10,... | collective-permute-start | bytes 147464 | tf_op jit(solution)/shard_map/ppermute | solution.py:219
  30.3 1.7 %collective-permute-start.11 = (bf16[192,128]{1,0:T(8,128)(2,1)S(1)}, bf16[192,128]{1,0:T(8,128)(2,1)S(1)}, u32[]{:S(2)}, u32[]{:S(2)}) collective-permute-start(bf16[192,128]{1,0:T(8,128)(2,1)S(1)} %get-tuple-element.32), channel_id=1, source_target_pairs={{0,4},{1,5},{2,6},{3,7},{4,0},{5,1},{6,2},{7,3},{8,12},{9,13},{10,... | collective-permute-start | bytes 147464 | tf_op jit(solution)/shard_map/ppermute | solution.py:219
  32.1 0.5 %collective-permute-start.12 = (bf16[192,128]{1,0:T(8,128)(2,1)S(1)}, bf16[192,128]{1,0:T(8,128)(2,1)S(1)}, u32[]{:S(2)}, u32[]{:S(2)}) collective-permute-start(bf16[192,128]{1,0:T(8,128)(2,1)S(1)} %get-tuple-element.33), channel_id=1, source_target_pairs={{0,2},{1,3},{2,0},{3,1},{4,6},{5,7},{6,4},{7,5},{8,10},{9,11},{10,... | collective-permute-start | bytes 147464 | tf_op jit(solution)/shard_map/ppermute | solution.py:219
  32.6 0.7 %collective-permute-start.13 = (bf16[192,128]{1,0:T(8,128)(2,1)S(1)}, bf16[192,128]{1,0:T(8,128)(2,1)S(1)}, u32[]{:S(2)}, u32[]{:S(2)}) collective-permute-start(bf16[192,128]{1,0:T(8,128)(2,1)S(1)} %get-tuple-element.34), channel_id=1, source_target_pairs={{0,1},{1,0},{2,3},{3,2},{4,5},{5,4},{6,7},{7,6},{8,9},{9,8},{10,11... | collective-permute-start | bytes 147464 | tf_op jit(solution)/shard_map/ppermute | solution.py:219
  33.3 0.4 %collective-permute-done.9.refs_3_ = bf16[192,128]{1,0:T(8,128)(2,1)S(1)} collective-permute-done((bf16[192,128]{1,0:T(8,128)(2,1)S(1)}, bf16[192,128]{1,0:T(8,128)(2,1)S(1)}, u32[]{:S(2)}, u32[]{:S(2)}) %collective-permute-start.9) | collective-permute-done | bytes 49184 | tf_op jit(solution)/shard_map/ppermute | solution.py:219
  33.7 1.2 %collective-permute-done.10.refs_4_ = bf16[192,128]{1,0:T(8,128)(2,1)S(1)} collective-permute-done((bf16[192,128]{1,0:T(8,128)(2,1)S(1)}, bf16[192,128]{1,0:T(8,128)(2,1)S(1)}, u32[]{:S(2)}, u32[]{:S(2)}) %collective-permute-start.10) | collective-permute-done | bytes 49184 | tf_op jit(solution)/shard_map/ppermute | solution.py:219
  34.8 0.5 %collective-permute-done.11.refs_5_ = bf16[192,128]{1,0:T(8,128)(2,1)S(1)} collective-permute-done((bf16[192,128]{1,0:T(8,128)(2,1)S(1)}, bf16[192,128]{1,0:T(8,128)(2,1)S(1)}, u32[]{:S(2)}, u32[]{:S(2)}) %collective-permute-start.11) | collective-permute-done | bytes 49184 | tf_op jit(solution)/shard_map/ppermute | solution.py:219
  35.3 0.8 %collective-permute-done.12.refs_6_ = bf16[192,128]{1,0:T(8,128)(2,1)S(1)} collective-permute-done((bf16[192,128]{1,0:T(8,128)(2,1)S(1)}, bf16[192,128]{1,0:T(8,128)(2,1)S(1)}, u32[]{:S(2)}, u32[]{:S(2)}) %collective-permute-start.12) | collective-permute-done | bytes 49184 | tf_op jit(solution)/shard_map/ppermute | solution.py:219
  36.2 0.5 %collective-permute-done.13.refs_7_ = bf16[192,128]{1,0:T(8,128)(2,1)S(1)} collective-permute-done((bf16[192,128]{1,0:T(8,128)(2,1)S(1)}, bf16[192,128]{1,0:T(8,128)(2,1)S(1)}, u32[]{:S(2)}, u32[]{:S(2)}) %collective-permute-start.13) | collective-permute-done | bytes 49184 | tf_op jit(solution)/shard_map/ppermute | solution.py:219
  36.7 0.9 %unpack.1 = (bf16[128,512]{1,0:T(8,128)(2,1)}, bf16[128,512]{1,0:T(8,128)(2,1)}, bf16[128,512]{1,0:T(8,128)(2,1)}) custom-call(bf16[192,128]{1,0:T(8,128)(2,1)S(1)} %get-tuple-element.27.refs_0_, bf16[192,128]{1,0:T(8,128)(2,1)S(1)} %collective-permute-done.7.refs_1_, bf16[192,128]{1,0:T(8,128)(2,1)S(1)} %collective-permute-done.8.refs_2_, ...), custom_call_target="tpu_custom_call" | custom-call | tf_op jit(solution)/shard_map/unpack/pallas_call | solution.py:280
  (14 shorter events, 0.6 us)
Async XLA Ops:
  2.1 10.9 %collective-permute-start = (bf16[2,128,128]{2,1,0:T(8,128)(2,1)S(1)}, bf16[2,128,128]{2,1,0:T(8,128)(2,1)S(1)}, u32[]{:S(2)}, u32[]{:S(2)}) collective-permute-start(bf16[2,128,128]{2,1,0:T(8,128)(2,1)S(1)} %get-tuple-element.20), channel_id=1, source_target_pairs={{0,4},{1,5},{2,6},{3,7},{4,0},{5,1},{6,2},{7,3},{8,12},{9,13},{10,... | collective-permute-start | bytes 196616 | tf_op jit(solution)/shard_map/ppermute | solution.py:219
  6.2 8.1 %collective-permute-start.1 = (bf16[2,128,128]{2,1,0:T(8,128)(2,1)S(1)}, bf16[2,128,128]{2,1,0:T(8,128)(2,1)S(1)}, u32[]{:S(2)}, u32[]{:S(2)}) collective-permute-start(bf16[2,128,128]{2,1,0:T(8,128)(2,1)S(1)} %get-tuple-element.21), channel_id=1, source_target_pairs={{0,6},{1,7},{2,4},{3,5},{4,2},{5,3},{6,0},{7,1},{8,14},{9,15},{10,... | collective-permute-start | bytes 196616 | tf_op jit(solution)/shard_map/ppermute | solution.py:219
  7.5 5.3 %copy-start = (s32[16,3]{0,1:T(4,128)S(1)}, s32[16,3]{0,1:T(4,128)}, u32[]{:S(2)}) copy-start(s32[16,3]{0,1:T(4,128)} %param.10) | copy-start | bytes 580
  7.5 7.3 %collective-permute-start.2 = (bf16[2,128,128]{2,1,0:T(8,128)(2,1)S(1)}, bf16[2,128,128]{2,1,0:T(8,128)(2,1)S(1)}, u32[]{:S(2)}, u32[]{:S(2)}) collective-permute-start(bf16[2,128,128]{2,1,0:T(8,128)(2,1)S(1)} %get-tuple-element.22), channel_id=1, source_target_pairs={{0,3},{1,2},{2,1},{3,0},{4,7},{5,6},{6,5},{7,4},{8,11},{9,10},{10,... | collective-permute-start | bytes 196616 | tf_op jit(solution)/shard_map/ppermute | solution.py:219
  8.7 7.4 %collective-permute-start.3 = (bf16[2,128,128]{2,1,0:T(8,128)(2,1)S(1)}, bf16[2,128,128]{2,1,0:T(8,128)(2,1)S(1)}, u32[]{:S(2)}, u32[]{:S(2)}) collective-permute-start(bf16[2,128,128]{2,1,0:T(8,128)(2,1)S(1)} %get-tuple-element.23), channel_id=1, source_target_pairs={{0,7},{1,6},{2,5},{3,4},{4,3},{5,2},{6,1},{7,0},{8,15},{9,14},{10,... | collective-permute-start | bytes 196616 | tf_op jit(solution)/shard_map/ppermute | solution.py:219
  11.6 8.0 %collective-permute-start.4 = (bf16[2,128,128]{2,1,0:T(8,128)(2,1)S(1)}, bf16[2,128,128]{2,1,0:T(8,128)(2,1)S(1)}, u32[]{:S(2)}, u32[]{:S(2)}) collective-permute-start(bf16[2,128,128]{2,1,0:T(8,128)(2,1)S(1)} %get-tuple-element.24), channel_id=1, source_target_pairs={{0,5},{1,4},{2,7},{3,6},{4,1},{5,0},{6,3},{7,2},{8,13},{9,12},{10,... | collective-permute-start | bytes 196616 | tf_op jit(solution)/shard_map/ppermute | solution.py:219
  13.0 1.7 %copy-start.1 = (s32[2]{0:T(128)S(1)}, s32[2]{0:T(128)}, u32[]{:S(2)}) copy-start(s32[2]{0:T(128)} %param.11) | copy-start | bytes 28
  13.0 6.5 %collective-permute-start.5 = (bf16[2,128,128]{2,1,0:T(8,128)(2,1)S(1)}, bf16[2,128,128]{2,1,0:T(8,128)(2,1)S(1)}, u32[]{:S(2)}, u32[]{:S(2)}) collective-permute-start(bf16[2,128,128]{2,1,0:T(8,128)(2,1)S(1)} %get-tuple-element.25), channel_id=1, source_target_pairs={{0,2},{1,3},{2,0},{3,1},{4,6},{5,7},{6,4},{7,5},{8,10},{9,11},{10,... | collective-permute-start | bytes 196616 | tf_op jit(solution)/shard_map/ppermute | solution.py:219
  14.2 5.7 %collective-permute-start.6 = (bf16[2,128,128]{2,1,0:T(8,128)(2,1)S(1)}, bf16[2,128,128]{2,1,0:T(8,128)(2,1)S(1)}, u32[]{:S(2)}, u32[]{:S(2)}) collective-permute-start(bf16[2,128,128]{2,1,0:T(8,128)(2,1)S(1)} %get-tuple-element.26), channel_id=1, source_target_pairs={{0,1},{1,0},{2,3},{3,2},{4,5},{5,4},{6,7},{7,6},{8,9},{9,8},{10,11... | collective-permute-start | bytes 196616 | tf_op jit(solution)/shard_map/ppermute | solution.py:219
  23.0 9.1 %collective-permute-start.7 = (bf16[192,128]{1,0:T(8,128)(2,1)S(1)}, bf16[192,128]{1,0:T(8,128)(2,1)S(1)}, u32[]{:S(2)}, u32[]{:S(2)}) collective-permute-start(bf16[192,128]{1,0:T(8,128)(2,1)S(1)} %get-tuple-element.28), channel_id=1, source_target_pairs={{0,6},{1,7},{2,4},{3,5},{4,2},{5,3},{6,0},{7,1},{8,14},{9,15},{10,... | collective-permute-start | bytes 147464 | tf_op jit(solution)/shard_map/ppermute | solution.py:219
  26.0 6.6 %collective-permute-start.8 = (bf16[192,128]{1,0:T(8,128)(2,1)S(1)}, bf16[192,128]{1,0:T(8,128)(2,1)S(1)}, u32[]{:S(2)}, u32[]{:S(2)}) collective-permute-start(bf16[192,128]{1,0:T(8,128)(2,1)S(1)} %get-tuple-element.29), channel_id=1, source_target_pairs={{0,5},{1,4},{2,7},{3,6},{4,1},{5,0},{6,3},{7,2},{8,13},{9,12},{10,... | collective-permute-start | bytes 147464 | tf_op jit(solution)/shard_map/ppermute | solution.py:219
  26.8 6.9 %collective-permute-start.9 = (bf16[192,128]{1,0:T(8,128)(2,1)S(1)}, bf16[192,128]{1,0:T(8,128)(2,1)S(1)}, u32[]{:S(2)}, u32[]{:S(2)}) collective-permute-start(bf16[192,128]{1,0:T(8,128)(2,1)S(1)} %get-tuple-element.30), channel_id=1, source_target_pairs={{0,7},{1,6},{2,5},{3,4},{4,3},{5,2},{6,1},{7,0},{8,15},{9,14},{10,... | collective-permute-start | bytes 147464 | tf_op jit(solution)/shard_map/ppermute | solution.py:219
  29.6 5.2 %collective-permute-start.10 = (bf16[192,128]{1,0:T(8,128)(2,1)S(1)}, bf16[192,128]{1,0:T(8,128)(2,1)S(1)}, u32[]{:S(2)}, u32[]{:S(2)}) collective-permute-start(bf16[192,128]{1,0:T(8,128)(2,1)S(1)} %get-tuple-element.31), channel_id=1, source_target_pairs={{0,3},{1,2},{2,1},{3,0},{4,7},{5,6},{6,5},{7,4},{8,11},{9,10},{10,... | collective-permute-start | bytes 147464 | tf_op jit(solution)/shard_map/ppermute | solution.py:219
  30.3 5.0 %collective-permute-start.11 = (bf16[192,128]{1,0:T(8,128)(2,1)S(1)}, bf16[192,128]{1,0:T(8,128)(2,1)S(1)}, u32[]{:S(2)}, u32[]{:S(2)}) collective-permute-start(bf16[192,128]{1,0:T(8,128)(2,1)S(1)} %get-tuple-element.32), channel_id=1, source_target_pairs={{0,4},{1,5},{2,6},{3,7},{4,0},{5,1},{6,2},{7,3},{8,12},{9,13},{10,... | collective-permute-start | bytes 147464 | tf_op jit(solution)/shard_map/ppermute | solution.py:219
  32.1 4.1 %collective-permute-start.12 = (bf16[192,128]{1,0:T(8,128)(2,1)S(1)}, bf16[192,128]{1,0:T(8,128)(2,1)S(1)}, u32[]{:S(2)}, u32[]{:S(2)}) collective-permute-start(bf16[192,128]{1,0:T(8,128)(2,1)S(1)} %get-tuple-element.33), channel_id=1, source_target_pairs={{0,2},{1,3},{2,0},{3,1},{4,6},{5,7},{6,4},{7,5},{8,10},{9,11},{10,... | collective-permute-start | bytes 147464 | tf_op jit(solution)/shard_map/ppermute | solution.py:219
  32.6 4.1 %collective-permute-start.13 = (bf16[192,128]{1,0:T(8,128)(2,1)S(1)}, bf16[192,128]{1,0:T(8,128)(2,1)S(1)}, u32[]{:S(2)}, u32[]{:S(2)}) collective-permute-start(bf16[192,128]{1,0:T(8,128)(2,1)S(1)} %get-tuple-element.34), channel_id=1, source_target_pairs={{0,1},{1,0},{2,3},{3,2},{4,5},{5,4},{6,7},{7,6},{8,9},{9,8},{10,11... | collective-permute-start | bytes 147464 | tf_op jit(solution)/shard_map/ppermute | solution.py:219

commit v9 on v8

--- a/solution.py
+++ b/solution.py
@@ -14,8 +14,8 @@
 GLOBAL = 2
 HEAD = 64
 LANES = 2 * HEAD
-PARTNERS_IN = (0, 4, 6, 3, 7, 5, 2, 1)
-PARTNERS_BACK = (0, 6, 5, 7, 3, 4, 2, 1)
+PARTNERS_IN = (0, 6, 5, 7, 3, 4, 2, 1)
+PARTNERS_BACK = (0, 2, 6, 3, 5, 4, 1)
 NEAR = (2, 3, 1, 0)
 PACK_GRANT = 427 * 2**17
 MASKED = -1e30
@@ -59,7 +59,8 @@
 
 
 def unpack_kernel(*refs):
-    in_refs = dict(zip(PARTNERS_BACK, refs[:HEADS]))
+    in_refs = dict(zip(PARTNERS_BACK + (7,), refs))
+    in_refs[6] = in_refs[6].at[0]
     gq_ref, gk_ref, gv_ref = refs[HEADS:]
     rows = gq_ref.shape[0]
     low = low_lanes((rows, LANES))
@@ -86,8 +87,9 @@
 def attend_kernel(alone, scale, table_ref, *rest):
     if alone:
         in_refs = dict(zip(PARTNERS_IN, rest[:HEADS]))
-        out_refs = rest[HEADS : 2 * HEADS]
-        sent_ref, gq_ref, acc_ref = rest[2 * HEADS :]
+        out_refs = dict(zip(PARTNERS_BACK, rest[HEADS:]))
+        out_refs[6], out_refs[7] = out_refs[6].at[0], out_refs[6].at[1]
+        sent_ref, gq_ref, acc_ref = rest[HEADS + len(PARTNERS_BACK) :]
         place = lax.rem(lax.axis_index("seq"), HEADS)
         for m in range(HEADS):
             sent_ref[lax.bitwise_xor(place, m)] = in_refs[m][...]
@@ -211,13 +213,26 @@
             out_refs[m][queries:] = gq_ref[tile]
 
 
-def exchange(parts, partners):
-    group = lax.axis_size("seq")
-    arrived = list(parts)
-    for m in partners[1:]:
-        route = [(i, i ^ m) for i in range(group)]
-        arrived[m] = lax.ppermute(parts[m], "seq", route)
-    return arrived
+def send(part, m):
+    return lax.ppermute(part, "seq", [(i, i ^ m) for i in range(lax.axis_size("seq"))])
+
+
+def second_kernel(got_ref, out_ref):
+    out_ref[...] = got_ref[1]
+
+
+def send_back(back):
+    got = [back[0]] + [send(part, m) for part, m in zip(back[1:], PARTNERS_BACK[1:])]
+    vmem = pl.BlockSpec(memory_space=pltpu.VMEM)
+    relayed = pl.pallas_call(
+        second_kernel,
+        out_shape=jax.ShapeDtypeStruct(back[0].shape, back[0].dtype),
+        in_specs=[vmem],
+        out_specs=vmem,
+        compiler_params=pltpu.CompilerParams(vmem_limit_bytes=8 * 2**20),
+        name="second",
+    )(got[PARTNERS_BACK.index(6)])
+    return got + [send(relayed, 1)]
 
 
 def moved(block, ranges, distance, ways, wrap=True):
@@ -257,15 +272,20 @@
         compiler_params=pltpu.CompilerParams(vmem_limit_bytes=PACK_GRANT),
         name="pack",
     )(queries, key_vectors, value_vectors, output_grad)
-    sent = [part.reshape(2, 2, BLOCK, LANES) for part in exchange(packed, PARTNERS_IN)]
+    sent = list(packed)
+    for m in PARTNERS_IN[1:]:
+        sent[m] = send(packed[m], m)
+    sent = [part.reshape(2, 2, BLOCK, LANES) for part in sent]
 
     kernel = functools.partial(attend_kernel, alone, scale)
+    back_shape = (rows + BLOCK, LANES)
     if alone:
+        back_shapes = [(2, *back_shape) if m == 6 else back_shape for m in PARTNERS_BACK]
         back = pl.pallas_call(
             kernel,
-            out_shape=[jax.ShapeDtypeStruct((rows + BLOCK, LANES), half_type)] * HEADS,
+            out_shape=[jax.ShapeDtypeStruct(shape, half_type) for shape in back_shapes],
             in_specs=[smem] + [vmem] * HEADS,
-            out_specs=[vmem] * HEADS,
+            out_specs=[vmem] * len(back_shapes),
             scratch_shapes=[
                 pltpu.VMEM((ways, 2, 2, BLOCK, LANES), half_type),
                 pltpu.VMEM((ways, BLOCK, LANES), half_type),
@@ -276,15 +296,15 @@
         )(jnp.concatenate([rand_pick.reshape(-1), global_ids]), *[sent[m] for m in PARTNERS_IN])
     else:
         back = spread_out(kernel, sent, rand_pick, global_ids, ways, ranges, blocks)
-    received = exchange(back, PARTNERS_BACK)
+    received = send_back(back)
     return pl.pallas_call(
         unpack_kernel,
         out_shape=[jax.ShapeDtypeStruct((rows, width), half_type)] * 3,
-        in_specs=[vmem] * HEADS,
+        in_specs=[vmem] * len(received),
         out_specs=[vmem] * 3,
         compiler_params=pltpu.CompilerParams(vmem_limit_bytes=8 * 2**20),
         name="unpack",
-    )(*[received[m] for m in PARTNERS_BACK])
+    )(*received)
 
 
 def spread_out(kernel, sent, rand_pick, global_ids, ways, ranges, blocks):
@@ -334,7 +354,7 @@
         base += blocks + 1
     grads = total.astype(jnp.bfloat16).reshape(ways, 2 * BLOCK, LANES)
     back = jnp.take(jnp.concatenate([grads, grad_query], axis=1), order, axis=0)
-    return [back[m] for m in range(ways)]
+    return [back[6:] if m == 6 else back[m] for m in PARTNERS_BACK]
 
 
 def solution(mesh):

time: 37.8 us -> 38.3 us (1.013)
  starting transfers between devices: 22.8 us -> 23.9 us
  waiting for transfers between devices: 8.42 us -> 7.84 us
    ppermute x14, starting transfers between devices: 22.8 us -> 23.9 us  [send(): lax.ppermute(part, 'seq', [(i, i ^ m) for i in range(lax.axis_size('seq'))])]
    ppermute x14, waiting for transfers between devices: 8.42 us -> 7.84 us  [send(): lax.ppermute(part, 'seq', [(i, i ^ m) for i in range(lax.axis_size('seq'))])]
    pallas_call x1 -> x2, Pallas kernels: 3.08 us -> 3.09 us  [the longest x1 3.08 us: on_device(): pl.pallas_call(kernel, out_shape=[jax.ShapeDtypeStruct(shape, half_type)...]
  transfers between devices with their start and end apart: 14 -> 14, of which waited for: 8 -> 6; matrix products, arithmetic and copies ran while one was open for 1% -> 1% of each run, Pallas kernels for 0% -> 0%
where the time goes in v9:
time: 38.3 us; the launch traced here: 38.1 us
  starting transfers between devices  23.9 us (62%)
  waiting for transfers between devices  7.84 us (20%)
  Pallas kernels  5.43 us (14%)
  between operations  0.68 us (2%)
    ppermute x14, starting transfers between devices, send(): lax.ppermute(part, 'seq', [(i, i ^ m) for i in range(lax.axis_size('seq'))])  23.9 us
    ppermute x14, waiting for transfers between devices, send(): lax.ppermute(part, 'seq', [(i, i ^ m) for i in range(lax.axis_size('seq'))])  7.84 us
    pallas_call x1, Pallas kernels, on_device(): pl.pallas_call(kernel, out_shape=[jax.ShapeDtypeStruct(shape, half_type)...  3.08 us
    pallas_call x1, Pallas kernels, on_device(): pl.pallas_call(pack_kernel, out_shape=[jax.ShapeDtypeStruct((2, rows, LAN...  1.42 us
    pallas_call x1, Pallas kernels, on_device(): pl.pallas_call(unpack_kernel, out_shape=[jax.ShapeDtypeStruct((rows, widt...  0.92 us
  transfers between devices with their start and end apart: 14, of which 6 were waited for; matrix products, arithmetic and copies ran while one was open for 1% of the time, Pallas kernels for 0%

profile of v9, /device:TPU:0, one launch (start us, length us, event | category | flops | bytes accessed | tf_op | source)
XLA Modules:
  0.0 38.1 jit_solution(9649579456031290283)
XLA Ops:
  0.6 1.4 %pack.1 = (bf16[2,128,128]{2,1,0:T(8,128)(2,1)S(1)}, bf16[2,128,128]{2,1,0:T(8,128)(2,1)S(1)}, bf16[2,128,128]{2,1,0:T(8,128)(2,1)S(1)}, bf16[2,128,128]{2,1,0:T...) custom-call(bf16[128,512]{1,0:T(8,128)(2,1)} %refs_0_.1, ...), custom_call_target="tpu_custom_call" | custom-call | tf_op jit(solution)/shard_map/pack/pallas_call | solution.py:263
  2.1 5.1 %collective-permute-start = (bf16[2,128,128]{2,1,0:T(8,128)(2,1)S(1)}, bf16[2,128,128]{2,1,0:T(8,128)(2,1)S(1)}, u32[]{:S(2)}, u32[]{:S(2)}) collective-permute-start(bf16[2,128,128]{2,1,0:T(8,128)(2,1)S(1)} %get-tuple-element.19), channel_id=1, source_target_pairs={{0,6},{1,7},{2,4},{3,5},{4,2},{5,3},{6,0},{7,1},{8,14},{9,15},{10,... | collective-permute-start | bytes 196616 | tf_op jit(solution)/shard_map/ppermute | solution.py:217
  7.2 0.4 collective-permute-start.1
  7.5 2.4 %collective-permute-start.2 = (bf16[2,128,128]{2,1,0:T(8,128)(2,1)S(1)}, bf16[2,128,128]{2,1,0:T(8,128)(2,1)S(1)}, u32[]{:S(2)}, u32[]{:S(2)}) collective-permute-start(bf16[2,128,128]{2,1,0:T(8,128)(2,1)S(1)} %get-tuple-element.21), channel_id=1, source_target_pairs={{0,7},{1,6},{2,5},{3,4},{4,3},{5,2},{6,1},{7,0},{8,15},{9,14},{10,... | collective-permute-start | bytes 196616 | tf_op jit(solution)/shard_map/ppermute | solution.py:217
  10.0 2.5 %collective-permute-start.3 = (bf16[2,128,128]{2,1,0:T(8,128)(2,1)S(1)}, bf16[2,128,128]{2,1,0:T(8,128)(2,1)S(1)}, u32[]{:S(2)}, u32[]{:S(2)}) collective-permute-start(bf16[2,128,128]{2,1,0:T(8,128)(2,1)S(1)} %get-tuple-element.22), channel_id=1, source_target_pairs={{0,3},{1,2},{2,1},{3,0},{4,7},{5,6},{6,5},{7,4},{8,11},{9,10},{10,... | collective-permute-start | bytes 196616 | tf_op jit(solution)/shard_map/ppermute | solution.py:217
  12.5 0.3 collective-permute-start.4
  12.8 0.1 copy.10
  12.9 0.1 reshape.33
  13.0 0.5 %collective-permute-start.5 = (bf16[2,128,128]{2,1,0:T(8,128)(2,1)S(1)}, bf16[2,128,128]{2,1,0:T(8,128)(2,1)S(1)}, u32[]{:S(2)}, u32[]{:S(2)}) collective-permute-start(bf16[2,128,128]{2,1,0:T(8,128)(2,1)S(1)} %get-tuple-element.24), channel_id=1, source_target_pairs={{0,2},{1,3},{2,0},{3,1},{4,6},{5,7},{6,4},{7,5},{8,10},{9,11},{10,... | collective-permute-start | bytes 196616 | tf_op jit(solution)/shard_map/ppermute | solution.py:217
  13.5 2.5 %collective-permute-done.1 = bf16[2,128,128]{2,1,0:T(8,128)(2,1)S(1)} collective-permute-done((bf16[2,128,128]{2,1,0:T(8,128)(2,1)S(1)}, bf16[2,128,128]{2,1,0:T(8,128)(2,1)S(1)}, u32[]{:S(2)}, u32[]{:S(2)}) %collective-permute-start.1) | collective-permute-done | bytes 65568 | tf_op jit(solution)/shard_map/ppermute | solution.py:217
  16.0 1.4 %collective-permute-start.6 = (bf16[2,128,128]{2,1,0:T(8,128)(2,1)S(1)}, bf16[2,128,128]{2,1,0:T(8,128)(2,1)S(1)}, u32[]{:S(2)}, u32[]{:S(2)}) collective-permute-start(bf16[2,128,128]{2,1,0:T(8,128)(2,1)S(1)} %get-tuple-element.25), channel_id=1, source_target_pairs={{0,1},{1,0},{2,3},{3,2},{4,5},{5,4},{6,7},{7,6},{8,9},{9,8},{10,11... | collective-permute-start | bytes 196616 | tf_op jit(solution)/shard_map/ppermute | solution.py:217
  17.4 0.1 pad_add_fusion.table_ref
  17.5 1.4 %collective-permute-done.4 = bf16[2,128,128]{2,1,0:T(8,128)(2,1)S(1)} collective-permute-done((bf16[2,128,128]{2,1,0:T(8,128)(2,1)S(1)}, bf16[2,128,128]{2,1,0:T(8,128)(2,1)S(1)}, u32[]{:S(2)}, u32[]{:S(2)}) %collective-permute-start.4) | collective-permute-done | bytes 65568 | tf_op jit(solution)/shard_map/ppermute | solution.py:217
  18.9 1.4 %collective-permute-done.6 = bf16[2,128,128]{2,1,0:T(8,128)(2,1)S(1)} collective-permute-done((bf16[2,128,128]{2,1,0:T(8,128)(2,1)S(1)}, bf16[2,128,128]{2,1,0:T(8,128)(2,1)S(1)}, u32[]{:S(2)}, u32[]{:S(2)}) %collective-permute-start.6) | collective-permute-done | bytes 65568 | tf_op jit(solution)/shard_map/ppermute | solution.py:217
  20.3 3.1 %attend.1 = (bf16[192,128]{1,0:T(8,128)(2,1)S(1)}, bf16[192,128]{1,0:T(8,128)(2,1)S(1)}, bf16[2,192,128]{2,1,0:T(8,128)(2,1)S(1)}, bf16[192,128]{1,0:T(8,128)(2,...) custom-call(s32[50]{0:T(128)S(1)} %pad_add_fusion.table_ref, ...), custom_call_target="tpu_custom_call" | custom-call | tf_op jit(solution)/shard_map/attend/pallas_call | solution.py:284
  23.4 3.3 %collective-permute-start.8 = (bf16[2,192,128]{2,1,0:T(8,128)(2,1)S(1)}, bf16[2,192,128]{2,1,0:T(8,128)(2,1)S(1)}, u32[]{:S(2)}, u32[]{:S(2)}) collective-permute-start(bf16[2,192,128]{2,1,0:T(8,128)(2,1)S(1)} %get-tuple-element.28), channel_id=1, source_target_pairs={{0,6},{1,7},{2,4},{3,5},{4,2},{5,3},{6,0},{7,1},{8,14},{9,15},{10,... | collective-permute-start | bytes 294920 | tf_op jit(solution)/shard_map/ppermute | solution.py:217
  26.7 1.5 %collective-permute-start.9 = (bf16[192,128]{1,0:T(8,128)(2,1)S(1)}, bf16[192,128]{1,0:T(8,128)(2,1)S(1)}, u32[]{:S(2)}, u32[]{:S(2)}) collective-permute-start(bf16[192,128]{1,0:T(8,128)(2,1)S(1)} %get-tuple-element.29), channel_id=1, source_target_pairs={{0,3},{1,2},{2,1},{3,0},{4,7},{5,6},{6,5},{7,4},{8,11},{9,10},{10,... | collective-permute-start | bytes 147464 | tf_op jit(solution)/shard_map/ppermute | solution.py:217
  28.2 0.5 %collective-permute-start.10 = (bf16[192,128]{1,0:T(8,128)(2,1)S(1)}, bf16[192,128]{1,0:T(8,128)(2,1)S(1)}, u32[]{:S(2)}, u32[]{:S(2)}) collective-permute-start(bf16[192,128]{1,0:T(8,128)(2,1)S(1)} %get-tuple-element.30), channel_id=1, source_target_pairs={{0,5},{1,4},{2,7},{3,6},{4,1},{5,0},{6,3},{7,2},{8,13},{9,12},{10,... | collective-permute-start | bytes 147464 | tf_op jit(solution)/shard_map/ppermute | solution.py:217
  28.7 3.8 %collective-permute-start.11 = (bf16[192,128]{1,0:T(8,128)(2,1)S(1)}, bf16[192,128]{1,0:T(8,128)(2,1)S(1)}, u32[]{:S(2)}, u32[]{:S(2)}) collective-permute-start(bf16[192,128]{1,0:T(8,128)(2,1)S(1)} %get-tuple-element.31), channel_id=1, source_target_pairs={{0,4},{1,5},{2,6},{3,7},{4,0},{5,1},{6,2},{7,3},{8,12},{9,13},{10,... | collective-permute-start | bytes 147464 | tf_op jit(solution)/shard_map/ppermute | solution.py:217
  32.6 2.1 %collective-permute-start.13 = (bf16[192,128]{1,0:T(8,128)(2,1)S(1)}, bf16[192,128]{1,0:T(8,128)(2,1)S(1)}, u32[]{:S(2)}, u32[]{:S(2)}) collective-permute-start(bf16[192,128]{1,0:T(8,128)(2,1)S(1)} %second.1), channel_id=1, source_target_pairs={{0,1},{1,0},{2,3},{3,2},{4,5},{5,4},{6,7},{7,6},{8,9},{9,8},{10,11... | collective-permute-start | bytes 147464 | tf_op jit(solution)/shard_map/ppermute | solution.py:217
  34.7 1.0 %collective-permute-done.11.refs_5_ = bf16[192,128]{1,0:T(8,128)(2,1)S(1)} collective-permute-done((bf16[192,128]{1,0:T(8,128)(2,1)S(1)}, bf16[192,128]{1,0:T(8,128)(2,1)S(1)}, u32[]{:S(2)}, u32[]{:S(2)}) %collective-permute-start.11) | collective-permute-done | bytes 49184 | tf_op jit(solution)/shard_map/ppermute | solution.py:217
  35.7 1.0 %collective-permute-done.12.refs_6_ = bf16[192,128]{1,0:T(8,128)(2,1)S(1)} collective-permute-done((bf16[192,128]{1,0:T(8,128)(2,1)S(1)}, bf16[192,128]{1,0:T(8,128)(2,1)S(1)}, u32[]{:S(2)}, u32[]{:S(2)}) %collective-permute-start.12) | collective-permute-done | bytes 49184 | tf_op jit(solution)/shard_map/ppermute | solution.py:217
  36.7 0.5 %collective-permute-done.13.refs_7_ = bf16[192,128]{1,0:T(8,128)(2,1)S(1)} collective-permute-done((bf16[192,128]{1,0:T(8,128)(2,1)S(1)}, bf16[192,128]{1,0:T(8,128)(2,1)S(1)}, u32[]{:S(2)}, u32[]{:S(2)}) %collective-permute-start.13) | collective-permute-done | bytes 49184 | tf_op jit(solution)/shard_map/ppermute | solution.py:217
  37.2 0.9 %unpack.1 = (bf16[128,512]{1,0:T(8,128)(2,1)}, bf16[128,512]{1,0:T(8,128)(2,1)}, bf16[128,512]{1,0:T(8,128)(2,1)}) custom-call(bf16[192,128]{1,0:T(8,128)(2,1)S(1)} %get-tuple-element.26.refs_0_, bf16[192,128]{1,0:T(8,128)(2,1)S(1)} %collective-permute-done.7.refs_1_, bf16[2,192,128]{2,1,0:T(8,128)(2,1)S(1)} %collective-permute-done.8.got_ref.refs_2_, ...), custom_call_target="tpu_custom_call" | custom-call | tf_op jit(solution)/shard_map/unpack/pallas_call | solution.py:300
  (15 shorter events, 0.1 us)
Async XLA Ops:
  2.1 10.9 %collective-permute-start = (bf16[2,128,128]{2,1,0:T(8,128)(2,1)S(1)}, bf16[2,128,128]{2,1,0:T(8,128)(2,1)S(1)}, u32[]{:S(2)}, u32[]{:S(2)}) collective-permute-start(bf16[2,128,128]{2,1,0:T(8,128)(2,1)S(1)} %get-tuple-element.19), channel_id=1, source_target_pairs={{0,6},{1,7},{2,4},{3,5},{4,2},{5,3},{6,0},{7,1},{8,14},{9,15},{10,... | collective-permute-start | bytes 196616 | tf_op jit(solution)/shard_map/ppermute | solution.py:217
  7.2 8.9 %collective-permute-start.1 = (bf16[2,128,128]{2,1,0:T(8,128)(2,1)S(1)}, bf16[2,128,128]{2,1,0:T(8,128)(2,1)S(1)}, u32[]{:S(2)}, u32[]{:S(2)}) collective-permute-start(bf16[2,128,128]{2,1,0:T(8,128)(2,1)S(1)} %get-tuple-element.20), channel_id=1, source_target_pairs={{0,5},{1,4},{2,7},{3,6},{4,1},{5,0},{6,3},{7,2},{8,13},{9,12},{10,... | collective-permute-start | bytes 196616 | tf_op jit(solution)/shard_map/ppermute | solution.py:217
  7.5 5.3 %copy-start = (s32[16,3]{0,1:T(4,128)S(1)}, s32[16,3]{0,1:T(4,128)}, u32[]{:S(2)}) copy-start(s32[16,3]{0,1:T(4,128)} %param.10) | copy-start | bytes 580
  7.5 9.9 %collective-permute-start.2 = (bf16[2,128,128]{2,1,0:T(8,128)(2,1)S(1)}, bf16[2,128,128]{2,1,0:T(8,128)(2,1)S(1)}, u32[]{:S(2)}, u32[]{:S(2)}) collective-permute-start(bf16[2,128,128]{2,1,0:T(8,128)(2,1)S(1)} %get-tuple-element.21), channel_id=1, source_target_pairs={{0,7},{1,6},{2,5},{3,4},{4,3},{5,2},{6,1},{7,0},{8,15},{9,14},{10,... | collective-permute-start | bytes 196616 | tf_op jit(solution)/shard_map/ppermute | solution.py:217
  10.0 7.5 %collective-permute-start.3 = (bf16[2,128,128]{2,1,0:T(8,128)(2,1)S(1)}, bf16[2,128,128]{2,1,0:T(8,128)(2,1)S(1)}, u32[]{:S(2)}, u32[]{:S(2)}) collective-permute-start(bf16[2,128,128]{2,1,0:T(8,128)(2,1)S(1)} %get-tuple-element.22), channel_id=1, source_target_pairs={{0,3},{1,2},{2,1},{3,0},{4,7},{5,6},{6,5},{7,4},{8,11},{9,10},{10,... | collective-permute-start | bytes 196616 | tf_op jit(solution)/shard_map/ppermute | solution.py:217
  12.5 6.4 %collective-permute-start.4 = (bf16[2,128,128]{2,1,0:T(8,128)(2,1)S(1)}, bf16[2,128,128]{2,1,0:T(8,128)(2,1)S(1)}, u32[]{:S(2)}, u32[]{:S(2)}) collective-permute-start(bf16[2,128,128]{2,1,0:T(8,128)(2,1)S(1)} %get-tuple-element.23), channel_id=1, source_target_pairs={{0,4},{1,5},{2,6},{3,7},{4,0},{5,1},{6,2},{7,3},{8,12},{9,13},{10,... | collective-permute-start | bytes 196616 | tf_op jit(solution)/shard_map/ppermute | solution.py:217
  13.0 4.4 %copy-start.1 = (s32[2]{0:T(128)S(1)}, s32[2]{0:T(128)}, u32[]{:S(2)}) copy-start(s32[2]{0:T(128)} %param.11) | copy-start | bytes 28
  13.0 5.8 %collective-permute-start.5 = (bf16[2,128,128]{2,1,0:T(8,128)(2,1)S(1)}, bf16[2,128,128]{2,1,0:T(8,128)(2,1)S(1)}, u32[]{:S(2)}, u32[]{:S(2)}) collective-permute-start(bf16[2,128,128]{2,1,0:T(8,128)(2,1)S(1)} %get-tuple-element.24), channel_id=1, source_target_pairs={{0,2},{1,3},{2,0},{3,1},{4,6},{5,7},{6,4},{7,5},{8,10},{9,11},{10,... | collective-permute-start | bytes 196616 | tf_op jit(solution)/shard_map/ppermute | solution.py:217
  16.0 4.3 %collective-permute-start.6 = (bf16[2,128,128]{2,1,0:T(8,128)(2,1)S(1)}, bf16[2,128,128]{2,1,0:T(8,128)(2,1)S(1)}, u32[]{:S(2)}, u32[]{:S(2)}) collective-permute-start(bf16[2,128,128]{2,1,0:T(8,128)(2,1)S(1)} %get-tuple-element.25), channel_id=1, source_target_pairs={{0,1},{1,0},{2,3},{3,2},{4,5},{5,4},{6,7},{7,6},{8,9},{9,8},{10,11... | collective-permute-start | bytes 196616 | tf_op jit(solution)/shard_map/ppermute | solution.py:217
  23.4 9.2 %collective-permute-start.8 = (bf16[2,192,128]{2,1,0:T(8,128)(2,1)S(1)}, bf16[2,192,128]{2,1,0:T(8,128)(2,1)S(1)}, u32[]{:S(2)}, u32[]{:S(2)}) collective-permute-start(bf16[2,192,128]{2,1,0:T(8,128)(2,1)S(1)} %get-tuple-element.28), channel_id=1, source_target_pairs={{0,6},{1,7},{2,4},{3,5},{4,2},{5,3},{6,0},{7,1},{8,14},{9,15},{10,... | collective-permute-start | bytes 294920 | tf_op jit(solution)/shard_map/ppermute | solution.py:217
  26.7 5.9 %collective-permute-start.7 = (bf16[192,128]{1,0:T(8,128)(2,1)S(1)}, bf16[192,128]{1,0:T(8,128)(2,1)S(1)}, u32[]{:S(2)}, u32[]{:S(2)}) collective-permute-start(bf16[192,128]{1,0:T(8,128)(2,1)S(1)} %get-tuple-element.27), channel_id=1, source_target_pairs={{0,2},{1,3},{2,0},{3,1},{4,6},{5,7},{6,4},{7,5},{8,10},{9,11},{10,... | collective-permute-start | bytes 147464 | tf_op jit(solution)/shard_map/ppermute | solution.py:217
  26.7 8.0 %collective-permute-start.9 = (bf16[192,128]{1,0:T(8,128)(2,1)S(1)}, bf16[192,128]{1,0:T(8,128)(2,1)S(1)}, u32[]{:S(2)}, u32[]{:S(2)}) collective-permute-start(bf16[192,128]{1,0:T(8,128)(2,1)S(1)} %get-tuple-element.29), channel_id=1, source_target_pairs={{0,3},{1,2},{2,1},{3,0},{4,7},{5,6},{6,5},{7,4},{8,11},{9,10},{10,... | collective-permute-start | bytes 147464 | tf_op jit(solution)/shard_map/ppermute | solution.py:217
  28.2 6.5 %collective-permute-start.10 = (bf16[192,128]{1,0:T(8,128)(2,1)S(1)}, bf16[192,128]{1,0:T(8,128)(2,1)S(1)}, u32[]{:S(2)}, u32[]{:S(2)}) collective-permute-start(bf16[192,128]{1,0:T(8,128)(2,1)S(1)} %get-tuple-element.30), channel_id=1, source_target_pairs={{0,5},{1,4},{2,7},{3,6},{4,1},{5,0},{6,3},{7,2},{8,13},{9,12},{10,... | collective-permute-start | bytes 147464 | tf_op jit(solution)/shard_map/ppermute | solution.py:217
  28.7 6.9 %collective-permute-start.11 = (bf16[192,128]{1,0:T(8,128)(2,1)S(1)}, bf16[192,128]{1,0:T(8,128)(2,1)S(1)}, u32[]{:S(2)}, u32[]{:S(2)}) collective-permute-start(bf16[192,128]{1,0:T(8,128)(2,1)S(1)} %get-tuple-element.31), channel_id=1, source_target_pairs={{0,4},{1,5},{2,6},{3,7},{4,0},{5,1},{6,2},{7,3},{8,12},{9,13},{10,... | collective-permute-start | bytes 147464 | tf_op jit(solution)/shard_map/ppermute | solution.py:217
  32.6 4.1 %collective-permute-start.12 = (bf16[192,128]{1,0:T(8,128)(2,1)S(1)}, bf16[192,128]{1,0:T(8,128)(2,1)S(1)}, u32[]{:S(2)}, u32[]{:S(2)}) collective-permute-start(bf16[192,128]{1,0:T(8,128)(2,1)S(1)} %get-tuple-element.32), channel_id=1, source_target_pairs={{0,1},{1,0},{2,3},{3,2},{4,5},{5,4},{6,7},{7,6},{8,9},{9,8},{10,11... | collective-permute-start | bytes 147464 | tf_op jit(solution)/shard_map/ppermute | solution.py:217
  32.6 4.6 %collective-permute-start.13 = (bf16[192,128]{1,0:T(8,128)(2,1)S(1)}, bf16[192,128]{1,0:T(8,128)(2,1)S(1)}, u32[]{:S(2)}, u32[]{:S(2)}) collective-permute-start(bf16[192,128]{1,0:T(8,128)(2,1)S(1)} %second.1), channel_id=1, source_target_pairs={{0,1},{1,0},{2,3},{3,2},{4,5},{5,4},{6,7},{7,6},{8,9},{9,8},{10,11... | collective-permute-start | bytes 147464 | tf_op jit(solution)/shard_map/ppermute | solution.py:217

commit v10 on v8

--- a/solution.py
+++ b/solution.py
@@ -83,16 +83,25 @@
         gq_ref[BLOCK:, lanes] = second.astype(jnp.bfloat16)
 
 
-def attend_kernel(alone, scale, table_ref, *rest):
+def attend_kernel(alone, scale, ints_ref, *rest):
     if alone:
         in_refs = dict(zip(PARTNERS_IN, rest[:HEADS]))
         out_refs = rest[HEADS : 2 * HEADS]
-        sent_ref, gq_ref, acc_ref = rest[2 * HEADS :]
+        sent_ref, pool_ref, gq_ref, acc_ref, swapped_ref, table_ref, sem = rest[2 * HEADS :]
+    else:
+        sent_ref, pool_ref, gq_ref, acc_ref, swapped_ref, table_ref, sem = rest
+    fetch = pltpu.make_async_copy(ints_ref, table_ref, sem)
+    fetch.start()
+    if alone:
         place = lax.rem(lax.axis_index("seq"), HEADS)
         for m in range(HEADS):
-            sent_ref[lax.bitwise_xor(place, m)] = in_refs[m][...]
-    else:
-        sent_ref, pool_ref, gq_ref, acc_ref = rest
+            tile = lax.bitwise_xor(place, m)
+            sent_ref[tile] = in_refs[m][1]
+            for half in range(2):
+                pool_ref[2 * tile + half] = in_refs[m][0, half]
+    for entry in range(pool_ref.shape[0]):
+        swapped = swap_halves(pool_ref[entry].astype(jnp.float32))
+        swapped_ref[entry] = swapped.astype(jnp.bfloat16)
     tiles = sent_ref.shape[0]
     blocks = 2 * tiles
     queries = 2 * BLOCK
@@ -100,11 +109,7 @@
     zero = jnp.zeros((BLOCK, LANES), jnp.bfloat16)
     fixed = blocks * RAND
     acc_ref[...] = jnp.zeros_like(acc_ref)
-
-    def pooled(entry):
-        if alone:
-            return sent_ref[entry // 2, 0, entry % 2]
-        return pool_ref[entry]
+    fetch.wait()
 
     def chosen(tile):
         first = 2 * tile
@@ -135,9 +140,9 @@
     def multiply(tile):
         pairs = chosen(tile)
         keys = jnp.concatenate(
-            [jnp.concatenate([pooled(a), pooled(b)], axis=1) for a, b in pairs], axis=0
+            [jnp.concatenate([pool_ref[a], pool_ref[b]], axis=1) for a, b in pairs], axis=0
         )
-        first, second = sent_ref[tile, 1, 0], sent_ref[tile, 1, 1]
+        first, second = sent_ref[tile, 0], sent_ref[tile, 1]
         rows = [
             [jnp.where(low, first * scale, zero), zero],
             [zero, jnp.where(low, second * scale, zero)],
@@ -148,7 +153,7 @@
         products = lax.dot_general(
             keys, sides, (((1,), (1,)), ((), ())), preferred_element_type=jnp.float32
         )
-        return pairs, keys, sides, products
+        return pairs, sides, products
 
     def weigh(tile, products):
         scores, grad_probs = products[:, :queries], products[:, queries:]
@@ -174,17 +179,18 @@
         grad_half = (probs * (grad_probs - row_dot)).astype(jnp.bfloat16)
         return grad_half, probs_half
 
-    def gather(tile, pairs, keys, sides, grad_half, probs_half):
+    def gather(tile, pairs, sides, grad_half, probs_half):
         both = jnp.concatenate([grad_half, probs_half], axis=1)
         key_grads = jnp.dot(both, sides, preferred_element_type=jnp.float32)
+        keys = jnp.concatenate(
+            [jnp.where(low, pool_ref[a], swapped_ref[b]) for a, b in pairs], axis=0
+        )
         grad_query = lax.dot_general(
             grad_half, keys, (((0,), (0,)), ((), ())), preferred_element_type=jnp.float32
         )
         grad_query = grad_query * scale
-        folded = jnp.where(
-            low, grad_query[:BLOCK, :LANES], swap_halves(grad_query[BLOCK:, LANES:])
-        ).astype(jnp.bfloat16)
-        gq_ref[tile] = folded
+        folded = jnp.where(low, grad_query[:BLOCK], grad_query[BLOCK:])
+        gq_ref[tile] = folded.astype(jnp.bfloat16)
         for place, (a, b) in enumerate(pairs):
             part = key_grads[place * BLOCK : (place + 1) * BLOCK]
             if place < 2 + GLOBAL:
@@ -200,8 +206,8 @@
         if 0 <= step - 1 < tiles:
             weighed[step - 1] = weigh(step - 1, ahead[step - 1][-1])
         if step >= 2:
-            pairs, keys, sides, _ = ahead.pop(step - 2)
-            gather(step - 2, pairs, keys, sides, *weighed.pop(step - 2))
+            pairs, sides, _ = ahead.pop(step - 2)
+            gather(step - 2, pairs, sides, *weighed.pop(step - 2))
     if alone:
         for m in range(HEADS):
             tile = lax.bitwise_xor(place, m)
@@ -241,7 +247,6 @@
     blocks = ways * rows // BLOCK
     scale = 1.0 / math.sqrt(width // HEADS)
     vmem = pl.BlockSpec(memory_space=pltpu.VMEM)
-    smem = pl.BlockSpec(memory_space=pltpu.SMEM)
     half_type = jnp.bfloat16
 
     anywhere = pl.BlockSpec(memory_space=pl.ANY)
@@ -264,12 +269,16 @@
         back = pl.pallas_call(
             kernel,
             out_shape=[jax.ShapeDtypeStruct((rows + BLOCK, LANES), half_type)] * HEADS,
-            in_specs=[smem] + [vmem] * HEADS,
+            in_specs=[anywhere] + [vmem] * HEADS,
             out_specs=[vmem] * HEADS,
             scratch_shapes=[
-                pltpu.VMEM((ways, 2, 2, BLOCK, LANES), half_type),
+                pltpu.VMEM((ways, 2, BLOCK, LANES), half_type),
+                pltpu.VMEM((blocks, BLOCK, LANES), half_type),
                 pltpu.VMEM((ways, BLOCK, LANES), half_type),
                 pltpu.VMEM((blocks, BLOCK, LANES), jnp.float32),
+                pltpu.VMEM((blocks, BLOCK, LANES), half_type),
+                pltpu.SMEM((blocks * RAND + GLOBAL,), jnp.int32),
+                pltpu.SemaphoreType.DMA,
             ],
             compiler_params=pltpu.CompilerParams(vmem_limit_bytes=24 * 2**20),
             name="attend",
@@ -289,7 +298,6 @@
 
 def spread_out(kernel, sent, rand_pick, global_ids, ways, ranges, blocks):
     vmem = pl.BlockSpec(memory_space=pltpu.VMEM)
-    smem = pl.BlockSpec(memory_space=pltpu.SMEM)
     mine = lax.axis_index("seq") // ways
     order = lax.bitwise_xor(lax.axis_index("seq") % ways, jnp.arange(ways, dtype=jnp.int32))
     sent = jnp.take(jnp.stack(sent), order, axis=0)
@@ -314,11 +322,16 @@
             jax.ShapeDtypeStruct((ways, BLOCK, LANES), jnp.bfloat16),
             jax.ShapeDtypeStruct(pool.shape, jnp.float32),
         ],
-        in_specs=[smem, vmem, vmem],
+        in_specs=[pl.BlockSpec(memory_space=pl.ANY), vmem, vmem],
         out_specs=[vmem] * 2,
+        scratch_shapes=[
+            pltpu.VMEM(pool.shape, pool.dtype),
+            pltpu.SMEM(table.shape, jnp.int32),
+            pltpu.SemaphoreType.DMA,
+        ],
         compiler_params=pltpu.CompilerParams(vmem_limit_bytes=24 * 2**20),
         name="attend",
-    )(table, sent, pool)
+    )(table, sent[:, 1], pool)
     total = totals[:blocks]
     total = total.at[-1].add(moved(totals[blocks], ranges, -1, ways, False))
     total = total.at[0].add(moved(totals[blocks + 1], ranges, 1, ways, False))

time: 37.8 us -> 37.9 us (level)
  no operation moved by 1% of the time
where the time goes in v10:
time: 37.9 us; the launch traced here: 37.7 us
  starting transfers between devices  22.8 us (60%)
  waiting for transfers between devices  8.42 us (22%)
  Pallas kernels  5.55 us (15%)
  between operations  0.68 us (2%)
    ppermute x14, starting transfers between devices, exchange(): arrived[m] = lax.ppermute(parts[m], 'seq', route)  22.8 us
    ppermute x14, waiting for transfers between devices, exchange(): arrived[m] = lax.ppermute(parts[m], 'seq', route)  8.42 us
    pallas_call x1, Pallas kernels, on_device(): pl.pallas_call(kernel, out_shape=[jax.ShapeDtypeStruct((rows + BLOCK, LAN...  3.21 us
    pallas_call x1, Pallas kernels, on_device(): pl.pallas_call(pack_kernel, out_shape=[jax.ShapeDtypeStruct((2, rows, LAN...  1.42 us
    pallas_call x1, Pallas kernels, on_device(): pl.pallas_call(unpack_kernel, out_shape=[jax.ShapeDtypeStruct((rows, widt...  0.92 us
  transfers between devices with their start and end apart: 14, of which 8 were waited for; matrix products, arithmetic and copies ran while one was open for 1% of the time, Pallas kernels for 0%

profile of v10, /device:TPU:0, one launch (start us, length us, event | category | flops | bytes accessed | tf_op | source)
XLA Modules:
  0.0 37.7 jit_solution(7424180402039735918)
XLA Ops:
  0.6 1.4 %pack.1 = (bf16[2,128,128]{2,1,0:T(8,128)(2,1)S(1)}, bf16[2,128,128]{2,1,0:T(8,128)(2,1)S(1)}, bf16[2,128,128]{2,1,0:T(8,128)(2,1)S(1)}, bf16[2,128,128]{2,1,0:T...) custom-call(bf16[128,512]{1,0:T(8,128)(2,1)} %refs_0_.1, ...), custom_call_target="tpu_custom_call" | custom-call | tf_op jit(solution)/shard_map/pack/pallas_call | solution.py:253
  2.1 4.1 %collective-permute-start = (bf16[2,128,128]{2,1,0:T(8,128)(2,1)S(1)}, bf16[2,128,128]{2,1,0:T(8,128)(2,1)S(1)}, u32[]{:S(2)}, u32[]{:S(2)}) collective-permute-start(bf16[2,128,128]{2,1,0:T(8,128)(2,1)S(1)} %get-tuple-element.20), channel_id=1, source_target_pairs={{0,4},{1,5},{2,6},{3,7},{4,0},{5,1},{6,2},{7,3},{8,12},{9,13},{10,... | collective-permute-start | bytes 196616 | tf_op jit(solution)/shard_map/ppermute | solution.py:225
  6.2 1.3 %collective-permute-start.1 = (bf16[2,128,128]{2,1,0:T(8,128)(2,1)S(1)}, bf16[2,128,128]{2,1,0:T(8,128)(2,1)S(1)}, u32[]{:S(2)}, u32[]{:S(2)}) collective-permute-start(bf16[2,128,128]{2,1,0:T(8,128)(2,1)S(1)} %get-tuple-element.21), channel_id=1, source_target_pairs={{0,6},{1,7},{2,4},{3,5},{4,2},{5,3},{6,0},{7,1},{8,14},{9,15},{10,... | collective-permute-start | bytes 196616 | tf_op jit(solution)/shard_map/ppermute | solution.py:225
  7.5 1.2 %collective-permute-start.2 = (bf16[2,128,128]{2,1,0:T(8,128)(2,1)S(1)}, bf16[2,128,128]{2,1,0:T(8,128)(2,1)S(1)}, u32[]{:S(2)}, u32[]{:S(2)}) collective-permute-start(bf16[2,128,128]{2,1,0:T(8,128)(2,1)S(1)} %get-tuple-element.22), channel_id=1, source_target_pairs={{0,3},{1,2},{2,1},{3,0},{4,7},{5,6},{6,5},{7,4},{8,11},{9,10},{10,... | collective-permute-start | bytes 196616 | tf_op jit(solution)/shard_map/ppermute | solution.py:225
  8.7 2.9 %collective-permute-start.3 = (bf16[2,128,128]{2,1,0:T(8,128)(2,1)S(1)}, bf16[2,128,128]{2,1,0:T(8,128)(2,1)S(1)}, u32[]{:S(2)}, u32[]{:S(2)}) collective-permute-start(bf16[2,128,128]{2,1,0:T(8,128)(2,1)S(1)} %get-tuple-element.23), channel_id=1, source_target_pairs={{0,7},{1,6},{2,5},{3,4},{4,3},{5,2},{6,1},{7,0},{8,15},{9,14},{10,... | collective-permute-start | bytes 196616 | tf_op jit(solution)/shard_map/ppermute | solution.py:225
  11.6 1.3 %collective-permute-start.4 = (bf16[2,128,128]{2,1,0:T(8,128)(2,1)S(1)}, bf16[2,128,128]{2,1,0:T(8,128)(2,1)S(1)}, u32[]{:S(2)}, u32[]{:S(2)}) collective-permute-start(bf16[2,128,128]{2,1,0:T(8,128)(2,1)S(1)} %get-tuple-element.24), channel_id=1, source_target_pairs={{0,5},{1,4},{2,7},{3,6},{4,1},{5,0},{6,3},{7,2},{8,13},{9,12},{10,... | collective-permute-start | bytes 196616 | tf_op jit(solution)/shard_map/ppermute | solution.py:225
  13.0 1.2 %collective-permute-start.5 = (bf16[2,128,128]{2,1,0:T(8,128)(2,1)S(1)}, bf16[2,128,128]{2,1,0:T(8,128)(2,1)S(1)}, u32[]{:S(2)}, u32[]{:S(2)}) collective-permute-start(bf16[2,128,128]{2,1,0:T(8,128)(2,1)S(1)} %get-tuple-element.25), channel_id=1, source_target_pairs={{0,2},{1,3},{2,0},{3,1},{4,6},{5,7},{6,4},{7,5},{8,10},{9,11},{10,... | collective-permute-start | bytes 196616 | tf_op jit(solution)/shard_map/ppermute | solution.py:225
  14.2 0.5 %collective-permute-start.6 = (bf16[2,128,128]{2,1,0:T(8,128)(2,1)S(1)}, bf16[2,128,128]{2,1,0:T(8,128)(2,1)S(1)}, u32[]{:S(2)}, u32[]{:S(2)}) collective-permute-start(bf16[2,128,128]{2,1,0:T(8,128)(2,1)S(1)} %get-tuple-element.26), channel_id=1, source_target_pairs={{0,1},{1,0},{2,3},{3,2},{4,5},{5,4},{6,7},{7,6},{8,9},{9,8},{10,11... | collective-permute-start | bytes 196616 | tf_op jit(solution)/shard_map/ppermute | solution.py:225
  14.8 1.2 %collective-permute-done.3 = bf16[2,128,128]{2,1,0:T(8,128)(2,1)S(1)} collective-permute-done((bf16[2,128,128]{2,1,0:T(8,128)(2,1)S(1)}, bf16[2,128,128]{2,1,0:T(8,128)(2,1)S(1)}, u32[]{:S(2)}, u32[]{:S(2)}) %collective-permute-start.3) | collective-permute-done | bytes 65568 | tf_op jit(solution)/shard_map/ppermute | solution.py:225
  16.1 3.5 %collective-permute-done.4 = bf16[2,128,128]{2,1,0:T(8,128)(2,1)S(1)} collective-permute-done((bf16[2,128,128]{2,1,0:T(8,128)(2,1)S(1)}, bf16[2,128,128]{2,1,0:T(8,128)(2,1)S(1)}, u32[]{:S(2)}, u32[]{:S(2)}) %collective-permute-start.4) | collective-permute-done | bytes 65568 | tf_op jit(solution)/shard_map/ppermute | solution.py:225
  19.9 3.2 %attend.1 = (bf16[192,128]{1,0:T(8,128)(2,1)S(1)}, bf16[192,128]{1,0:T(8,128)(2,1)S(1)}, bf16[192,128]{1,0:T(8,128)(2,1)S(1)}, bf16[192,128]{1,0:T(8,128)(2,1)S(...) custom-call(s32[50]{0:T(128)S(1)} %pad_add_fusion.ints_ref, ...), custom_call_target="tpu_custom_call" | custom-call | tf_op jit(solution)/shard_map/attend/pallas_call | solution.py:269
  23.1 3.0 %collective-permute-start.7 = (bf16[192,128]{1,0:T(8,128)(2,1)S(1)}, bf16[192,128]{1,0:T(8,128)(2,1)S(1)}, u32[]{:S(2)}, u32[]{:S(2)}) collective-permute-start(bf16[192,128]{1,0:T(8,128)(2,1)S(1)} %get-tuple-element.28), channel_id=1, source_target_pairs={{0,6},{1,7},{2,4},{3,5},{4,2},{5,3},{6,0},{7,1},{8,14},{9,15},{10,... | collective-permute-start | bytes 147464 | tf_op jit(solution)/shard_map/ppermute | solution.py:225
  26.1 0.8 %collective-permute-start.8 = (bf16[192,128]{1,0:T(8,128)(2,1)S(1)}, bf16[192,128]{1,0:T(8,128)(2,1)S(1)}, u32[]{:S(2)}, u32[]{:S(2)}) collective-permute-start(bf16[192,128]{1,0:T(8,128)(2,1)S(1)} %get-tuple-element.29), channel_id=1, source_target_pairs={{0,5},{1,4},{2,7},{3,6},{4,1},{5,0},{6,3},{7,2},{8,13},{9,12},{10,... | collective-permute-start | bytes 147464 | tf_op jit(solution)/shard_map/ppermute | solution.py:225
  26.9 2.8 %collective-permute-start.9 = (bf16[192,128]{1,0:T(8,128)(2,1)S(1)}, bf16[192,128]{1,0:T(8,128)(2,1)S(1)}, u32[]{:S(2)}, u32[]{:S(2)}) collective-permute-start(bf16[192,128]{1,0:T(8,128)(2,1)S(1)} %get-tuple-element.30), channel_id=1, source_target_pairs={{0,7},{1,6},{2,5},{3,4},{4,3},{5,2},{6,1},{7,0},{8,15},{9,14},{10,... | collective-permute-start | bytes 147464 | tf_op jit(solution)/shard_map/ppermute | solution.py:225
  29.7 0.7 %collective-permute-start.10 = (bf16[192,128]{1,0:T(8,128)(2,1)S(1)}, bf16[192,128]{1,0:T(8,128)(2,1)S(1)}, u32[]{:S(2)}, u32[]{:S(2)}) collective-permute-start(bf16[192,128]{1,0:T(8,128)(2,1)S(1)} %get-tuple-element.31), channel_id=1, source_target_pairs={{0,3},{1,2},{2,1},{3,0},{4,7},{5,6},{6,5},{7,4},{8,11},{9,10},{10,... | collective-permute-start | bytes 147464 | tf_op jit(solution)/shard_map/ppermute | solution.py:225
  30.5 1.7 %collective-permute-start.11 = (bf16[192,128]{1,0:T(8,128)(2,1)S(1)}, bf16[192,128]{1,0:T(8,128)(2,1)S(1)}, u32[]{:S(2)}, u32[]{:S(2)}) collective-permute-start(bf16[192,128]{1,0:T(8,128)(2,1)S(1)} %get-tuple-element.32), channel_id=1, source_target_pairs={{0,4},{1,5},{2,6},{3,7},{4,0},{5,1},{6,2},{7,3},{8,12},{9,13},{10,... | collective-permute-start | bytes 147464 | tf_op jit(solution)/shard_map/ppermute | solution.py:225
  32.2 0.5 %collective-permute-start.12 = (bf16[192,128]{1,0:T(8,128)(2,1)S(1)}, bf16[192,128]{1,0:T(8,128)(2,1)S(1)}, u32[]{:S(2)}, u32[]{:S(2)}) collective-permute-start(bf16[192,128]{1,0:T(8,128)(2,1)S(1)} %get-tuple-element.33), channel_id=1, source_target_pairs={{0,2},{1,3},{2,0},{3,1},{4,6},{5,7},{6,4},{7,5},{8,10},{9,11},{10,... | collective-permute-start | bytes 147464 | tf_op jit(solution)/shard_map/ppermute | solution.py:225
  32.7 0.7 %collective-permute-start.13 = (bf16[192,128]{1,0:T(8,128)(2,1)S(1)}, bf16[192,128]{1,0:T(8,128)(2,1)S(1)}, u32[]{:S(2)}, u32[]{:S(2)}) collective-permute-start(bf16[192,128]{1,0:T(8,128)(2,1)S(1)} %get-tuple-element.34), channel_id=1, source_target_pairs={{0,1},{1,0},{2,3},{3,2},{4,5},{5,4},{6,7},{7,6},{8,9},{9,8},{10,11... | collective-permute-start | bytes 147464 | tf_op jit(solution)/shard_map/ppermute | solution.py:225
  33.4 0.4 %collective-permute-done.9.refs_3_ = bf16[192,128]{1,0:T(8,128)(2,1)S(1)} collective-permute-done((bf16[192,128]{1,0:T(8,128)(2,1)S(1)}, bf16[192,128]{1,0:T(8,128)(2,1)S(1)}, u32[]{:S(2)}, u32[]{:S(2)}) %collective-permute-start.9) | collective-permute-done | bytes 49184 | tf_op jit(solution)/shard_map/ppermute | solution.py:225
  33.8 1.2 %collective-permute-done.10.refs_4_ = bf16[192,128]{1,0:T(8,128)(2,1)S(1)} collective-permute-done((bf16[192,128]{1,0:T(8,128)(2,1)S(1)}, bf16[192,128]{1,0:T(8,128)(2,1)S(1)}, u32[]{:S(2)}, u32[]{:S(2)}) %collective-permute-start.10) | collective-permute-done | bytes 49184 | tf_op jit(solution)/shard_map/ppermute | solution.py:225
  35.0 0.5 %collective-permute-done.11.refs_5_ = bf16[192,128]{1,0:T(8,128)(2,1)S(1)} collective-permute-done((bf16[192,128]{1,0:T(8,128)(2,1)S(1)}, bf16[192,128]{1,0:T(8,128)(2,1)S(1)}, u32[]{:S(2)}, u32[]{:S(2)}) %collective-permute-start.11) | collective-permute-done | bytes 49184 | tf_op jit(solution)/shard_map/ppermute | solution.py:225
  35.4 0.8 %collective-permute-done.12.refs_6_ = bf16[192,128]{1,0:T(8,128)(2,1)S(1)} collective-permute-done((bf16[192,128]{1,0:T(8,128)(2,1)S(1)}, bf16[192,128]{1,0:T(8,128)(2,1)S(1)}, u32[]{:S(2)}, u32[]{:S(2)}) %collective-permute-start.12) | collective-permute-done | bytes 49184 | tf_op jit(solution)/shard_map/ppermute | solution.py:225
  36.3 0.5 %collective-permute-done.13.refs_7_ = bf16[192,128]{1,0:T(8,128)(2,1)S(1)} collective-permute-done((bf16[192,128]{1,0:T(8,128)(2,1)S(1)}, bf16[192,128]{1,0:T(8,128)(2,1)S(1)}, u32[]{:S(2)}, u32[]{:S(2)}) %collective-permute-start.13) | collective-permute-done | bytes 49184 | tf_op jit(solution)/shard_map/ppermute | solution.py:225
  36.8 0.9 %unpack.1 = (bf16[128,512]{1,0:T(8,128)(2,1)}, bf16[128,512]{1,0:T(8,128)(2,1)}, bf16[128,512]{1,0:T(8,128)(2,1)}) custom-call(bf16[192,128]{1,0:T(8,128)(2,1)S(1)} %get-tuple-element.27.refs_0_, bf16[192,128]{1,0:T(8,128)(2,1)S(1)} %collective-permute-done.7.refs_1_, bf16[192,128]{1,0:T(8,128)(2,1)S(1)} %collective-permute-done.8.refs_2_, ...), custom_call_target="tpu_custom_call" | custom-call | tf_op jit(solution)/shard_map/unpack/pallas_call | solution.py:289
  (14 shorter events, 0.6 us)
Async XLA Ops:
  2.1 10.9 %collective-permute-start = (bf16[2,128,128]{2,1,0:T(8,128)(2,1)S(1)}, bf16[2,128,128]{2,1,0:T(8,128)(2,1)S(1)}, u32[]{:S(2)}, u32[]{:S(2)}) collective-permute-start(bf16[2,128,128]{2,1,0:T(8,128)(2,1)S(1)} %get-tuple-element.20), channel_id=1, source_target_pairs={{0,4},{1,5},{2,6},{3,7},{4,0},{5,1},{6,2},{7,3},{8,12},{9,13},{10,... | collective-permute-start | bytes 196616 | tf_op jit(solution)/shard_map/ppermute | solution.py:225
  6.2 8.1 %collective-permute-start.1 = (bf16[2,128,128]{2,1,0:T(8,128)(2,1)S(1)}, bf16[2,128,128]{2,1,0:T(8,128)(2,1)S(1)}, u32[]{:S(2)}, u32[]{:S(2)}) collective-permute-start(bf16[2,128,128]{2,1,0:T(8,128)(2,1)S(1)} %get-tuple-element.21), channel_id=1, source_target_pairs={{0,6},{1,7},{2,4},{3,5},{4,2},{5,3},{6,0},{7,1},{8,14},{9,15},{10,... | collective-permute-start | bytes 196616 | tf_op jit(solution)/shard_map/ppermute | solution.py:225
  7.5 5.3 %copy-start = (s32[16,3]{0,1:T(4,128)S(1)}, s32[16,3]{0,1:T(4,128)}, u32[]{:S(2)}) copy-start(s32[16,3]{0,1:T(4,128)} %param.10) | copy-start | bytes 580
  7.5 7.3 %collective-permute-start.2 = (bf16[2,128,128]{2,1,0:T(8,128)(2,1)S(1)}, bf16[2,128,128]{2,1,0:T(8,128)(2,1)S(1)}, u32[]{:S(2)}, u32[]{:S(2)}) collective-permute-start(bf16[2,128,128]{2,1,0:T(8,128)(2,1)S(1)} %get-tuple-element.22), channel_id=1, source_target_pairs={{0,3},{1,2},{2,1},{3,0},{4,7},{5,6},{6,5},{7,4},{8,11},{9,10},{10,... | collective-permute-start | bytes 196616 | tf_op jit(solution)/shard_map/ppermute | solution.py:225
  8.7 7.4 %collective-permute-start.3 = (bf16[2,128,128]{2,1,0:T(8,128)(2,1)S(1)}, bf16[2,128,128]{2,1,0:T(8,128)(2,1)S(1)}, u32[]{:S(2)}, u32[]{:S(2)}) collective-permute-start(bf16[2,128,128]{2,1,0:T(8,128)(2,1)S(1)} %get-tuple-element.23), channel_id=1, source_target_pairs={{0,7},{1,6},{2,5},{3,4},{4,3},{5,2},{6,1},{7,0},{8,15},{9,14},{10,... | collective-permute-start | bytes 196616 | tf_op jit(solution)/shard_map/ppermute | solution.py:225
  11.6 8.0 %collective-permute-start.4 = (bf16[2,128,128]{2,1,0:T(8,128)(2,1)S(1)}, bf16[2,128,128]{2,1,0:T(8,128)(2,1)S(1)}, u32[]{:S(2)}, u32[]{:S(2)}) collective-permute-start(bf16[2,128,128]{2,1,0:T(8,128)(2,1)S(1)} %get-tuple-element.24), channel_id=1, source_target_pairs={{0,5},{1,4},{2,7},{3,6},{4,1},{5,0},{6,3},{7,2},{8,13},{9,12},{10,... | collective-permute-start | bytes 196616 | tf_op jit(solution)/shard_map/ppermute | solution.py:225
  13.0 1.7 %copy-start.1 = (s32[2]{0:T(128)S(1)}, s32[2]{0:T(128)}, u32[]{:S(2)}) copy-start(s32[2]{0:T(128)} %param.11) | copy-start | bytes 28
  13.0 6.5 %collective-permute-start.5 = (bf16[2,128,128]{2,1,0:T(8,128)(2,1)S(1)}, bf16[2,128,128]{2,1,0:T(8,128)(2,1)S(1)}, u32[]{:S(2)}, u32[]{:S(2)}) collective-permute-start(bf16[2,128,128]{2,1,0:T(8,128)(2,1)S(1)} %get-tuple-element.25), channel_id=1, source_target_pairs={{0,2},{1,3},{2,0},{3,1},{4,6},{5,7},{6,4},{7,5},{8,10},{9,11},{10,... | collective-permute-start | bytes 196616 | tf_op jit(solution)/shard_map/ppermute | solution.py:225
  14.2 5.7 %collective-permute-start.6 = (bf16[2,128,128]{2,1,0:T(8,128)(2,1)S(1)}, bf16[2,128,128]{2,1,0:T(8,128)(2,1)S(1)}, u32[]{:S(2)}, u32[]{:S(2)}) collective-permute-start(bf16[2,128,128]{2,1,0:T(8,128)(2,1)S(1)} %get-tuple-element.26), channel_id=1, source_target_pairs={{0,1},{1,0},{2,3},{3,2},{4,5},{5,4},{6,7},{7,6},{8,9},{9,8},{10,11... | collective-permute-start | bytes 196616 | tf_op jit(solution)/shard_map/ppermute | solution.py:225
  23.1 9.1 %collective-permute-start.7 = (bf16[192,128]{1,0:T(8,128)(2,1)S(1)}, bf16[192,128]{1,0:T(8,128)(2,1)S(1)}, u32[]{:S(2)}, u32[]{:S(2)}) collective-permute-start(bf16[192,128]{1,0:T(8,128)(2,1)S(1)} %get-tuple-element.28), channel_id=1, source_target_pairs={{0,6},{1,7},{2,4},{3,5},{4,2},{5,3},{6,0},{7,1},{8,14},{9,15},{10,... | collective-permute-start | bytes 147464 | tf_op jit(solution)/shard_map/ppermute | solution.py:225
  26.1 6.6 %collective-permute-start.8 = (bf16[192,128]{1,0:T(8,128)(2,1)S(1)}, bf16[192,128]{1,0:T(8,128)(2,1)S(1)}, u32[]{:S(2)}, u32[]{:S(2)}) collective-permute-start(bf16[192,128]{1,0:T(8,128)(2,1)S(1)} %get-tuple-element.29), channel_id=1, source_target_pairs={{0,5},{1,4},{2,7},{3,6},{4,1},{5,0},{6,3},{7,2},{8,13},{9,12},{10,... | collective-permute-start | bytes 147464 | tf_op jit(solution)/shard_map/ppermute | solution.py:225
  26.9 6.9 %collective-permute-start.9 = (bf16[192,128]{1,0:T(8,128)(2,1)S(1)}, bf16[192,128]{1,0:T(8,128)(2,1)S(1)}, u32[]{:S(2)}, u32[]{:S(2)}) collective-permute-start(bf16[192,128]{1,0:T(8,128)(2,1)S(1)} %get-tuple-element.30), channel_id=1, source_target_pairs={{0,7},{1,6},{2,5},{3,4},{4,3},{5,2},{6,1},{7,0},{8,15},{9,14},{10,... | collective-permute-start | bytes 147464 | tf_op jit(solution)/shard_map/ppermute | solution.py:225
  29.7 5.2 %collective-permute-start.10 = (bf16[192,128]{1,0:T(8,128)(2,1)S(1)}, bf16[192,128]{1,0:T(8,128)(2,1)S(1)}, u32[]{:S(2)}, u32[]{:S(2)}) collective-permute-start(bf16[192,128]{1,0:T(8,128)(2,1)S(1)} %get-tuple-element.31), channel_id=1, source_target_pairs={{0,3},{1,2},{2,1},{3,0},{4,7},{5,6},{6,5},{7,4},{8,11},{9,10},{10,... | collective-permute-start | bytes 147464 | tf_op jit(solution)/shard_map/ppermute | solution.py:225
  30.5 5.0 %collective-permute-start.11 = (bf16[192,128]{1,0:T(8,128)(2,1)S(1)}, bf16[192,128]{1,0:T(8,128)(2,1)S(1)}, u32[]{:S(2)}, u32[]{:S(2)}) collective-permute-start(bf16[192,128]{1,0:T(8,128)(2,1)S(1)} %get-tuple-element.32), channel_id=1, source_target_pairs={{0,4},{1,5},{2,6},{3,7},{4,0},{5,1},{6,2},{7,3},{8,12},{9,13},{10,... | collective-permute-start | bytes 147464 | tf_op jit(solution)/shard_map/ppermute | solution.py:225
  32.2 4.1 %collective-permute-start.12 = (bf16[192,128]{1,0:T(8,128)(2,1)S(1)}, bf16[192,128]{1,0:T(8,128)(2,1)S(1)}, u32[]{:S(2)}, u32[]{:S(2)}) collective-permute-start(bf16[192,128]{1,0:T(8,128)(2,1)S(1)} %get-tuple-element.33), channel_id=1, source_target_pairs={{0,2},{1,3},{2,0},{3,1},{4,6},{5,7},{6,4},{7,5},{8,10},{9,11},{10,... | collective-permute-start | bytes 147464 | tf_op jit(solution)/shard_map/ppermute | solution.py:225
  32.7 4.1 %collective-permute-start.13 = (bf16[192,128]{1,0:T(8,128)(2,1)S(1)}, bf16[192,128]{1,0:T(8,128)(2,1)S(1)}, u32[]{:S(2)}, u32[]{:S(2)}) collective-permute-start(bf16[192,128]{1,0:T(8,128)(2,1)S(1)} %get-tuple-element.34), channel_id=1, source_target_pairs={{0,1},{1,0},{2,3},{3,2},{4,5},{5,4},{6,7},{7,6},{8,9},{9,8},{10,11... | collective-permute-start | bytes 147464 | tf_op jit(solution)/shard_map/ppermute | solution.py:225

commit v11 on v8

--- a/solution.py
+++ b/solution.py
@@ -83,16 +83,19 @@
         gq_ref[BLOCK:, lanes] = second.astype(jnp.bfloat16)
 
 
-def attend_kernel(alone, scale, table_ref, *rest):
+def attend_kernel(alone, scale, ints_ref, *rest):
     if alone:
         in_refs = dict(zip(PARTNERS_IN, rest[:HEADS]))
         out_refs = rest[HEADS : 2 * HEADS]
-        sent_ref, gq_ref, acc_ref = rest[2 * HEADS :]
+        sent_ref, gq_ref, acc_ref, table_ref, sem = rest[2 * HEADS :]
+    else:
+        sent_ref, pool_ref, gq_ref, acc_ref, table_ref, sem = rest
+    fetch = pltpu.make_async_copy(ints_ref, table_ref, sem)
+    fetch.start()
+    if alone:
         place = lax.rem(lax.axis_index("seq"), HEADS)
         for m in range(HEADS):
             sent_ref[lax.bitwise_xor(place, m)] = in_refs[m][...]
-    else:
-        sent_ref, pool_ref, gq_ref, acc_ref = rest
     tiles = sent_ref.shape[0]
     blocks = 2 * tiles
     queries = 2 * BLOCK
@@ -100,6 +103,7 @@
     zero = jnp.zeros((BLOCK, LANES), jnp.bfloat16)
     fixed = blocks * RAND
     acc_ref[...] = jnp.zeros_like(acc_ref)
+    fetch.wait()
 
     def pooled(entry):
         if alone:
@@ -168,10 +172,10 @@
         row_max = jnp.max(scores, axis=0, keepdims=True)
         expo = jnp.exp(scores - row_max)
         row_total = jnp.sum(expo, axis=0, keepdims=True)
-        probs = expo * (1.0 / row_total)
-        probs_half = probs.astype(jnp.bfloat16)
+        inverse = 1.0 / row_total
+        probs_half = (expo * inverse).astype(jnp.bfloat16)
         row_dot = jnp.sum(probs_half.astype(jnp.float32) * grad_probs, axis=0, keepdims=True)
-        grad_half = (probs * (grad_probs - row_dot)).astype(jnp.bfloat16)
+        grad_half = (expo * ((grad_probs - row_dot) * inverse)).astype(jnp.bfloat16)
         return grad_half, probs_half
 
     def gather(tile, pairs, keys, sides, grad_half, probs_half):
@@ -241,7 +245,6 @@
     blocks = ways * rows // BLOCK
     scale = 1.0 / math.sqrt(width // HEADS)
     vmem = pl.BlockSpec(memory_space=pltpu.VMEM)
-    smem = pl.BlockSpec(memory_space=pltpu.SMEM)
     half_type = jnp.bfloat16
 
     anywhere = pl.BlockSpec(memory_space=pl.ANY)
@@ -264,12 +267,14 @@
         back = pl.pallas_call(
             kernel,
             out_shape=[jax.ShapeDtypeStruct((rows + BLOCK, LANES), half_type)] * HEADS,
-            in_specs=[smem] + [vmem] * HEADS,
+            in_specs=[anywhere] + [vmem] * HEADS,
             out_specs=[vmem] * HEADS,
             scratch_shapes=[
                 pltpu.VMEM((ways, 2, 2, BLOCK, LANES), half_type),
                 pltpu.VMEM((ways, BLOCK, LANES), half_type),
                 pltpu.VMEM((blocks, BLOCK, LANES), jnp.float32),
+                pltpu.SMEM((blocks * RAND + GLOBAL,), jnp.int32),
+                pltpu.SemaphoreType.DMA,
             ],
             compiler_params=pltpu.CompilerParams(vmem_limit_bytes=24 * 2**20),
             name="attend",
@@ -289,7 +294,6 @@
 
 def spread_out(kernel, sent, rand_pick, global_ids, ways, ranges, blocks):
     vmem = pl.BlockSpec(memory_space=pltpu.VMEM)
-    smem = pl.BlockSpec(memory_space=pltpu.SMEM)
     mine = lax.axis_index("seq") // ways
     order = lax.bitwise_xor(lax.axis_index("seq") % ways, jnp.arange(ways, dtype=jnp.int32))
     sent = jnp.take(jnp.stack(sent), order, axis=0)
@@ -314,8 +318,9 @@
             jax.ShapeDtypeStruct((ways, BLOCK, LANES), jnp.bfloat16),
             jax.ShapeDtypeStruct(pool.shape, jnp.float32),
         ],
-        in_specs=[smem, vmem, vmem],
+        in_specs=[pl.BlockSpec(memory_space=pl.ANY), vmem, vmem],
         out_specs=[vmem] * 2,
+        scratch_shapes=[pltpu.SMEM(table.shape, jnp.int32), pltpu.SemaphoreType.DMA],
         compiler_params=pltpu.CompilerParams(vmem_limit_bytes=24 * 2**20),
         name="attend",
     )(table, sent, pool)

time: 37.8 us -> 37.8 us (level)
  no operation moved by 1% of the time
where the time goes in v11:
time: 37.8 us; the launch traced here: 37.6 us
  starting transfers between devices  22.8 us (60%)
  waiting for transfers between devices  8.43 us (22%)
  Pallas kernels  5.44 us (14%)
  between operations  0.68 us (2%)
    ppermute x14, starting transfers between devices, exchange(): arrived[m] = lax.ppermute(parts[m], 'seq', route)  22.8 us
    ppermute x14, waiting for transfers between devices, exchange(): arrived[m] = lax.ppermute(parts[m], 'seq', route)  8.43 us
    pallas_call x1, Pallas kernels, on_device(): pl.pallas_call(kernel, out_shape=[jax.ShapeDtypeStruct((rows + BLOCK, LAN...  3.1 us
    pallas_call x1, Pallas kernels, on_device(): pl.pallas_call(pack_kernel, out_shape=[jax.ShapeDtypeStruct((2, rows, LAN...  1.42 us
    pallas_call x1, Pallas kernels, on_device(): pl.pallas_call(unpack_kernel, out_shape=[jax.ShapeDtypeStruct((rows, widt...  0.92 us
  transfers between devices with their start and end apart: 14, of which 8 were waited for; matrix products, arithmetic and copies ran while one was open for 1% of the time, Pallas kernels for 0%

profile of v11, /device:TPU:0, one launch (start us, length us, event | category | flops | bytes accessed | tf_op | source)
XLA Modules:
  0.0 37.6 jit_solution(3284522426096002378)
XLA Ops:
  0.6 1.4 %pack.1 = (bf16[2,128,128]{2,1,0:T(8,128)(2,1)S(1)}, bf16[2,128,128]{2,1,0:T(8,128)(2,1)S(1)}, bf16[2,128,128]{2,1,0:T(8,128)(2,1)S(1)}, bf16[2,128,128]{2,1,0:T...) custom-call(bf16[128,512]{1,0:T(8,128)(2,1)} %refs_0_.1, ...), custom_call_target="tpu_custom_call" | custom-call | tf_op jit(solution)/shard_map/pack/pallas_call | solution.py:251
  2.1 4.1 %collective-permute-start = (bf16[2,128,128]{2,1,0:T(8,128)(2,1)S(1)}, bf16[2,128,128]{2,1,0:T(8,128)(2,1)S(1)}, u32[]{:S(2)}, u32[]{:S(2)}) collective-permute-start(bf16[2,128,128]{2,1,0:T(8,128)(2,1)S(1)} %get-tuple-element.20), channel_id=1, source_target_pairs={{0,4},{1,5},{2,6},{3,7},{4,0},{5,1},{6,2},{7,3},{8,12},{9,13},{10,... | collective-permute-start | bytes 196616 | tf_op jit(solution)/shard_map/ppermute | solution.py:223
  6.2 1.3 %collective-permute-start.1 = (bf16[2,128,128]{2,1,0:T(8,128)(2,1)S(1)}, bf16[2,128,128]{2,1,0:T(8,128)(2,1)S(1)}, u32[]{:S(2)}, u32[]{:S(2)}) collective-permute-start(bf16[2,128,128]{2,1,0:T(8,128)(2,1)S(1)} %get-tuple-element.21), channel_id=1, source_target_pairs={{0,6},{1,7},{2,4},{3,5},{4,2},{5,3},{6,0},{7,1},{8,14},{9,15},{10,... | collective-permute-start | bytes 196616 | tf_op jit(solution)/shard_map/ppermute | solution.py:223
  7.5 1.2 %collective-permute-start.2 = (bf16[2,128,128]{2,1,0:T(8,128)(2,1)S(1)}, bf16[2,128,128]{2,1,0:T(8,128)(2,1)S(1)}, u32[]{:S(2)}, u32[]{:S(2)}) collective-permute-start(bf16[2,128,128]{2,1,0:T(8,128)(2,1)S(1)} %get-tuple-element.22), channel_id=1, source_target_pairs={{0,3},{1,2},{2,1},{3,0},{4,7},{5,6},{6,5},{7,4},{8,11},{9,10},{10,... | collective-permute-start | bytes 196616 | tf_op jit(solution)/shard_map/ppermute | solution.py:223
  8.7 2.9 %collective-permute-start.3 = (bf16[2,128,128]{2,1,0:T(8,128)(2,1)S(1)}, bf16[2,128,128]{2,1,0:T(8,128)(2,1)S(1)}, u32[]{:S(2)}, u32[]{:S(2)}) collective-permute-start(bf16[2,128,128]{2,1,0:T(8,128)(2,1)S(1)} %get-tuple-element.23), channel_id=1, source_target_pairs={{0,7},{1,6},{2,5},{3,4},{4,3},{5,2},{6,1},{7,0},{8,15},{9,14},{10,... | collective-permute-start | bytes 196616 | tf_op jit(solution)/shard_map/ppermute | solution.py:223
  11.6 1.3 %collective-permute-start.4 = (bf16[2,128,128]{2,1,0:T(8,128)(2,1)S(1)}, bf16[2,128,128]{2,1,0:T(8,128)(2,1)S(1)}, u32[]{:S(2)}, u32[]{:S(2)}) collective-permute-start(bf16[2,128,128]{2,1,0:T(8,128)(2,1)S(1)} %get-tuple-element.24), channel_id=1, source_target_pairs={{0,5},{1,4},{2,7},{3,6},{4,1},{5,0},{6,3},{7,2},{8,13},{9,12},{10,... | collective-permute-start | bytes 196616 | tf_op jit(solution)/shard_map/ppermute | solution.py:223
  13.0 1.2 %collective-permute-start.5 = (bf16[2,128,128]{2,1,0:T(8,128)(2,1)S(1)}, bf16[2,128,128]{2,1,0:T(8,128)(2,1)S(1)}, u32[]{:S(2)}, u32[]{:S(2)}) collective-permute-start(bf16[2,128,128]{2,1,0:T(8,128)(2,1)S(1)} %get-tuple-element.25), channel_id=1, source_target_pairs={{0,2},{1,3},{2,0},{3,1},{4,6},{5,7},{6,4},{7,5},{8,10},{9,11},{10,... | collective-permute-start | bytes 196616 | tf_op jit(solution)/shard_map/ppermute | solution.py:223
  14.2 0.5 %collective-permute-start.6 = (bf16[2,128,128]{2,1,0:T(8,128)(2,1)S(1)}, bf16[2,128,128]{2,1,0:T(8,128)(2,1)S(1)}, u32[]{:S(2)}, u32[]{:S(2)}) collective-permute-start(bf16[2,128,128]{2,1,0:T(8,128)(2,1)S(1)} %get-tuple-element.26), channel_id=1, source_target_pairs={{0,1},{1,0},{2,3},{3,2},{4,5},{5,4},{6,7},{7,6},{8,9},{9,8},{10,11... | collective-permute-start | bytes 196616 | tf_op jit(solution)/shard_map/ppermute | solution.py:223
  14.8 1.2 %collective-permute-done.3 = bf16[2,128,128]{2,1,0:T(8,128)(2,1)S(1)} collective-permute-done((bf16[2,128,128]{2,1,0:T(8,128)(2,1)S(1)}, bf16[2,128,128]{2,1,0:T(8,128)(2,1)S(1)}, u32[]{:S(2)}, u32[]{:S(2)}) %collective-permute-start.3) | collective-permute-done | bytes 65568 | tf_op jit(solution)/shard_map/ppermute | solution.py:223
  16.1 3.5 %collective-permute-done.4 = bf16[2,128,128]{2,1,0:T(8,128)(2,1)S(1)} collective-permute-done((bf16[2,128,128]{2,1,0:T(8,128)(2,1)S(1)}, bf16[2,128,128]{2,1,0:T(8,128)(2,1)S(1)}, u32[]{:S(2)}, u32[]{:S(2)}) %collective-permute-start.4) | collective-permute-done | bytes 65568 | tf_op jit(solution)/shard_map/ppermute | solution.py:223
  19.9 3.1 %attend.1 = (bf16[192,128]{1,0:T(8,128)(2,1)S(1)}, bf16[192,128]{1,0:T(8,128)(2,1)S(1)}, bf16[192,128]{1,0:T(8,128)(2,1)S(1)}, bf16[192,128]{1,0:T(8,128)(2,1)S(...) custom-call(s32[50]{0:T(128)S(1)} %pad_add_fusion.ints_ref, ...), custom_call_target="tpu_custom_call" | custom-call | tf_op jit(solution)/shard_map/attend/pallas_call | solution.py:267
  23.0 3.0 %collective-permute-start.7 = (bf16[192,128]{1,0:T(8,128)(2,1)S(1)}, bf16[192,128]{1,0:T(8,128)(2,1)S(1)}, u32[]{:S(2)}, u32[]{:S(2)}) collective-permute-start(bf16[192,128]{1,0:T(8,128)(2,1)S(1)} %get-tuple-element.28), channel_id=1, source_target_pairs={{0,6},{1,7},{2,4},{3,5},{4,2},{5,3},{6,0},{7,1},{8,14},{9,15},{10,... | collective-permute-start | bytes 147464 | tf_op jit(solution)/shard_map/ppermute | solution.py:223
  26.0 0.8 %collective-permute-start.8 = (bf16[192,128]{1,0:T(8,128)(2,1)S(1)}, bf16[192,128]{1,0:T(8,128)(2,1)S(1)}, u32[]{:S(2)}, u32[]{:S(2)}) collective-permute-start(bf16[192,128]{1,0:T(8,128)(2,1)S(1)} %get-tuple-element.29), channel_id=1, source_target_pairs={{0,5},{1,4},{2,7},{3,6},{4,1},{5,0},{6,3},{7,2},{8,13},{9,12},{10,... | collective-permute-start | bytes 147464 | tf_op jit(solution)/shard_map/ppermute | solution.py:223
  26.8 2.8 %collective-permute-start.9 = (bf16[192,128]{1,0:T(8,128)(2,1)S(1)}, bf16[192,128]{1,0:T(8,128)(2,1)S(1)}, u32[]{:S(2)}, u32[]{:S(2)}) collective-permute-start(bf16[192,128]{1,0:T(8,128)(2,1)S(1)} %get-tuple-element.30), channel_id=1, source_target_pairs={{0,7},{1,6},{2,5},{3,4},{4,3},{5,2},{6,1},{7,0},{8,15},{9,14},{10,... | collective-permute-start | bytes 147464 | tf_op jit(solution)/shard_map/ppermute | solution.py:223
  29.6 0.7 %collective-permute-start.10 = (bf16[192,128]{1,0:T(8,128)(2,1)S(1)}, bf16[192,128]{1,0:T(8,128)(2,1)S(1)}, u32[]{:S(2)}, u32[]{:S(2)}) collective-permute-start(bf16[192,128]{1,0:T(8,128)(2,1)S(1)} %get-tuple-element.31), channel_id=1, source_target_pairs={{0,3},{1,2},{2,1},{3,0},{4,7},{5,6},{6,5},{7,4},{8,11},{9,10},{10,... | collective-permute-start | bytes 147464 | tf_op jit(solution)/shard_map/ppermute | solution.py:223
  30.4 1.7 %collective-permute-start.11 = (bf16[192,128]{1,0:T(8,128)(2,1)S(1)}, bf16[192,128]{1,0:T(8,128)(2,1)S(1)}, u32[]{:S(2)}, u32[]{:S(2)}) collective-permute-start(bf16[192,128]{1,0:T(8,128)(2,1)S(1)} %get-tuple-element.32), channel_id=1, source_target_pairs={{0,4},{1,5},{2,6},{3,7},{4,0},{5,1},{6,2},{7,3},{8,12},{9,13},{10,... | collective-permute-start | bytes 147464 | tf_op jit(solution)/shard_map/ppermute | solution.py:223
  32.1 0.5 %collective-permute-start.12 = (bf16[192,128]{1,0:T(8,128)(2,1)S(1)}, bf16[192,128]{1,0:T(8,128)(2,1)S(1)}, u32[]{:S(2)}, u32[]{:S(2)}) collective-permute-start(bf16[192,128]{1,0:T(8,128)(2,1)S(1)} %get-tuple-element.33), channel_id=1, source_target_pairs={{0,2},{1,3},{2,0},{3,1},{4,6},{5,7},{6,4},{7,5},{8,10},{9,11},{10,... | collective-permute-start | bytes 147464 | tf_op jit(solution)/shard_map/ppermute | solution.py:223
  32.6 0.7 %collective-permute-start.13 = (bf16[192,128]{1,0:T(8,128)(2,1)S(1)}, bf16[192,128]{1,0:T(8,128)(2,1)S(1)}, u32[]{:S(2)}, u32[]{:S(2)}) collective-permute-start(bf16[192,128]{1,0:T(8,128)(2,1)S(1)} %get-tuple-element.34), channel_id=1, source_target_pairs={{0,1},{1,0},{2,3},{3,2},{4,5},{5,4},{6,7},{7,6},{8,9},{9,8},{10,11... | collective-permute-start | bytes 147464 | tf_op jit(solution)/shard_map/ppermute | solution.py:223
  33.3 0.4 %collective-permute-done.9.refs_3_ = bf16[192,128]{1,0:T(8,128)(2,1)S(1)} collective-permute-done((bf16[192,128]{1,0:T(8,128)(2,1)S(1)}, bf16[192,128]{1,0:T(8,128)(2,1)S(1)}, u32[]{:S(2)}, u32[]{:S(2)}) %collective-permute-start.9) | collective-permute-done | bytes 49184 | tf_op jit(solution)/shard_map/ppermute | solution.py:223
  33.7 1.2 %collective-permute-done.10.refs_4_ = bf16[192,128]{1,0:T(8,128)(2,1)S(1)} collective-permute-done((bf16[192,128]{1,0:T(8,128)(2,1)S(1)}, bf16[192,128]{1,0:T(8,128)(2,1)S(1)}, u32[]{:S(2)}, u32[]{:S(2)}) %collective-permute-start.10) | collective-permute-done | bytes 49184 | tf_op jit(solution)/shard_map/ppermute | solution.py:223
  34.9 0.5 %collective-permute-done.11.refs_5_ = bf16[192,128]{1,0:T(8,128)(2,1)S(1)} collective-permute-done((bf16[192,128]{1,0:T(8,128)(2,1)S(1)}, bf16[192,128]{1,0:T(8,128)(2,1)S(1)}, u32[]{:S(2)}, u32[]{:S(2)}) %collective-permute-start.11) | collective-permute-done | bytes 49184 | tf_op jit(solution)/shard_map/ppermute | solution.py:223
  35.3 0.8 %collective-permute-done.12.refs_6_ = bf16[192,128]{1,0:T(8,128)(2,1)S(1)} collective-permute-done((bf16[192,128]{1,0:T(8,128)(2,1)S(1)}, bf16[192,128]{1,0:T(8,128)(2,1)S(1)}, u32[]{:S(2)}, u32[]{:S(2)}) %collective-permute-start.12) | collective-permute-done | bytes 49184 | tf_op jit(solution)/shard_map/ppermute | solution.py:223
  36.2 0.5 %collective-permute-done.13.refs_7_ = bf16[192,128]{1,0:T(8,128)(2,1)S(1)} collective-permute-done((bf16[192,128]{1,0:T(8,128)(2,1)S(1)}, bf16[192,128]{1,0:T(8,128)(2,1)S(1)}, u32[]{:S(2)}, u32[]{:S(2)}) %collective-permute-start.13) | collective-permute-done | bytes 49184 | tf_op jit(solution)/shard_map/ppermute | solution.py:223
  36.7 0.9 %unpack.1 = (bf16[128,512]{1,0:T(8,128)(2,1)}, bf16[128,512]{1,0:T(8,128)(2,1)}, bf16[128,512]{1,0:T(8,128)(2,1)}) custom-call(bf16[192,128]{1,0:T(8,128)(2,1)S(1)} %get-tuple-element.27.refs_0_, bf16[192,128]{1,0:T(8,128)(2,1)S(1)} %collective-permute-done.7.refs_1_, bf16[192,128]{1,0:T(8,128)(2,1)S(1)} %collective-permute-done.8.refs_2_, ...), custom_call_target="tpu_custom_call" | custom-call | tf_op jit(solution)/shard_map/unpack/pallas_call | solution.py:285
  (14 shorter events, 0.6 us)
Async XLA Ops:
  2.1 10.9 %collective-permute-start = (bf16[2,128,128]{2,1,0:T(8,128)(2,1)S(1)}, bf16[2,128,128]{2,1,0:T(8,128)(2,1)S(1)}, u32[]{:S(2)}, u32[]{:S(2)}) collective-permute-start(bf16[2,128,128]{2,1,0:T(8,128)(2,1)S(1)} %get-tuple-element.20), channel_id=1, source_target_pairs={{0,4},{1,5},{2,6},{3,7},{4,0},{5,1},{6,2},{7,3},{8,12},{9,13},{10,... | collective-permute-start | bytes 196616 | tf_op jit(solution)/shard_map/ppermute | solution.py:223
  6.2 8.1 %collective-permute-start.1 = (bf16[2,128,128]{2,1,0:T(8,128)(2,1)S(1)}, bf16[2,128,128]{2,1,0:T(8,128)(2,1)S(1)}, u32[]{:S(2)}, u32[]{:S(2)}) collective-permute-start(bf16[2,128,128]{2,1,0:T(8,128)(2,1)S(1)} %get-tuple-element.21), channel_id=1, source_target_pairs={{0,6},{1,7},{2,4},{3,5},{4,2},{5,3},{6,0},{7,1},{8,14},{9,15},{10,... | collective-permute-start | bytes 196616 | tf_op jit(solution)/shard_map/ppermute | solution.py:223
  7.5 5.3 %copy-start = (s32[16,3]{0,1:T(4,128)S(1)}, s32[16,3]{0,1:T(4,128)}, u32[]{:S(2)}) copy-start(s32[16,3]{0,1:T(4,128)} %param.10) | copy-start | bytes 580
  7.5 7.3 %collective-permute-start.2 = (bf16[2,128,128]{2,1,0:T(8,128)(2,1)S(1)}, bf16[2,128,128]{2,1,0:T(8,128)(2,1)S(1)}, u32[]{:S(2)}, u32[]{:S(2)}) collective-permute-start(bf16[2,128,128]{2,1,0:T(8,128)(2,1)S(1)} %get-tuple-element.22), channel_id=1, source_target_pairs={{0,3},{1,2},{2,1},{3,0},{4,7},{5,6},{6,5},{7,4},{8,11},{9,10},{10,... | collective-permute-start | bytes 196616 | tf_op jit(solution)/shard_map/ppermute | solution.py:223
  8.7 7.4 %collective-permute-start.3 = (bf16[2,128,128]{2,1,0:T(8,128)(2,1)S(1)}, bf16[2,128,128]{2,1,0:T(8,128)(2,1)S(1)}, u32[]{:S(2)}, u32[]{:S(2)}) collective-permute-start(bf16[2,128,128]{2,1,0:T(8,128)(2,1)S(1)} %get-tuple-element.23), channel_id=1, source_target_pairs={{0,7},{1,6},{2,5},{3,4},{4,3},{5,2},{6,1},{7,0},{8,15},{9,14},{10,... | collective-permute-start | bytes 196616 | tf_op jit(solution)/shard_map/ppermute | solution.py:223
  11.6 8.0 %collective-permute-start.4 = (bf16[2,128,128]{2,1,0:T(8,128)(2,1)S(1)}, bf16[2,128,128]{2,1,0:T(8,128)(2,1)S(1)}, u32[]{:S(2)}, u32[]{:S(2)}) collective-permute-start(bf16[2,128,128]{2,1,0:T(8,128)(2,1)S(1)} %get-tuple-element.24), channel_id=1, source_target_pairs={{0,5},{1,4},{2,7},{3,6},{4,1},{5,0},{6,3},{7,2},{8,13},{9,12},{10,... | collective-permute-start | bytes 196616 | tf_op jit(solution)/shard_map/ppermute | solution.py:223
  13.0 1.7 %copy-start.1 = (s32[2]{0:T(128)S(1)}, s32[2]{0:T(128)}, u32[]{:S(2)}) copy-start(s32[2]{0:T(128)} %param.11) | copy-start | bytes 28
  13.0 6.5 %collective-permute-start.5 = (bf16[2,128,128]{2,1,0:T(8,128)(2,1)S(1)}, bf16[2,128,128]{2,1,0:T(8,128)(2,1)S(1)}, u32[]{:S(2)}, u32[]{:S(2)}) collective-permute-start(bf16[2,128,128]{2,1,0:T(8,128)(2,1)S(1)} %get-tuple-element.25), channel_id=1, source_target_pairs={{0,2},{1,3},{2,0},{3,1},{4,6},{5,7},{6,4},{7,5},{8,10},{9,11},{10,... | collective-permute-start | bytes 196616 | tf_op jit(solution)/shard_map/ppermute | solution.py:223
  14.2 5.7 %collective-permute-start.6 = (bf16[2,128,128]{2,1,0:T(8,128)(2,1)S(1)}, bf16[2,128,128]{2,1,0:T(8,128)(2,1)S(1)}, u32[]{:S(2)}, u32[]{:S(2)}) collective-permute-start(bf16[2,128,128]{2,1,0:T(8,128)(2,1)S(1)} %get-tuple-element.26), channel_id=1, source_target_pairs={{0,1},{1,0},{2,3},{3,2},{4,5},{5,4},{6,7},{7,6},{8,9},{9,8},{10,11... | collective-permute-start | bytes 196616 | tf_op jit(solution)/shard_map/ppermute | solution.py:223
  23.0 9.1 %collective-permute-start.7 = (bf16[192,128]{1,0:T(8,128)(2,1)S(1)}, bf16[192,128]{1,0:T(8,128)(2,1)S(1)}, u32[]{:S(2)}, u32[]{:S(2)}) collective-permute-start(bf16[192,128]{1,0:T(8,128)(2,1)S(1)} %get-tuple-element.28), channel_id=1, source_target_pairs={{0,6},{1,7},{2,4},{3,5},{4,2},{5,3},{6,0},{7,1},{8,14},{9,15},{10,... | collective-permute-start | bytes 147464 | tf_op jit(solution)/shard_map/ppermute | solution.py:223
  26.0 6.6 %collective-permute-start.8 = (bf16[192,128]{1,0:T(8,128)(2,1)S(1)}, bf16[192,128]{1,0:T(8,128)(2,1)S(1)}, u32[]{:S(2)}, u32[]{:S(2)}) collective-permute-start(bf16[192,128]{1,0:T(8,128)(2,1)S(1)} %get-tuple-element.29), channel_id=1, source_target_pairs={{0,5},{1,4},{2,7},{3,6},{4,1},{5,0},{6,3},{7,2},{8,13},{9,12},{10,... | collective-permute-start | bytes 147464 | tf_op jit(solution)/shard_map/ppermute | solution.py:223
  26.8 6.9 %collective-permute-start.9 = (bf16[192,128]{1,0:T(8,128)(2,1)S(1)}, bf16[192,128]{1,0:T(8,128)(2,1)S(1)}, u32[]{:S(2)}, u32[]{:S(2)}) collective-permute-start(bf16[192,128]{1,0:T(8,128)(2,1)S(1)} %get-tuple-element.30), channel_id=1, source_target_pairs={{0,7},{1,6},{2,5},{3,4},{4,3},{5,2},{6,1},{7,0},{8,15},{9,14},{10,... | collective-permute-start | bytes 147464 | tf_op jit(solution)/shard_map/ppermute | solution.py:223
  29.6 5.2 %collective-permute-start.10 = (bf16[192,128]{1,0:T(8,128)(2,1)S(1)}, bf16[192,128]{1,0:T(8,128)(2,1)S(1)}, u32[]{:S(2)}, u32[]{:S(2)}) collective-permute-start(bf16[192,128]{1,0:T(8,128)(2,1)S(1)} %get-tuple-element.31), channel_id=1, source_target_pairs={{0,3},{1,2},{2,1},{3,0},{4,7},{5,6},{6,5},{7,4},{8,11},{9,10},{10,... | collective-permute-start | bytes 147464 | tf_op jit(solution)/shard_map/ppermute | solution.py:223
  30.4 5.0 %collective-permute-start.11 = (bf16[192,128]{1,0:T(8,128)(2,1)S(1)}, bf16[192,128]{1,0:T(8,128)(2,1)S(1)}, u32[]{:S(2)}, u32[]{:S(2)}) collective-permute-start(bf16[192,128]{1,0:T(8,128)(2,1)S(1)} %get-tuple-element.32), channel_id=1, source_target_pairs={{0,4},{1,5},{2,6},{3,7},{4,0},{5,1},{6,2},{7,3},{8,12},{9,13},{10,... | collective-permute-start | bytes 147464 | tf_op jit(solution)/shard_map/ppermute | solution.py:223
  32.1 4.1 %collective-permute-start.12 = (bf16[192,128]{1,0:T(8,128)(2,1)S(1)}, bf16[192,128]{1,0:T(8,128)(2,1)S(1)}, u32[]{:S(2)}, u32[]{:S(2)}) collective-permute-start(bf16[192,128]{1,0:T(8,128)(2,1)S(1)} %get-tuple-element.33), channel_id=1, source_target_pairs={{0,2},{1,3},{2,0},{3,1},{4,6},{5,7},{6,4},{7,5},{8,10},{9,11},{10,... | collective-permute-start | bytes 147464 | tf_op jit(solution)/shard_map/ppermute | solution.py:223
  32.6 4.1 %collective-permute-start.13 = (bf16[192,128]{1,0:T(8,128)(2,1)S(1)}, bf16[192,128]{1,0:T(8,128)(2,1)S(1)}, u32[]{:S(2)}, u32[]{:S(2)}) collective-permute-start(bf16[192,128]{1,0:T(8,128)(2,1)S(1)} %get-tuple-element.34), channel_id=1, source_target_pairs={{0,1},{1,0},{2,3},{3,2},{4,5},{5,4},{6,7},{7,6},{8,9},{9,8},{10,11... | collective-permute-start | bytes 147464 | tf_op jit(solution)/shard_map/ppermute | solution.py:223

commit v12 on v11

--- a/solution.py
+++ b/solution.py
@@ -63,7 +63,6 @@
     gq_ref, gk_ref, gv_ref = refs[HEADS:]
     rows = gq_ref.shape[0]
     low = low_lanes((rows, LANES))
-    low_block = low_lanes((BLOCK, LANES))
     place = lax.rem(lax.axis_index("seq"), HEADS)
     odd_place = lax.rem(place, 2) == 1
     for near in range(HEADS // 2):
@@ -77,19 +76,17 @@
         gv = jnp.where(low, swap_halves(even[:rows]), odd[:rows])
         gk_ref[:, lanes] = gk.astype(jnp.bfloat16)
         gv_ref[:, lanes] = gv.astype(jnp.bfloat16)
-        first = jnp.where(low_block, even[rows:], swap_halves(odd[rows:]))
-        second = jnp.where(low_block, swap_halves(even[rows:]), odd[rows:])
-        gq_ref[:BLOCK, lanes] = first.astype(jnp.bfloat16)
-        gq_ref[BLOCK:, lanes] = second.astype(jnp.bfloat16)
+        gq = jnp.concatenate([even[rows:], odd[rows:]], axis=0).T
+        gq_ref[:, lanes] = gq.astype(jnp.bfloat16)
 
 
 def attend_kernel(alone, scale, ints_ref, *rest):
     if alone:
         in_refs = dict(zip(PARTNERS_IN, rest[:HEADS]))
         out_refs = rest[HEADS : 2 * HEADS]
-        sent_ref, gq_ref, acc_ref, table_ref, sem = rest[2 * HEADS :]
+        sent_ref, gq_ref, acc_ref, turned_ref, table_ref, sem = rest[2 * HEADS :]
     else:
-        sent_ref, pool_ref, gq_ref, acc_ref, table_ref, sem = rest
+        sent_ref, pool_ref, gq_ref, acc_ref, turned_ref, table_ref, sem = rest
     fetch = pltpu.make_async_copy(ints_ref, table_ref, sem)
     fetch.start()
     if alone:
@@ -103,12 +100,21 @@
     zero = jnp.zeros((BLOCK, LANES), jnp.bfloat16)
     fixed = blocks * RAND
     acc_ref[...] = jnp.zeros_like(acc_ref)
-    fetch.wait()
 
     def pooled(entry):
         if alone:
             return sent_ref[entry // 2, 0, entry % 2]
         return pool_ref[entry]
+
+    entries = acc_ref.shape[0]
+    for entry in range(0, entries, 2):
+        after = min(entry + 1, entries - 1)
+        two = jnp.concatenate([pooled(entry), pooled(after)], axis=0).astype(jnp.float32)
+        keys = two.T[:HEAD]
+        swapped = swap_halves(keys)
+        turned_ref[entry] = jnp.where(low, keys, swapped).astype(jnp.bfloat16)
+        turned_ref[after] = jnp.where(low, swapped, keys).astype(jnp.bfloat16)
+    fetch.wait()
 
     def chosen(tile):
         first = 2 * tile
@@ -149,10 +155,18 @@
             [zero, jnp.where(low, zero, second)],
         ]
         sides = jnp.concatenate([jnp.concatenate(row, axis=1) for row in rows], axis=0)
-        products = lax.dot_general(
-            keys, sides, (((1,), (1,)), ((), ())), preferred_element_type=jnp.float32
-        )
-        return pairs, keys, sides, products
+        turned = jnp.concatenate([first, second], axis=0).astype(jnp.float32).T
+        turned = turned.astype(jnp.bfloat16)
+        above, below = turned[:HEAD] * scale, turned[HEAD:]
+        rows = [
+            [jnp.where(low, above, zero), zero],
+            [zero, jnp.where(low, below, zero)],
+            [jnp.where(low, zero, above), zero],
+            [zero, jnp.where(low, zero, below)],
+        ]
+        turned = jnp.concatenate([jnp.concatenate(row, axis=1) for row in rows], axis=0)
+        products = jnp.dot(keys, turned, preferred_element_type=jnp.float32)
+        return pairs, sides, products
 
     def weigh(tile, products):
         scores, grad_probs = products[:, :queries], products[:, queries:]
@@ -178,17 +192,19 @@
         grad_half = (expo * ((grad_probs - row_dot) * inverse)).astype(jnp.bfloat16)
         return grad_half, probs_half
 
-    def gather(tile, pairs, keys, sides, grad_half, probs_half):
+    def gather(tile, pairs, sides, grad_half, probs_half):
         both = jnp.concatenate([grad_half, probs_half], axis=1)
         key_grads = jnp.dot(both, sides, preferred_element_type=jnp.float32)
-        grad_query = lax.dot_general(
-            grad_half, keys, (((0,), (0,)), ((), ())), preferred_element_type=jnp.float32
+        turned = []
+        for side in range(2):
+            halves = [turned_ref[pair[side]] for pair in pairs]
+            whole = [jnp.where(low, halves[i], halves[i + 1]) for i in range(0, len(pairs), 2)]
+            turned.append(jnp.concatenate(whole, axis=1))
+        grad_query = jnp.dot(
+            jnp.concatenate(turned, axis=0), grad_half, preferred_element_type=jnp.float32
         )
-        grad_query = grad_query * scale
-        folded = jnp.where(
-            low, grad_query[:BLOCK, :LANES], swap_halves(grad_query[BLOCK:, LANES:])
-        ).astype(jnp.bfloat16)
-        gq_ref[tile] = folded
+        grad_query = jnp.where(low, grad_query[:HEAD], grad_query[HEAD:]) * scale
+        gq_ref[tile] = grad_query.astype(jnp.bfloat16)
         for place, (a, b) in enumerate(pairs):
             part = key_grads[place * BLOCK : (place + 1) * BLOCK]
             if place < 2 + GLOBAL:
@@ -204,8 +220,8 @@
         if 0 <= step - 1 < tiles:
             weighed[step - 1] = weigh(step - 1, ahead[step - 1][-1])
         if step >= 2:
-            pairs, keys, sides, _ = ahead.pop(step - 2)
-            gather(step - 2, pairs, keys, sides, *weighed.pop(step - 2))
+            pairs, sides, _ = ahead.pop(step - 2)
+            gather(step - 2, pairs, sides, *weighed.pop(step - 2))
     if alone:
         for m in range(HEADS):
             tile = lax.bitwise_xor(place, m)
@@ -273,6 +289,7 @@
                 pltpu.VMEM((ways, 2, 2, BLOCK, LANES), half_type),
                 pltpu.VMEM((ways, BLOCK, LANES), half_type),
                 pltpu.VMEM((blocks, BLOCK, LANES), jnp.float32),
+                pltpu.VMEM((blocks, HEAD, LANES), half_type),
                 pltpu.SMEM((blocks * RAND + GLOBAL,), jnp.int32),
                 pltpu.SemaphoreType.DMA,
             ],
@@ -320,7 +337,11 @@
         ],
         in_specs=[pl.BlockSpec(memory_space=pl.ANY), vmem, vmem],
         out_specs=[vmem] * 2,
-        scratch_shapes=[pltpu.SMEM(table.shape, jnp.int32), pltpu.SemaphoreType.DMA],
+        scratch_shapes=[
+            pltpu.VMEM((pool.shape[0], HEAD, LANES), pool.dtype),
+            pltpu.SMEM(table.shape, jnp.int32),
+            pltpu.SemaphoreType.DMA,
+        ],
         compiler_params=pltpu.CompilerParams(vmem_limit_bytes=24 * 2**20),
         name="attend",
     )(table, sent, pool)

time: 37.8 us -> 37.9 us (level)
  no operation moved by 1% of the time
where the time goes in v12:
time: 37.9 us; the launch traced here: 37.7 us
  starting transfers between devices  22.8 us (60%)
  waiting for transfers between devices  8.42 us (22%)
  Pallas kernels  5.59 us (15%)
  between operations  0.68 us (2%)
    ppermute x14, starting transfers between devices, exchange(): arrived[m] = lax.ppermute(parts[m], 'seq', route)  22.8 us
    ppermute x14, waiting for transfers between devices, exchange(): arrived[m] = lax.ppermute(parts[m], 'seq', route)  8.42 us
    pallas_call x1, Pallas kernels, on_device(): pl.pallas_call(kernel, out_shape=[jax.ShapeDtypeStruct((rows + BLOCK, LAN...  3.24 us
    pallas_call x1, Pallas kernels, on_device(): pl.pallas_call(pack_kernel, out_shape=[jax.ShapeDtypeStruct((2, rows, LAN...  1.42 us
    pallas_call x1, Pallas kernels, on_device(): pl.pallas_call(unpack_kernel, out_shape=[jax.ShapeDtypeStruct((rows, widt...  0.93 us
  transfers between devices with their start and end apart: 14, of which 8 were waited for; matrix products, arithmetic and copies ran while one was open for 1% of the time, Pallas kernels for 0%

profile of v12, /device:TPU:0, one launch (start us, length us, event | category | flops | bytes accessed | tf_op | source)
XLA Modules:
  0.0 37.7 jit_solution(10568628928623611869)
XLA Ops:
  0.6 1.4 %pack.1 = (bf16[2,128,128]{2,1,0:T(8,128)(2,1)S(1)}, bf16[2,128,128]{2,1,0:T(8,128)(2,1)S(1)}, bf16[2,128,128]{2,1,0:T(8,128)(2,1)S(1)}, bf16[2,128,128]{2,1,0:T...) custom-call(bf16[128,512]{1,0:T(8,128)(2,1)} %refs_0_.1, ...), custom_call_target="tpu_custom_call" | custom-call | tf_op jit(solution)/shard_map/pack/pallas_call | solution.py:267
  2.1 4.1 %collective-permute-start = (bf16[2,128,128]{2,1,0:T(8,128)(2,1)S(1)}, bf16[2,128,128]{2,1,0:T(8,128)(2,1)S(1)}, u32[]{:S(2)}, u32[]{:S(2)}) collective-permute-start(bf16[2,128,128]{2,1,0:T(8,128)(2,1)S(1)} %get-tuple-element.20), channel_id=1, source_target_pairs={{0,4},{1,5},{2,6},{3,7},{4,0},{5,1},{6,2},{7,3},{8,12},{9,13},{10,... | collective-permute-start | bytes 196616 | tf_op jit(solution)/shard_map/ppermute | solution.py:239
  6.2 1.3 %collective-permute-start.1 = (bf16[2,128,128]{2,1,0:T(8,128)(2,1)S(1)}, bf16[2,128,128]{2,1,0:T(8,128)(2,1)S(1)}, u32[]{:S(2)}, u32[]{:S(2)}) collective-permute-start(bf16[2,128,128]{2,1,0:T(8,128)(2,1)S(1)} %get-tuple-element.21), channel_id=1, source_target_pairs={{0,6},{1,7},{2,4},{3,5},{4,2},{5,3},{6,0},{7,1},{8,14},{9,15},{10,... | collective-permute-start | bytes 196616 | tf_op jit(solution)/shard_map/ppermute | solution.py:239
  7.5 1.2 %collective-permute-start.2 = (bf16[2,128,128]{2,1,0:T(8,128)(2,1)S(1)}, bf16[2,128,128]{2,1,0:T(8,128)(2,1)S(1)}, u32[]{:S(2)}, u32[]{:S(2)}) collective-permute-start(bf16[2,128,128]{2,1,0:T(8,128)(2,1)S(1)} %get-tuple-element.22), channel_id=1, source_target_pairs={{0,3},{1,2},{2,1},{3,0},{4,7},{5,6},{6,5},{7,4},{8,11},{9,10},{10,... | collective-permute-start | bytes 196616 | tf_op jit(solution)/shard_map/ppermute | solution.py:239
  8.7 2.9 %collective-permute-start.3 = (bf16[2,128,128]{2,1,0:T(8,128)(2,1)S(1)}, bf16[2,128,128]{2,1,0:T(8,128)(2,1)S(1)}, u32[]{:S(2)}, u32[]{:S(2)}) collective-permute-start(bf16[2,128,128]{2,1,0:T(8,128)(2,1)S(1)} %get-tuple-element.23), channel_id=1, source_target_pairs={{0,7},{1,6},{2,5},{3,4},{4,3},{5,2},{6,1},{7,0},{8,15},{9,14},{10,... | collective-permute-start | bytes 196616 | tf_op jit(solution)/shard_map/ppermute | solution.py:239
  11.6 1.3 %collective-permute-start.4 = (bf16[2,128,128]{2,1,0:T(8,128)(2,1)S(1)}, bf16[2,128,128]{2,1,0:T(8,128)(2,1)S(1)}, u32[]{:S(2)}, u32[]{:S(2)}) collective-permute-start(bf16[2,128,128]{2,1,0:T(8,128)(2,1)S(1)} %get-tuple-element.24), channel_id=1, source_target_pairs={{0,5},{1,4},{2,7},{3,6},{4,1},{5,0},{6,3},{7,2},{8,13},{9,12},{10,... | collective-permute-start | bytes 196616 | tf_op jit(solution)/shard_map/ppermute | solution.py:239
  13.0 1.2 %collective-permute-start.5 = (bf16[2,128,128]{2,1,0:T(8,128)(2,1)S(1)}, bf16[2,128,128]{2,1,0:T(8,128)(2,1)S(1)}, u32[]{:S(2)}, u32[]{:S(2)}) collective-permute-start(bf16[2,128,128]{2,1,0:T(8,128)(2,1)S(1)} %get-tuple-element.25), channel_id=1, source_target_pairs={{0,2},{1,3},{2,0},{3,1},{4,6},{5,7},{6,4},{7,5},{8,10},{9,11},{10,... | collective-permute-start | bytes 196616 | tf_op jit(solution)/shard_map/ppermute | solution.py:239
  14.2 0.5 %collective-permute-start.6 = (bf16[2,128,128]{2,1,0:T(8,128)(2,1)S(1)}, bf16[2,128,128]{2,1,0:T(8,128)(2,1)S(1)}, u32[]{:S(2)}, u32[]{:S(2)}) collective-permute-start(bf16[2,128,128]{2,1,0:T(8,128)(2,1)S(1)} %get-tuple-element.26), channel_id=1, source_target_pairs={{0,1},{1,0},{2,3},{3,2},{4,5},{5,4},{6,7},{7,6},{8,9},{9,8},{10,11... | collective-permute-start | bytes 196616 | tf_op jit(solution)/shard_map/ppermute | solution.py:239
  14.8 1.2 %collective-permute-done.3 = bf16[2,128,128]{2,1,0:T(8,128)(2,1)S(1)} collective-permute-done((bf16[2,128,128]{2,1,0:T(8,128)(2,1)S(1)}, bf16[2,128,128]{2,1,0:T(8,128)(2,1)S(1)}, u32[]{:S(2)}, u32[]{:S(2)}) %collective-permute-start.3) | collective-permute-done | bytes 65568 | tf_op jit(solution)/shard_map/ppermute | solution.py:239
  16.1 3.5 %collective-permute-done.4 = bf16[2,128,128]{2,1,0:T(8,128)(2,1)S(1)} collective-permute-done((bf16[2,128,128]{2,1,0:T(8,128)(2,1)S(1)}, bf16[2,128,128]{2,1,0:T(8,128)(2,1)S(1)}, u32[]{:S(2)}, u32[]{:S(2)}) %collective-permute-start.4) | collective-permute-done | bytes 65568 | tf_op jit(solution)/shard_map/ppermute | solution.py:239
  19.9 3.2 %attend.1 = (bf16[192,128]{1,0:T(8,128)(2,1)S(1)}, bf16[192,128]{1,0:T(8,128)(2,1)S(1)}, bf16[192,128]{1,0:T(8,128)(2,1)S(1)}, bf16[192,128]{1,0:T(8,128)(2,1)S(...) custom-call(s32[50]{0:T(128)S(1)} %pad_add_fusion.ints_ref, ...), custom_call_target="tpu_custom_call" | custom-call | tf_op jit(solution)/shard_map/attend/pallas_call | solution.py:283
  23.1 3.0 %collective-permute-start.7 = (bf16[192,128]{1,0:T(8,128)(2,1)S(1)}, bf16[192,128]{1,0:T(8,128)(2,1)S(1)}, u32[]{:S(2)}, u32[]{:S(2)}) collective-permute-start(bf16[192,128]{1,0:T(8,128)(2,1)S(1)} %get-tuple-element.28), channel_id=1, source_target_pairs={{0,6},{1,7},{2,4},{3,5},{4,2},{5,3},{6,0},{7,1},{8,14},{9,15},{10,... | collective-permute-start | bytes 147464 | tf_op jit(solution)/shard_map/ppermute | solution.py:239
  26.1 0.8 %collective-permute-start.8 = (bf16[192,128]{1,0:T(8,128)(2,1)S(1)}, bf16[192,128]{1,0:T(8,128)(2,1)S(1)}, u32[]{:S(2)}, u32[]{:S(2)}) collective-permute-start(bf16[192,128]{1,0:T(8,128)(2,1)S(1)} %get-tuple-element.29), channel_id=1, source_target_pairs={{0,5},{1,4},{2,7},{3,6},{4,1},{5,0},{6,3},{7,2},{8,13},{9,12},{10,... | collective-permute-start | bytes 147464 | tf_op jit(solution)/shard_map/ppermute | solution.py:239
  26.9 2.8 %collective-permute-start.9 = (bf16[192,128]{1,0:T(8,128)(2,1)S(1)}, bf16[192,128]{1,0:T(8,128)(2,1)S(1)}, u32[]{:S(2)}, u32[]{:S(2)}) collective-permute-start(bf16[192,128]{1,0:T(8,128)(2,1)S(1)} %get-tuple-element.30), channel_id=1, source_target_pairs={{0,7},{1,6},{2,5},{3,4},{4,3},{5,2},{6,1},{7,0},{8,15},{9,14},{10,... | collective-permute-start | bytes 147464 | tf_op jit(solution)/shard_map/ppermute | solution.py:239
  29.8 0.7 %collective-permute-start.10 = (bf16[192,128]{1,0:T(8,128)(2,1)S(1)}, bf16[192,128]{1,0:T(8,128)(2,1)S(1)}, u32[]{:S(2)}, u32[]{:S(2)}) collective-permute-start(bf16[192,128]{1,0:T(8,128)(2,1)S(1)} %get-tuple-element.31), channel_id=1, source_target_pairs={{0,3},{1,2},{2,1},{3,0},{4,7},{5,6},{6,5},{7,4},{8,11},{9,10},{10,... | collective-permute-start | bytes 147464 | tf_op jit(solution)/shard_map/ppermute | solution.py:239
  30.5 1.7 %collective-permute-start.11 = (bf16[192,128]{1,0:T(8,128)(2,1)S(1)}, bf16[192,128]{1,0:T(8,128)(2,1)S(1)}, u32[]{:S(2)}, u32[]{:S(2)}) collective-permute-start(bf16[192,128]{1,0:T(8,128)(2,1)S(1)} %get-tuple-element.32), channel_id=1, source_target_pairs={{0,4},{1,5},{2,6},{3,7},{4,0},{5,1},{6,2},{7,3},{8,12},{9,13},{10,... | collective-permute-start | bytes 147464 | tf_op jit(solution)/shard_map/ppermute | solution.py:239
  32.2 0.5 %collective-permute-start.12 = (bf16[192,128]{1,0:T(8,128)(2,1)S(1)}, bf16[192,128]{1,0:T(8,128)(2,1)S(1)}, u32[]{:S(2)}, u32[]{:S(2)}) collective-permute-start(bf16[192,128]{1,0:T(8,128)(2,1)S(1)} %get-tuple-element.33), channel_id=1, source_target_pairs={{0,2},{1,3},{2,0},{3,1},{4,6},{5,7},{6,4},{7,5},{8,10},{9,11},{10,... | collective-permute-start | bytes 147464 | tf_op jit(solution)/shard_map/ppermute | solution.py:239
  32.7 0.7 %collective-permute-start.13 = (bf16[192,128]{1,0:T(8,128)(2,1)S(1)}, bf16[192,128]{1,0:T(8,128)(2,1)S(1)}, u32[]{:S(2)}, u32[]{:S(2)}) collective-permute-start(bf16[192,128]{1,0:T(8,128)(2,1)S(1)} %get-tuple-element.34), channel_id=1, source_target_pairs={{0,1},{1,0},{2,3},{3,2},{4,5},{5,4},{6,7},{7,6},{8,9},{9,8},{10,11... | collective-permute-start | bytes 147464 | tf_op jit(solution)/shard_map/ppermute | solution.py:239
  33.5 0.4 %collective-permute-done.9.refs_3_ = bf16[192,128]{1,0:T(8,128)(2,1)S(1)} collective-permute-done((bf16[192,128]{1,0:T(8,128)(2,1)S(1)}, bf16[192,128]{1,0:T(8,128)(2,1)S(1)}, u32[]{:S(2)}, u32[]{:S(2)}) %collective-permute-start.9) | collective-permute-done | bytes 49184 | tf_op jit(solution)/shard_map/ppermute | solution.py:239
  33.8 1.2 %collective-permute-done.10.refs_4_ = bf16[192,128]{1,0:T(8,128)(2,1)S(1)} collective-permute-done((bf16[192,128]{1,0:T(8,128)(2,1)S(1)}, bf16[192,128]{1,0:T(8,128)(2,1)S(1)}, u32[]{:S(2)}, u32[]{:S(2)}) %collective-permute-start.10) | collective-permute-done | bytes 49184 | tf_op jit(solution)/shard_map/ppermute | solution.py:239
  35.0 0.5 %collective-permute-done.11.refs_5_ = bf16[192,128]{1,0:T(8,128)(2,1)S(1)} collective-permute-done((bf16[192,128]{1,0:T(8,128)(2,1)S(1)}, bf16[192,128]{1,0:T(8,128)(2,1)S(1)}, u32[]{:S(2)}, u32[]{:S(2)}) %collective-permute-start.11) | collective-permute-done | bytes 49184 | tf_op jit(solution)/shard_map/ppermute | solution.py:239
  35.5 0.8 %collective-permute-done.12.refs_6_ = bf16[192,128]{1,0:T(8,128)(2,1)S(1)} collective-permute-done((bf16[192,128]{1,0:T(8,128)(2,1)S(1)}, bf16[192,128]{1,0:T(8,128)(2,1)S(1)}, u32[]{:S(2)}, u32[]{:S(2)}) %collective-permute-start.12) | collective-permute-done | bytes 49184 | tf_op jit(solution)/shard_map/ppermute | solution.py:239
  36.3 0.5 %collective-permute-done.13.refs_7_ = bf16[192,128]{1,0:T(8,128)(2,1)S(1)} collective-permute-done((bf16[192,128]{1,0:T(8,128)(2,1)S(1)}, bf16[192,128]{1,0:T(8,128)(2,1)S(1)}, u32[]{:S(2)}, u32[]{:S(2)}) %collective-permute-start.13) | collective-permute-done | bytes 49184 | tf_op jit(solution)/shard_map/ppermute | solution.py:239
  36.8 0.9 %unpack.1 = (bf16[128,512]{1,0:T(8,128)(2,1)}, bf16[128,512]{1,0:T(8,128)(2,1)}, bf16[128,512]{1,0:T(8,128)(2,1)}) custom-call(bf16[192,128]{1,0:T(8,128)(2,1)S(1)} %get-tuple-element.27.refs_0_, bf16[192,128]{1,0:T(8,128)(2,1)S(1)} %collective-permute-done.7.refs_1_, bf16[192,128]{1,0:T(8,128)(2,1)S(1)} %collective-permute-done.8.refs_2_, ...), custom_call_target="tpu_custom_call" | custom-call | tf_op jit(solution)/shard_map/unpack/pallas_call | solution.py:302
  (14 shorter events, 0.6 us)
Async XLA Ops:
  2.1 10.9 %collective-permute-start = (bf16[2,128,128]{2,1,0:T(8,128)(2,1)S(1)}, bf16[2,128,128]{2,1,0:T(8,128)(2,1)S(1)}, u32[]{:S(2)}, u32[]{:S(2)}) collective-permute-start(bf16[2,128,128]{2,1,0:T(8,128)(2,1)S(1)} %get-tuple-element.20), channel_id=1, source_target_pairs={{0,4},{1,5},{2,6},{3,7},{4,0},{5,1},{6,2},{7,3},{8,12},{9,13},{10,... | collective-permute-start | bytes 196616 | tf_op jit(solution)/shard_map/ppermute | solution.py:239
  6.2 8.1 %collective-permute-start.1 = (bf16[2,128,128]{2,1,0:T(8,128)(2,1)S(1)}, bf16[2,128,128]{2,1,0:T(8,128)(2,1)S(1)}, u32[]{:S(2)}, u32[]{:S(2)}) collective-permute-start(bf16[2,128,128]{2,1,0:T(8,128)(2,1)S(1)} %get-tuple-element.21), channel_id=1, source_target_pairs={{0,6},{1,7},{2,4},{3,5},{4,2},{5,3},{6,0},{7,1},{8,14},{9,15},{10,... | collective-permute-start | bytes 196616 | tf_op jit(solution)/shard_map/ppermute | solution.py:239
  7.5 5.3 %copy-start = (s32[16,3]{0,1:T(4,128)S(1)}, s32[16,3]{0,1:T(4,128)}, u32[]{:S(2)}) copy-start(s32[16,3]{0,1:T(4,128)} %param.10) | copy-start | bytes 580
  7.5 7.3 %collective-permute-start.2 = (bf16[2,128,128]{2,1,0:T(8,128)(2,1)S(1)}, bf16[2,128,128]{2,1,0:T(8,128)(2,1)S(1)}, u32[]{:S(2)}, u32[]{:S(2)}) collective-permute-start(bf16[2,128,128]{2,1,0:T(8,128)(2,1)S(1)} %get-tuple-element.22), channel_id=1, source_target_pairs={{0,3},{1,2},{2,1},{3,0},{4,7},{5,6},{6,5},{7,4},{8,11},{9,10},{10,... | collective-permute-start | bytes 196616 | tf_op jit(solution)/shard_map/ppermute | solution.py:239
  8.7 7.4 %collective-permute-start.3 = (bf16[2,128,128]{2,1,0:T(8,128)(2,1)S(1)}, bf16[2,128,128]{2,1,0:T(8,128)(2,1)S(1)}, u32[]{:S(2)}, u32[]{:S(2)}) collective-permute-start(bf16[2,128,128]{2,1,0:T(8,128)(2,1)S(1)} %get-tuple-element.23), channel_id=1, source_target_pairs={{0,7},{1,6},{2,5},{3,4},{4,3},{5,2},{6,1},{7,0},{8,15},{9,14},{10,... | collective-permute-start | bytes 196616 | tf_op jit(solution)/shard_map/ppermute | solution.py:239
  11.6 8.0 %collective-permute-start.4 = (bf16[2,128,128]{2,1,0:T(8,128)(2,1)S(1)}, bf16[2,128,128]{2,1,0:T(8,128)(2,1)S(1)}, u32[]{:S(2)}, u32[]{:S(2)}) collective-permute-start(bf16[2,128,128]{2,1,0:T(8,128)(2,1)S(1)} %get-tuple-element.24), channel_id=1, source_target_pairs={{0,5},{1,4},{2,7},{3,6},{4,1},{5,0},{6,3},{7,2},{8,13},{9,12},{10,... | collective-permute-start | bytes 196616 | tf_op jit(solution)/shard_map/ppermute | solution.py:239
  13.0 1.7 %copy-start.1 = (s32[2]{0:T(128)S(1)}, s32[2]{0:T(128)}, u32[]{:S(2)}) copy-start(s32[2]{0:T(128)} %param.11) | copy-start | bytes 28
  13.0 6.5 %collective-permute-start.5 = (bf16[2,128,128]{2,1,0:T(8,128)(2,1)S(1)}, bf16[2,128,128]{2,1,0:T(8,128)(2,1)S(1)}, u32[]{:S(2)}, u32[]{:S(2)}) collective-permute-start(bf16[2,128,128]{2,1,0:T(8,128)(2,1)S(1)} %get-tuple-element.25), channel_id=1, source_target_pairs={{0,2},{1,3},{2,0},{3,1},{4,6},{5,7},{6,4},{7,5},{8,10},{9,11},{10,... | collective-permute-start | bytes 196616 | tf_op jit(solution)/shard_map/ppermute | solution.py:239
  14.2 5.7 %collective-permute-start.6 = (bf16[2,128,128]{2,1,0:T(8,128)(2,1)S(1)}, bf16[2,128,128]{2,1,0:T(8,128)(2,1)S(1)}, u32[]{:S(2)}, u32[]{:S(2)}) collective-permute-start(bf16[2,128,128]{2,1,0:T(8,128)(2,1)S(1)} %get-tuple-element.26), channel_id=1, source_target_pairs={{0,1},{1,0},{2,3},{3,2},{4,5},{5,4},{6,7},{7,6},{8,9},{9,8},{10,11... | collective-permute-start | bytes 196616 | tf_op jit(solution)/shard_map/ppermute | solution.py:239
  23.1 9.1 %collective-permute-start.7 = (bf16[192,128]{1,0:T(8,128)(2,1)S(1)}, bf16[192,128]{1,0:T(8,128)(2,1)S(1)}, u32[]{:S(2)}, u32[]{:S(2)}) collective-permute-start(bf16[192,128]{1,0:T(8,128)(2,1)S(1)} %get-tuple-element.28), channel_id=1, source_target_pairs={{0,6},{1,7},{2,4},{3,5},{4,2},{5,3},{6,0},{7,1},{8,14},{9,15},{10,... | collective-permute-start | bytes 147464 | tf_op jit(solution)/shard_map/ppermute | solution.py:239
  26.1 6.6 %collective-permute-start.8 = (bf16[192,128]{1,0:T(8,128)(2,1)S(1)}, bf16[192,128]{1,0:T(8,128)(2,1)S(1)}, u32[]{:S(2)}, u32[]{:S(2)}) collective-permute-start(bf16[192,128]{1,0:T(8,128)(2,1)S(1)} %get-tuple-element.29), channel_id=1, source_target_pairs={{0,5},{1,4},{2,7},{3,6},{4,1},{5,0},{6,3},{7,2},{8,13},{9,12},{10,... | collective-permute-start | bytes 147464 | tf_op jit(solution)/shard_map/ppermute | solution.py:239
  26.9 6.9 %collective-permute-start.9 = (bf16[192,128]{1,0:T(8,128)(2,1)S(1)}, bf16[192,128]{1,0:T(8,128)(2,1)S(1)}, u32[]{:S(2)}, u32[]{:S(2)}) collective-permute-start(bf16[192,128]{1,0:T(8,128)(2,1)S(1)} %get-tuple-element.30), channel_id=1, source_target_pairs={{0,7},{1,6},{2,5},{3,4},{4,3},{5,2},{6,1},{7,0},{8,15},{9,14},{10,... | collective-permute-start | bytes 147464 | tf_op jit(solution)/shard_map/ppermute | solution.py:239
  29.8 5.2 %collective-permute-start.10 = (bf16[192,128]{1,0:T(8,128)(2,1)S(1)}, bf16[192,128]{1,0:T(8,128)(2,1)S(1)}, u32[]{:S(2)}, u32[]{:S(2)}) collective-permute-start(bf16[192,128]{1,0:T(8,128)(2,1)S(1)} %get-tuple-element.31), channel_id=1, source_target_pairs={{0,3},{1,2},{2,1},{3,0},{4,7},{5,6},{6,5},{7,4},{8,11},{9,10},{10,... | collective-permute-start | bytes 147464 | tf_op jit(solution)/shard_map/ppermute | solution.py:239
  30.5 5.0 %collective-permute-start.11 = (bf16[192,128]{1,0:T(8,128)(2,1)S(1)}, bf16[192,128]{1,0:T(8,128)(2,1)S(1)}, u32[]{:S(2)}, u32[]{:S(2)}) collective-permute-start(bf16[192,128]{1,0:T(8,128)(2,1)S(1)} %get-tuple-element.32), channel_id=1, source_target_pairs={{0,4},{1,5},{2,6},{3,7},{4,0},{5,1},{6,2},{7,3},{8,12},{9,13},{10,... | collective-permute-start | bytes 147464 | tf_op jit(solution)/shard_map/ppermute | solution.py:239
  32.2 4.1 %collective-permute-start.12 = (bf16[192,128]{1,0:T(8,128)(2,1)S(1)}, bf16[192,128]{1,0:T(8,128)(2,1)S(1)}, u32[]{:S(2)}, u32[]{:S(2)}) collective-permute-start(bf16[192,128]{1,0:T(8,128)(2,1)S(1)} %get-tuple-element.33), channel_id=1, source_target_pairs={{0,2},{1,3},{2,0},{3,1},{4,6},{5,7},{6,4},{7,5},{8,10},{9,11},{10,... | collective-permute-start | bytes 147464 | tf_op jit(solution)/shard_map/ppermute | solution.py:239
  32.7 4.1 %collective-permute-start.13 = (bf16[192,128]{1,0:T(8,128)(2,1)S(1)}, bf16[192,128]{1,0:T(8,128)(2,1)S(1)}, u32[]{:S(2)}, u32[]{:S(2)}) collective-permute-start(bf16[192,128]{1,0:T(8,128)(2,1)S(1)} %get-tuple-element.34), channel_id=1, source_target_pairs={{0,1},{1,0},{2,3},{3,2},{4,5},{5,4},{6,7},{7,6},{8,9},{9,8},{10,11... | collective-permute-start | bytes 147464 | tf_op jit(solution)/shard_map/ppermute | solution.py:239

commit v13 on v11

--- a/solution.py
+++ b/solution.py
@@ -16,7 +16,6 @@
 LANES = 2 * HEAD
 PARTNERS_IN = (0, 4, 6, 3, 7, 5, 2, 1)
 PARTNERS_BACK = (0, 6, 5, 7, 3, 4, 2, 1)
-NEAR = (2, 3, 1, 0)
 PACK_GRANT = 427 * 2**17
 MASKED = -1e30
 
@@ -32,23 +31,19 @@
 def pack_kernel(*refs):
     in_refs, out_refs = refs[:4], refs[4 : 4 + HEADS]
     held_ref, in_sems = refs[4 + HEADS :]
-    rows = held_ref.shape[2]
+    copies = [pltpu.make_async_copy(in_refs[i], held_ref.at[i], in_sems.at[i]) for i in range(4)]
+    for copy in copies:
+        copy.start()
+    rows = held_ref.shape[1]
     low = low_lanes((rows, LANES))
     place = lax.rem(lax.axis_index("seq"), HEADS)
     odd_place = lax.rem(place, 2) == 1
-    arriving = {}
-    for near in NEAR:
+    for copy in copies:
+        copy.wait()
+    for near in range(HEADS // 2):
         pair = lax.bitwise_xor(place // 2, near)
         lanes = pl.ds(pl.multiple_of(pair * LANES, LANES), LANES)
-        for kind, ref in enumerate(in_refs):
-            arriving[near, kind] = pltpu.make_async_copy(
-                ref.at[:, lanes], held_ref.at[near, kind], in_sems.at[near, kind]
-            )
-            arriving[near, kind].start()
-    for near in NEAR:
-        for kind in range(4):
-            arriving[near, kind].wait()
-        q, k, v, g = [held_ref[near, kind].astype(jnp.float32) for kind in range(4)]
+        q, k, v, g = [held_ref[i, :, lanes].astype(jnp.float32) for i in range(4)]
         for kind, (first, second) in enumerate(((k, v), (q, g))):
             even = jnp.where(low, first, swap_halves(second))
             odd = jnp.where(low, swap_halves(first), second)
@@ -60,36 +55,44 @@
 
 def unpack_kernel(*refs):
     in_refs = dict(zip(PARTNERS_BACK, refs[:HEADS]))
-    gq_ref, gk_ref, gv_ref = refs[HEADS:]
-    rows = gq_ref.shape[0]
+    out_refs, held_ref, sems = refs[HEADS : HEADS + 3], refs[-2], refs[-1]
+    rows = held_ref.shape[1]
     low = low_lanes((rows, LANES))
     low_block = low_lanes((BLOCK, LANES))
     place = lax.rem(lax.axis_index("seq"), HEADS)
     odd_place = lax.rem(place, 2) == 1
-    for near in range(HEADS // 2):
-        pair = lax.bitwise_xor(place // 2, near)
-        lanes = pl.ds(pl.multiple_of(pair * LANES, LANES), LANES)
-        same = in_refs[2 * near][...].astype(jnp.float32)
-        other = in_refs[2 * near + 1][...].astype(jnp.float32)
-        even = jnp.where(odd_place, other, same)
-        odd = jnp.where(odd_place, same, other)
-        gk = jnp.where(low, even[:rows], swap_halves(odd[:rows]))
-        gv = jnp.where(low, swap_halves(even[:rows]), odd[:rows])
-        gk_ref[:, lanes] = gk.astype(jnp.bfloat16)
-        gv_ref[:, lanes] = gv.astype(jnp.bfloat16)
-        first = jnp.where(low_block, even[rows:], swap_halves(odd[rows:]))
-        second = jnp.where(low_block, swap_halves(even[rows:]), odd[rows:])
-        gq_ref[:BLOCK, lanes] = first.astype(jnp.bfloat16)
-        gq_ref[BLOCK:, lanes] = second.astype(jnp.bfloat16)
+    copies = [pltpu.make_async_copy(held_ref.at[i], out_refs[i], sems.at[i]) for i in range(3)]
+    for kind in (1, 2, 0):
+        for near in range(HEADS // 2):
+            pair = lax.bitwise_xor(place // 2, near)
+            lanes = pl.ds(pl.multiple_of(pair * LANES, LANES), LANES)
+            part = slice(rows, rows + BLOCK) if kind == 0 else slice(0, rows)
+            same = in_refs[2 * near][part].astype(jnp.float32)
+            other = in_refs[2 * near + 1][part].astype(jnp.float32)
+            even = jnp.where(odd_place, other, same)
+            odd = jnp.where(odd_place, same, other)
+            if kind == 1:
+                whole = jnp.where(low, even, swap_halves(odd))
+            elif kind == 2:
+                whole = jnp.where(low, swap_halves(even), odd)
+            else:
+                first = jnp.where(low_block, even, swap_halves(odd))
+                second = jnp.where(low_block, swap_halves(even), odd)
+                whole = jnp.concatenate([first, second], axis=0)
+            held_ref[kind, :, lanes] = whole.astype(jnp.bfloat16)
+        copies[kind].start()
+    for copy in copies:
+        copy.wait()
 
 
 def attend_kernel(alone, scale, ints_ref, *rest):
     if alone:
         in_refs = dict(zip(PARTNERS_IN, rest[:HEADS]))
         out_refs = rest[HEADS : 2 * HEADS]
-        sent_ref, gq_ref, acc_ref, table_ref, sem = rest[2 * HEADS :]
+        sent_ref, gq_ref, acc_ref, *rest = rest[2 * HEADS :]
     else:
-        sent_ref, pool_ref, gq_ref, acc_ref, table_ref, sem = rest
+        sent_ref, pool_ref, gq_ref, acc_ref, *rest = rest
+    global_ref, global_acc_ref, table_ref, sem = rest
     fetch = pltpu.make_async_copy(ints_ref, table_ref, sem)
     fetch.start()
     if alone:
@@ -110,37 +113,40 @@
             return sent_ref[entry // 2, 0, entry % 2]
         return pool_ref[entry]
 
-    def chosen(tile):
+    for slot in range(GLOBAL):
+        entry = table_ref[fixed + slot] if alone else blocks + 2 + slot
+        global_ref[slot] = pooled(entry)
+        global_acc_ref[slot] = jnp.zeros((BLOCK, LANES), jnp.float32)
+
+    def window(tile):
         first = 2 * tile
-        pairs = [(first, first), (first + 1, first + 1)]
-        for slot in range(GLOBAL):
-            entry = table_ref[fixed + slot] if alone else blocks + 2 + slot
-            pairs.append((entry, entry))
         before, after = first - 1, first + 2
         if alone:
-            before, after = max(before, 0), min(after, blocks - 1)
+            return first, first + 1, max(before, 0), min(after, blocks - 1)
+        before = before if tile > 0 else blocks
+        after = after if tile < tiles - 1 else blocks + 1
+        return first, first + 1, before, after
+
+    def random(block, slot):
+        if alone:
+            here = (block - (slot + 1) * blocks // 4) % blocks
+            back = (here - 1) % blocks
         else:
-            before = before if tile > 0 else blocks
-            after = after if tile < tiles - 1 else blocks + 1
-        pairs.append((before, after))
-        for slot in range(RAND):
-            picked = []
-            for block in (first, first + 1):
-                pick = table_ref[block * RAND + slot]
-                if alone:
-                    behind = block + blocks - (slot + 1) * blocks // 4 - pick
-                    picked.append(lax.rem(behind, blocks))
-                else:
-                    base = blocks + 2 + GLOBAL + slot * (blocks + 1)
-                    picked.append(base + block + 1 - pick)
-            pairs.append(tuple(picked))
-        return pairs
+            back = blocks + 2 + GLOBAL + slot * (blocks + 1) + block
+            here = back + 1
+        return here, back, table_ref[block * RAND + slot] == 1
+
+    def drawn(block, slot):
+        here, back, picked = random(block, slot)
+        return jnp.where(picked, pooled(back), pooled(here))
 
     def multiply(tile):
-        pairs = chosen(tile)
-        keys = jnp.concatenate(
-            [jnp.concatenate([pooled(a), pooled(b)], axis=1) for a, b in pairs], axis=0
-        )
+        one, two, before, after = window(tile)
+        pairs = [(pooled(one), pooled(one)), (pooled(two), pooled(two))]
+        pairs += [(global_ref[slot], global_ref[slot]) for slot in range(GLOBAL)]
+        pairs.append((pooled(before), pooled(after)))
+        pairs += [(drawn(one, slot), drawn(two, slot)) for slot in range(RAND)]
+        keys = jnp.concatenate([jnp.concatenate(pair, axis=1) for pair in pairs], axis=0)
         first, second = sent_ref[tile, 1, 0], sent_ref[tile, 1, 1]
         rows = [
             [jnp.where(low, first * scale, zero), zero],
@@ -152,7 +158,7 @@
         products = lax.dot_general(
             keys, sides, (((1,), (1,)), ((), ())), preferred_element_type=jnp.float32
         )
-        return pairs, keys, sides, products
+        return keys, sides, products
 
     def weigh(tile, products):
         scores, grad_probs = products[:, :queries], products[:, queries:]
@@ -178,7 +184,7 @@
         grad_half = (expo * ((grad_probs - row_dot) * inverse)).astype(jnp.bfloat16)
         return grad_half, probs_half
 
-    def gather(tile, pairs, keys, sides, grad_half, probs_half):
+    def gather(tile, keys, sides, grad_half, probs_half):
         both = jnp.concatenate([grad_half, probs_half], axis=1)
         key_grads = jnp.dot(both, sides, preferred_element_type=jnp.float32)
         grad_query = lax.dot_general(
@@ -189,13 +195,22 @@
             low, grad_query[:BLOCK, :LANES], swap_halves(grad_query[BLOCK:, LANES:])
         ).astype(jnp.bfloat16)
         gq_ref[tile] = folded
-        for place, (a, b) in enumerate(pairs):
-            part = key_grads[place * BLOCK : (place + 1) * BLOCK]
-            if place < 2 + GLOBAL:
-                acc_ref[a] += part[:, :LANES] + part[:, LANES:]
-            else:
-                acc_ref[a] += part[:, :LANES]
-                acc_ref[b] += part[:, LANES:]
+        parts = [key_grads[i * BLOCK : (i + 1) * BLOCK] for i in range(3 + GLOBAL + RAND)]
+        one, two, before, after = window(tile)
+        acc_ref[one] += parts[0][:, :LANES] + parts[0][:, LANES:]
+        acc_ref[two] += parts[1][:, :LANES] + parts[1][:, LANES:]
+        for slot in range(GLOBAL):
+            part = parts[2 + slot]
+            global_acc_ref[slot] += part[:, :LANES] + part[:, LANES:]
+        acc_ref[before] += parts[2 + GLOBAL][:, :LANES]
+        acc_ref[after] += parts[2 + GLOBAL][:, LANES:]
+        for slot in range(RAND):
+            part = parts[3 + GLOBAL + slot]
+            for side, block in enumerate((one, two)):
+                here, back, picked = random(block, slot)
+                mine = part[:, side * LANES : (side + 1) * LANES]
+                acc_ref[back] += jnp.where(picked, mine, 0.0)
+                acc_ref[here] += jnp.where(picked, 0.0, mine)
 
     ahead, weighed = {}, {}
     for step in range(tiles + 2):
@@ -204,8 +219,11 @@
         if 0 <= step - 1 < tiles:
             weighed[step - 1] = weigh(step - 1, ahead[step - 1][-1])
         if step >= 2:
-            pairs, keys, sides, _ = ahead.pop(step - 2)
-            gather(step - 2, pairs, keys, sides, *weighed.pop(step - 2))
+            keys, sides, _ = ahead.pop(step - 2)
+            gather(step - 2, keys, sides, *weighed.pop(step - 2))
+    for slot in range(GLOBAL):
+        entry = table_ref[fixed + slot] if alone else blocks + 2 + slot
+        acc_ref[entry] += global_acc_ref[slot]
     if alone:
         for m in range(HEADS):
             tile = lax.bitwise_xor(place, m)
@@ -254,8 +272,8 @@
         in_specs=[anywhere] * 4,
         out_specs=[vmem] * HEADS,
         scratch_shapes=[
-            pltpu.VMEM((HEADS // 2, 4, rows, LANES), half_type),
-            pltpu.SemaphoreType.DMA((HEADS // 2, 4)),
+            pltpu.VMEM((4, rows, width), half_type),
+            pltpu.SemaphoreType.DMA((4,)),
         ],
         compiler_params=pltpu.CompilerParams(vmem_limit_bytes=PACK_GRANT),
         name="pack",
@@ -273,6 +291,8 @@
                 pltpu.VMEM((ways, 2, 2, BLOCK, LANES), half_type),
                 pltpu.VMEM((ways, BLOCK, LANES), half_type),
                 pltpu.VMEM((blocks, BLOCK, LANES), jnp.float32),
+                pltpu.VMEM((GLOBAL, BLOCK, LANES), half_type),
+                pltpu.VMEM((GLOBAL, BLOCK, LANES), jnp.float32),
                 pltpu.SMEM((blocks * RAND + GLOBAL,), jnp.int32),
                 pltpu.SemaphoreType.DMA,
             ],
@@ -286,7 +306,11 @@
         unpack_kernel,
         out_shape=[jax.ShapeDtypeStruct((rows, width), half_type)] * 3,
         in_specs=[vmem] * HEADS,
-        out_specs=[vmem] * 3,
+        out_specs=[anywhere] * 3,
+        scratch_shapes=[
+            pltpu.VMEM((3, rows, width), half_type),
+            pltpu.SemaphoreType.DMA((3,)),
+        ],
         compiler_params=pltpu.CompilerParams(vmem_limit_bytes=8 * 2**20),
         name="unpack",
     )(*[received[m] for m in PARTNERS_BACK])
@@ -320,7 +344,12 @@
         ],
         in_specs=[pl.BlockSpec(memory_space=pl.ANY), vmem, vmem],
         out_specs=[vmem] * 2,
-        scratch_shapes=[pltpu.SMEM(table.shape, jnp.int32), pltpu.SemaphoreType.DMA],
+        scratch_shapes=[
+            pltpu.VMEM((GLOBAL, BLOCK, LANES), pool.dtype),
+            pltpu.VMEM((GLOBAL, BLOCK, LANES), jnp.float32),
+            pltpu.SMEM(table.shape, jnp.int32),
+            pltpu.SemaphoreType.DMA,
+        ],
         compiler_params=pltpu.CompilerParams(vmem_limit_bytes=24 * 2**20),
         name="attend",
     )(table, sent, pool)

time: 37.8 us -> 37.7 us (level)
  no operation moved by 1% of the time
where the time goes in v13:
time: 37.7 us; the launch traced here: 37.6 us
  starting transfers between devices  22.8 us (60%)
  waiting for transfers between devices  8.43 us (22%)
  Pallas kernels  5.43 us (14%)
  between operations  0.68 us (2%)
    ppermute x14, starting transfers between devices, exchange(): arrived[m] = lax.ppermute(parts[m], 'seq', route)  22.8 us
    ppermute x14, waiting for transfers between devices, exchange(): arrived[m] = lax.ppermute(parts[m], 'seq', route)  8.43 us
    pallas_call x1, Pallas kernels, on_device(): pl.pallas_call(kernel, out_shape=[jax.ShapeDtypeStruct((rows + BLOCK, LAN...  3.18 us
    pallas_call x1, Pallas kernels, on_device(): pl.pallas_call(pack_kernel, out_shape=[jax.ShapeDtypeStruct((2, rows, LAN...  1.35 us
    pallas_call x1, Pallas kernels, on_device(): pl.pallas_call(unpack_kernel, out_shape=[jax.ShapeDtypeStruct((rows, widt...  0.9 us
  transfers between devices with their start and end apart: 14, of which 8 were waited for; matrix products, arithmetic and copies ran while one was open for 1% of the time, Pallas kernels for 0%

profile of v13, /device:TPU:0, one launch (start us, length us, event | category | flops | bytes accessed | tf_op | source)
XLA Modules:
  0.0 37.6 jit_solution(8507961023479802823)
XLA Ops:
  0.6 1.4 %pack.1 = (bf16[2,128,128]{2,1,0:T(8,128)(2,1)S(1)}, bf16[2,128,128]{2,1,0:T(8,128)(2,1)S(1)}, bf16[2,128,128]{2,1,0:T(8,128)(2,1)S(1)}, bf16[2,128,128]{2,1,0:T...) custom-call(bf16[128,512]{1,0:T(8,128)(2,1)} %refs_0_.1, ...), custom_call_target="tpu_custom_call" | custom-call | tf_op jit(solution)/shard_map/pack/pallas_call | solution.py:269
  2.0 4.1 %collective-permute-start = (bf16[2,128,128]{2,1,0:T(8,128)(2,1)S(1)}, bf16[2,128,128]{2,1,0:T(8,128)(2,1)S(1)}, u32[]{:S(2)}, u32[]{:S(2)}) collective-permute-start(bf16[2,128,128]{2,1,0:T(8,128)(2,1)S(1)} %get-tuple-element.20), channel_id=1, source_target_pairs={{0,4},{1,5},{2,6},{3,7},{4,0},{5,1},{6,2},{7,3},{8,12},{9,13},{10,... | collective-permute-start | bytes 196616 | tf_op jit(solution)/shard_map/ppermute | solution.py:241
  6.1 1.4 %collective-permute-start.1 = (bf16[2,128,128]{2,1,0:T(8,128)(2,1)S(1)}, bf16[2,128,128]{2,1,0:T(8,128)(2,1)S(1)}, u32[]{:S(2)}, u32[]{:S(2)}) collective-permute-start(bf16[2,128,128]{2,1,0:T(8,128)(2,1)S(1)} %get-tuple-element.21), channel_id=1, source_target_pairs={{0,6},{1,7},{2,4},{3,5},{4,2},{5,3},{6,0},{7,1},{8,14},{9,15},{10,... | collective-permute-start | bytes 196616 | tf_op jit(solution)/shard_map/ppermute | solution.py:241
  7.4 1.2 %collective-permute-start.2 = (bf16[2,128,128]{2,1,0:T(8,128)(2,1)S(1)}, bf16[2,128,128]{2,1,0:T(8,128)(2,1)S(1)}, u32[]{:S(2)}, u32[]{:S(2)}) collective-permute-start(bf16[2,128,128]{2,1,0:T(8,128)(2,1)S(1)} %get-tuple-element.22), channel_id=1, source_target_pairs={{0,3},{1,2},{2,1},{3,0},{4,7},{5,6},{6,5},{7,4},{8,11},{9,10},{10,... | collective-permute-start | bytes 196616 | tf_op jit(solution)/shard_map/ppermute | solution.py:241
  8.6 2.9 %collective-permute-start.3 = (bf16[2,128,128]{2,1,0:T(8,128)(2,1)S(1)}, bf16[2,128,128]{2,1,0:T(8,128)(2,1)S(1)}, u32[]{:S(2)}, u32[]{:S(2)}) collective-permute-start(bf16[2,128,128]{2,1,0:T(8,128)(2,1)S(1)} %get-tuple-element.23), channel_id=1, source_target_pairs={{0,7},{1,6},{2,5},{3,4},{4,3},{5,2},{6,1},{7,0},{8,15},{9,14},{10,... | collective-permute-start | bytes 196616 | tf_op jit(solution)/shard_map/ppermute | solution.py:241
  11.5 1.3 %collective-permute-start.4 = (bf16[2,128,128]{2,1,0:T(8,128)(2,1)S(1)}, bf16[2,128,128]{2,1,0:T(8,128)(2,1)S(1)}, u32[]{:S(2)}, u32[]{:S(2)}) collective-permute-start(bf16[2,128,128]{2,1,0:T(8,128)(2,1)S(1)} %get-tuple-element.24), channel_id=1, source_target_pairs={{0,5},{1,4},{2,7},{3,6},{4,1},{5,0},{6,3},{7,2},{8,13},{9,12},{10,... | collective-permute-start | bytes 196616 | tf_op jit(solution)/shard_map/ppermute | solution.py:241
  13.0 1.2 %collective-permute-start.5 = (bf16[2,128,128]{2,1,0:T(8,128)(2,1)S(1)}, bf16[2,128,128]{2,1,0:T(8,128)(2,1)S(1)}, u32[]{:S(2)}, u32[]{:S(2)}) collective-permute-start(bf16[2,128,128]{2,1,0:T(8,128)(2,1)S(1)} %get-tuple-element.25), channel_id=1, source_target_pairs={{0,2},{1,3},{2,0},{3,1},{4,6},{5,7},{6,4},{7,5},{8,10},{9,11},{10,... | collective-permute-start | bytes 196616 | tf_op jit(solution)/shard_map/ppermute | solution.py:241
  14.2 0.5 %collective-permute-start.6 = (bf16[2,128,128]{2,1,0:T(8,128)(2,1)S(1)}, bf16[2,128,128]{2,1,0:T(8,128)(2,1)S(1)}, u32[]{:S(2)}, u32[]{:S(2)}) collective-permute-start(bf16[2,128,128]{2,1,0:T(8,128)(2,1)S(1)} %get-tuple-element.26), channel_id=1, source_target_pairs={{0,1},{1,0},{2,3},{3,2},{4,5},{5,4},{6,7},{7,6},{8,9},{9,8},{10,11... | collective-permute-start | bytes 196616 | tf_op jit(solution)/shard_map/ppermute | solution.py:241
  14.8 1.2 %collective-permute-done.3 = bf16[2,128,128]{2,1,0:T(8,128)(2,1)S(1)} collective-permute-done((bf16[2,128,128]{2,1,0:T(8,128)(2,1)S(1)}, bf16[2,128,128]{2,1,0:T(8,128)(2,1)S(1)}, u32[]{:S(2)}, u32[]{:S(2)}) %collective-permute-start.3) | collective-permute-done | bytes 65568 | tf_op jit(solution)/shard_map/ppermute | solution.py:241
  16.0 3.5 %collective-permute-done.4 = bf16[2,128,128]{2,1,0:T(8,128)(2,1)S(1)} collective-permute-done((bf16[2,128,128]{2,1,0:T(8,128)(2,1)S(1)}, bf16[2,128,128]{2,1,0:T(8,128)(2,1)S(1)}, u32[]{:S(2)}, u32[]{:S(2)}) %collective-permute-start.4) | collective-permute-done | bytes 65568 | tf_op jit(solution)/shard_map/ppermute | solution.py:241
  19.8 3.2 %attend.1 = (bf16[192,128]{1,0:T(8,128)(2,1)S(1)}, bf16[192,128]{1,0:T(8,128)(2,1)S(1)}, bf16[192,128]{1,0:T(8,128)(2,1)S(1)}, bf16[192,128]{1,0:T(8,128)(2,1)S(...) custom-call(s32[50]{0:T(128)S(1)} %pad_add_fusion.ints_ref, ...), custom_call_target="tpu_custom_call" | custom-call | tf_op jit(solution)/shard_map/attend/pallas_call | solution.py:285
  23.0 3.0 %collective-permute-start.7 = (bf16[192,128]{1,0:T(8,128)(2,1)S(1)}, bf16[192,128]{1,0:T(8,128)(2,1)S(1)}, u32[]{:S(2)}, u32[]{:S(2)}) collective-permute-start(bf16[192,128]{1,0:T(8,128)(2,1)S(1)} %get-tuple-element.28), channel_id=1, source_target_pairs={{0,6},{1,7},{2,4},{3,5},{4,2},{5,3},{6,0},{7,1},{8,14},{9,15},{10,... | collective-permute-start | bytes 147464 | tf_op jit(solution)/shard_map/ppermute | solution.py:241
  26.0 0.8 %collective-permute-start.8 = (bf16[192,128]{1,0:T(8,128)(2,1)S(1)}, bf16[192,128]{1,0:T(8,128)(2,1)S(1)}, u32[]{:S(2)}, u32[]{:S(2)}) collective-permute-start(bf16[192,128]{1,0:T(8,128)(2,1)S(1)} %get-tuple-element.29), channel_id=1, source_target_pairs={{0,5},{1,4},{2,7},{3,6},{4,1},{5,0},{6,3},{7,2},{8,13},{9,12},{10,... | collective-permute-start | bytes 147464 | tf_op jit(solution)/shard_map/ppermute | solution.py:241
  26.8 2.8 %collective-permute-start.9 = (bf16[192,128]{1,0:T(8,128)(2,1)S(1)}, bf16[192,128]{1,0:T(8,128)(2,1)S(1)}, u32[]{:S(2)}, u32[]{:S(2)}) collective-permute-start(bf16[192,128]{1,0:T(8,128)(2,1)S(1)} %get-tuple-element.30), channel_id=1, source_target_pairs={{0,7},{1,6},{2,5},{3,4},{4,3},{5,2},{6,1},{7,0},{8,15},{9,14},{10,... | collective-permute-start | bytes 147464 | tf_op jit(solution)/shard_map/ppermute | solution.py:241
  29.6 0.7 %collective-permute-start.10 = (bf16[192,128]{1,0:T(8,128)(2,1)S(1)}, bf16[192,128]{1,0:T(8,128)(2,1)S(1)}, u32[]{:S(2)}, u32[]{:S(2)}) collective-permute-start(bf16[192,128]{1,0:T(8,128)(2,1)S(1)} %get-tuple-element.31), channel_id=1, source_target_pairs={{0,3},{1,2},{2,1},{3,0},{4,7},{5,6},{6,5},{7,4},{8,11},{9,10},{10,... | collective-permute-start | bytes 147464 | tf_op jit(solution)/shard_map/ppermute | solution.py:241
  30.4 1.7 %collective-permute-start.11 = (bf16[192,128]{1,0:T(8,128)(2,1)S(1)}, bf16[192,128]{1,0:T(8,128)(2,1)S(1)}, u32[]{:S(2)}, u32[]{:S(2)}) collective-permute-start(bf16[192,128]{1,0:T(8,128)(2,1)S(1)} %get-tuple-element.32), channel_id=1, source_target_pairs={{0,4},{1,5},{2,6},{3,7},{4,0},{5,1},{6,2},{7,3},{8,12},{9,13},{10,... | collective-permute-start | bytes 147464 | tf_op jit(solution)/shard_map/ppermute | solution.py:241
  32.1 0.5 %collective-permute-start.12 = (bf16[192,128]{1,0:T(8,128)(2,1)S(1)}, bf16[192,128]{1,0:T(8,128)(2,1)S(1)}, u32[]{:S(2)}, u32[]{:S(2)}) collective-permute-start(bf16[192,128]{1,0:T(8,128)(2,1)S(1)} %get-tuple-element.33), channel_id=1, source_target_pairs={{0,2},{1,3},{2,0},{3,1},{4,6},{5,7},{6,4},{7,5},{8,10},{9,11},{10,... | collective-permute-start | bytes 147464 | tf_op jit(solution)/shard_map/ppermute | solution.py:241
  32.6 0.7 %collective-permute-start.13 = (bf16[192,128]{1,0:T(8,128)(2,1)S(1)}, bf16[192,128]{1,0:T(8,128)(2,1)S(1)}, u32[]{:S(2)}, u32[]{:S(2)}) collective-permute-start(bf16[192,128]{1,0:T(8,128)(2,1)S(1)} %get-tuple-element.34), channel_id=1, source_target_pairs={{0,1},{1,0},{2,3},{3,2},{4,5},{5,4},{6,7},{7,6},{8,9},{9,8},{10,11... | collective-permute-start | bytes 147464 | tf_op jit(solution)/shard_map/ppermute | solution.py:241
  33.3 0.4 %collective-permute-done.9.refs_3_ = bf16[192,128]{1,0:T(8,128)(2,1)S(1)} collective-permute-done((bf16[192,128]{1,0:T(8,128)(2,1)S(1)}, bf16[192,128]{1,0:T(8,128)(2,1)S(1)}, u32[]{:S(2)}, u32[]{:S(2)}) %collective-permute-start.9) | collective-permute-done | bytes 49184 | tf_op jit(solution)/shard_map/ppermute | solution.py:241
  33.7 1.2 %collective-permute-done.10.refs_4_ = bf16[192,128]{1,0:T(8,128)(2,1)S(1)} collective-permute-done((bf16[192,128]{1,0:T(8,128)(2,1)S(1)}, bf16[192,128]{1,0:T(8,128)(2,1)S(1)}, u32[]{:S(2)}, u32[]{:S(2)}) %collective-permute-start.10) | collective-permute-done | bytes 49184 | tf_op jit(solution)/shard_map/ppermute | solution.py:241
  34.9 0.5 %collective-permute-done.11.refs_5_ = bf16[192,128]{1,0:T(8,128)(2,1)S(1)} collective-permute-done((bf16[192,128]{1,0:T(8,128)(2,1)S(1)}, bf16[192,128]{1,0:T(8,128)(2,1)S(1)}, u32[]{:S(2)}, u32[]{:S(2)}) %collective-permute-start.11) | collective-permute-done | bytes 49184 | tf_op jit(solution)/shard_map/ppermute | solution.py:241
  35.4 0.8 %collective-permute-done.12.refs_6_ = bf16[192,128]{1,0:T(8,128)(2,1)S(1)} collective-permute-done((bf16[192,128]{1,0:T(8,128)(2,1)S(1)}, bf16[192,128]{1,0:T(8,128)(2,1)S(1)}, u32[]{:S(2)}, u32[]{:S(2)}) %collective-permute-start.12) | collective-permute-done | bytes 49184 | tf_op jit(solution)/shard_map/ppermute | solution.py:241
  36.2 0.5 %collective-permute-done.13.refs_7_ = bf16[192,128]{1,0:T(8,128)(2,1)S(1)} collective-permute-done((bf16[192,128]{1,0:T(8,128)(2,1)S(1)}, bf16[192,128]{1,0:T(8,128)(2,1)S(1)}, u32[]{:S(2)}, u32[]{:S(2)}) %collective-permute-start.13) | collective-permute-done | bytes 49184 | tf_op jit(solution)/shard_map/ppermute | solution.py:241
  36.7 0.9 %unpack.1 = (bf16[128,512]{1,0:T(8,128)(2,1)}, bf16[128,512]{1,0:T(8,128)(2,1)}, bf16[128,512]{1,0:T(8,128)(2,1)}) custom-call(bf16[192,128]{1,0:T(8,128)(2,1)S(1)} %get-tuple-element.27.refs_0_, bf16[192,128]{1,0:T(8,128)(2,1)S(1)} %collective-permute-done.7.refs_1_, bf16[192,128]{1,0:T(8,128)(2,1)S(1)} %collective-permute-done.8.refs_2_, ...), custom_call_target="tpu_custom_call" | custom-call | tf_op jit(solution)/shard_map/unpack/pallas_call | solution.py:305
  (14 shorter events, 0.6 us)
Async XLA Ops:
  2.0 10.9 %collective-permute-start = (bf16[2,128,128]{2,1,0:T(8,128)(2,1)S(1)}, bf16[2,128,128]{2,1,0:T(8,128)(2,1)S(1)}, u32[]{:S(2)}, u32[]{:S(2)}) collective-permute-start(bf16[2,128,128]{2,1,0:T(8,128)(2,1)S(1)} %get-tuple-element.20), channel_id=1, source_target_pairs={{0,4},{1,5},{2,6},{3,7},{4,0},{5,1},{6,2},{7,3},{8,12},{9,13},{10,... | collective-permute-start | bytes 196616 | tf_op jit(solution)/shard_map/ppermute | solution.py:241
  6.1 8.1 %collective-permute-start.1 = (bf16[2,128,128]{2,1,0:T(8,128)(2,1)S(1)}, bf16[2,128,128]{2,1,0:T(8,128)(2,1)S(1)}, u32[]{:S(2)}, u32[]{:S(2)}) collective-permute-start(bf16[2,128,128]{2,1,0:T(8,128)(2,1)S(1)} %get-tuple-element.21), channel_id=1, source_target_pairs={{0,6},{1,7},{2,4},{3,5},{4,2},{5,3},{6,0},{7,1},{8,14},{9,15},{10,... | collective-permute-start | bytes 196616 | tf_op jit(solution)/shard_map/ppermute | solution.py:241
  7.4 5.3 %copy-start = (s32[16,3]{0,1:T(4,128)S(1)}, s32[16,3]{0,1:T(4,128)}, u32[]{:S(2)}) copy-start(s32[16,3]{0,1:T(4,128)} %param.10) | copy-start | bytes 580
  7.4 7.3 %collective-permute-start.2 = (bf16[2,128,128]{2,1,0:T(8,128)(2,1)S(1)}, bf16[2,128,128]{2,1,0:T(8,128)(2,1)S(1)}, u32[]{:S(2)}, u32[]{:S(2)}) collective-permute-start(bf16[2,128,128]{2,1,0:T(8,128)(2,1)S(1)} %get-tuple-element.22), channel_id=1, source_target_pairs={{0,3},{1,2},{2,1},{3,0},{4,7},{5,6},{6,5},{7,4},{8,11},{9,10},{10,... | collective-permute-start | bytes 196616 | tf_op jit(solution)/shard_map/ppermute | solution.py:241
  8.6 7.4 %collective-permute-start.3 = (bf16[2,128,128]{2,1,0:T(8,128)(2,1)S(1)}, bf16[2,128,128]{2,1,0:T(8,128)(2,1)S(1)}, u32[]{:S(2)}, u32[]{:S(2)}) collective-permute-start(bf16[2,128,128]{2,1,0:T(8,128)(2,1)S(1)} %get-tuple-element.23), channel_id=1, source_target_pairs={{0,7},{1,6},{2,5},{3,4},{4,3},{5,2},{6,1},{7,0},{8,15},{9,14},{10,... | collective-permute-start | bytes 196616 | tf_op jit(solution)/shard_map/ppermute | solution.py:241
  11.5 8.0 %collective-permute-start.4 = (bf16[2,128,128]{2,1,0:T(8,128)(2,1)S(1)}, bf16[2,128,128]{2,1,0:T(8,128)(2,1)S(1)}, u32[]{:S(2)}, u32[]{:S(2)}) collective-permute-start(bf16[2,128,128]{2,1,0:T(8,128)(2,1)S(1)} %get-tuple-element.24), channel_id=1, source_target_pairs={{0,5},{1,4},{2,7},{3,6},{4,1},{5,0},{6,3},{7,2},{8,13},{9,12},{10,... | collective-permute-start | bytes 196616 | tf_op jit(solution)/shard_map/ppermute | solution.py:241
  12.9 1.7 %copy-start.1 = (s32[2]{0:T(128)S(1)}, s32[2]{0:T(128)}, u32[]{:S(2)}) copy-start(s32[2]{0:T(128)} %param.11) | copy-start | bytes 28
  13.0 6.5 %collective-permute-start.5 = (bf16[2,128,128]{2,1,0:T(8,128)(2,1)S(1)}, bf16[2,128,128]{2,1,0:T(8,128)(2,1)S(1)}, u32[]{:S(2)}, u32[]{:S(2)}) collective-permute-start(bf16[2,128,128]{2,1,0:T(8,128)(2,1)S(1)} %get-tuple-element.25), channel_id=1, source_target_pairs={{0,2},{1,3},{2,0},{3,1},{4,6},{5,7},{6,4},{7,5},{8,10},{9,11},{10,... | collective-permute-start | bytes 196616 | tf_op jit(solution)/shard_map/ppermute | solution.py:241
  14.2 5.7 %collective-permute-start.6 = (bf16[2,128,128]{2,1,0:T(8,128)(2,1)S(1)}, bf16[2,128,128]{2,1,0:T(8,128)(2,1)S(1)}, u32[]{:S(2)}, u32[]{:S(2)}) collective-permute-start(bf16[2,128,128]{2,1,0:T(8,128)(2,1)S(1)} %get-tuple-element.26), channel_id=1, source_target_pairs={{0,1},{1,0},{2,3},{3,2},{4,5},{5,4},{6,7},{7,6},{8,9},{9,8},{10,11... | collective-permute-start | bytes 196616 | tf_op jit(solution)/shard_map/ppermute | solution.py:241
  23.0 9.1 %collective-permute-start.7 = (bf16[192,128]{1,0:T(8,128)(2,1)S(1)}, bf16[192,128]{1,0:T(8,128)(2,1)S(1)}, u32[]{:S(2)}, u32[]{:S(2)}) collective-permute-start(bf16[192,128]{1,0:T(8,128)(2,1)S(1)} %get-tuple-element.28), channel_id=1, source_target_pairs={{0,6},{1,7},{2,4},{3,5},{4,2},{5,3},{6,0},{7,1},{8,14},{9,15},{10,... | collective-permute-start | bytes 147464 | tf_op jit(solution)/shard_map/ppermute | solution.py:241
  26.0 6.6 %collective-permute-start.8 = (bf16[192,128]{1,0:T(8,128)(2,1)S(1)}, bf16[192,128]{1,0:T(8,128)(2,1)S(1)}, u32[]{:S(2)}, u32[]{:S(2)}) collective-permute-start(bf16[192,128]{1,0:T(8,128)(2,1)S(1)} %get-tuple-element.29), channel_id=1, source_target_pairs={{0,5},{1,4},{2,7},{3,6},{4,1},{5,0},{6,3},{7,2},{8,13},{9,12},{10,... | collective-permute-start | bytes 147464 | tf_op jit(solution)/shard_map/ppermute | solution.py:241
  26.8 6.9 %collective-permute-start.9 = (bf16[192,128]{1,0:T(8,128)(2,1)S(1)}, bf16[192,128]{1,0:T(8,128)(2,1)S(1)}, u32[]{:S(2)}, u32[]{:S(2)}) collective-permute-start(bf16[192,128]{1,0:T(8,128)(2,1)S(1)} %get-tuple-element.30), channel_id=1, source_target_pairs={{0,7},{1,6},{2,5},{3,4},{4,3},{5,2},{6,1},{7,0},{8,15},{9,14},{10,... | collective-permute-start | bytes 147464 | tf_op jit(solution)/shard_map/ppermute | solution.py:241
  29.6 5.2 %collective-permute-start.10 = (bf16[192,128]{1,0:T(8,128)(2,1)S(1)}, bf16[192,128]{1,0:T(8,128)(2,1)S(1)}, u32[]{:S(2)}, u32[]{:S(2)}) collective-permute-start(bf16[192,128]{1,0:T(8,128)(2,1)S(1)} %get-tuple-element.31), channel_id=1, source_target_pairs={{0,3},{1,2},{2,1},{3,0},{4,7},{5,6},{6,5},{7,4},{8,11},{9,10},{10,... | collective-permute-start | bytes 147464 | tf_op jit(solution)/shard_map/ppermute | solution.py:241
  30.4 5.0 %collective-permute-start.11 = (bf16[192,128]{1,0:T(8,128)(2,1)S(1)}, bf16[192,128]{1,0:T(8,128)(2,1)S(1)}, u32[]{:S(2)}, u32[]{:S(2)}) collective-permute-start(bf16[192,128]{1,0:T(8,128)(2,1)S(1)} %get-tuple-element.32), channel_id=1, source_target_pairs={{0,4},{1,5},{2,6},{3,7},{4,0},{5,1},{6,2},{7,3},{8,12},{9,13},{10,... | collective-permute-start | bytes 147464 | tf_op jit(solution)/shard_map/ppermute | solution.py:241
  32.1 4.1 %collective-permute-start.12 = (bf16[192,128]{1,0:T(8,128)(2,1)S(1)}, bf16[192,128]{1,0:T(8,128)(2,1)S(1)}, u32[]{:S(2)}, u32[]{:S(2)}) collective-permute-start(bf16[192,128]{1,0:T(8,128)(2,1)S(1)} %get-tuple-element.33), channel_id=1, source_target_pairs={{0,2},{1,3},{2,0},{3,1},{4,6},{5,7},{6,4},{7,5},{8,10},{9,11},{10,... | collective-permute-start | bytes 147464 | tf_op jit(solution)/shard_map/ppermute | solution.py:241
  32.6 4.1 %collective-permute-start.13 = (bf16[192,128]{1,0:T(8,128)(2,1)S(1)}, bf16[192,128]{1,0:T(8,128)(2,1)S(1)}, u32[]{:S(2)}, u32[]{:S(2)}) collective-permute-start(bf16[192,128]{1,0:T(8,128)(2,1)S(1)} %get-tuple-element.34), channel_id=1, source_target_pairs={{0,1},{1,0},{2,3},{3,2},{4,5},{5,4},{6,7},{7,6},{8,9},{9,8},{10,11... | collective-permute-start | bytes 147464 | tf_op jit(solution)/shard_map/ppermute | solution.py:241

commit v14 on v11

--- a/solution.py
+++ b/solution.py
@@ -16,7 +16,6 @@
 LANES = 2 * HEAD
 PARTNERS_IN = (0, 4, 6, 3, 7, 5, 2, 1)
 PARTNERS_BACK = (0, 6, 5, 7, 3, 4, 2, 1)
-NEAR = (2, 3, 1, 0)
 PACK_GRANT = 427 * 2**17
 MASKED = -1e30
 
@@ -27,28 +26,28 @@
 
 def swap_halves(block):
     return pltpu.roll(block, HEAD, 1)
+
+
+def folded(reduce, rows):
+    return reduce(reduce(rows.reshape(-1, BLOCK, rows.shape[1]), axis=0), axis=0, keepdims=True)
 
 
 def pack_kernel(*refs):
     in_refs, out_refs = refs[:4], refs[4 : 4 + HEADS]
     held_ref, in_sems = refs[4 + HEADS :]
-    rows = held_ref.shape[2]
+    copies = [pltpu.make_async_copy(in_refs[i], held_ref.at[i], in_sems.at[i]) for i in range(4)]
+    for copy in copies:
+        copy.start()
+    rows = held_ref.shape[1]
     low = low_lanes((rows, LANES))
     place = lax.rem(lax.axis_index("seq"), HEADS)
     odd_place = lax.rem(place, 2) == 1
-    arriving = {}
-    for near in NEAR:
+    for copy in copies:
+        copy.wait()
+    for near in range(HEADS // 2):
         pair = lax.bitwise_xor(place // 2, near)
         lanes = pl.ds(pl.multiple_of(pair * LANES, LANES), LANES)
-        for kind, ref in enumerate(in_refs):
-            arriving[near, kind] = pltpu.make_async_copy(
-                ref.at[:, lanes], held_ref.at[near, kind], in_sems.at[near, kind]
-            )
-            arriving[near, kind].start()
-    for near in NEAR:
-        for kind in range(4):
-            arriving[near, kind].wait()
-        q, k, v, g = [held_ref[near, kind].astype(jnp.float32) for kind in range(4)]
+        q, k, v, g = [held_ref[i, :, lanes].astype(jnp.float32) for i in range(4)]
         for kind, (first, second) in enumerate(((k, v), (q, g))):
             even = jnp.where(low, first, swap_halves(second))
             odd = jnp.where(low, swap_halves(first), second)
@@ -60,27 +59,34 @@
 
 def unpack_kernel(*refs):
     in_refs = dict(zip(PARTNERS_BACK, refs[:HEADS]))
-    gq_ref, gk_ref, gv_ref = refs[HEADS:]
-    rows = gq_ref.shape[0]
+    out_refs, held_ref, sems = refs[HEADS : HEADS + 3], refs[-2], refs[-1]
+    rows = held_ref.shape[1]
     low = low_lanes((rows, LANES))
     low_block = low_lanes((BLOCK, LANES))
     place = lax.rem(lax.axis_index("seq"), HEADS)
     odd_place = lax.rem(place, 2) == 1
-    for near in range(HEADS // 2):
-        pair = lax.bitwise_xor(place // 2, near)
-        lanes = pl.ds(pl.multiple_of(pair * LANES, LANES), LANES)
-        same = in_refs[2 * near][...].astype(jnp.float32)
-        other = in_refs[2 * near + 1][...].astype(jnp.float32)
-        even = jnp.where(odd_place, other, same)
-        odd = jnp.where(odd_place, same, other)
-        gk = jnp.where(low, even[:rows], swap_halves(odd[:rows]))
-        gv = jnp.where(low, swap_halves(even[:rows]), odd[:rows])
-        gk_ref[:, lanes] = gk.astype(jnp.bfloat16)
-        gv_ref[:, lanes] = gv.astype(jnp.bfloat16)
-        first = jnp.where(low_block, even[rows:], swap_halves(odd[rows:]))
-        second = jnp.where(low_block, swap_halves(even[rows:]), odd[rows:])
-        gq_ref[:BLOCK, lanes] = first.astype(jnp.bfloat16)
-        gq_ref[BLOCK:, lanes] = second.astype(jnp.bfloat16)
+    copies = [pltpu.make_async_copy(held_ref.at[i], out_refs[i], sems.at[i]) for i in range(3)]
+    for kind in (1, 2, 0):
+        for near in range(HEADS // 2):
+            pair = lax.bitwise_xor(place // 2, near)
+            lanes = pl.ds(pl.multiple_of(pair * LANES, LANES), LANES)
+            part = slice(rows, rows + BLOCK) if kind == 0 else slice(0, rows)
+            same = in_refs[2 * near][part].astype(jnp.float32)
+            other = in_refs[2 * near + 1][part].astype(jnp.float32)
+            even = jnp.where(odd_place, other, same)
+            odd = jnp.where(odd_place, same, other)
+            if kind == 1:
+                whole = jnp.where(low, even, swap_halves(odd))
+            elif kind == 2:
+                whole = jnp.where(low, swap_halves(even), odd)
+            else:
+                first = jnp.where(low_block, even, swap_halves(odd))
+                second = jnp.where(low_block, swap_halves(even), odd)
+                whole = jnp.concatenate([first, second], axis=0)
+            held_ref[kind, :, lanes] = whole.astype(jnp.bfloat16)
+        copies[kind].start()
+    for copy in copies:
+        copy.wait()
 
 
 def attend_kernel(alone, scale, ints_ref, *rest):
@@ -169,12 +175,12 @@
                     keep = jnp.logical_or(keep, table_ref[fixed + GLOBAL] < last)
             masked = jnp.where(keep, scores[edge : edge + BLOCK], MASKED)
             scores = jnp.concatenate([scores[:edge], masked, scores[edge + BLOCK :]], axis=0)
-        row_max = jnp.max(scores, axis=0, keepdims=True)
+        row_max = folded(jnp.max, scores)
         expo = jnp.exp(scores - row_max)
-        row_total = jnp.sum(expo, axis=0, keepdims=True)
+        row_total = folded(jnp.sum, expo)
         inverse = 1.0 / row_total
         probs_half = (expo * inverse).astype(jnp.bfloat16)
-        row_dot = jnp.sum(probs_half.astype(jnp.float32) * grad_probs, axis=0, keepdims=True)
+        row_dot = folded(jnp.sum, probs_half.astype(jnp.float32) * grad_probs)
         grad_half = (expo * ((grad_probs - row_dot) * inverse)).astype(jnp.bfloat16)
         return grad_half, probs_half
 
@@ -185,10 +191,10 @@
             grad_half, keys, (((0,), (0,)), ((), ())), preferred_element_type=jnp.float32
         )
         grad_query = grad_query * scale
-        folded = jnp.where(
+        grad_query = jnp.where(
             low, grad_query[:BLOCK, :LANES], swap_halves(grad_query[BLOCK:, LANES:])
-        ).astype(jnp.bfloat16)
-        gq_ref[tile] = folded
+        )
+        gq_ref[tile] = grad_query.astype(jnp.bfloat16)
         for place, (a, b) in enumerate(pairs):
             part = key_grads[place * BLOCK : (place + 1) * BLOCK]
             if place < 2 + GLOBAL:
@@ -254,8 +260,8 @@
         in_specs=[anywhere] * 4,
         out_specs=[vmem] * HEADS,
         scratch_shapes=[
-            pltpu.VMEM((HEADS // 2, 4, rows, LANES), half_type),
-            pltpu.SemaphoreType.DMA((HEADS // 2, 4)),
+            pltpu.VMEM((4, rows, width), half_type),
+            pltpu.SemaphoreType.DMA((4,)),
         ],
         compiler_params=pltpu.CompilerParams(vmem_limit_bytes=PACK_GRANT),
         name="pack",
@@ -286,7 +292,11 @@
         unpack_kernel,
         out_shape=[jax.ShapeDtypeStruct((rows, width), half_type)] * 3,
         in_specs=[vmem] * HEADS,
-        out_specs=[vmem] * 3,
+        out_specs=[anywhere] * 3,
+        scratch_shapes=[
+            pltpu.VMEM((3, rows, width), half_type),
+            pltpu.SemaphoreType.DMA((3,)),
+        ],
         compiler_params=pltpu.CompilerParams(vmem_limit_bytes=8 * 2**20),
         name="unpack",
     )(*[received[m] for m in PARTNERS_BACK])
@@ -320,7 +330,10 @@
         ],
         in_specs=[pl.BlockSpec(memory_space=pl.ANY), vmem, vmem],
         out_specs=[vmem] * 2,
-        scratch_shapes=[pltpu.SMEM(table.shape, jnp.int32), pltpu.SemaphoreType.DMA],
+        scratch_shapes=[
+            pltpu.SMEM(table.shape, jnp.int32),
+            pltpu.SemaphoreType.DMA,
+        ],
         compiler_params=pltpu.CompilerParams(vmem_limit_bytes=24 * 2**20),
         name="attend",
     )(table, sent, pool)

time: 37.8 us -> 37.7 us (level)
  no operation moved by 1% of the time
where the time goes in v14:
time: 37.7 us; the launch traced here: 37.5 us
  starting transfers between devices  22.8 us (60%)
  waiting for transfers between devices  8.43 us (22%)
  Pallas kernels  5.35 us (14%)
  between operations  0.68 us (2%)
    ppermute x14, starting transfers between devices, exchange(): arrived[m] = lax.ppermute(parts[m], 'seq', route)  22.8 us
    ppermute x14, waiting for transfers between devices, exchange(): arrived[m] = lax.ppermute(parts[m], 'seq', route)  8.43 us
    pallas_call x1, Pallas kernels, on_device(): pl.pallas_call(kernel, out_shape=[jax.ShapeDtypeStruct((rows + BLOCK, LAN...  3.1 us
    pallas_call x1, Pallas kernels, on_device(): pl.pallas_call(pack_kernel, out_shape=[jax.ShapeDtypeStruct((2, rows, LAN...  1.35 us
    pallas_call x1, Pallas kernels, on_device(): pl.pallas_call(unpack_kernel, out_shape=[jax.ShapeDtypeStruct((rows, widt...  0.9 us
  transfers between devices with their start and end apart: 14, of which 8 were waited for; matrix products, arithmetic and copies ran while one was open for 1% of the time, Pallas kernels for 0%

profile of v14, /device:TPU:0, one launch (start us, length us, event | category | flops | bytes accessed | tf_op | source)
XLA Modules:
  0.0 37.5 jit_solution(7888822854064363779)
XLA Ops:
  0.6 1.4 %pack.1 = (bf16[2,128,128]{2,1,0:T(8,128)(2,1)S(1)}, bf16[2,128,128]{2,1,0:T(8,128)(2,1)S(1)}, bf16[2,128,128]{2,1,0:T(8,128)(2,1)S(1)}, bf16[2,128,128]{2,1,0:T...) custom-call(bf16[128,512]{1,0:T(8,128)(2,1)} %refs_0_.1, ...), custom_call_target="tpu_custom_call" | custom-call | tf_op jit(solution)/shard_map/pack/pallas_call | solution.py:257
  2.0 4.1 %collective-permute-start = (bf16[2,128,128]{2,1,0:T(8,128)(2,1)S(1)}, bf16[2,128,128]{2,1,0:T(8,128)(2,1)S(1)}, u32[]{:S(2)}, u32[]{:S(2)}) collective-permute-start(bf16[2,128,128]{2,1,0:T(8,128)(2,1)S(1)} %get-tuple-element.20), channel_id=1, source_target_pairs={{0,4},{1,5},{2,6},{3,7},{4,0},{5,1},{6,2},{7,3},{8,12},{9,13},{10,... | collective-permute-start | bytes 196616 | tf_op jit(solution)/shard_map/ppermute | solution.py:229
  6.1 1.4 %collective-permute-start.1 = (bf16[2,128,128]{2,1,0:T(8,128)(2,1)S(1)}, bf16[2,128,128]{2,1,0:T(8,128)(2,1)S(1)}, u32[]{:S(2)}, u32[]{:S(2)}) collective-permute-start(bf16[2,128,128]{2,1,0:T(8,128)(2,1)S(1)} %get-tuple-element.21), channel_id=1, source_target_pairs={{0,6},{1,7},{2,4},{3,5},{4,2},{5,3},{6,0},{7,1},{8,14},{9,15},{10,... | collective-permute-start | bytes 196616 | tf_op jit(solution)/shard_map/ppermute | solution.py:229
  7.4 1.2 %collective-permute-start.2 = (bf16[2,128,128]{2,1,0:T(8,128)(2,1)S(1)}, bf16[2,128,128]{2,1,0:T(8,128)(2,1)S(1)}, u32[]{:S(2)}, u32[]{:S(2)}) collective-permute-start(bf16[2,128,128]{2,1,0:T(8,128)(2,1)S(1)} %get-tuple-element.22), channel_id=1, source_target_pairs={{0,3},{1,2},{2,1},{3,0},{4,7},{5,6},{6,5},{7,4},{8,11},{9,10},{10,... | collective-permute-start | bytes 196616 | tf_op jit(solution)/shard_map/ppermute | solution.py:229
  8.6 2.9 %collective-permute-start.3 = (bf16[2,128,128]{2,1,0:T(8,128)(2,1)S(1)}, bf16[2,128,128]{2,1,0:T(8,128)(2,1)S(1)}, u32[]{:S(2)}, u32[]{:S(2)}) collective-permute-start(bf16[2,128,128]{2,1,0:T(8,128)(2,1)S(1)} %get-tuple-element.23), channel_id=1, source_target_pairs={{0,7},{1,6},{2,5},{3,4},{4,3},{5,2},{6,1},{7,0},{8,15},{9,14},{10,... | collective-permute-start | bytes 196616 | tf_op jit(solution)/shard_map/ppermute | solution.py:229
  11.5 1.3 %collective-permute-start.4 = (bf16[2,128,128]{2,1,0:T(8,128)(2,1)S(1)}, bf16[2,128,128]{2,1,0:T(8,128)(2,1)S(1)}, u32[]{:S(2)}, u32[]{:S(2)}) collective-permute-start(bf16[2,128,128]{2,1,0:T(8,128)(2,1)S(1)} %get-tuple-element.24), channel_id=1, source_target_pairs={{0,5},{1,4},{2,7},{3,6},{4,1},{5,0},{6,3},{7,2},{8,13},{9,12},{10,... | collective-permute-start | bytes 196616 | tf_op jit(solution)/shard_map/ppermute | solution.py:229
  13.0 1.2 %collective-permute-start.5 = (bf16[2,128,128]{2,1,0:T(8,128)(2,1)S(1)}, bf16[2,128,128]{2,1,0:T(8,128)(2,1)S(1)}, u32[]{:S(2)}, u32[]{:S(2)}) collective-permute-start(bf16[2,128,128]{2,1,0:T(8,128)(2,1)S(1)} %get-tuple-element.25), channel_id=1, source_target_pairs={{0,2},{1,3},{2,0},{3,1},{4,6},{5,7},{6,4},{7,5},{8,10},{9,11},{10,... | collective-permute-start | bytes 196616 | tf_op jit(solution)/shard_map/ppermute | solution.py:229
  14.2 0.5 %collective-permute-start.6 = (bf16[2,128,128]{2,1,0:T(8,128)(2,1)S(1)}, bf16[2,128,128]{2,1,0:T(8,128)(2,1)S(1)}, u32[]{:S(2)}, u32[]{:S(2)}) collective-permute-start(bf16[2,128,128]{2,1,0:T(8,128)(2,1)S(1)} %get-tuple-element.26), channel_id=1, source_target_pairs={{0,1},{1,0},{2,3},{3,2},{4,5},{5,4},{6,7},{7,6},{8,9},{9,8},{10,11... | collective-permute-start | bytes 196616 | tf_op jit(solution)/shard_map/ppermute | solution.py:229
  14.8 1.2 %collective-permute-done.3 = bf16[2,128,128]{2,1,0:T(8,128)(2,1)S(1)} collective-permute-done((bf16[2,128,128]{2,1,0:T(8,128)(2,1)S(1)}, bf16[2,128,128]{2,1,0:T(8,128)(2,1)S(1)}, u32[]{:S(2)}, u32[]{:S(2)}) %collective-permute-start.3) | collective-permute-done | bytes 65568 | tf_op jit(solution)/shard_map/ppermute | solution.py:229
  16.0 3.5 %collective-permute-done.4 = bf16[2,128,128]{2,1,0:T(8,128)(2,1)S(1)} collective-permute-done((bf16[2,128,128]{2,1,0:T(8,128)(2,1)S(1)}, bf16[2,128,128]{2,1,0:T(8,128)(2,1)S(1)}, u32[]{:S(2)}, u32[]{:S(2)}) %collective-permute-start.4) | collective-permute-done | bytes 65568 | tf_op jit(solution)/shard_map/ppermute | solution.py:229
  19.8 3.1 %attend.1 = (bf16[192,128]{1,0:T(8,128)(2,1)S(1)}, bf16[192,128]{1,0:T(8,128)(2,1)S(1)}, bf16[192,128]{1,0:T(8,128)(2,1)S(1)}, bf16[192,128]{1,0:T(8,128)(2,1)S(...) custom-call(s32[50]{0:T(128)S(1)} %pad_add_fusion.ints_ref, ...), custom_call_target="tpu_custom_call" | custom-call | tf_op jit(solution)/shard_map/attend/pallas_call | solution.py:273
  22.9 3.0 %collective-permute-start.7 = (bf16[192,128]{1,0:T(8,128)(2,1)S(1)}, bf16[192,128]{1,0:T(8,128)(2,1)S(1)}, u32[]{:S(2)}, u32[]{:S(2)}) collective-permute-start(bf16[192,128]{1,0:T(8,128)(2,1)S(1)} %get-tuple-element.28), channel_id=1, source_target_pairs={{0,6},{1,7},{2,4},{3,5},{4,2},{5,3},{6,0},{7,1},{8,14},{9,15},{10,... | collective-permute-start | bytes 147464 | tf_op jit(solution)/shard_map/ppermute | solution.py:229
  25.9 0.8 %collective-permute-start.8 = (bf16[192,128]{1,0:T(8,128)(2,1)S(1)}, bf16[192,128]{1,0:T(8,128)(2,1)S(1)}, u32[]{:S(2)}, u32[]{:S(2)}) collective-permute-start(bf16[192,128]{1,0:T(8,128)(2,1)S(1)} %get-tuple-element.29), channel_id=1, source_target_pairs={{0,5},{1,4},{2,7},{3,6},{4,1},{5,0},{6,3},{7,2},{8,13},{9,12},{10,... | collective-permute-start | bytes 147464 | tf_op jit(solution)/shard_map/ppermute | solution.py:229
  26.7 2.8 %collective-permute-start.9 = (bf16[192,128]{1,0:T(8,128)(2,1)S(1)}, bf16[192,128]{1,0:T(8,128)(2,1)S(1)}, u32[]{:S(2)}, u32[]{:S(2)}) collective-permute-start(bf16[192,128]{1,0:T(8,128)(2,1)S(1)} %get-tuple-element.30), channel_id=1, source_target_pairs={{0,7},{1,6},{2,5},{3,4},{4,3},{5,2},{6,1},{7,0},{8,15},{9,14},{10,... | collective-permute-start | bytes 147464 | tf_op jit(solution)/shard_map/ppermute | solution.py:229
  29.5 0.7 %collective-permute-start.10 = (bf16[192,128]{1,0:T(8,128)(2,1)S(1)}, bf16[192,128]{1,0:T(8,128)(2,1)S(1)}, u32[]{:S(2)}, u32[]{:S(2)}) collective-permute-start(bf16[192,128]{1,0:T(8,128)(2,1)S(1)} %get-tuple-element.31), channel_id=1, source_target_pairs={{0,3},{1,2},{2,1},{3,0},{4,7},{5,6},{6,5},{7,4},{8,11},{9,10},{10,... | collective-permute-start | bytes 147464 | tf_op jit(solution)/shard_map/ppermute | solution.py:229
  30.3 1.7 %collective-permute-start.11 = (bf16[192,128]{1,0:T(8,128)(2,1)S(1)}, bf16[192,128]{1,0:T(8,128)(2,1)S(1)}, u32[]{:S(2)}, u32[]{:S(2)}) collective-permute-start(bf16[192,128]{1,0:T(8,128)(2,1)S(1)} %get-tuple-element.32), channel_id=1, source_target_pairs={{0,4},{1,5},{2,6},{3,7},{4,0},{5,1},{6,2},{7,3},{8,12},{9,13},{10,... | collective-permute-start | bytes 147464 | tf_op jit(solution)/shard_map/ppermute | solution.py:229
  32.0 0.5 %collective-permute-start.12 = (bf16[192,128]{1,0:T(8,128)(2,1)S(1)}, bf16[192,128]{1,0:T(8,128)(2,1)S(1)}, u32[]{:S(2)}, u32[]{:S(2)}) collective-permute-start(bf16[192,128]{1,0:T(8,128)(2,1)S(1)} %get-tuple-element.33), channel_id=1, source_target_pairs={{0,2},{1,3},{2,0},{3,1},{4,6},{5,7},{6,4},{7,5},{8,10},{9,11},{10,... | collective-permute-start | bytes 147464 | tf_op jit(solution)/shard_map/ppermute | solution.py:229
  32.5 0.7 %collective-permute-start.13 = (bf16[192,128]{1,0:T(8,128)(2,1)S(1)}, bf16[192,128]{1,0:T(8,128)(2,1)S(1)}, u32[]{:S(2)}, u32[]{:S(2)}) collective-permute-start(bf16[192,128]{1,0:T(8,128)(2,1)S(1)} %get-tuple-element.34), channel_id=1, source_target_pairs={{0,1},{1,0},{2,3},{3,2},{4,5},{5,4},{6,7},{7,6},{8,9},{9,8},{10,11... | collective-permute-start | bytes 147464 | tf_op jit(solution)/shard_map/ppermute | solution.py:229
  33.2 0.4 %collective-permute-done.9.refs_3_ = bf16[192,128]{1,0:T(8,128)(2,1)S(1)} collective-permute-done((bf16[192,128]{1,0:T(8,128)(2,1)S(1)}, bf16[192,128]{1,0:T(8,128)(2,1)S(1)}, u32[]{:S(2)}, u32[]{:S(2)}) %collective-permute-start.9) | collective-permute-done | bytes 49184 | tf_op jit(solution)/shard_map/ppermute | solution.py:229
  33.6 1.2 %collective-permute-done.10.refs_4_ = bf16[192,128]{1,0:T(8,128)(2,1)S(1)} collective-permute-done((bf16[192,128]{1,0:T(8,128)(2,1)S(1)}, bf16[192,128]{1,0:T(8,128)(2,1)S(1)}, u32[]{:S(2)}, u32[]{:S(2)}) %collective-permute-start.10) | collective-permute-done | bytes 49184 | tf_op jit(solution)/shard_map/ppermute | solution.py:229
  34.8 0.5 %collective-permute-done.11.refs_5_ = bf16[192,128]{1,0:T(8,128)(2,1)S(1)} collective-permute-done((bf16[192,128]{1,0:T(8,128)(2,1)S(1)}, bf16[192,128]{1,0:T(8,128)(2,1)S(1)}, u32[]{:S(2)}, u32[]{:S(2)}) %collective-permute-start.11) | collective-permute-done | bytes 49184 | tf_op jit(solution)/shard_map/ppermute | solution.py:229
  35.3 0.8 %collective-permute-done.12.refs_6_ = bf16[192,128]{1,0:T(8,128)(2,1)S(1)} collective-permute-done((bf16[192,128]{1,0:T(8,128)(2,1)S(1)}, bf16[192,128]{1,0:T(8,128)(2,1)S(1)}, u32[]{:S(2)}, u32[]{:S(2)}) %collective-permute-start.12) | collective-permute-done | bytes 49184 | tf_op jit(solution)/shard_map/ppermute | solution.py:229
  36.1 0.5 %collective-permute-done.13.refs_7_ = bf16[192,128]{1,0:T(8,128)(2,1)S(1)} collective-permute-done((bf16[192,128]{1,0:T(8,128)(2,1)S(1)}, bf16[192,128]{1,0:T(8,128)(2,1)S(1)}, u32[]{:S(2)}, u32[]{:S(2)}) %collective-permute-start.13) | collective-permute-done | bytes 49184 | tf_op jit(solution)/shard_map/ppermute | solution.py:229
  36.6 0.9 %unpack.1 = (bf16[128,512]{1,0:T(8,128)(2,1)}, bf16[128,512]{1,0:T(8,128)(2,1)}, bf16[128,512]{1,0:T(8,128)(2,1)}) custom-call(bf16[192,128]{1,0:T(8,128)(2,1)S(1)} %get-tuple-element.27.refs_0_, bf16[192,128]{1,0:T(8,128)(2,1)S(1)} %collective-permute-done.7.refs_1_, bf16[192,128]{1,0:T(8,128)(2,1)S(1)} %collective-permute-done.8.refs_2_, ...), custom_call_target="tpu_custom_call" | custom-call | tf_op jit(solution)/shard_map/unpack/pallas_call | solution.py:291
  (14 shorter events, 0.6 us)
Async XLA Ops:
  2.0 10.9 %collective-permute-start = (bf16[2,128,128]{2,1,0:T(8,128)(2,1)S(1)}, bf16[2,128,128]{2,1,0:T(8,128)(2,1)S(1)}, u32[]{:S(2)}, u32[]{:S(2)}) collective-permute-start(bf16[2,128,128]{2,1,0:T(8,128)(2,1)S(1)} %get-tuple-element.20), channel_id=1, source_target_pairs={{0,4},{1,5},{2,6},{3,7},{4,0},{5,1},{6,2},{7,3},{8,12},{9,13},{10,... | collective-permute-start | bytes 196616 | tf_op jit(solution)/shard_map/ppermute | solution.py:229
  6.1 8.1 %collective-permute-start.1 = (bf16[2,128,128]{2,1,0:T(8,128)(2,1)S(1)}, bf16[2,128,128]{2,1,0:T(8,128)(2,1)S(1)}, u32[]{:S(2)}, u32[]{:S(2)}) collective-permute-start(bf16[2,128,128]{2,1,0:T(8,128)(2,1)S(1)} %get-tuple-element.21), channel_id=1, source_target_pairs={{0,6},{1,7},{2,4},{3,5},{4,2},{5,3},{6,0},{7,1},{8,14},{9,15},{10,... | collective-permute-start | bytes 196616 | tf_op jit(solution)/shard_map/ppermute | solution.py:229
  7.4 5.3 %copy-start = (s32[16,3]{0,1:T(4,128)S(1)}, s32[16,3]{0,1:T(4,128)}, u32[]{:S(2)}) copy-start(s32[16,3]{0,1:T(4,128)} %param.10) | copy-start | bytes 580
  7.4 7.3 %collective-permute-start.2 = (bf16[2,128,128]{2,1,0:T(8,128)(2,1)S(1)}, bf16[2,128,128]{2,1,0:T(8,128)(2,1)S(1)}, u32[]{:S(2)}, u32[]{:S(2)}) collective-permute-start(bf16[2,128,128]{2,1,0:T(8,128)(2,1)S(1)} %get-tuple-element.22), channel_id=1, source_target_pairs={{0,3},{1,2},{2,1},{3,0},{4,7},{5,6},{6,5},{7,4},{8,11},{9,10},{10,... | collective-permute-start | bytes 196616 | tf_op jit(solution)/shard_map/ppermute | solution.py:229
  8.6 7.4 %collective-permute-start.3 = (bf16[2,128,128]{2,1,0:T(8,128)(2,1)S(1)}, bf16[2,128,128]{2,1,0:T(8,128)(2,1)S(1)}, u32[]{:S(2)}, u32[]{:S(2)}) collective-permute-start(bf16[2,128,128]{2,1,0:T(8,128)(2,1)S(1)} %get-tuple-element.23), channel_id=1, source_target_pairs={{0,7},{1,6},{2,5},{3,4},{4,3},{5,2},{6,1},{7,0},{8,15},{9,14},{10,... | collective-permute-start | bytes 196616 | tf_op jit(solution)/shard_map/ppermute | solution.py:229
  11.5 8.0 %collective-permute-start.4 = (bf16[2,128,128]{2,1,0:T(8,128)(2,1)S(1)}, bf16[2,128,128]{2,1,0:T(8,128)(2,1)S(1)}, u32[]{:S(2)}, u32[]{:S(2)}) collective-permute-start(bf16[2,128,128]{2,1,0:T(8,128)(2,1)S(1)} %get-tuple-element.24), channel_id=1, source_target_pairs={{0,5},{1,4},{2,7},{3,6},{4,1},{5,0},{6,3},{7,2},{8,13},{9,12},{10,... | collective-permute-start | bytes 196616 | tf_op jit(solution)/shard_map/ppermute | solution.py:229
  12.9 1.7 %copy-start.1 = (s32[2]{0:T(128)S(1)}, s32[2]{0:T(128)}, u32[]{:S(2)}) copy-start(s32[2]{0:T(128)} %param.11) | copy-start | bytes 28
  13.0 6.5 %collective-permute-start.5 = (bf16[2,128,128]{2,1,0:T(8,128)(2,1)S(1)}, bf16[2,128,128]{2,1,0:T(8,128)(2,1)S(1)}, u32[]{:S(2)}, u32[]{:S(2)}) collective-permute-start(bf16[2,128,128]{2,1,0:T(8,128)(2,1)S(1)} %get-tuple-element.25), channel_id=1, source_target_pairs={{0,2},{1,3},{2,0},{3,1},{4,6},{5,7},{6,4},{7,5},{8,10},{9,11},{10,... | collective-permute-start | bytes 196616 | tf_op jit(solution)/shard_map/ppermute | solution.py:229
  14.2 5.7 %collective-permute-start.6 = (bf16[2,128,128]{2,1,0:T(8,128)(2,1)S(1)}, bf16[2,128,128]{2,1,0:T(8,128)(2,1)S(1)}, u32[]{:S(2)}, u32[]{:S(2)}) collective-permute-start(bf16[2,128,128]{2,1,0:T(8,128)(2,1)S(1)} %get-tuple-element.26), channel_id=1, source_target_pairs={{0,1},{1,0},{2,3},{3,2},{4,5},{5,4},{6,7},{7,6},{8,9},{9,8},{10,11... | collective-permute-start | bytes 196616 | tf_op jit(solution)/shard_map/ppermute | solution.py:229
  22.9 9.1 %collective-permute-start.7 = (bf16[192,128]{1,0:T(8,128)(2,1)S(1)}, bf16[192,128]{1,0:T(8,128)(2,1)S(1)}, u32[]{:S(2)}, u32[]{:S(2)}) collective-permute-start(bf16[192,128]{1,0:T(8,128)(2,1)S(1)} %get-tuple-element.28), channel_id=1, source_target_pairs={{0,6},{1,7},{2,4},{3,5},{4,2},{5,3},{6,0},{7,1},{8,14},{9,15},{10,... | collective-permute-start | bytes 147464 | tf_op jit(solution)/shard_map/ppermute | solution.py:229
  25.9 6.6 %collective-permute-start.8 = (bf16[192,128]{1,0:T(8,128)(2,1)S(1)}, bf16[192,128]{1,0:T(8,128)(2,1)S(1)}, u32[]{:S(2)}, u32[]{:S(2)}) collective-permute-start(bf16[192,128]{1,0:T(8,128)(2,1)S(1)} %get-tuple-element.29), channel_id=1, source_target_pairs={{0,5},{1,4},{2,7},{3,6},{4,1},{5,0},{6,3},{7,2},{8,13},{9,12},{10,... | collective-permute-start | bytes 147464 | tf_op jit(solution)/shard_map/ppermute | solution.py:229
  26.7 6.9 %collective-permute-start.9 = (bf16[192,128]{1,0:T(8,128)(2,1)S(1)}, bf16[192,128]{1,0:T(8,128)(2,1)S(1)}, u32[]{:S(2)}, u32[]{:S(2)}) collective-permute-start(bf16[192,128]{1,0:T(8,128)(2,1)S(1)} %get-tuple-element.30), channel_id=1, source_target_pairs={{0,7},{1,6},{2,5},{3,4},{4,3},{5,2},{6,1},{7,0},{8,15},{9,14},{10,... | collective-permute-start | bytes 147464 | tf_op jit(solution)/shard_map/ppermute | solution.py:229
  29.5 5.2 %collective-permute-start.10 = (bf16[192,128]{1,0:T(8,128)(2,1)S(1)}, bf16[192,128]{1,0:T(8,128)(2,1)S(1)}, u32[]{:S(2)}, u32[]{:S(2)}) collective-permute-start(bf16[192,128]{1,0:T(8,128)(2,1)S(1)} %get-tuple-element.31), channel_id=1, source_target_pairs={{0,3},{1,2},{2,1},{3,0},{4,7},{5,6},{6,5},{7,4},{8,11},{9,10},{10,... | collective-permute-start | bytes 147464 | tf_op jit(solution)/shard_map/ppermute | solution.py:229
  30.3 5.0 %collective-permute-start.11 = (bf16[192,128]{1,0:T(8,128)(2,1)S(1)}, bf16[192,128]{1,0:T(8,128)(2,1)S(1)}, u32[]{:S(2)}, u32[]{:S(2)}) collective-permute-start(bf16[192,128]{1,0:T(8,128)(2,1)S(1)} %get-tuple-element.32), channel_id=1, source_target_pairs={{0,4},{1,5},{2,6},{3,7},{4,0},{5,1},{6,2},{7,3},{8,12},{9,13},{10,... | collective-permute-start | bytes 147464 | tf_op jit(solution)/shard_map/ppermute | solution.py:229
  32.0 4.1 %collective-permute-start.12 = (bf16[192,128]{1,0:T(8,128)(2,1)S(1)}, bf16[192,128]{1,0:T(8,128)(2,1)S(1)}, u32[]{:S(2)}, u32[]{:S(2)}) collective-permute-start(bf16[192,128]{1,0:T(8,128)(2,1)S(1)} %get-tuple-element.33), channel_id=1, source_target_pairs={{0,2},{1,3},{2,0},{3,1},{4,6},{5,7},{6,4},{7,5},{8,10},{9,11},{10,... | collective-permute-start | bytes 147464 | tf_op jit(solution)/shard_map/ppermute | solution.py:229
  32.5 4.1 %collective-permute-start.13 = (bf16[192,128]{1,0:T(8,128)(2,1)S(1)}, bf16[192,128]{1,0:T(8,128)(2,1)S(1)}, u32[]{:S(2)}, u32[]{:S(2)}) collective-permute-start(bf16[192,128]{1,0:T(8,128)(2,1)S(1)} %get-tuple-element.34), channel_id=1, source_target_pairs={{0,1},{1,0},{2,3},{3,2},{4,5},{5,4},{6,7},{7,6},{8,9},{9,8},{10,11... | collective-permute-start | bytes 147464 | tf_op jit(solution)/shard_map/ppermute | solution.py:229

commit v15 on v14

--- a/solution.py
+++ b/solution.py
@@ -14,8 +14,8 @@
 GLOBAL = 2
 HEAD = 64
 LANES = 2 * HEAD
-PARTNERS_IN = (0, 4, 6, 3, 7, 5, 2, 1)
-PARTNERS_BACK = (0, 6, 5, 7, 3, 4, 2, 1)
+PARTNERS_IN = (0, 4, 5, 2, 3, 7, 6, 1)
+PARTNERS_BACK = (0, 2, 6, 4, 7, 5, 1, 3)
 PACK_GRANT = 427 * 2**17
 MASKED = -1e30
 

time: 37.7 us -> 37.1 us (0.984)
  waiting for transfers between devices: 8.43 us -> 6.38 us
  starting transfers between devices: 22.8 us -> 24.3 us
    ppermute x14, waiting for transfers between devices: 8.43 us -> 6.38 us  [exchange(): arrived[m] = lax.ppermute(parts[m], 'seq', route)]
    ppermute x14, starting transfers between devices: 22.8 us -> 24.3 us  [exchange(): arrived[m] = lax.ppermute(parts[m], 'seq', route)]
  transfers between devices with their start and end apart: 14 -> 14, of which waited for: 8 -> 5; matrix products, arithmetic and copies ran while one was open for 1% -> 1% of each run, Pallas kernels for 0% -> 0%
where the time goes in v15:
time: 37.1 us; the launch traced here: 37 us
  starting transfers between devices  24.3 us (65%)
  waiting for transfers between devices  6.38 us (17%)
  Pallas kernels  5.34 us (14%)
  between operations  0.69 us (2%)
    ppermute x14, starting transfers between devices, exchange(): arrived[m] = lax.ppermute(parts[m], 'seq', route)  24.3 us
    ppermute x14, waiting for transfers between devices, exchange(): arrived[m] = lax.ppermute(parts[m], 'seq', route)  6.38 us
    pallas_call x1, Pallas kernels, on_device(): pl.pallas_call(kernel, out_shape=[jax.ShapeDtypeStruct((rows + BLOCK, LAN...  3.09 us
    pallas_call x1, Pallas kernels, on_device(): pl.pallas_call(pack_kernel, out_shape=[jax.ShapeDtypeStruct((2, rows, LAN...  1.35 us
    pallas_call x1, Pallas kernels, on_device(): pl.pallas_call(unpack_kernel, out_shape=[jax.ShapeDtypeStruct((rows, widt...  0.9 us
  transfers between devices with their start and end apart: 14, of which 5 were waited for; matrix products, arithmetic and copies ran while one was open for 1% of the time, Pallas kernels for 0%

profile of v15, /device:TPU:0, one launch (start us, length us, event | category | flops | bytes accessed | tf_op | source)
XLA Modules:
  0.0 37.0 jit_solution(14525919082926590349)
XLA Ops:
  0.6 1.4 %pack.1 = (bf16[2,128,128]{2,1,0:T(8,128)(2,1)S(1)}, bf16[2,128,128]{2,1,0:T(8,128)(2,1)S(1)}, bf16[2,128,128]{2,1,0:T(8,128)(2,1)S(1)}, bf16[2,128,128]{2,1,0:T...) custom-call(bf16[128,512]{1,0:T(8,128)(2,1)} %refs_0_.1, ...), custom_call_target="tpu_custom_call" | custom-call | tf_op jit(solution)/shard_map/pack/pallas_call | solution.py:257
  2.0 4.1 %collective-permute-start = (bf16[2,128,128]{2,1,0:T(8,128)(2,1)S(1)}, bf16[2,128,128]{2,1,0:T(8,128)(2,1)S(1)}, u32[]{:S(2)}, u32[]{:S(2)}) collective-permute-start(bf16[2,128,128]{2,1,0:T(8,128)(2,1)S(1)} %get-tuple-element.20), channel_id=1, source_target_pairs={{0,4},{1,5},{2,6},{3,7},{4,0},{5,1},{6,2},{7,3},{8,12},{9,13},{10,... | collective-permute-start | bytes 196616 | tf_op jit(solution)/shard_map/ppermute | solution.py:229
  6.1 1.3 %collective-permute-start.1 = (bf16[2,128,128]{2,1,0:T(8,128)(2,1)S(1)}, bf16[2,128,128]{2,1,0:T(8,128)(2,1)S(1)}, u32[]{:S(2)}, u32[]{:S(2)}) collective-permute-start(bf16[2,128,128]{2,1,0:T(8,128)(2,1)S(1)} %get-tuple-element.21), channel_id=1, source_target_pairs={{0,5},{1,4},{2,7},{3,6},{4,1},{5,0},{6,3},{7,2},{8,13},{9,12},{10,... | collective-permute-start | bytes 196616 | tf_op jit(solution)/shard_map/ppermute | solution.py:229
  7.4 1.6 %collective-permute-start.2 = (bf16[2,128,128]{2,1,0:T(8,128)(2,1)S(1)}, bf16[2,128,128]{2,1,0:T(8,128)(2,1)S(1)}, u32[]{:S(2)}, u32[]{:S(2)}) collective-permute-start(bf16[2,128,128]{2,1,0:T(8,128)(2,1)S(1)} %get-tuple-element.22), channel_id=1, source_target_pairs={{0,2},{1,3},{2,0},{3,1},{4,6},{5,7},{6,4},{7,5},{8,10},{9,11},{10,... | collective-permute-start | bytes 196616 | tf_op jit(solution)/shard_map/ppermute | solution.py:229
  8.9 0.2 collective-permute-start.3
  9.1 4.8 %collective-permute-start.4 = (bf16[2,128,128]{2,1,0:T(8,128)(2,1)S(1)}, bf16[2,128,128]{2,1,0:T(8,128)(2,1)S(1)}, u32[]{:S(2)}, u32[]{:S(2)}) collective-permute-start(bf16[2,128,128]{2,1,0:T(8,128)(2,1)S(1)} %get-tuple-element.24), channel_id=1, source_target_pairs={{0,7},{1,6},{2,5},{3,4},{4,3},{5,2},{6,1},{7,0},{8,15},{9,14},{10,... | collective-permute-start | bytes 196616 | tf_op jit(solution)/shard_map/ppermute | solution.py:229
  13.9 0.1 copy.10
  14.0 0.1 reshape.33
  14.1 0.9 %collective-permute-start.5 = (bf16[2,128,128]{2,1,0:T(8,128)(2,1)S(1)}, bf16[2,128,128]{2,1,0:T(8,128)(2,1)S(1)}, u32[]{:S(2)}, u32[]{:S(2)}) collective-permute-start(bf16[2,128,128]{2,1,0:T(8,128)(2,1)S(1)} %get-tuple-element.25), channel_id=1, source_target_pairs={{0,6},{1,7},{2,4},{3,5},{4,2},{5,3},{6,0},{7,1},{8,14},{9,15},{10,... | collective-permute-start | bytes 196616 | tf_op jit(solution)/shard_map/ppermute | solution.py:229
  14.9 1.3 %collective-permute-start.6 = (bf16[2,128,128]{2,1,0:T(8,128)(2,1)S(1)}, bf16[2,128,128]{2,1,0:T(8,128)(2,1)S(1)}, u32[]{:S(2)}, u32[]{:S(2)}) collective-permute-start(bf16[2,128,128]{2,1,0:T(8,128)(2,1)S(1)} %get-tuple-element.26), channel_id=1, source_target_pairs={{0,1},{1,0},{2,3},{3,2},{4,5},{5,4},{6,7},{7,6},{8,9},{9,8},{10,11... | collective-permute-start | bytes 196616 | tf_op jit(solution)/shard_map/ppermute | solution.py:229
  16.2 0.1 pad_add_fusion.ints_ref
  16.3 0.7 %collective-permute-done.4 = bf16[2,128,128]{2,1,0:T(8,128)(2,1)S(1)} collective-permute-done((bf16[2,128,128]{2,1,0:T(8,128)(2,1)S(1)}, bf16[2,128,128]{2,1,0:T(8,128)(2,1)S(1)}, u32[]{:S(2)}, u32[]{:S(2)}) %collective-permute-start.4) | collective-permute-done | bytes 65568 | tf_op jit(solution)/shard_map/ppermute | solution.py:229
  17.0 3.3 %collective-permute-done.5 = bf16[2,128,128]{2,1,0:T(8,128)(2,1)S(1)} collective-permute-done((bf16[2,128,128]{2,1,0:T(8,128)(2,1)S(1)}, bf16[2,128,128]{2,1,0:T(8,128)(2,1)S(1)}, u32[]{:S(2)}, u32[]{:S(2)}) %collective-permute-start.5) | collective-permute-done | bytes 65568 | tf_op jit(solution)/shard_map/ppermute | solution.py:229
  20.2 3.1 %attend.1 = (bf16[192,128]{1,0:T(8,128)(2,1)S(1)}, bf16[192,128]{1,0:T(8,128)(2,1)S(1)}, bf16[192,128]{1,0:T(8,128)(2,1)S(1)}, bf16[192,128]{1,0:T(8,128)(2,1)S(...) custom-call(s32[50]{0:T(128)S(1)} %pad_add_fusion.ints_ref, ...), custom_call_target="tpu_custom_call" | custom-call | tf_op jit(solution)/shard_map/attend/pallas_call | solution.py:273
  23.4 2.1 %collective-permute-start.8 = (bf16[192,128]{1,0:T(8,128)(2,1)S(1)}, bf16[192,128]{1,0:T(8,128)(2,1)S(1)}, u32[]{:S(2)}, u32[]{:S(2)}) collective-permute-start(bf16[192,128]{1,0:T(8,128)(2,1)S(1)} %get-tuple-element.29), channel_id=1, source_target_pairs={{0,6},{1,7},{2,4},{3,5},{4,2},{5,3},{6,0},{7,1},{8,14},{9,15},{10,... | collective-permute-start | bytes 147464 | tf_op jit(solution)/shard_map/ppermute | solution.py:229
  25.5 1.4 %collective-permute-start.9 = (bf16[192,128]{1,0:T(8,128)(2,1)S(1)}, bf16[192,128]{1,0:T(8,128)(2,1)S(1)}, u32[]{:S(2)}, u32[]{:S(2)}) collective-permute-start(bf16[192,128]{1,0:T(8,128)(2,1)S(1)} %get-tuple-element.30), channel_id=1, source_target_pairs={{0,4},{1,5},{2,6},{3,7},{4,0},{5,1},{6,2},{7,3},{8,12},{9,13},{10,... | collective-permute-start | bytes 147464 | tf_op jit(solution)/shard_map/ppermute | solution.py:229
  26.9 2.0 %collective-permute-start.10 = (bf16[192,128]{1,0:T(8,128)(2,1)S(1)}, bf16[192,128]{1,0:T(8,128)(2,1)S(1)}, u32[]{:S(2)}, u32[]{:S(2)}) collective-permute-start(bf16[192,128]{1,0:T(8,128)(2,1)S(1)} %get-tuple-element.31), channel_id=1, source_target_pairs={{0,7},{1,6},{2,5},{3,4},{4,3},{5,2},{6,1},{7,0},{8,15},{9,14},{10,... | collective-permute-start | bytes 147464 | tf_op jit(solution)/shard_map/ppermute | solution.py:229
  28.9 1.3 %collective-permute-start.11 = (bf16[192,128]{1,0:T(8,128)(2,1)S(1)}, bf16[192,128]{1,0:T(8,128)(2,1)S(1)}, u32[]{:S(2)}, u32[]{:S(2)}) collective-permute-start(bf16[192,128]{1,0:T(8,128)(2,1)S(1)} %get-tuple-element.32), channel_id=1, source_target_pairs={{0,5},{1,4},{2,7},{3,6},{4,1},{5,0},{6,3},{7,2},{8,13},{9,12},{10,... | collective-permute-start | bytes 147464 | tf_op jit(solution)/shard_map/ppermute | solution.py:229
  30.2 0.7 %collective-permute-start.12 = (bf16[192,128]{1,0:T(8,128)(2,1)S(1)}, bf16[192,128]{1,0:T(8,128)(2,1)S(1)}, u32[]{:S(2)}, u32[]{:S(2)}) collective-permute-start(bf16[192,128]{1,0:T(8,128)(2,1)S(1)} %get-tuple-element.33), channel_id=1, source_target_pairs={{0,1},{1,0},{2,3},{3,2},{4,5},{5,4},{6,7},{7,6},{8,9},{9,8},{10,11... | collective-permute-start | bytes 147464 | tf_op jit(solution)/shard_map/ppermute | solution.py:229
  31.0 2.7 %collective-permute-start.13 = (bf16[192,128]{1,0:T(8,128)(2,1)S(1)}, bf16[192,128]{1,0:T(8,128)(2,1)S(1)}, u32[]{:S(2)}, u32[]{:S(2)}) collective-permute-start(bf16[192,128]{1,0:T(8,128)(2,1)S(1)} %get-tuple-element.34), channel_id=1, source_target_pairs={{0,3},{1,2},{2,1},{3,0},{4,7},{5,6},{6,5},{7,4},{8,11},{9,10},{10,... | collective-permute-start | bytes 147464 | tf_op jit(solution)/shard_map/ppermute | solution.py:229
  33.6 0.1 collective-permute-done.10.refs_4_
  33.8 1.8 %collective-permute-done.11.refs_5_ = bf16[192,128]{1,0:T(8,128)(2,1)S(1)} collective-permute-done((bf16[192,128]{1,0:T(8,128)(2,1)S(1)}, bf16[192,128]{1,0:T(8,128)(2,1)S(1)}, u32[]{:S(2)}, u32[]{:S(2)}) %collective-permute-start.11) | collective-permute-done | bytes 49184 | tf_op jit(solution)/shard_map/ppermute | solution.py:229
  35.6 0.5 %collective-permute-done.13.refs_7_ = bf16[192,128]{1,0:T(8,128)(2,1)S(1)} collective-permute-done((bf16[192,128]{1,0:T(8,128)(2,1)S(1)}, bf16[192,128]{1,0:T(8,128)(2,1)S(1)}, u32[]{:S(2)}, u32[]{:S(2)}) %collective-permute-start.13) | collective-permute-done | bytes 49184 | tf_op jit(solution)/shard_map/ppermute | solution.py:229
  36.1 0.9 %unpack.1 = (bf16[128,512]{1,0:T(8,128)(2,1)}, bf16[128,512]{1,0:T(8,128)(2,1)}, bf16[128,512]{1,0:T(8,128)(2,1)}) custom-call(bf16[192,128]{1,0:T(8,128)(2,1)S(1)} %get-tuple-element.27.refs_0_, bf16[192,128]{1,0:T(8,128)(2,1)S(1)} %collective-permute-done.7.refs_1_, bf16[192,128]{1,0:T(8,128)(2,1)S(1)} %collective-permute-done.8.refs_2_, ...), custom_call_target="tpu_custom_call" | custom-call | tf_op jit(solution)/shard_map/unpack/pallas_call | solution.py:291
  (14 shorter events, 0.1 us)
Async XLA Ops:
  2.0 12.1 %collective-permute-start = (bf16[2,128,128]{2,1,0:T(8,128)(2,1)S(1)}, bf16[2,128,128]{2,1,0:T(8,128)(2,1)S(1)}, u32[]{:S(2)}, u32[]{:S(2)}) collective-permute-start(bf16[2,128,128]{2,1,0:T(8,128)(2,1)S(1)} %get-tuple-element.20), channel_id=1, source_target_pairs={{0,4},{1,5},{2,6},{3,7},{4,0},{5,1},{6,2},{7,3},{8,12},{9,13},{10,... | collective-permute-start | bytes 196616 | tf_op jit(solution)/shard_map/ppermute | solution.py:229
  6.1 8.8 %collective-permute-start.1 = (bf16[2,128,128]{2,1,0:T(8,128)(2,1)S(1)}, bf16[2,128,128]{2,1,0:T(8,128)(2,1)S(1)}, u32[]{:S(2)}, u32[]{:S(2)}) collective-permute-start(bf16[2,128,128]{2,1,0:T(8,128)(2,1)S(1)} %get-tuple-element.21), channel_id=1, source_target_pairs={{0,5},{1,4},{2,7},{3,6},{4,1},{5,0},{6,3},{7,2},{8,13},{9,12},{10,... | collective-permute-start | bytes 196616 | tf_op jit(solution)/shard_map/ppermute | solution.py:229
  7.4 6.5 %copy-start = (s32[16,3]{0,1:T(4,128)S(1)}, s32[16,3]{0,1:T(4,128)}, u32[]{:S(2)}) copy-start(s32[16,3]{0,1:T(4,128)} %param.10) | copy-start | bytes 580
  7.4 8.9 %collective-permute-start.2 = (bf16[2,128,128]{2,1,0:T(8,128)(2,1)S(1)}, bf16[2,128,128]{2,1,0:T(8,128)(2,1)S(1)}, u32[]{:S(2)}, u32[]{:S(2)}) collective-permute-start(bf16[2,128,128]{2,1,0:T(8,128)(2,1)S(1)} %get-tuple-element.22), channel_id=1, source_target_pairs={{0,2},{1,3},{2,0},{3,1},{4,6},{5,7},{6,4},{7,5},{8,10},{9,11},{10,... | collective-permute-start | bytes 196616 | tf_op jit(solution)/shard_map/ppermute | solution.py:229
  8.9 7.4 %collective-permute-start.3 = (bf16[2,128,128]{2,1,0:T(8,128)(2,1)S(1)}, bf16[2,128,128]{2,1,0:T(8,128)(2,1)S(1)}, u32[]{:S(2)}, u32[]{:S(2)}) collective-permute-start(bf16[2,128,128]{2,1,0:T(8,128)(2,1)S(1)} %get-tuple-element.23), channel_id=1, source_target_pairs={{0,3},{1,2},{2,1},{3,0},{4,7},{5,6},{6,5},{7,4},{8,11},{9,10},{10,... | collective-permute-start | bytes 196616 | tf_op jit(solution)/shard_map/ppermute | solution.py:229
  9.1 7.9 %collective-permute-start.4 = (bf16[2,128,128]{2,1,0:T(8,128)(2,1)S(1)}, bf16[2,128,128]{2,1,0:T(8,128)(2,1)S(1)}, u32[]{:S(2)}, u32[]{:S(2)}) collective-permute-start(bf16[2,128,128]{2,1,0:T(8,128)(2,1)S(1)} %get-tuple-element.24), channel_id=1, source_target_pairs={{0,7},{1,6},{2,5},{3,4},{4,3},{5,2},{6,1},{7,0},{8,15},{9,14},{10,... | collective-permute-start | bytes 196616 | tf_op jit(solution)/shard_map/ppermute | solution.py:229
  14.1 2.2 %copy-start.1 = (s32[2]{0:T(128)S(1)}, s32[2]{0:T(128)}, u32[]{:S(2)}) copy-start(s32[2]{0:T(128)} %param.11) | copy-start | bytes 28
  14.1 6.1 %collective-permute-start.5 = (bf16[2,128,128]{2,1,0:T(8,128)(2,1)S(1)}, bf16[2,128,128]{2,1,0:T(8,128)(2,1)S(1)}, u32[]{:S(2)}, u32[]{:S(2)}) collective-permute-start(bf16[2,128,128]{2,1,0:T(8,128)(2,1)S(1)} %get-tuple-element.25), channel_id=1, source_target_pairs={{0,6},{1,7},{2,4},{3,5},{4,2},{5,3},{6,0},{7,1},{8,14},{9,15},{10,... | collective-permute-start | bytes 196616 | tf_op jit(solution)/shard_map/ppermute | solution.py:229
  14.9 5.3 %collective-permute-start.6 = (bf16[2,128,128]{2,1,0:T(8,128)(2,1)S(1)}, bf16[2,128,128]{2,1,0:T(8,128)(2,1)S(1)}, u32[]{:S(2)}, u32[]{:S(2)}) collective-permute-start(bf16[2,128,128]{2,1,0:T(8,128)(2,1)S(1)} %get-tuple-element.26), channel_id=1, source_target_pairs={{0,1},{1,0},{2,3},{3,2},{4,5},{5,4},{6,7},{7,6},{8,9},{9,8},{10,11... | collective-permute-start | bytes 196616 | tf_op jit(solution)/shard_map/ppermute | solution.py:229
  23.3 6.9 %collective-permute-start.7 = (bf16[192,128]{1,0:T(8,128)(2,1)S(1)}, bf16[192,128]{1,0:T(8,128)(2,1)S(1)}, u32[]{:S(2)}, u32[]{:S(2)}) collective-permute-start(bf16[192,128]{1,0:T(8,128)(2,1)S(1)} %get-tuple-element.28), channel_id=1, source_target_pairs={{0,2},{1,3},{2,0},{3,1},{4,6},{5,7},{6,4},{7,5},{8,10},{9,11},{10,... | collective-permute-start | bytes 147464 | tf_op jit(solution)/shard_map/ppermute | solution.py:229
  23.4 7.6 %collective-permute-start.8 = (bf16[192,128]{1,0:T(8,128)(2,1)S(1)}, bf16[192,128]{1,0:T(8,128)(2,1)S(1)}, u32[]{:S(2)}, u32[]{:S(2)}) collective-permute-start(bf16[192,128]{1,0:T(8,128)(2,1)S(1)} %get-tuple-element.29), channel_id=1, source_target_pairs={{0,6},{1,7},{2,4},{3,5},{4,2},{5,3},{6,0},{7,1},{8,14},{9,15},{10,... | collective-permute-start | bytes 147464 | tf_op jit(solution)/shard_map/ppermute | solution.py:229
  25.5 8.1 %collective-permute-start.9 = (bf16[192,128]{1,0:T(8,128)(2,1)S(1)}, bf16[192,128]{1,0:T(8,128)(2,1)S(1)}, u32[]{:S(2)}, u32[]{:S(2)}) collective-permute-start(bf16[192,128]{1,0:T(8,128)(2,1)S(1)} %get-tuple-element.30), channel_id=1, source_target_pairs={{0,4},{1,5},{2,6},{3,7},{4,0},{5,1},{6,2},{7,3},{8,12},{9,13},{10,... | collective-permute-start | bytes 147464 | tf_op jit(solution)/shard_map/ppermute | solution.py:229
  26.9 6.9 %collective-permute-start.10 = (bf16[192,128]{1,0:T(8,128)(2,1)S(1)}, bf16[192,128]{1,0:T(8,128)(2,1)S(1)}, u32[]{:S(2)}, u32[]{:S(2)}) collective-permute-start(bf16[192,128]{1,0:T(8,128)(2,1)S(1)} %get-tuple-element.31), channel_id=1, source_target_pairs={{0,7},{1,6},{2,5},{3,4},{4,3},{5,2},{6,1},{7,0},{8,15},{9,14},{10,... | collective-permute-start | bytes 147464 | tf_op jit(solution)/shard_map/ppermute | solution.py:229
  28.9 6.7 %collective-permute-start.11 = (bf16[192,128]{1,0:T(8,128)(2,1)S(1)}, bf16[192,128]{1,0:T(8,128)(2,1)S(1)}, u32[]{:S(2)}, u32[]{:S(2)}) collective-permute-start(bf16[192,128]{1,0:T(8,128)(2,1)S(1)} %get-tuple-element.32), channel_id=1, source_target_pairs={{0,5},{1,4},{2,7},{3,6},{4,1},{5,0},{6,3},{7,2},{8,13},{9,12},{10,... | collective-permute-start | bytes 147464 | tf_op jit(solution)/shard_map/ppermute | solution.py:229
  30.2 5.4 %collective-permute-start.12 = (bf16[192,128]{1,0:T(8,128)(2,1)S(1)}, bf16[192,128]{1,0:T(8,128)(2,1)S(1)}, u32[]{:S(2)}, u32[]{:S(2)}) collective-permute-start(bf16[192,128]{1,0:T(8,128)(2,1)S(1)} %get-tuple-element.33), channel_id=1, source_target_pairs={{0,1},{1,0},{2,3},{3,2},{4,5},{5,4},{6,7},{7,6},{8,9},{9,8},{10,11... | collective-permute-start | bytes 147464 | tf_op jit(solution)/shard_map/ppermute | solution.py:229
  31.0 5.1 %collective-permute-start.13 = (bf16[192,128]{1,0:T(8,128)(2,1)S(1)}, bf16[192,128]{1,0:T(8,128)(2,1)S(1)}, u32[]{:S(2)}, u32[]{:S(2)}) collective-permute-start(bf16[192,128]{1,0:T(8,128)(2,1)S(1)} %get-tuple-element.34), channel_id=1, source_target_pairs={{0,3},{1,2},{2,1},{3,0},{4,7},{5,6},{6,5},{7,4},{8,11},{9,10},{10,... | collective-permute-start | bytes 147464 | tf_op jit(solution)/shard_map/ppermute | solution.py:229

commit v16 on v15

--- a/solution.py
+++ b/solution.py
@@ -14,8 +14,8 @@
 GLOBAL = 2
 HEAD = 64
 LANES = 2 * HEAD
-PARTNERS_IN = (0, 4, 5, 2, 3, 7, 6, 1)
-PARTNERS_BACK = (0, 2, 6, 4, 7, 5, 1, 3)
+PARTNERS_IN = (0, 4, 5, 2, 7, 3, 6, 1)
+PARTNERS_BACK = (0, 4, 6, 5, 7, 3, 1, 2)
 PACK_GRANT = 427 * 2**17
 MASKED = -1e30
 

time: 37.1 us -> 36.3 us (0.978)
  waiting for transfers between devices: 6.38 us -> 5.57 us
    ppermute x14, waiting for transfers between devices: 6.38 us -> 5.57 us  [exchange(): arrived[m] = lax.ppermute(parts[m], 'seq', route)]
where the time goes in v16:
time: 36.3 us; the launch traced here: 36.2 us
  starting transfers between devices  24.3 us (67%)
  waiting for transfers between devices  5.57 us (15%)
  Pallas kernels  5.35 us (15%)
  between operations  0.68 us (2%)
    ppermute x14, starting transfers between devices, exchange(): arrived[m] = lax.ppermute(parts[m], 'seq', route)  24.3 us
    ppermute x14, waiting for transfers between devices, exchange(): arrived[m] = lax.ppermute(parts[m], 'seq', route)  5.57 us
    pallas_call x1, Pallas kernels, on_device(): pl.pallas_call(kernel, out_shape=[jax.ShapeDtypeStruct((rows + BLOCK, LAN...  3.1 us
    pallas_call x1, Pallas kernels, on_device(): pl.pallas_call(pack_kernel, out_shape=[jax.ShapeDtypeStruct((2, rows, LAN...  1.35 us
    pallas_call x1, Pallas kernels, on_device(): pl.pallas_call(unpack_kernel, out_shape=[jax.ShapeDtypeStruct((rows, widt...  0.9 us
  transfers between devices with their start and end apart: 14, of which 5 were waited for; matrix products, arithmetic and copies ran while one was open for 1% of the time, Pallas kernels for 0%

profile of v16, /device:TPU:0, one launch (start us, length us, event | category | flops | bytes accessed | tf_op | source)
XLA Modules:
  0.0 36.2 jit_solution(7320640014092849159)
XLA Ops:
  0.6 1.4 %pack.1 = (bf16[2,128,128]{2,1,0:T(8,128)(2,1)S(1)}, bf16[2,128,128]{2,1,0:T(8,128)(2,1)S(1)}, bf16[2,128,128]{2,1,0:T(8,128)(2,1)S(1)}, bf16[2,128,128]{2,1,0:T...) custom-call(bf16[128,512]{1,0:T(8,128)(2,1)} %refs_0_.1, ...), custom_call_target="tpu_custom_call" | custom-call | tf_op jit(solution)/shard_map/pack/pallas_call | solution.py:257
  2.0 4.1 %collective-permute-start = (bf16[2,128,128]{2,1,0:T(8,128)(2,1)S(1)}, bf16[2,128,128]{2,1,0:T(8,128)(2,1)S(1)}, u32[]{:S(2)}, u32[]{:S(2)}) collective-permute-start(bf16[2,128,128]{2,1,0:T(8,128)(2,1)S(1)} %get-tuple-element.20), channel_id=1, source_target_pairs={{0,4},{1,5},{2,6},{3,7},{4,0},{5,1},{6,2},{7,3},{8,12},{9,13},{10,... | collective-permute-start | bytes 196616 | tf_op jit(solution)/shard_map/ppermute | solution.py:229
  6.1 1.3 %collective-permute-start.1 = (bf16[2,128,128]{2,1,0:T(8,128)(2,1)S(1)}, bf16[2,128,128]{2,1,0:T(8,128)(2,1)S(1)}, u32[]{:S(2)}, u32[]{:S(2)}) collective-permute-start(bf16[2,128,128]{2,1,0:T(8,128)(2,1)S(1)} %get-tuple-element.21), channel_id=1, source_target_pairs={{0,5},{1,4},{2,7},{3,6},{4,1},{5,0},{6,3},{7,2},{8,13},{9,12},{10,... | collective-permute-start | bytes 196616 | tf_op jit(solution)/shard_map/ppermute | solution.py:229
  7.4 1.6 %collective-permute-start.2 = (bf16[2,128,128]{2,1,0:T(8,128)(2,1)S(1)}, bf16[2,128,128]{2,1,0:T(8,128)(2,1)S(1)}, u32[]{:S(2)}, u32[]{:S(2)}) collective-permute-start(bf16[2,128,128]{2,1,0:T(8,128)(2,1)S(1)} %get-tuple-element.22), channel_id=1, source_target_pairs={{0,2},{1,3},{2,0},{3,1},{4,6},{5,7},{6,4},{7,5},{8,10},{9,11},{10,... | collective-permute-start | bytes 196616 | tf_op jit(solution)/shard_map/ppermute | solution.py:229
  8.9 2.4 %collective-permute-start.3 = (bf16[2,128,128]{2,1,0:T(8,128)(2,1)S(1)}, bf16[2,128,128]{2,1,0:T(8,128)(2,1)S(1)}, u32[]{:S(2)}, u32[]{:S(2)}) collective-permute-start(bf16[2,128,128]{2,1,0:T(8,128)(2,1)S(1)} %get-tuple-element.23), channel_id=1, source_target_pairs={{0,7},{1,6},{2,5},{3,4},{4,3},{5,2},{6,1},{7,0},{8,15},{9,14},{10,... | collective-permute-start | bytes 196616 | tf_op jit(solution)/shard_map/ppermute | solution.py:229
  11.4 1.6 %collective-permute-start.4 = (bf16[2,128,128]{2,1,0:T(8,128)(2,1)S(1)}, bf16[2,128,128]{2,1,0:T(8,128)(2,1)S(1)}, u32[]{:S(2)}, u32[]{:S(2)}) collective-permute-start(bf16[2,128,128]{2,1,0:T(8,128)(2,1)S(1)} %get-tuple-element.24), channel_id=1, source_target_pairs={{0,3},{1,2},{2,1},{3,0},{4,7},{5,6},{6,5},{7,4},{8,11},{9,10},{10,... | collective-permute-start | bytes 196616 | tf_op jit(solution)/shard_map/ppermute | solution.py:229
  13.0 0.1 copy.10
  13.1 0.1 reshape.33
  13.2 1.7 %collective-permute-start.5 = (bf16[2,128,128]{2,1,0:T(8,128)(2,1)S(1)}, bf16[2,128,128]{2,1,0:T(8,128)(2,1)S(1)}, u32[]{:S(2)}, u32[]{:S(2)}) collective-permute-start(bf16[2,128,128]{2,1,0:T(8,128)(2,1)S(1)} %get-tuple-element.25), channel_id=1, source_target_pairs={{0,6},{1,7},{2,4},{3,5},{4,2},{5,3},{6,0},{7,1},{8,14},{9,15},{10,... | collective-permute-start | bytes 196616 | tf_op jit(solution)/shard_map/ppermute | solution.py:229
  14.9 1.3 %collective-permute-start.6 = (bf16[2,128,128]{2,1,0:T(8,128)(2,1)S(1)}, bf16[2,128,128]{2,1,0:T(8,128)(2,1)S(1)}, u32[]{:S(2)}, u32[]{:S(2)}) collective-permute-start(bf16[2,128,128]{2,1,0:T(8,128)(2,1)S(1)} %get-tuple-element.26), channel_id=1, source_target_pairs={{0,1},{1,0},{2,3},{3,2},{4,5},{5,4},{6,7},{7,6},{8,9},{9,8},{10,11... | collective-permute-start | bytes 196616 | tf_op jit(solution)/shard_map/ppermute | solution.py:229
  16.3 1.3 %collective-permute-done.4 = bf16[2,128,128]{2,1,0:T(8,128)(2,1)S(1)} collective-permute-done((bf16[2,128,128]{2,1,0:T(8,128)(2,1)S(1)}, bf16[2,128,128]{2,1,0:T(8,128)(2,1)S(1)}, u32[]{:S(2)}, u32[]{:S(2)}) %collective-permute-start.4) | collective-permute-done | bytes 65568 | tf_op jit(solution)/shard_map/ppermute | solution.py:229
  17.6 1.7 %collective-permute-done.5 = bf16[2,128,128]{2,1,0:T(8,128)(2,1)S(1)} collective-permute-done((bf16[2,128,128]{2,1,0:T(8,128)(2,1)S(1)}, bf16[2,128,128]{2,1,0:T(8,128)(2,1)S(1)}, u32[]{:S(2)}, u32[]{:S(2)}) %collective-permute-start.5) | collective-permute-done | bytes 65568 | tf_op jit(solution)/shard_map/ppermute | solution.py:229
  19.3 3.1 %attend.1 = (bf16[192,128]{1,0:T(8,128)(2,1)S(1)}, bf16[192,128]{1,0:T(8,128)(2,1)S(1)}, bf16[192,128]{1,0:T(8,128)(2,1)S(1)}, bf16[192,128]{1,0:T(8,128)(2,1)S(...) custom-call(s32[50]{0:T(128)S(1)} %pad_add_fusion.ints_ref, ...), custom_call_target="tpu_custom_call" | custom-call | tf_op jit(solution)/shard_map/attend/pallas_call | solution.py:273
  22.4 1.4 %collective-permute-start.7 = (bf16[192,128]{1,0:T(8,128)(2,1)S(1)}, bf16[192,128]{1,0:T(8,128)(2,1)S(1)}, u32[]{:S(2)}, u32[]{:S(2)}) collective-permute-start(bf16[192,128]{1,0:T(8,128)(2,1)S(1)} %get-tuple-element.28), channel_id=1, source_target_pairs={{0,4},{1,5},{2,6},{3,7},{4,0},{5,1},{6,2},{7,3},{8,12},{9,13},{10,... | collective-permute-start | bytes 147464 | tf_op jit(solution)/shard_map/ppermute | solution.py:229
  23.9 1.4 %collective-permute-start.8 = (bf16[192,128]{1,0:T(8,128)(2,1)S(1)}, bf16[192,128]{1,0:T(8,128)(2,1)S(1)}, u32[]{:S(2)}, u32[]{:S(2)}) collective-permute-start(bf16[192,128]{1,0:T(8,128)(2,1)S(1)} %get-tuple-element.29), channel_id=1, source_target_pairs={{0,6},{1,7},{2,4},{3,5},{4,2},{5,3},{6,0},{7,1},{8,14},{9,15},{10,... | collective-permute-start | bytes 147464 | tf_op jit(solution)/shard_map/ppermute | solution.py:229
  25.2 2.8 %collective-permute-start.9 = (bf16[192,128]{1,0:T(8,128)(2,1)S(1)}, bf16[192,128]{1,0:T(8,128)(2,1)S(1)}, u32[]{:S(2)}, u32[]{:S(2)}) collective-permute-start(bf16[192,128]{1,0:T(8,128)(2,1)S(1)} %get-tuple-element.30), channel_id=1, source_target_pairs={{0,5},{1,4},{2,7},{3,6},{4,1},{5,0},{6,3},{7,2},{8,13},{9,12},{10,... | collective-permute-start | bytes 147464 | tf_op jit(solution)/shard_map/ppermute | solution.py:229
  28.1 1.2 %collective-permute-start.10 = (bf16[192,128]{1,0:T(8,128)(2,1)S(1)}, bf16[192,128]{1,0:T(8,128)(2,1)S(1)}, u32[]{:S(2)}, u32[]{:S(2)}) collective-permute-start(bf16[192,128]{1,0:T(8,128)(2,1)S(1)} %get-tuple-element.31), channel_id=1, source_target_pairs={{0,7},{1,6},{2,5},{3,4},{4,3},{5,2},{6,1},{7,0},{8,15},{9,14},{10,... | collective-permute-start | bytes 147464 | tf_op jit(solution)/shard_map/ppermute | solution.py:229
  29.2 1.3 %collective-permute-start.11 = (bf16[192,128]{1,0:T(8,128)(2,1)S(1)}, bf16[192,128]{1,0:T(8,128)(2,1)S(1)}, u32[]{:S(2)}, u32[]{:S(2)}) collective-permute-start(bf16[192,128]{1,0:T(8,128)(2,1)S(1)} %get-tuple-element.32), channel_id=1, source_target_pairs={{0,3},{1,2},{2,1},{3,0},{4,7},{5,6},{6,5},{7,4},{8,11},{9,10},{10,... | collective-permute-start | bytes 147464 | tf_op jit(solution)/shard_map/ppermute | solution.py:229
  30.5 0.6 %collective-permute-start.12 = (bf16[192,128]{1,0:T(8,128)(2,1)S(1)}, bf16[192,128]{1,0:T(8,128)(2,1)S(1)}, u32[]{:S(2)}, u32[]{:S(2)}) collective-permute-start(bf16[192,128]{1,0:T(8,128)(2,1)S(1)} %get-tuple-element.33), channel_id=1, source_target_pairs={{0,1},{1,0},{2,3},{3,2},{4,5},{5,4},{6,7},{7,6},{8,9},{9,8},{10,11... | collective-permute-start | bytes 147464 | tf_op jit(solution)/shard_map/ppermute | solution.py:229
  31.1 1.6 %collective-permute-start.13 = (bf16[192,128]{1,0:T(8,128)(2,1)S(1)}, bf16[192,128]{1,0:T(8,128)(2,1)S(1)}, u32[]{:S(2)}, u32[]{:S(2)}) collective-permute-start(bf16[192,128]{1,0:T(8,128)(2,1)S(1)} %get-tuple-element.34), channel_id=1, source_target_pairs={{0,2},{1,3},{2,0},{3,1},{4,6},{5,7},{6,4},{7,5},{8,10},{9,11},{10,... | collective-permute-start | bytes 147464 | tf_op jit(solution)/shard_map/ppermute | solution.py:229
  32.7 0.6 %collective-permute-done.9.refs_3_ = bf16[192,128]{1,0:T(8,128)(2,1)S(1)} collective-permute-done((bf16[192,128]{1,0:T(8,128)(2,1)S(1)}, bf16[192,128]{1,0:T(8,128)(2,1)S(1)}, u32[]{:S(2)}, u32[]{:S(2)}) %collective-permute-start.9) | collective-permute-done | bytes 49184 | tf_op jit(solution)/shard_map/ppermute | solution.py:229
  33.4 1.5 %collective-permute-done.10.refs_4_ = bf16[192,128]{1,0:T(8,128)(2,1)S(1)} collective-permute-done((bf16[192,128]{1,0:T(8,128)(2,1)S(1)}, bf16[192,128]{1,0:T(8,128)(2,1)S(1)}, u32[]{:S(2)}, u32[]{:S(2)}) %collective-permute-start.10) | collective-permute-done | bytes 49184 | tf_op jit(solution)/shard_map/ppermute | solution.py:229
  34.9 0.4 %collective-permute-done.12.refs_6_ = bf16[192,128]{1,0:T(8,128)(2,1)S(1)} collective-permute-done((bf16[192,128]{1,0:T(8,128)(2,1)S(1)}, bf16[192,128]{1,0:T(8,128)(2,1)S(1)}, u32[]{:S(2)}, u32[]{:S(2)}) %collective-permute-start.12) | collective-permute-done | bytes 49184 | tf_op jit(solution)/shard_map/ppermute | solution.py:229
  35.3 0.9 %unpack.1 = (bf16[128,512]{1,0:T(8,128)(2,1)}, bf16[128,512]{1,0:T(8,128)(2,1)}, bf16[128,512]{1,0:T(8,128)(2,1)}) custom-call(bf16[192,128]{1,0:T(8,128)(2,1)S(1)} %get-tuple-element.27.refs_0_, bf16[192,128]{1,0:T(8,128)(2,1)S(1)} %collective-permute-done.7.refs_1_, bf16[192,128]{1,0:T(8,128)(2,1)S(1)} %collective-permute-done.8.refs_2_, ...), custom_call_target="tpu_custom_call" | custom-call | tf_op jit(solution)/shard_map/unpack/pallas_call | solution.py:291
  (14 shorter events, 0.1 us)
Async XLA Ops:
  2.0 11.2 %collective-permute-start = (bf16[2,128,128]{2,1,0:T(8,128)(2,1)S(1)}, bf16[2,128,128]{2,1,0:T(8,128)(2,1)S(1)}, u32[]{:S(2)}, u32[]{:S(2)}) collective-permute-start(bf16[2,128,128]{2,1,0:T(8,128)(2,1)S(1)} %get-tuple-element.20), channel_id=1, source_target_pairs={{0,4},{1,5},{2,6},{3,7},{4,0},{5,1},{6,2},{7,3},{8,12},{9,13},{10,... | collective-permute-start | bytes 196616 | tf_op jit(solution)/shard_map/ppermute | solution.py:229
  6.1 8.8 %collective-permute-start.1 = (bf16[2,128,128]{2,1,0:T(8,128)(2,1)S(1)}, bf16[2,128,128]{2,1,0:T(8,128)(2,1)S(1)}, u32[]{:S(2)}, u32[]{:S(2)}) collective-permute-start(bf16[2,128,128]{2,1,0:T(8,128)(2,1)S(1)} %get-tuple-element.21), channel_id=1, source_target_pairs={{0,5},{1,4},{2,7},{3,6},{4,1},{5,0},{6,3},{7,2},{8,13},{9,12},{10,... | collective-permute-start | bytes 196616 | tf_op jit(solution)/shard_map/ppermute | solution.py:229
  7.4 5.6 %copy-start = (s32[16,3]{0,1:T(4,128)S(1)}, s32[16,3]{0,1:T(4,128)}, u32[]{:S(2)}) copy-start(s32[16,3]{0,1:T(4,128)} %param.10) | copy-start | bytes 580
  7.4 8.9 %collective-permute-start.2 = (bf16[2,128,128]{2,1,0:T(8,128)(2,1)S(1)}, bf16[2,128,128]{2,1,0:T(8,128)(2,1)S(1)}, u32[]{:S(2)}, u32[]{:S(2)}) collective-permute-start(bf16[2,128,128]{2,1,0:T(8,128)(2,1)S(1)} %get-tuple-element.22), channel_id=1, source_target_pairs={{0,2},{1,3},{2,0},{3,1},{4,6},{5,7},{6,4},{7,5},{8,10},{9,11},{10,... | collective-permute-start | bytes 196616 | tf_op jit(solution)/shard_map/ppermute | solution.py:229
  8.9 7.4 %collective-permute-start.3 = (bf16[2,128,128]{2,1,0:T(8,128)(2,1)S(1)}, bf16[2,128,128]{2,1,0:T(8,128)(2,1)S(1)}, u32[]{:S(2)}, u32[]{:S(2)}) collective-permute-start(bf16[2,128,128]{2,1,0:T(8,128)(2,1)S(1)} %get-tuple-element.23), channel_id=1, source_target_pairs={{0,7},{1,6},{2,5},{3,4},{4,3},{5,2},{6,1},{7,0},{8,15},{9,14},{10,... | collective-permute-start | bytes 196616 | tf_op jit(solution)/shard_map/ppermute | solution.py:229
  11.4 6.2 %collective-permute-start.4 = (bf16[2,128,128]{2,1,0:T(8,128)(2,1)S(1)}, bf16[2,128,128]{2,1,0:T(8,128)(2,1)S(1)}, u32[]{:S(2)}, u32[]{:S(2)}) collective-permute-start(bf16[2,128,128]{2,1,0:T(8,128)(2,1)S(1)} %get-tuple-element.24), channel_id=1, source_target_pairs={{0,3},{1,2},{2,1},{3,0},{4,7},{5,6},{6,5},{7,4},{8,11},{9,10},{10,... | collective-permute-start | bytes 196616 | tf_op jit(solution)/shard_map/ppermute | solution.py:229
  13.2 3.1 %copy-start.1 = (s32[2]{0:T(128)S(1)}, s32[2]{0:T(128)}, u32[]{:S(2)}) copy-start(s32[2]{0:T(128)} %param.11) | copy-start | bytes 28
  13.2 6.1 %collective-permute-start.5 = (bf16[2,128,128]{2,1,0:T(8,128)(2,1)S(1)}, bf16[2,128,128]{2,1,0:T(8,128)(2,1)S(1)}, u32[]{:S(2)}, u32[]{:S(2)}) collective-permute-start(bf16[2,128,128]{2,1,0:T(8,128)(2,1)S(1)} %get-tuple-element.25), channel_id=1, source_target_pairs={{0,6},{1,7},{2,4},{3,5},{4,2},{5,3},{6,0},{7,1},{8,14},{9,15},{10,... | collective-permute-start | bytes 196616 | tf_op jit(solution)/shard_map/ppermute | solution.py:229
  14.9 4.4 %collective-permute-start.6 = (bf16[2,128,128]{2,1,0:T(8,128)(2,1)S(1)}, bf16[2,128,128]{2,1,0:T(8,128)(2,1)S(1)}, u32[]{:S(2)}, u32[]{:S(2)}) collective-permute-start(bf16[2,128,128]{2,1,0:T(8,128)(2,1)S(1)} %get-tuple-element.26), channel_id=1, source_target_pairs={{0,1},{1,0},{2,3},{3,2},{4,5},{5,4},{6,7},{7,6},{8,9},{9,8},{10,11... | collective-permute-start | bytes 196616 | tf_op jit(solution)/shard_map/ppermute | solution.py:229
  22.4 8.1 %collective-permute-start.7 = (bf16[192,128]{1,0:T(8,128)(2,1)S(1)}, bf16[192,128]{1,0:T(8,128)(2,1)S(1)}, u32[]{:S(2)}, u32[]{:S(2)}) collective-permute-start(bf16[192,128]{1,0:T(8,128)(2,1)S(1)} %get-tuple-element.28), channel_id=1, source_target_pairs={{0,4},{1,5},{2,6},{3,7},{4,0},{5,1},{6,2},{7,3},{8,12},{9,13},{10,... | collective-permute-start | bytes 147464 | tf_op jit(solution)/shard_map/ppermute | solution.py:229
  23.9 7.2 %collective-permute-start.8 = (bf16[192,128]{1,0:T(8,128)(2,1)S(1)}, bf16[192,128]{1,0:T(8,128)(2,1)S(1)}, u32[]{:S(2)}, u32[]{:S(2)}) collective-permute-start(bf16[192,128]{1,0:T(8,128)(2,1)S(1)} %get-tuple-element.29), channel_id=1, source_target_pairs={{0,6},{1,7},{2,4},{3,5},{4,2},{5,3},{6,0},{7,1},{8,14},{9,15},{10,... | collective-permute-start | bytes 147464 | tf_op jit(solution)/shard_map/ppermute | solution.py:229
  25.2 8.1 %collective-permute-start.9 = (bf16[192,128]{1,0:T(8,128)(2,1)S(1)}, bf16[192,128]{1,0:T(8,128)(2,1)S(1)}, u32[]{:S(2)}, u32[]{:S(2)}) collective-permute-start(bf16[192,128]{1,0:T(8,128)(2,1)S(1)} %get-tuple-element.30), channel_id=1, source_target_pairs={{0,5},{1,4},{2,7},{3,6},{4,1},{5,0},{6,3},{7,2},{8,13},{9,12},{10,... | collective-permute-start | bytes 147464 | tf_op jit(solution)/shard_map/ppermute | solution.py:229
  28.1 6.8 %collective-permute-start.10 = (bf16[192,128]{1,0:T(8,128)(2,1)S(1)}, bf16[192,128]{1,0:T(8,128)(2,1)S(1)}, u32[]{:S(2)}, u32[]{:S(2)}) collective-permute-start(bf16[192,128]{1,0:T(8,128)(2,1)S(1)} %get-tuple-element.31), channel_id=1, source_target_pairs={{0,7},{1,6},{2,5},{3,4},{4,3},{5,2},{6,1},{7,0},{8,15},{9,14},{10,... | collective-permute-start | bytes 147464 | tf_op jit(solution)/shard_map/ppermute | solution.py:229
  29.2 5.7 %collective-permute-start.11 = (bf16[192,128]{1,0:T(8,128)(2,1)S(1)}, bf16[192,128]{1,0:T(8,128)(2,1)S(1)}, u32[]{:S(2)}, u32[]{:S(2)}) collective-permute-start(bf16[192,128]{1,0:T(8,128)(2,1)S(1)} %get-tuple-element.32), channel_id=1, source_target_pairs={{0,3},{1,2},{2,1},{3,0},{4,7},{5,6},{6,5},{7,4},{8,11},{9,10},{10,... | collective-permute-start | bytes 147464 | tf_op jit(solution)/shard_map/ppermute | solution.py:229
  30.5 4.8 %collective-permute-start.12 = (bf16[192,128]{1,0:T(8,128)(2,1)S(1)}, bf16[192,128]{1,0:T(8,128)(2,1)S(1)}, u32[]{:S(2)}, u32[]{:S(2)}) collective-permute-start(bf16[192,128]{1,0:T(8,128)(2,1)S(1)} %get-tuple-element.33), channel_id=1, source_target_pairs={{0,1},{1,0},{2,3},{3,2},{4,5},{5,4},{6,7},{7,6},{8,9},{9,8},{10,11... | collective-permute-start | bytes 147464 | tf_op jit(solution)/shard_map/ppermute | solution.py:229
  31.1 4.2 %collective-permute-start.13 = (bf16[192,128]{1,0:T(8,128)(2,1)S(1)}, bf16[192,128]{1,0:T(8,128)(2,1)S(1)}, u32[]{:S(2)}, u32[]{:S(2)}) collective-permute-start(bf16[192,128]{1,0:T(8,128)(2,1)S(1)} %get-tuple-element.34), channel_id=1, source_target_pairs={{0,2},{1,3},{2,0},{3,1},{4,6},{5,7},{6,4},{7,5},{8,10},{9,11},{10,... | collective-permute-start | bytes 147464 | tf_op jit(solution)/shard_map/ppermute | solution.py:229

commit v17 on v16

--- a/solution.py
+++ b/solution.py
@@ -15,7 +15,7 @@
 HEAD = 64
 LANES = 2 * HEAD
 PARTNERS_IN = (0, 4, 5, 2, 7, 3, 6, 1)
-PARTNERS_BACK = (0, 4, 6, 5, 7, 3, 1, 2)
+PARTNERS_BACK = (0, 4, 7, 5, 6, 3, 1, 2)
 PACK_GRANT = 427 * 2**17
 MASKED = -1e30
 

time: 36.3 us -> 36.5 us (level)
  starting transfers between devices: 24.3 us -> 25 us
  waiting for transfers between devices: 5.57 us -> 5.09 us
    ppermute x14, starting transfers between devices: 24.3 us -> 25 us  [exchange(): arrived[m] = lax.ppermute(parts[m], 'seq', route)]
    ppermute x14, waiting for transfers between devices: 5.57 us -> 5.09 us  [exchange(): arrived[m] = lax.ppermute(parts[m], 'seq', route)]
  transfers between devices with their start and end apart: 14 -> 14, of which waited for: 5 -> 6; matrix products, arithmetic and copies ran while one was open for 1% -> 1% of each run, Pallas kernels for 0% -> 0%
where the time goes in v17:
time: 36.5 us; the launch traced here: 36.4 us
  starting transfers between devices  25 us (68%)
  Pallas kernels  5.35 us (15%)
  waiting for transfers between devices  5.09 us (14%)
  between operations  0.68 us (2%)
    ppermute x14, starting transfers between devices, exchange(): arrived[m] = lax.ppermute(parts[m], 'seq', route)  25 us
    ppermute x14, waiting for transfers between devices, exchange(): arrived[m] = lax.ppermute(parts[m], 'seq', route)  5.09 us
    pallas_call x1, Pallas kernels, on_device(): pl.pallas_call(kernel, out_shape=[jax.ShapeDtypeStruct((rows + BLOCK, LAN...  3.1 us
    pallas_call x1, Pallas kernels, on_device(): pl.pallas_call(pack_kernel, out_shape=[jax.ShapeDtypeStruct((2, rows, LAN...  1.35 us
    pallas_call x1, Pallas kernels, on_device(): pl.pallas_call(unpack_kernel, out_shape=[jax.ShapeDtypeStruct((rows, widt...  0.9 us
  transfers between devices with their start and end apart: 14, of which 6 were waited for; matrix products, arithmetic and copies ran while one was open for 1% of the time, Pallas kernels for 0%

profile of v17, /device:TPU:0, one launch (start us, length us, event | category | flops | bytes accessed | tf_op | source)
XLA Modules:
  0.0 36.4 jit_solution(298745422078035818)
XLA Ops:
  0.6 1.4 %pack.1 = (bf16[2,128,128]{2,1,0:T(8,128)(2,1)S(1)}, bf16[2,128,128]{2,1,0:T(8,128)(2,1)S(1)}, bf16[2,128,128]{2,1,0:T(8,128)(2,1)S(1)}, bf16[2,128,128]{2,1,0:T...) custom-call(bf16[128,512]{1,0:T(8,128)(2,1)} %refs_0_.1, ...), custom_call_target="tpu_custom_call" | custom-call | tf_op jit(solution)/shard_map/pack/pallas_call | solution.py:257
  2.0 4.1 %collective-permute-start = (bf16[2,128,128]{2,1,0:T(8,128)(2,1)S(1)}, bf16[2,128,128]{2,1,0:T(8,128)(2,1)S(1)}, u32[]{:S(2)}, u32[]{:S(2)}) collective-permute-start(bf16[2,128,128]{2,1,0:T(8,128)(2,1)S(1)} %get-tuple-element.20), channel_id=1, source_target_pairs={{0,4},{1,5},{2,6},{3,7},{4,0},{5,1},{6,2},{7,3},{8,12},{9,13},{10,... | collective-permute-start | bytes 196616 | tf_op jit(solution)/shard_map/ppermute | solution.py:229
  6.1 1.3 %collective-permute-start.1 = (bf16[2,128,128]{2,1,0:T(8,128)(2,1)S(1)}, bf16[2,128,128]{2,1,0:T(8,128)(2,1)S(1)}, u32[]{:S(2)}, u32[]{:S(2)}) collective-permute-start(bf16[2,128,128]{2,1,0:T(8,128)(2,1)S(1)} %get-tuple-element.21), channel_id=1, source_target_pairs={{0,5},{1,4},{2,7},{3,6},{4,1},{5,0},{6,3},{7,2},{8,13},{9,12},{10,... | collective-permute-start | bytes 196616 | tf_op jit(solution)/shard_map/ppermute | solution.py:229
  7.4 1.6 %collective-permute-start.2 = (bf16[2,128,128]{2,1,0:T(8,128)(2,1)S(1)}, bf16[2,128,128]{2,1,0:T(8,128)(2,1)S(1)}, u32[]{:S(2)}, u32[]{:S(2)}) collective-permute-start(bf16[2,128,128]{2,1,0:T(8,128)(2,1)S(1)} %get-tuple-element.22), channel_id=1, source_target_pairs={{0,2},{1,3},{2,0},{3,1},{4,6},{5,7},{6,4},{7,5},{8,10},{9,11},{10,... | collective-permute-start | bytes 196616 | tf_op jit(solution)/shard_map/ppermute | solution.py:229
  8.9 2.4 %collective-permute-start.3 = (bf16[2,128,128]{2,1,0:T(8,128)(2,1)S(1)}, bf16[2,128,128]{2,1,0:T(8,128)(2,1)S(1)}, u32[]{:S(2)}, u32[]{:S(2)}) collective-permute-start(bf16[2,128,128]{2,1,0:T(8,128)(2,1)S(1)} %get-tuple-element.23), channel_id=1, source_target_pairs={{0,7},{1,6},{2,5},{3,4},{4,3},{5,2},{6,1},{7,0},{8,15},{9,14},{10,... | collective-permute-start | bytes 196616 | tf_op jit(solution)/shard_map/ppermute | solution.py:229
  11.4 1.6 %collective-permute-start.4 = (bf16[2,128,128]{2,1,0:T(8,128)(2,1)S(1)}, bf16[2,128,128]{2,1,0:T(8,128)(2,1)S(1)}, u32[]{:S(2)}, u32[]{:S(2)}) collective-permute-start(bf16[2,128,128]{2,1,0:T(8,128)(2,1)S(1)} %get-tuple-element.24), channel_id=1, source_target_pairs={{0,3},{1,2},{2,1},{3,0},{4,7},{5,6},{6,5},{7,4},{8,11},{9,10},{10,... | collective-permute-start | bytes 196616 | tf_op jit(solution)/shard_map/ppermute | solution.py:229
  13.1 0.1 reshape.33
  13.2 1.7 %collective-permute-start.5 = (bf16[2,128,128]{2,1,0:T(8,128)(2,1)S(1)}, bf16[2,128,128]{2,1,0:T(8,128)(2,1)S(1)}, u32[]{:S(2)}, u32[]{:S(2)}) collective-permute-start(bf16[2,128,128]{2,1,0:T(8,128)(2,1)S(1)} %get-tuple-element.25), channel_id=1, source_target_pairs={{0,6},{1,7},{2,4},{3,5},{4,2},{5,3},{6,0},{7,1},{8,14},{9,15},{10,... | collective-permute-start | bytes 196616 | tf_op jit(solution)/shard_map/ppermute | solution.py:229
  14.9 1.3 %collective-permute-start.6 = (bf16[2,128,128]{2,1,0:T(8,128)(2,1)S(1)}, bf16[2,128,128]{2,1,0:T(8,128)(2,1)S(1)}, u32[]{:S(2)}, u32[]{:S(2)}) collective-permute-start(bf16[2,128,128]{2,1,0:T(8,128)(2,1)S(1)} %get-tuple-element.26), channel_id=1, source_target_pairs={{0,1},{1,0},{2,3},{3,2},{4,5},{5,4},{6,7},{7,6},{8,9},{9,8},{10,11... | collective-permute-start | bytes 196616 | tf_op jit(solution)/shard_map/ppermute | solution.py:229
  16.3 1.3 %collective-permute-done.4 = bf16[2,128,128]{2,1,0:T(8,128)(2,1)S(1)} collective-permute-done((bf16[2,128,128]{2,1,0:T(8,128)(2,1)S(1)}, bf16[2,128,128]{2,1,0:T(8,128)(2,1)S(1)}, u32[]{:S(2)}, u32[]{:S(2)}) %collective-permute-start.4) | collective-permute-done | bytes 65568 | tf_op jit(solution)/shard_map/ppermute | solution.py:229
  17.6 1.7 %collective-permute-done.5 = bf16[2,128,128]{2,1,0:T(8,128)(2,1)S(1)} collective-permute-done((bf16[2,128,128]{2,1,0:T(8,128)(2,1)S(1)}, bf16[2,128,128]{2,1,0:T(8,128)(2,1)S(1)}, u32[]{:S(2)}, u32[]{:S(2)}) %collective-permute-start.5) | collective-permute-done | bytes 65568 | tf_op jit(solution)/shard_map/ppermute | solution.py:229
  19.3 3.1 %attend.1 = (bf16[192,128]{1,0:T(8,128)(2,1)S(1)}, bf16[192,128]{1,0:T(8,128)(2,1)S(1)}, bf16[192,128]{1,0:T(8,128)(2,1)S(1)}, bf16[192,128]{1,0:T(8,128)(2,1)S(...) custom-call(s32[50]{0:T(128)S(1)} %pad_add_fusion.ints_ref, ...), custom_call_target="tpu_custom_call" | custom-call | tf_op jit(solution)/shard_map/attend/pallas_call | solution.py:273
  22.4 1.4 %collective-permute-start.7 = (bf16[192,128]{1,0:T(8,128)(2,1)S(1)}, bf16[192,128]{1,0:T(8,128)(2,1)S(1)}, u32[]{:S(2)}, u32[]{:S(2)}) collective-permute-start(bf16[192,128]{1,0:T(8,128)(2,1)S(1)} %get-tuple-element.28), channel_id=1, source_target_pairs={{0,4},{1,5},{2,6},{3,7},{4,0},{5,1},{6,2},{7,3},{8,12},{9,13},{10,... | collective-permute-start | bytes 147464 | tf_op jit(solution)/shard_map/ppermute | solution.py:229
  23.9 2.2 %collective-permute-start.8 = (bf16[192,128]{1,0:T(8,128)(2,1)S(1)}, bf16[192,128]{1,0:T(8,128)(2,1)S(1)}, u32[]{:S(2)}, u32[]{:S(2)}) collective-permute-start(bf16[192,128]{1,0:T(8,128)(2,1)S(1)} %get-tuple-element.29), channel_id=1, source_target_pairs={{0,7},{1,6},{2,5},{3,4},{4,3},{5,2},{6,1},{7,0},{8,15},{9,14},{10,... | collective-permute-start | bytes 147464 | tf_op jit(solution)/shard_map/ppermute | solution.py:229
  26.1 2.0 %collective-permute-start.9 = (bf16[192,128]{1,0:T(8,128)(2,1)S(1)}, bf16[192,128]{1,0:T(8,128)(2,1)S(1)}, u32[]{:S(2)}, u32[]{:S(2)}) collective-permute-start(bf16[192,128]{1,0:T(8,128)(2,1)S(1)} %get-tuple-element.30), channel_id=1, source_target_pairs={{0,5},{1,4},{2,7},{3,6},{4,1},{5,0},{6,3},{7,2},{8,13},{9,12},{10,... | collective-permute-start | bytes 147464 | tf_op jit(solution)/shard_map/ppermute | solution.py:229
  28.1 1.2 %collective-permute-start.10 = (bf16[192,128]{1,0:T(8,128)(2,1)S(1)}, bf16[192,128]{1,0:T(8,128)(2,1)S(1)}, u32[]{:S(2)}, u32[]{:S(2)}) collective-permute-start(bf16[192,128]{1,0:T(8,128)(2,1)S(1)} %get-tuple-element.31), channel_id=1, source_target_pairs={{0,6},{1,7},{2,4},{3,5},{4,2},{5,3},{6,0},{7,1},{8,14},{9,15},{10,... | collective-permute-start | bytes 147464 | tf_op jit(solution)/shard_map/ppermute | solution.py:229
  29.2 1.3 %collective-permute-start.11 = (bf16[192,128]{1,0:T(8,128)(2,1)S(1)}, bf16[192,128]{1,0:T(8,128)(2,1)S(1)}, u32[]{:S(2)}, u32[]{:S(2)}) collective-permute-start(bf16[192,128]{1,0:T(8,128)(2,1)S(1)} %get-tuple-element.32), channel_id=1, source_target_pairs={{0,3},{1,2},{2,1},{3,0},{4,7},{5,6},{6,5},{7,4},{8,11},{9,10},{10,... | collective-permute-start | bytes 147464 | tf_op jit(solution)/shard_map/ppermute | solution.py:229
  30.5 0.8 %collective-permute-start.12 = (bf16[192,128]{1,0:T(8,128)(2,1)S(1)}, bf16[192,128]{1,0:T(8,128)(2,1)S(1)}, u32[]{:S(2)}, u32[]{:S(2)}) collective-permute-start(bf16[192,128]{1,0:T(8,128)(2,1)S(1)} %get-tuple-element.33), channel_id=1, source_target_pairs={{0,1},{1,0},{2,3},{3,2},{4,5},{5,4},{6,7},{7,6},{8,9},{9,8},{10,11... | collective-permute-start | bytes 147464 | tf_op jit(solution)/shard_map/ppermute | solution.py:229
  31.3 2.1 %collective-permute-start.13 = (bf16[192,128]{1,0:T(8,128)(2,1)S(1)}, bf16[192,128]{1,0:T(8,128)(2,1)S(1)}, u32[]{:S(2)}, u32[]{:S(2)}) collective-permute-start(bf16[192,128]{1,0:T(8,128)(2,1)S(1)} %get-tuple-element.34), channel_id=1, source_target_pairs={{0,2},{1,3},{2,0},{3,1},{4,6},{5,7},{6,4},{7,5},{8,10},{9,11},{10,... | collective-permute-start | bytes 147464 | tf_op jit(solution)/shard_map/ppermute | solution.py:229
  33.4 0.4 %collective-permute-done.9.refs_3_ = bf16[192,128]{1,0:T(8,128)(2,1)S(1)} collective-permute-done((bf16[192,128]{1,0:T(8,128)(2,1)S(1)}, bf16[192,128]{1,0:T(8,128)(2,1)S(1)}, u32[]{:S(2)}, u32[]{:S(2)}) %collective-permute-start.9) | collective-permute-done | bytes 49184 | tf_op jit(solution)/shard_map/ppermute | solution.py:229
  33.8 0.6 %collective-permute-done.10.refs_4_ = bf16[192,128]{1,0:T(8,128)(2,1)S(1)} collective-permute-done((bf16[192,128]{1,0:T(8,128)(2,1)S(1)}, bf16[192,128]{1,0:T(8,128)(2,1)S(1)}, u32[]{:S(2)}, u32[]{:S(2)}) %collective-permute-start.10) | collective-permute-done | bytes 49184 | tf_op jit(solution)/shard_map/ppermute | solution.py:229
  34.4 0.5 %collective-permute-done.12.refs_6_ = bf16[192,128]{1,0:T(8,128)(2,1)S(1)} collective-permute-done((bf16[192,128]{1,0:T(8,128)(2,1)S(1)}, bf16[192,128]{1,0:T(8,128)(2,1)S(1)}, u32[]{:S(2)}, u32[]{:S(2)}) %collective-permute-start.12) | collective-permute-done | bytes 49184 | tf_op jit(solution)/shard_map/ppermute | solution.py:229
  34.9 0.6 %collective-permute-done.13.refs_7_ = bf16[192,128]{1,0:T(8,128)(2,1)S(1)} collective-permute-done((bf16[192,128]{1,0:T(8,128)(2,1)S(1)}, bf16[192,128]{1,0:T(8,128)(2,1)S(1)}, u32[]{:S(2)}, u32[]{:S(2)}) %collective-permute-start.13) | collective-permute-done | bytes 49184 | tf_op jit(solution)/shard_map/ppermute | solution.py:229
  35.5 0.9 %unpack.1 = (bf16[128,512]{1,0:T(8,128)(2,1)}, bf16[128,512]{1,0:T(8,128)(2,1)}, bf16[128,512]{1,0:T(8,128)(2,1)}) custom-call(bf16[192,128]{1,0:T(8,128)(2,1)S(1)} %get-tuple-element.27.refs_0_, bf16[192,128]{1,0:T(8,128)(2,1)S(1)} %collective-permute-done.7.refs_1_, bf16[192,128]{1,0:T(8,128)(2,1)S(1)} %collective-permute-done.8.refs_2_, ...), custom_call_target="tpu_custom_call" | custom-call | tf_op jit(solution)/shard_map/unpack/pallas_call | solution.py:291
  (14 shorter events, 0.2 us)
Async XLA Ops:
  2.0 11.2 %collective-permute-start = (bf16[2,128,128]{2,1,0:T(8,128)(2,1)S(1)}, bf16[2,128,128]{2,1,0:T(8,128)(2,1)S(1)}, u32[]{:S(2)}, u32[]{:S(2)}) collective-permute-start(bf16[2,128,128]{2,1,0:T(8,128)(2,1)S(1)} %get-tuple-element.20), channel_id=1, source_target_pairs={{0,4},{1,5},{2,6},{3,7},{4,0},{5,1},{6,2},{7,3},{8,12},{9,13},{10,... | collective-permute-start | bytes 196616 | tf_op jit(solution)/shard_map/ppermute | solution.py:229
  6.1 8.8 %collective-permute-start.1 = (bf16[2,128,128]{2,1,0:T(8,128)(2,1)S(1)}, bf16[2,128,128]{2,1,0:T(8,128)(2,1)S(1)}, u32[]{:S(2)}, u32[]{:S(2)}) collective-permute-start(bf16[2,128,128]{2,1,0:T(8,128)(2,1)S(1)} %get-tuple-element.21), channel_id=1, source_target_pairs={{0,5},{1,4},{2,7},{3,6},{4,1},{5,0},{6,3},{7,2},{8,13},{9,12},{10,... | collective-permute-start | bytes 196616 | tf_op jit(solution)/shard_map/ppermute | solution.py:229
  7.4 5.6 %copy-start = (s32[16,3]{0,1:T(4,128)S(1)}, s32[16,3]{0,1:T(4,128)}, u32[]{:S(2)}) copy-start(s32[16,3]{0,1:T(4,128)} %param.10) | copy-start | bytes 580
  7.4 8.9 %collective-permute-start.2 = (bf16[2,128,128]{2,1,0:T(8,128)(2,1)S(1)}, bf16[2,128,128]{2,1,0:T(8,128)(2,1)S(1)}, u32[]{:S(2)}, u32[]{:S(2)}) collective-permute-start(bf16[2,128,128]{2,1,0:T(8,128)(2,1)S(1)} %get-tuple-element.22), channel_id=1, source_target_pairs={{0,2},{1,3},{2,0},{3,1},{4,6},{5,7},{6,4},{7,5},{8,10},{9,11},{10,... | collective-permute-start | bytes 196616 | tf_op jit(solution)/shard_map/ppermute | solution.py:229
  8.9 7.4 %collective-permute-start.3 = (bf16[2,128,128]{2,1,0:T(8,128)(2,1)S(1)}, bf16[2,128,128]{2,1,0:T(8,128)(2,1)S(1)}, u32[]{:S(2)}, u32[]{:S(2)}) collective-permute-start(bf16[2,128,128]{2,1,0:T(8,128)(2,1)S(1)} %get-tuple-element.23), channel_id=1, source_target_pairs={{0,7},{1,6},{2,5},{3,4},{4,3},{5,2},{6,1},{7,0},{8,15},{9,14},{10,... | collective-permute-start | bytes 196616 | tf_op jit(solution)/shard_map/ppermute | solution.py:229
  11.4 6.2 %collective-permute-start.4 = (bf16[2,128,128]{2,1,0:T(8,128)(2,1)S(1)}, bf16[2,128,128]{2,1,0:T(8,128)(2,1)S(1)}, u32[]{:S(2)}, u32[]{:S(2)}) collective-permute-start(bf16[2,128,128]{2,1,0:T(8,128)(2,1)S(1)} %get-tuple-element.24), channel_id=1, source_target_pairs={{0,3},{1,2},{2,1},{3,0},{4,7},{5,6},{6,5},{7,4},{8,11},{9,10},{10,... | collective-permute-start | bytes 196616 | tf_op jit(solution)/shard_map/ppermute | solution.py:229
  13.2 3.1 %copy-start.1 = (s32[2]{0:T(128)S(1)}, s32[2]{0:T(128)}, u32[]{:S(2)}) copy-start(s32[2]{0:T(128)} %param.11) | copy-start | bytes 28
  13.2 6.1 %collective-permute-start.5 = (bf16[2,128,128]{2,1,0:T(8,128)(2,1)S(1)}, bf16[2,128,128]{2,1,0:T(8,128)(2,1)S(1)}, u32[]{:S(2)}, u32[]{:S(2)}) collective-permute-start(bf16[2,128,128]{2,1,0:T(8,128)(2,1)S(1)} %get-tuple-element.25), channel_id=1, source_target_pairs={{0,6},{1,7},{2,4},{3,5},{4,2},{5,3},{6,0},{7,1},{8,14},{9,15},{10,... | collective-permute-start | bytes 196616 | tf_op jit(solution)/shard_map/ppermute | solution.py:229
  14.9 4.4 %collective-permute-start.6 = (bf16[2,128,128]{2,1,0:T(8,128)(2,1)S(1)}, bf16[2,128,128]{2,1,0:T(8,128)(2,1)S(1)}, u32[]{:S(2)}, u32[]{:S(2)}) collective-permute-start(bf16[2,128,128]{2,1,0:T(8,128)(2,1)S(1)} %get-tuple-element.26), channel_id=1, source_target_pairs={{0,1},{1,0},{2,3},{3,2},{4,5},{5,4},{6,7},{7,6},{8,9},{9,8},{10,11... | collective-permute-start | bytes 196616 | tf_op jit(solution)/shard_map/ppermute | solution.py:229
  22.4 8.1 %collective-permute-start.7 = (bf16[192,128]{1,0:T(8,128)(2,1)S(1)}, bf16[192,128]{1,0:T(8,128)(2,1)S(1)}, u32[]{:S(2)}, u32[]{:S(2)}) collective-permute-start(bf16[192,128]{1,0:T(8,128)(2,1)S(1)} %get-tuple-element.28), channel_id=1, source_target_pairs={{0,4},{1,5},{2,6},{3,7},{4,0},{5,1},{6,2},{7,3},{8,12},{9,13},{10,... | collective-permute-start | bytes 147464 | tf_op jit(solution)/shard_map/ppermute | solution.py:229
  23.9 7.4 %collective-permute-start.8 = (bf16[192,128]{1,0:T(8,128)(2,1)S(1)}, bf16[192,128]{1,0:T(8,128)(2,1)S(1)}, u32[]{:S(2)}, u32[]{:S(2)}) collective-permute-start(bf16[192,128]{1,0:T(8,128)(2,1)S(1)} %get-tuple-element.29), channel_id=1, source_target_pairs={{0,7},{1,6},{2,5},{3,4},{4,3},{5,2},{6,1},{7,0},{8,15},{9,14},{10,... | collective-permute-start | bytes 147464 | tf_op jit(solution)/shard_map/ppermute | solution.py:229
  26.1 7.7 %collective-permute-start.9 = (bf16[192,128]{1,0:T(8,128)(2,1)S(1)}, bf16[192,128]{1,0:T(8,128)(2,1)S(1)}, u32[]{:S(2)}, u32[]{:S(2)}) collective-permute-start(bf16[192,128]{1,0:T(8,128)(2,1)S(1)} %get-tuple-element.30), channel_id=1, source_target_pairs={{0,5},{1,4},{2,7},{3,6},{4,1},{5,0},{6,3},{7,2},{8,13},{9,12},{10,... | collective-permute-start | bytes 147464 | tf_op jit(solution)/shard_map/ppermute | solution.py:229
  28.1 6.3 %collective-permute-start.10 = (bf16[192,128]{1,0:T(8,128)(2,1)S(1)}, bf16[192,128]{1,0:T(8,128)(2,1)S(1)}, u32[]{:S(2)}, u32[]{:S(2)}) collective-permute-start(bf16[192,128]{1,0:T(8,128)(2,1)S(1)} %get-tuple-element.31), channel_id=1, source_target_pairs={{0,6},{1,7},{2,4},{3,5},{4,2},{5,3},{6,0},{7,1},{8,14},{9,15},{10,... | collective-permute-start | bytes 147464 | tf_op jit(solution)/shard_map/ppermute | solution.py:229
  29.2 5.2 %collective-permute-start.11 = (bf16[192,128]{1,0:T(8,128)(2,1)S(1)}, bf16[192,128]{1,0:T(8,128)(2,1)S(1)}, u32[]{:S(2)}, u32[]{:S(2)}) collective-permute-start(bf16[192,128]{1,0:T(8,128)(2,1)S(1)} %get-tuple-element.32), channel_id=1, source_target_pairs={{0,3},{1,2},{2,1},{3,0},{4,7},{5,6},{6,5},{7,4},{8,11},{9,10},{10,... | collective-permute-start | bytes 147464 | tf_op jit(solution)/shard_map/ppermute | solution.py:229
  30.5 4.4 %collective-permute-start.12 = (bf16[192,128]{1,0:T(8,128)(2,1)S(1)}, bf16[192,128]{1,0:T(8,128)(2,1)S(1)}, u32[]{:S(2)}, u32[]{:S(2)}) collective-permute-start(bf16[192,128]{1,0:T(8,128)(2,1)S(1)} %get-tuple-element.33), channel_id=1, source_target_pairs={{0,1},{1,0},{2,3},{3,2},{4,5},{5,4},{6,7},{7,6},{8,9},{9,8},{10,11... | collective-permute-start | bytes 147464 | tf_op jit(solution)/shard_map/ppermute | solution.py:229
  31.3 4.2 %collective-permute-start.13 = (bf16[192,128]{1,0:T(8,128)(2,1)S(1)}, bf16[192,128]{1,0:T(8,128)(2,1)S(1)}, u32[]{:S(2)}, u32[]{:S(2)}) collective-permute-start(bf16[192,128]{1,0:T(8,128)(2,1)S(1)} %get-tuple-element.34), channel_id=1, source_target_pairs={{0,2},{1,3},{2,0},{3,1},{4,6},{5,7},{6,4},{7,5},{8,10},{9,11},{10,... | collective-permute-start | bytes 147464 | tf_op jit(solution)/shard_map/ppermute | solution.py:229

commit v18 on v17

--- a/solution.py
+++ b/solution.py
@@ -14,7 +14,7 @@
 GLOBAL = 2
 HEAD = 64
 LANES = 2 * HEAD
-PARTNERS_IN = (0, 4, 5, 2, 7, 3, 6, 1)
+PARTNERS_IN = (0, 4, 7, 3, 5, 2, 6, 1)
 PARTNERS_BACK = (0, 4, 7, 5, 6, 3, 1, 2)
 PACK_GRANT = 427 * 2**17
 MASKED = -1e30

time: 36.5 us -> 37.7 us (1.033)
  waiting for transfers between devices: 5.09 us -> 6.89 us
  starting transfers between devices: 25 us -> 24.4 us
    ppermute x14, waiting for transfers between devices: 5.09 us -> 6.89 us  [exchange(): arrived[m] = lax.ppermute(parts[m], 'seq', route)]
    ppermute x14, starting transfers between devices: 25 us -> 24.4 us  [exchange(): arrived[m] = lax.ppermute(parts[m], 'seq', route)]
  transfers between devices with their start and end apart: 14 -> 14, of which waited for: 6 -> 7; matrix products, arithmetic and copies ran while one was open for 1% -> 1% of each run, Pallas kernels for 0% -> 0%
where the time goes in v18:
time: 37.7 us; the launch traced here: 37.6 us
  starting transfers between devices  24.4 us (65%)
  waiting for transfers between devices  6.89 us (18%)
  Pallas kernels  5.35 us (14%)
  between operations  0.68 us (2%)
    ppermute x14, starting transfers between devices, exchange(): arrived[m] = lax.ppermute(parts[m], 'seq', route)  24.4 us
    ppermute x14, waiting for transfers between devices, exchange(): arrived[m] = lax.ppermute(parts[m], 'seq', route)  6.89 us
    pallas_call x1, Pallas kernels, on_device(): pl.pallas_call(kernel, out_shape=[jax.ShapeDtypeStruct((rows + BLOCK, LAN...  3.1 us
    pallas_call x1, Pallas kernels, on_device(): pl.pallas_call(pack_kernel, out_shape=[jax.ShapeDtypeStruct((2, rows, LAN...  1.35 us
    pallas_call x1, Pallas kernels, on_device(): pl.pallas_call(unpack_kernel, out_shape=[jax.ShapeDtypeStruct((rows, widt...  0.9 us
  transfers between devices with their start and end apart: 14, of which 7 were waited for; matrix products, arithmetic and copies ran while one was open for 1% of the time, Pallas kernels for 0%

profile of v18, /device:TPU:0, one launch (start us, length us, event | category | flops | bytes accessed | tf_op | source)
XLA Modules:
  0.0 37.6 jit_solution(3209385868804373961)
XLA Ops:
  0.6 1.4 %pack.1 = (bf16[2,128,128]{2,1,0:T(8,128)(2,1)S(1)}, bf16[2,128,128]{2,1,0:T(8,128)(2,1)S(1)}, bf16[2,128,128]{2,1,0:T(8,128)(2,1)S(1)}, bf16[2,128,128]{2,1,0:T...) custom-call(bf16[128,512]{1,0:T(8,128)(2,1)} %refs_0_.1, ...), custom_call_target="tpu_custom_call" | custom-call | tf_op jit(solution)/shard_map/pack/pallas_call | solution.py:257
  2.0 4.1 %collective-permute-start = (bf16[2,128,128]{2,1,0:T(8,128)(2,1)S(1)}, bf16[2,128,128]{2,1,0:T(8,128)(2,1)S(1)}, u32[]{:S(2)}, u32[]{:S(2)}) collective-permute-start(bf16[2,128,128]{2,1,0:T(8,128)(2,1)S(1)} %get-tuple-element.20), channel_id=1, source_target_pairs={{0,4},{1,5},{2,6},{3,7},{4,0},{5,1},{6,2},{7,3},{8,12},{9,13},{10,... | collective-permute-start | bytes 196616 | tf_op jit(solution)/shard_map/ppermute | solution.py:229
  6.1 2.3 %collective-permute-start.1 = (bf16[2,128,128]{2,1,0:T(8,128)(2,1)S(1)}, bf16[2,128,128]{2,1,0:T(8,128)(2,1)S(1)}, u32[]{:S(2)}, u32[]{:S(2)}) collective-permute-start(bf16[2,128,128]{2,1,0:T(8,128)(2,1)S(1)} %get-tuple-element.21), channel_id=1, source_target_pairs={{0,7},{1,6},{2,5},{3,4},{4,3},{5,2},{6,1},{7,0},{8,15},{9,14},{10,... | collective-permute-start | bytes 196616 | tf_op jit(solution)/shard_map/ppermute | solution.py:229
  8.4 0.2 collective-permute-start.2
  8.6 3.7 %collective-permute-start.3 = (bf16[2,128,128]{2,1,0:T(8,128)(2,1)S(1)}, bf16[2,128,128]{2,1,0:T(8,128)(2,1)S(1)}, u32[]{:S(2)}, u32[]{:S(2)}) collective-permute-start(bf16[2,128,128]{2,1,0:T(8,128)(2,1)S(1)} %get-tuple-element.23), channel_id=1, source_target_pairs={{0,5},{1,4},{2,7},{3,6},{4,1},{5,0},{6,3},{7,2},{8,13},{9,12},{10,... | collective-permute-start | bytes 196616 | tf_op jit(solution)/shard_map/ppermute | solution.py:229
  12.3 0.7 %collective-permute-start.4 = (bf16[2,128,128]{2,1,0:T(8,128)(2,1)S(1)}, bf16[2,128,128]{2,1,0:T(8,128)(2,1)S(1)}, u32[]{:S(2)}, u32[]{:S(2)}) collective-permute-start(bf16[2,128,128]{2,1,0:T(8,128)(2,1)S(1)} %get-tuple-element.24), channel_id=1, source_target_pairs={{0,2},{1,3},{2,0},{3,1},{4,6},{5,7},{6,4},{7,5},{8,10},{9,11},{10,... | collective-permute-start | bytes 196616 | tf_op jit(solution)/shard_map/ppermute | solution.py:229
  13.1 0.1 reshape.33
  13.2 1.8 %collective-permute-start.5 = (bf16[2,128,128]{2,1,0:T(8,128)(2,1)S(1)}, bf16[2,128,128]{2,1,0:T(8,128)(2,1)S(1)}, u32[]{:S(2)}, u32[]{:S(2)}) collective-permute-start(bf16[2,128,128]{2,1,0:T(8,128)(2,1)S(1)} %get-tuple-element.25), channel_id=1, source_target_pairs={{0,6},{1,7},{2,4},{3,5},{4,2},{5,3},{6,0},{7,1},{8,14},{9,15},{10,... | collective-permute-start | bytes 196616 | tf_op jit(solution)/shard_map/ppermute | solution.py:229
  15.0 1.6 %collective-permute-start.6 = (bf16[2,128,128]{2,1,0:T(8,128)(2,1)S(1)}, bf16[2,128,128]{2,1,0:T(8,128)(2,1)S(1)}, u32[]{:S(2)}, u32[]{:S(2)}) collective-permute-start(bf16[2,128,128]{2,1,0:T(8,128)(2,1)S(1)} %get-tuple-element.26), channel_id=1, source_target_pairs={{0,1},{1,0},{2,3},{3,2},{4,5},{5,4},{6,7},{7,6},{8,9},{9,8},{10,11... | collective-permute-start | bytes 196616 | tf_op jit(solution)/shard_map/ppermute | solution.py:229
  16.6 0.7 %collective-permute-done.3 = bf16[2,128,128]{2,1,0:T(8,128)(2,1)S(1)} collective-permute-done((bf16[2,128,128]{2,1,0:T(8,128)(2,1)S(1)}, bf16[2,128,128]{2,1,0:T(8,128)(2,1)S(1)}, u32[]{:S(2)}, u32[]{:S(2)}) %collective-permute-start.3) | collective-permute-done | bytes 65568 | tf_op jit(solution)/shard_map/ppermute | solution.py:229
  17.3 2.0 %collective-permute-done.5 = bf16[2,128,128]{2,1,0:T(8,128)(2,1)S(1)} collective-permute-done((bf16[2,128,128]{2,1,0:T(8,128)(2,1)S(1)}, bf16[2,128,128]{2,1,0:T(8,128)(2,1)S(1)}, u32[]{:S(2)}, u32[]{:S(2)}) %collective-permute-start.5) | collective-permute-done | bytes 65568 | tf_op jit(solution)/shard_map/ppermute | solution.py:229
  19.3 3.1 %attend.1 = (bf16[192,128]{1,0:T(8,128)(2,1)S(1)}, bf16[192,128]{1,0:T(8,128)(2,1)S(1)}, bf16[192,128]{1,0:T(8,128)(2,1)S(1)}, bf16[192,128]{1,0:T(8,128)(2,1)S(...) custom-call(s32[50]{0:T(128)S(1)} %pad_add_fusion.ints_ref, ...), custom_call_target="tpu_custom_call" | custom-call | tf_op jit(solution)/shard_map/attend/pallas_call | solution.py:273
  22.4 3.1 %collective-permute-start.7 = (bf16[192,128]{1,0:T(8,128)(2,1)S(1)}, bf16[192,128]{1,0:T(8,128)(2,1)S(1)}, u32[]{:S(2)}, u32[]{:S(2)}) collective-permute-start(bf16[192,128]{1,0:T(8,128)(2,1)S(1)} %get-tuple-element.28), channel_id=1, source_target_pairs={{0,4},{1,5},{2,6},{3,7},{4,0},{5,1},{6,2},{7,3},{8,12},{9,13},{10,... | collective-permute-start | bytes 147464 | tf_op jit(solution)/shard_map/ppermute | solution.py:229
  25.5 0.3 collective-permute-start.8
  25.8 1.9 %collective-permute-start.9 = (bf16[192,128]{1,0:T(8,128)(2,1)S(1)}, bf16[192,128]{1,0:T(8,128)(2,1)S(1)}, u32[]{:S(2)}, u32[]{:S(2)}) collective-permute-start(bf16[192,128]{1,0:T(8,128)(2,1)S(1)} %get-tuple-element.30), channel_id=1, source_target_pairs={{0,5},{1,4},{2,7},{3,6},{4,1},{5,0},{6,3},{7,2},{8,13},{9,12},{10,... | collective-permute-start | bytes 147464 | tf_op jit(solution)/shard_map/ppermute | solution.py:229
  27.6 1.7 %collective-permute-start.10 = (bf16[192,128]{1,0:T(8,128)(2,1)S(1)}, bf16[192,128]{1,0:T(8,128)(2,1)S(1)}, u32[]{:S(2)}, u32[]{:S(2)}) collective-permute-start(bf16[192,128]{1,0:T(8,128)(2,1)S(1)} %get-tuple-element.31), channel_id=1, source_target_pairs={{0,6},{1,7},{2,4},{3,5},{4,2},{5,3},{6,0},{7,1},{8,14},{9,15},{10,... | collective-permute-start | bytes 147464 | tf_op jit(solution)/shard_map/ppermute | solution.py:229
  29.4 1.0 %collective-permute-start.11 = (bf16[192,128]{1,0:T(8,128)(2,1)S(1)}, bf16[192,128]{1,0:T(8,128)(2,1)S(1)}, u32[]{:S(2)}, u32[]{:S(2)}) collective-permute-start(bf16[192,128]{1,0:T(8,128)(2,1)S(1)} %get-tuple-element.32), channel_id=1, source_target_pairs={{0,3},{1,2},{2,1},{3,0},{4,7},{5,6},{6,5},{7,4},{8,11},{9,10},{10,... | collective-permute-start | bytes 147464 | tf_op jit(solution)/shard_map/ppermute | solution.py:229
  30.3 1.9 %collective-permute-start.12 = (bf16[192,128]{1,0:T(8,128)(2,1)S(1)}, bf16[192,128]{1,0:T(8,128)(2,1)S(1)}, u32[]{:S(2)}, u32[]{:S(2)}) collective-permute-start(bf16[192,128]{1,0:T(8,128)(2,1)S(1)} %get-tuple-element.33), channel_id=1, source_target_pairs={{0,1},{1,0},{2,3},{3,2},{4,5},{5,4},{6,7},{7,6},{8,9},{9,8},{10,11... | collective-permute-start | bytes 147464 | tf_op jit(solution)/shard_map/ppermute | solution.py:229
  32.2 0.4 collective-permute-done.8.refs_2_
  32.6 0.3 collective-permute-start.13
  32.9 1.1 %collective-permute-done.10.refs_4_ = bf16[192,128]{1,0:T(8,128)(2,1)S(1)} collective-permute-done((bf16[192,128]{1,0:T(8,128)(2,1)S(1)}, bf16[192,128]{1,0:T(8,128)(2,1)S(1)}, u32[]{:S(2)}, u32[]{:S(2)}) %collective-permute-start.10) | collective-permute-done | bytes 49184 | tf_op jit(solution)/shard_map/ppermute | solution.py:229
  34.0 0.9 %collective-permute-done.11.refs_5_ = bf16[192,128]{1,0:T(8,128)(2,1)S(1)} collective-permute-done((bf16[192,128]{1,0:T(8,128)(2,1)S(1)}, bf16[192,128]{1,0:T(8,128)(2,1)S(1)}, u32[]{:S(2)}, u32[]{:S(2)}) %collective-permute-start.11) | collective-permute-done | bytes 49184 | tf_op jit(solution)/shard_map/ppermute | solution.py:229
  34.9 1.8 %collective-permute-done.13.refs_7_ = bf16[192,128]{1,0:T(8,128)(2,1)S(1)} collective-permute-done((bf16[192,128]{1,0:T(8,128)(2,1)S(1)}, bf16[192,128]{1,0:T(8,128)(2,1)S(1)}, u32[]{:S(2)}, u32[]{:S(2)}) %collective-permute-start.13) | collective-permute-done | bytes 49184 | tf_op jit(solution)/shard_map/ppermute | solution.py:229
  36.7 0.9 %unpack.1 = (bf16[128,512]{1,0:T(8,128)(2,1)}, bf16[128,512]{1,0:T(8,128)(2,1)}, bf16[128,512]{1,0:T(8,128)(2,1)}) custom-call(bf16[192,128]{1,0:T(8,128)(2,1)S(1)} %get-tuple-element.27.refs_0_, bf16[192,128]{1,0:T(8,128)(2,1)S(1)} %collective-permute-done.7.refs_1_, bf16[192,128]{1,0:T(8,128)(2,1)S(1)} %collective-permute-done.8.refs_2_, ...), custom_call_target="tpu_custom_call" | custom-call | tf_op jit(solution)/shard_map/unpack/pallas_call | solution.py:291
  (14 shorter events, 0.2 us)
Async XLA Ops:
  2.0 11.2 %collective-permute-start = (bf16[2,128,128]{2,1,0:T(8,128)(2,1)S(1)}, bf16[2,128,128]{2,1,0:T(8,128)(2,1)S(1)}, u32[]{:S(2)}, u32[]{:S(2)}) collective-permute-start(bf16[2,128,128]{2,1,0:T(8,128)(2,1)S(1)} %get-tuple-element.20), channel_id=1, source_target_pairs={{0,4},{1,5},{2,6},{3,7},{4,0},{5,1},{6,2},{7,3},{8,12},{9,13},{10,... | collective-permute-start | bytes 196616 | tf_op jit(solution)/shard_map/ppermute | solution.py:229
  6.1 8.9 %collective-permute-start.1 = (bf16[2,128,128]{2,1,0:T(8,128)(2,1)S(1)}, bf16[2,128,128]{2,1,0:T(8,128)(2,1)S(1)}, u32[]{:S(2)}, u32[]{:S(2)}) collective-permute-start(bf16[2,128,128]{2,1,0:T(8,128)(2,1)S(1)} %get-tuple-element.21), channel_id=1, source_target_pairs={{0,7},{1,6},{2,5},{3,4},{4,3},{5,2},{6,1},{7,0},{8,15},{9,14},{10,... | collective-permute-start | bytes 196616 | tf_op jit(solution)/shard_map/ppermute | solution.py:229
  8.4 4.6 %copy-start = (s32[16,3]{0,1:T(4,128)S(1)}, s32[16,3]{0,1:T(4,128)}, u32[]{:S(2)}) copy-start(s32[16,3]{0,1:T(4,128)} %param.10) | copy-start | bytes 580
  8.4 8.2 %collective-permute-start.2 = (bf16[2,128,128]{2,1,0:T(8,128)(2,1)S(1)}, bf16[2,128,128]{2,1,0:T(8,128)(2,1)S(1)}, u32[]{:S(2)}, u32[]{:S(2)}) collective-permute-start(bf16[2,128,128]{2,1,0:T(8,128)(2,1)S(1)} %get-tuple-element.22), channel_id=1, source_target_pairs={{0,3},{1,2},{2,1},{3,0},{4,7},{5,6},{6,5},{7,4},{8,11},{9,10},{10,... | collective-permute-start | bytes 196616 | tf_op jit(solution)/shard_map/ppermute | solution.py:229
  8.6 8.7 %collective-permute-start.3 = (bf16[2,128,128]{2,1,0:T(8,128)(2,1)S(1)}, bf16[2,128,128]{2,1,0:T(8,128)(2,1)S(1)}, u32[]{:S(2)}, u32[]{:S(2)}) collective-permute-start(bf16[2,128,128]{2,1,0:T(8,128)(2,1)S(1)} %get-tuple-element.23), channel_id=1, source_target_pairs={{0,5},{1,4},{2,7},{3,6},{4,1},{5,0},{6,3},{7,2},{8,13},{9,12},{10,... | collective-permute-start | bytes 196616 | tf_op jit(solution)/shard_map/ppermute | solution.py:229
  12.3 5.0 %collective-permute-start.4 = (bf16[2,128,128]{2,1,0:T(8,128)(2,1)S(1)}, bf16[2,128,128]{2,1,0:T(8,128)(2,1)S(1)}, u32[]{:S(2)}, u32[]{:S(2)}) collective-permute-start(bf16[2,128,128]{2,1,0:T(8,128)(2,1)S(1)} %get-tuple-element.24), channel_id=1, source_target_pairs={{0,2},{1,3},{2,0},{3,1},{4,6},{5,7},{6,4},{7,5},{8,10},{9,11},{10,... | collective-permute-start | bytes 196616 | tf_op jit(solution)/shard_map/ppermute | solution.py:229
  13.2 3.4 %copy-start.1 = (s32[2]{0:T(128)S(1)}, s32[2]{0:T(128)}, u32[]{:S(2)}) copy-start(s32[2]{0:T(128)} %param.11) | copy-start | bytes 28
  13.2 6.1 %collective-permute-start.5 = (bf16[2,128,128]{2,1,0:T(8,128)(2,1)S(1)}, bf16[2,128,128]{2,1,0:T(8,128)(2,1)S(1)}, u32[]{:S(2)}, u32[]{:S(2)}) collective-permute-start(bf16[2,128,128]{2,1,0:T(8,128)(2,1)S(1)} %get-tuple-element.25), channel_id=1, source_target_pairs={{0,6},{1,7},{2,4},{3,5},{4,2},{5,3},{6,0},{7,1},{8,14},{9,15},{10,... | collective-permute-start | bytes 196616 | tf_op jit(solution)/shard_map/ppermute | solution.py:229
  15.0 4.3 %collective-permute-start.6 = (bf16[2,128,128]{2,1,0:T(8,128)(2,1)S(1)}, bf16[2,128,128]{2,1,0:T(8,128)(2,1)S(1)}, u32[]{:S(2)}, u32[]{:S(2)}) collective-permute-start(bf16[2,128,128]{2,1,0:T(8,128)(2,1)S(1)} %get-tuple-element.26), channel_id=1, source_target_pairs={{0,1},{1,0},{2,3},{3,2},{4,5},{5,4},{6,7},{7,6},{8,9},{9,8},{10,11... | collective-permute-start | bytes 196616 | tf_op jit(solution)/shard_map/ppermute | solution.py:229
  22.4 7.9 %collective-permute-start.7 = (bf16[192,128]{1,0:T(8,128)(2,1)S(1)}, bf16[192,128]{1,0:T(8,128)(2,1)S(1)}, u32[]{:S(2)}, u32[]{:S(2)}) collective-permute-start(bf16[192,128]{1,0:T(8,128)(2,1)S(1)} %get-tuple-element.28), channel_id=1, source_target_pairs={{0,4},{1,5},{2,6},{3,7},{4,0},{5,1},{6,2},{7,3},{8,12},{9,13},{10,... | collective-permute-start | bytes 147464 | tf_op jit(solution)/shard_map/ppermute | solution.py:229
  25.5 7.1 %collective-permute-start.8 = (bf16[192,128]{1,0:T(8,128)(2,1)S(1)}, bf16[192,128]{1,0:T(8,128)(2,1)S(1)}, u32[]{:S(2)}, u32[]{:S(2)}) collective-permute-start(bf16[192,128]{1,0:T(8,128)(2,1)S(1)} %get-tuple-element.29), channel_id=1, source_target_pairs={{0,7},{1,6},{2,5},{3,4},{4,3},{5,2},{6,1},{7,0},{8,15},{9,14},{10,... | collective-permute-start | bytes 147464 | tf_op jit(solution)/shard_map/ppermute | solution.py:229
  25.8 7.1 %collective-permute-start.9 = (bf16[192,128]{1,0:T(8,128)(2,1)S(1)}, bf16[192,128]{1,0:T(8,128)(2,1)S(1)}, u32[]{:S(2)}, u32[]{:S(2)}) collective-permute-start(bf16[192,128]{1,0:T(8,128)(2,1)S(1)} %get-tuple-element.30), channel_id=1, source_target_pairs={{0,5},{1,4},{2,7},{3,6},{4,1},{5,0},{6,3},{7,2},{8,13},{9,12},{10,... | collective-permute-start | bytes 147464 | tf_op jit(solution)/shard_map/ppermute | solution.py:229
  27.6 6.3 %collective-permute-start.10 = (bf16[192,128]{1,0:T(8,128)(2,1)S(1)}, bf16[192,128]{1,0:T(8,128)(2,1)S(1)}, u32[]{:S(2)}, u32[]{:S(2)}) collective-permute-start(bf16[192,128]{1,0:T(8,128)(2,1)S(1)} %get-tuple-element.31), channel_id=1, source_target_pairs={{0,6},{1,7},{2,4},{3,5},{4,2},{5,3},{6,0},{7,1},{8,14},{9,15},{10,... | collective-permute-start | bytes 147464 | tf_op jit(solution)/shard_map/ppermute | solution.py:229
  29.4 5.5 %collective-permute-start.11 = (bf16[192,128]{1,0:T(8,128)(2,1)S(1)}, bf16[192,128]{1,0:T(8,128)(2,1)S(1)}, u32[]{:S(2)}, u32[]{:S(2)}) collective-permute-start(bf16[192,128]{1,0:T(8,128)(2,1)S(1)} %get-tuple-element.32), channel_id=1, source_target_pairs={{0,3},{1,2},{2,1},{3,0},{4,7},{5,6},{6,5},{7,4},{8,11},{9,10},{10,... | collective-permute-start | bytes 147464 | tf_op jit(solution)/shard_map/ppermute | solution.py:229
  30.3 4.6 %collective-permute-start.12 = (bf16[192,128]{1,0:T(8,128)(2,1)S(1)}, bf16[192,128]{1,0:T(8,128)(2,1)S(1)}, u32[]{:S(2)}, u32[]{:S(2)}) collective-permute-start(bf16[192,128]{1,0:T(8,128)(2,1)S(1)} %get-tuple-element.33), channel_id=1, source_target_pairs={{0,1},{1,0},{2,3},{3,2},{4,5},{5,4},{6,7},{7,6},{8,9},{9,8},{10,11... | collective-permute-start | bytes 147464 | tf_op jit(solution)/shard_map/ppermute | solution.py:229
  32.6 4.1 %collective-permute-start.13 = (bf16[192,128]{1,0:T(8,128)(2,1)S(1)}, bf16[192,128]{1,0:T(8,128)(2,1)S(1)}, u32[]{:S(2)}, u32[]{:S(2)}) collective-permute-start(bf16[192,128]{1,0:T(8,128)(2,1)S(1)} %get-tuple-element.34), channel_id=1, source_target_pairs={{0,2},{1,3},{2,0},{3,1},{4,6},{5,7},{6,4},{7,5},{8,10},{9,11},{10,... | collective-permute-start | bytes 147464 | tf_op jit(solution)/shard_map/ppermute | solution.py:229
